TPU v7x, 32 devices: a whole 2x2x4 slice. The times are simulated.
32 devices in a mesh: group: 2 (over y), row: 8 (over z, x), epoch: 2 (over core).
Axes of the slice: x: 2, y: 2, z: 4, core: 2. Of those that a mesh axis runs over, the one named last changes fastest.
Arguments:
- images: bfloat16 [8, 2048, 2048], P(('group', 'epoch'), 'row'), parts along dimension 0, may hold values from -6 to 6
- rate_vectors: int32 [2, 2], replicated, may hold values from -192 to 192
- epoch_times: int32 [4], replicated, may hold values from 0 to 127
Outputs:
- rate_images: float32 [4, 2048, 2048], P(('group', 'epoch'), 'row'), parts along dimension 0
There are 2 independent parts, one for each index of `group`. A program takes and returns all parts, laid end to end along the dimension named above; an argument that names none is the same for every part. Nothing has to cross between parts.
All inputs are finite; a program needn't handle non-finite values.
Results may differ from a plain program's by a relative error of at most 0.011.
Values may be sent and summed in bfloat16 or wider, within the bound.
No kernel may reach another device: no remote copies, remote signals or barrier semaphores. Data moves between devices by JAX's collectives and lax.ppermute only.
A program may use at most 128 MiB of HBM per device.

v0:
```python
import math

import jax
import jax.numpy as jnp
from jax import lax
from jax.sharding import PartitionSpec as P

SUBPIX = 16


def dft_tables(length):
    positions = jnp.arange(length, dtype=jnp.int32)
    turn_count = positions[:, None] * positions[None, :] % length
    angles = turn_count.astype(jnp.float32) * (2.0 * math.pi / length)
    factor = 1.0 / math.sqrt(length)
    return (
        (jnp.cos(angles) * factor).astype(jnp.bfloat16),
        (jnp.sin(angles) * factor).astype(jnp.bfloat16),
    )


def ramp_sums(spectrum, freq_rows, freq_cols, rate_vectors, time_steps, length):
    period = SUBPIX * length
    real_part = spectrum[:, 0].astype(jnp.float32)
    imag_part = spectrum[:, 1].astype(jnp.float32)

    def one_rate(rate_row):
        shift_y = rate_row[0] * time_steps % period
        shift_x = rate_row[1] * time_steps % period
        row_turns = shift_y[:, None] * freq_rows[None, :] % period
        col_turns = freq_cols[:, None] * shift_x[None, :] % period
        row_angles = row_turns.astype(jnp.float32) * (2.0 * math.pi / period)
        col_angles = col_turns.astype(jnp.float32) * (2.0 * math.pi / period)
        row_cos = jnp.cos(row_angles)[None]
        row_sin = jnp.sin(row_angles)[None]
        col_cos = jnp.cos(col_angles)[:, :, None]
        col_sin = jnp.sin(col_angles)[:, :, None]
        ramp_re = col_cos * row_cos - col_sin * row_sin
        ramp_im = col_sin * row_cos + col_cos * row_sin
        summed_re = jnp.sum(real_part * ramp_re - imag_part * ramp_im, axis=1)
        summed_im = jnp.sum(real_part * ramp_im + imag_part * ramp_re, axis=1)
        return jnp.stack([summed_re, summed_im], axis=1)

    return lax.map(one_rate, rate_vectors)


def local(images, rate_vectors, epoch_times):
    loc_epochs, loc_rows, length = images.shape
    row_count = lax.axis_size("row")
    epoch_count = lax.axis_size("epoch")
    row_pos = lax.axis_index("row")
    epoch_pos = lax.axis_index("epoch")
    loc_cols = length // row_count
    cosine, sine = dft_tables(length)
    stacked = jnp.stack([cosine, sine])
    stack_scale = 1.0 / math.sqrt(epoch_times.shape[0])
    sign_wide = jnp.array([1.0, -1.0], jnp.float32)[:, None]
    sign_narrow = jnp.array([1.0, -1.0], jnp.bfloat16)[:, None]
    row_terms = jnp.einsum("tcv,elc->vetl", stacked, images, preferred_element_type=jnp.float32)
    row_spectrum = (row_terms * sign_wide).astype(jnp.bfloat16)
    narrow = loc_cols // epoch_count
    gathered = lax.all_to_all(
        lax.all_to_all(row_spectrum, "row", split_axis=0, concat_axis=3, tiled=True),
        "epoch",
        split_axis=0,
        concat_axis=1,
        tiled=True,
    )
    products = jnp.einsum("vetr,wru->wvteu", gathered, stacked, preferred_element_type=jnp.float32)
    real_part = products[0, :, 0] + products[1, :, 1]
    imag_part = products[0, :, 1] - products[1, :, 0]
    spectra = jnp.stack([real_part, imag_part], axis=1).astype(jnp.bfloat16)
    freq_cols = row_pos * loc_cols + epoch_pos * narrow + jnp.arange(narrow, dtype=jnp.int32)
    freq_rows = jnp.arange(length, dtype=jnp.int32)
    rate_sums = ramp_sums(spectra, freq_rows, freq_cols, rate_vectors, epoch_times, length)
    rate_spectrum = (rate_sums * stack_scale).astype(jnp.bfloat16)
    products = jnp.einsum(
        "kvtu,wur->wkrtv", rate_spectrum, stacked, preferred_element_type=jnp.float32
    )
    real_part = products[0, :, :, 0] - products[1, :, :, 1]
    imag_part = products[0, :, :, 1] + products[1, :, :, 0]
    columns_back = jnp.stack([real_part, imag_part], axis=2).astype(jnp.bfloat16)
    returned = lax.all_to_all(
        lax.all_to_all(columns_back, "row", split_axis=1, concat_axis=3, tiled=True),
        "epoch",
        split_axis=0,
        concat_axis=3,
        tiled=True,
    )
    signed = returned * sign_narrow
    reshaped = signed.reshape(signed.shape[0], signed.shape[1], 2, epoch_count, row_count, narrow)
    inverse_table = stacked.reshape(2, row_count, epoch_count, narrow, length)
    result_rows = jnp.einsum(
        "krtjiw,tijwc->krc", reshaped, inverse_table, preferred_element_type=jnp.float32
    )
    return result_rows


def solution(mesh):
    in_specs = (P(("group", "epoch"), "row", None), P(), P())
    out_specs = P(("group", "epoch"), "row", None)
    return jax.shard_map(local, mesh=mesh, in_specs=in_specs, out_specs=out_specs, check_vma=False)
```

profile of v0, /device:TPU:0, one launch (start us, length us, event | category | flops | bytes accessed | tf_op | source)
XLA Modules:
  0.0 449.5 jit_solution(12149800663286219467)
XLA Ops:
  0.0 0.0 copy-start
  0.0 68.6 %multiply_convert_fusion.2 = (bf16[1,2048,2048]{1,2,0:T(8,128)(2,1)S(1)}, bf16[1,2048,2048]{1,2,0:T(8,128)(2,1)}) fusion(), kind=kLoop, calls=%fused_computation.64 | loop fusion | flops 75497472 | bytes 16777216 | tf_op jit(solution)/shard_map/convert_element_type | solution.py:18
  68.6 0.0 copy-done
  68.6 0.0 copy-done.7
  68.6 14.7 %fusion.49 = bf16[2048,2,2,256]{3,0,1,2:T(8,128)(2,1)S(1)} fusion(f32[2]{0:T(128)S(1)} %copy-done.7, bf16[1,2048,2048]{1,2,0:T(8,128)(2,1)S(1)} %get-tuple-element.189, bf16[1,2048,2048]{1,2,0:T(8,128)(2,1)} %get-tuple-element.190, bf16[2,256,2048]{2,1,0:T(8,128)(2,1)S(1)} %copy-done), kind=kOutput, calls=%fused_computation.78 | convolution fusion | flops 8627683328 | bytes 23068680 | tf_op jit(solution)/shard_map/tcv,elc->vetl/dot_general | solution.py:59
  83.3 0.0 copy-done.2
  83.3 19.1 %copy.52 = bf16[2048,2,2,256]{3,1,2,0:T(2,128)(2,1)} copy(bf16[2048,2,2,256]{3,0,1,2:T(8,128)(2,1)S(1)} %fusion.49) | data formatting | bytes 8388608 | tf_op jit(solution)/shard_map/convert_element_type | solution.py:60
  102.4 7.3 %all-to-all-start = ((bf16[2048,2,2,256]{3,1,2,0:T(2,128)(2,1)}), bf16[2048,2,2,256]{3,1,2,0:T(2,128)(2,1)}, u32[]{:S(2)}, u32[]{:S(2)}) async-start(bf16[2048,2,2,256]{3,1,2,0:T(2,128)(2,1)} %copy.52), calls=%async_computation | async-start | bytes 8388608 | tf_op jit(solution)/shard_map/all_to_all | solution.py:63
  109.7 93.3 %all-to-all-done = bf16[2048,2,2,256]{3,1,2,0:T(2,128)(2,1)} async-done(((bf16[2048,2,2,256]{3,1,2,0:T(2,128)(2,1)}), bf16[2048,2,2,256]{3,1,2,0:T(2,128)(2,1)}, u32[]{:S(2)}, u32[]{:S(2)}) %all-to-all-start) | async-done | bytes 4194336 | tf_op jit(solution)/shard_map/all_to_all | solution.py:63
  203.0 4.7 %copy.53 = bf16[2048,2,2,256]{3,0,2,1:T(8,128)(2,1)} copy(bf16[2048,2,2,256]{3,1,2,0:T(2,128)(2,1)} %all-to-all-done) | data formatting | bytes 8388608 | tf_op jit(solution)/shard_map/all_to_all | solution.py:63
  207.7 6.2 %copy.54 = bf16[256,2,2,8,256]{0,4,3,2,1:T(8,128)(2,1)} copy(bf16[256,2,2,8,256]{4,0,3,2,1:T(8,128)(2,1)} %bitcast.97) | data formatting | bytes 8388608 | tf_op jit(solution)/shard_map/all_to_all | solution.py:63
  213.9 11.2 %copy.55 = bf16[256,2,2,2048]{3,2,1,0:T(2,128)(2,1)} copy(bf16[256,2,2,2048]{0,3,2,1:T(8,128)(2,1)} %bitcast.98) | data formatting | bytes 8388608 | tf_op jit(solution)/shard_map/all_to_all | solution.py:63
  225.1 8.9 %all_to_all.72 = bf16[256,2,2,2048]{3,2,1,0:T(2,128)(2,1)S(1)} all-to-all(bf16[256,2,2,2048]{3,2,1,0:T(2,128)(2,1)} %copy.55), channel_id=1, replica_groups=mesh['group'=2,'row'=8,'epoch'=2] {'epoch'}, dimensions={0} | all-to-all | bytes 8388608 | tf_op jit(solution)/shard_map/all_to_all | solution.py:62
  234.0 2.3 copy.56
  236.3 0.0 slice-start.1
  236.4 2.5 copy.57
  238.8 0.0 slice-done.2
  238.8 0.0 slice-done.3
  238.8 1.6 slice-done.1
  240.4 22.7 %fusion.39 = f32[2,128,2,4,2048]{1,4,2,3,0:T(8,128)} fusion(bf16[128,4,2,2048,1]{3,0,2,1,4:T(8,128)(2,1)} %bitcast.107, bf16[1,2048,2048]{1,2,0:T(8,128)(2,1)S(1)} %bitcast.101, bf16[1,2048,2048]{1,2,0:T(8,128)(2,1)S(1)} %bitcast.103), kind=kOutput, calls=%fused_computation.71 | convolution fusion | flops 17213423616 | bytes 37748736 | tf_op jit(solution)/shard_map/vetr,wru->wvteu/dot_general | solution.py:69
  263.2 9.9 %fusion.58 = (f32[128,4,2048]{0,2,1:T(8,128)}, f32[128,4,2048]{0,2,1:T(8,128)}) fusion(f32[2,128,2,4,2048]{1,4,2,3,0:T(8,128)} %fusion.39), kind=kLoop, calls=%fused_computation.83 | loop fusion | flops 6291456 | bytes 25165824 | tf_op jit(solution)/shard_map/convert_element_type | solution.py:25
  273.1 5.5 %copy.58 = f32[128,4,2048]{2,1,0:T(4,128)} copy(f32[128,4,2048]{0,2,1:T(8,128)} %get-tuple-element.186) | data formatting | bytes 8388608
  278.6 5.5 %copy.59 = f32[128,4,2048]{2,1,0:T(4,128)} copy(f32[128,4,2048]{0,2,1:T(8,128)} %get-tuple-element.185) | data formatting | bytes 8388608
  284.1 0.0 copy-done.4
  284.1 39.6 %while.13 = (s32[]{:T(128)}, f32[2,128,2,2048]{3,2,1,0:T(2,128)}, s32[2,2]{1,0:T(2,128)S(1)}, s32[4]{0:T(128)S(1)}, f32[128,4,2048]{2,1,0:T(4,128)}, /*index=5*/f32[128,4,2048]{2,1,0:T(4,128)}, s32[]{:T(128)}, s32[]{:T(128)}) while((s32[]{:T(128)}, f32[2,128,2,2048]{3,2,1,0:T(2,128)}, s32[2,2]{1,0:T(2,128)S(1)}, s32[4]{0:T(128)S(1)}, ...), condition=%wide.region_3.4_spmd.clone, body=%wide.region_0.3_spmd.clone.sunk | while | flops 14802146 | bytes 19023572 | solution.py:44
  284.3 0.6 fusion.78
  284.9 1.2 and_select_fusion.3
  286.1 0.1 fusion.80
  286.2 0.1 copy.83
  286.3 0.1 copy.84
  286.4 0.3 fusion.79
  286.8 12.4 %subtract_reduce_fusion.2 = (f32[128,2048]{1,0:T(8,128)S(1)}, f32[128,2048]{1,0:T(8,128)S(1)}) fusion(f32[128,4,2048]{2,1,0:T(4,128)} %get-tuple-element.275, f32[128,4,2048]{2,1,0:T(4,128)} %get-tuple-element.274, f32[4,2048]{1,0:T(4,128)S(1)} %get-tuple-element.247, f32[128,4]{1,0:T(8,128)S(1)} %copy.83, f32[4,2048]{1,0:T(4,128)S(1)} %get-tuple-element.250, ...), kind=kLoop, calls=%fused_computation.3.clone.1 | loop fusion | flops 14155776 | bytes 10555392 | tf_op jit(solution)/shard_map/while/body/eval_jaxpr/reduce_sum | solution.py:40
  299.2 0.7 stack.43
  300.0 0.7 stack.44
  300.7 3.2 fusion.81
  303.9 0.6 fusion.78
  304.5 1.2 and_select_fusion.3
  305.7 0.1 fusion.80
  305.8 0.1 copy.83
  306.0 0.1 copy.84
  306.1 0.3 fusion.79
  306.4 12.4 %subtract_reduce_fusion.2 = (f32[128,2048]{1,0:T(8,128)S(1)}, f32[128,2048]{1,0:T(8,128)S(1)}) fusion(f32[128,4,2048]{2,1,0:T(4,128)} %get-tuple-element.275, f32[128,4,2048]{2,1,0:T(4,128)} %get-tuple-element.274, f32[4,2048]{1,0:T(4,128)S(1)} %get-tuple-element.247, f32[128,4]{1,0:T(8,128)S(1)} %copy.83, f32[4,2048]{1,0:T(4,128)S(1)} %get-tuple-element.250, ...), kind=kLoop, calls=%fused_computation.3.clone.1 | loop fusion | flops 14155776 | bytes 10555392 | tf_op jit(solution)/shard_map/while/body/eval_jaxpr/reduce_sum | solution.py:40
  318.9 0.7 stack.43
  319.6 0.7 stack.44
  320.3 3.3 fusion.81
  323.6 4.3 multiply_convert_fusion.5
  328.0 12.9 %fusion.44 = f32[2,2,2048,2,128]{4,2,3,1,0:T(8,128)S(1)} fusion(bf16[1,2048,2048]{1,2,0:T(8,128)(2,1)} %copy-done.2, bf16[1,2048,2048]{1,2,0:T(8,128)(2,1)} %get-tuple-element.190, bf16[2,128,2,2048]{3,2,1,0:T(2,128)(2,1)S(1)} %multiply_convert_fusion.5), kind=kOutput, calls=%fused_computation.72 | convolution fusion | flops 8623489024 | bytes 27262976 | tf_op jit(solution)/shard_map/kvtu,wur->wkrtv/dot_general | solution.py:77
  340.8 0.2 fusion.66
  341.1 0.2 fusion.67
  341.3 0.2 pad_maximum_fusion.4
  341.5 14.0 %copy.63 = bf16[2,2048,2,128]{3,0,2,1:T(2,128)(2,1)} copy(bf16[2,2048,2,128]{3,1,0,2:T(8,128)(2,1)S(1)} %pad_maximum_fusion.4) | data formatting | bytes 4194304 | tf_op jit(solution)/shard_map/stack | solution.py:82
  355.5 3.6 all-to-all-start.2
  359.1 71.3 %multiply_convert_fusion.1 = (bf16[1,8,2,128,2048]{4,3,0,2,1:T(8,128)(2,1)}, bf16[1,8,2,128,2048]{4,3,0,2,1:T(8,128)(2,1)}) fusion(s32[8,2,128]{2,1,0:T(2,128)S(1)} %multiply_add_fusion.1), kind=kLoop, calls=%fused_computation.61 | loop fusion | flops 75497472 | bytes 16785408 | tf_op jit(solution)/shard_map/convert_element_type | solution.py:17
  430.4 0.0 all-to-all-done.2
  430.4 1.6 copy.64
  432.0 2.9 copy.65
  434.8 0.0 copy-start.3
  434.8 0.0 copy-start.6
  434.8 5.8 %all_to_all.73 = bf16[2,256,2,1024]{1,3,2,0:T(8,128)(2,1)S(1)} all-to-all(bf16[2,256,2,1024]{1,3,2,0:T(8,128)(2,1)S(1)} %bitcast.105), channel_id=1, replica_groups=mesh['group'=2,'row'=8,'epoch'=2] {'epoch'}, dimensions={0} | all-to-all | bytes 4194304 | tf_op jit(solution)/shard_map/all_to_all | solution.py:83
  440.7 0.1 copy.66
  440.8 0.0 copy-done.3
  440.8 0.0 copy-done.6
  440.8 0.0 copy-start.1
  440.8 8.3 %fusion.52 = f32[1,256,2048]{2,1,0:T(8,128)} fusion(bf16[1,8,2,128,2048]{4,3,0,2,1:T(8,128)(2,1)} %get-tuple-element.188, bf16[1,8,2,128,2048]{4,3,0,2,1:T(8,128)(2,1)S(1)} %copy-done.3, bf16[256,2,2,8,128]{0,4,3,2,1:T(8,128)(2,1)S(1)} %bitcast.108, bf16[2]{0:T(256)(128)(2,1)S(1)} %copy-done.6), kind=kOutput, calls=%fused_computation.79 | convolution fusion | flops 4304404480 | bytes 20971524 | tf_op jit(solution)/shard_map/krtjiw,tijwc->krc/dot_general | solution.py:93
  (18 shorter events, 0.0 us)
Async XLA Ops:
  0.0 68.6 %copy-start = (bf16[2,256,2048]{2,1,0:T(8,128)(2,1)S(1)}, bf16[2,256,2048]{2,1,0:T(8,128)(2,1)}, u32[]{:S(2)}) copy-start(bf16[2,256,2048]{2,1,0:T(8,128)(2,1)} %param.7) | copy-start | bytes 6291460
  0.0 68.6 %copy-start.7 = (f32[2]{0:T(128)S(1)}, f32[2]{0:T(128)}, u32[]{:S(2)}) copy-start(f32[2]{0:T(128)} %constant.114.clone) | copy-start | bytes 28
  68.6 14.7 %copy-start.2 = (bf16[1,2048,2048]{1,2,0:T(8,128)(2,1)}, bf16[1,2048,2048]{1,2,0:T(8,128)(2,1)S(1)}, u32[]{:S(2)}) copy-start(bf16[1,2048,2048]{1,2,0:T(8,128)(2,1)S(1)} %get-tuple-element.189) | copy-start | bytes 25165828
  102.4 100.5 %all-to-all-start = ((bf16[2048,2,2,256]{3,1,2,0:T(2,128)(2,1)}), bf16[2048,2,2,256]{3,1,2,0:T(2,128)(2,1)}, u32[]{:S(2)}, u32[]{:S(2)}) async-start(bf16[2048,2,2,256]{3,1,2,0:T(2,128)(2,1)} %copy.52), calls=%async_computation | async-start | bytes 8388608 | tf_op jit(solution)/shard_map/all_to_all | solution.py:63
  225.1 13.7 %slice-start.2 = ((s8[8388608]{0:T(1024)(128)(4,1)}), s8[4194304]{0:T(1024)(128)(4,1)S(1)}, s32[]{:S(2)}) async-start(s8[8388608]{0:T(1024)(128)(4,1)} %bitcast.102), calls=%async_computation.6 | async-start | bytes 8388608
  234.0 4.8 %slice-start = ((s8[8388608]{0:T(1024)(128)(4,1)}), s8[4194304]{0:T(1024)(128)(4,1)S(1)}, s32[]{:S(2)}) async-start(s8[8388608]{0:T(1024)(128)(4,1)} %bitcast.100), calls=%async_computation.4 | async-start | bytes 8388608
  234.0 4.8 %slice-start.3 = ((s8[8388608]{0:T(1024)(128)(4,1)}), s8[4194304]{0:T(1024)(128)(4,1)S(1)}, s32[]{:S(2)}) async-start(s8[8388608]{0:T(1024)(128)(4,1)} %bitcast.102), calls=%async_computation.7 | async-start | bytes 8388608
  236.3 4.1 slice-start.1
  278.5 5.5 %copy-start.4 = (s32[4]{0:T(128)S(1)}, s32[4]{0:T(128)}, u32[]{:S(2)}) copy-start(s32[4]{0:T(128)} %param.9) | copy-start | bytes 52
  278.5 5.5 %copy-start.5 = (s32[2,2]{1,0:T(2,128)S(1)}, s32[2,2]{1,0:T(2,128)}, u32[]{:S(2)}) copy-start(s32[2,2]{1,0:T(2,128)} %param.8) | copy-start | bytes 52
  355.5 74.9 %all-to-all-start.2 = ((bf16[2,2048,2,128]{3,0,2,1:T(2,128)(2,1)}), bf16[2,2048,2,128]{3,0,2,1:T(2,128)(2,1)S(1)}, u32[]{:S(2)}, u32[]{:S(2)}) async-start(bf16[2,2048,2,128]{3,0,2,1:T(2,128)(2,1)} %copy.63), calls=%async_computation.2 | async-start | bytes 4194304 | tf_op jit(solution)/shard_map/all_to_all | solution.py:84
  434.8 6.0 %copy-start.3 = (bf16[1,8,2,128,2048]{4,3,0,2,1:T(8,128)(2,1)S(1)}, bf16[1,8,2,128,2048]{4,3,0,2,1:T(8,128)(2,1)}, u32[]{:S(2)}) copy-start(bf16[1,8,2,128,2048]{4,3,0,2,1:T(8,128)(2,1)} %get-tuple-element.187) | copy-start | bytes 25165828
  434.8 6.0 %copy-start.6 = (bf16[2]{0:T(256)(128)(2,1)S(1)}, bf16[2]{0:T(256)(128)(2,1)}, u32[]{:S(2)}) copy-start(bf16[2]{0:T(256)(128)(2,1)} %constant.115.clone) | copy-start | bytes 16
  440.8 8.3 %copy-start.1 = (bf16[2,256,2048]{2,1,0:T(8,128)(2,1)S(1)}, bf16[2,256,2048]{2,1,0:T(8,128)(2,1)}, u32[]{:S(2)}) copy-start(bf16[2,256,2048]{2,1,0:T(8,128)(2,1)} %param.7) | copy-start | bytes 6291460
where the time goes:
time: 458 us; the launch traced here: 450 us
  other arithmetic  189 us (41%)
  waiting for transfers between devices  93.3 us (20%)
  local copies, waits for them, and re-layouts  81.8 us (18%)
  matrix products  58.5 us (13%)
  blocking collectives  14.7 us (3%)
  starting transfers between devices  10.9 us (2%)
    all_to_all x1, waiting for transfers between devices, local(): lax.all_to_all(row_spectrum, 'row', split_axis=0, concat_axis=3, tiled=True)  93.3 us
    convert_element_type x1, other arithmetic, dft_tables(): (jnp.cos(angles) * factor).astype(jnp.bfloat16)  71.3 us
    convert_element_type x1, other arithmetic, dft_tables(): (jnp.sin(angles) * factor).astype(jnp.bfloat16)  68.6 us
    reduce_sum x2, other arithmetic, one_rate(): summed_re = jnp.sum(real_part * ramp_re - imag_part * ramp_im, axis=1)  24.9 us
    dot_general x1, matrix products, local(): jnp.einsum('vetr,wru->wvteu', gathered, stacked, preferred_element_type=j...  22.7 us
    all_to_all x3, local copies, waits for them, and re-layouts, local(): lax.all_to_all(row_spectrum, 'row', split_axis=0, concat_axis=3, tiled=True)  22.2 us
    convert_element_type x1, local copies, waits for them, and re-layouts, local(): row_spectrum = (row_terms * sign_wide).astype(jnp.bfloat16)  19.1 us
    dot_general x1, matrix products, local(): jnp.einsum('tcv,elc->vetl', stacked, images, preferred_element_type=jnp.f...  14.7 us
  transfers between devices with their start and end apart: 2, of which 1 were waited for; matrix products, arithmetic and copies ran while one was open for 16% of the time, Pallas kernels for 0%

commit v1 on v0

v1 whole, which is shorter than its diff:
```python
import functools
import math

import jax
import jax.numpy as jnp
import ml_dtypes
import numpy as np
from jax import lax
from jax.experimental import pallas as pl
from jax.experimental.pallas import tpu as pltpu
from jax.sharding import PartitionSpec as P

SUBPIX = 16
BLOCK = 256
VMEM_LIMIT = 56 * 1024 * 1024


def packed_table(length, cols):
    half = length // 2
    freqs = np.arange(half, dtype=np.int32)
    positions = np.arange(length, dtype=np.int32)
    turns = freqs[:, None] * positions[None, :] % length
    angles = turns.astype(np.float32) * np.float32(2.0 * math.pi / length)
    factor = np.float32(1.0 / math.sqrt(length))
    cosine = np.cos(angles) * factor
    sine = np.sin(angles) * factor
    sine[0] = np.where(positions % 2 == 0, factor, -factor)
    blocks = np.stack([cosine.reshape(-1, cols, length), sine.reshape(-1, cols, length)], axis=1)
    return blocks.reshape(length, length).astype(ml_dtypes.bfloat16)


def row_kernel(images_ref, table_ref, out_ref):
    loc_epochs, loc_rows, length = images_ref.shape
    dests, _, _, width = out_ref.shape
    pixels = images_ref[...].reshape(loc_epochs * loc_rows, length)
    terms = jnp.dot(pixels, table_ref[...], preferred_element_type=jnp.float32)
    terms = terms.astype(jnp.bfloat16)
    for dest in range(dests):
        part = terms[:, dest * width : (dest + 1) * width]
        out_ref[dest] = part.reshape(loc_epochs, loc_rows, width)


def row_transform(images, table_t, devices, width):
    loc_epochs, loc_rows, length = images.shape
    dests = BLOCK // width
    return pl.pallas_call(
        row_kernel,
        grid=(length // BLOCK,),
        in_specs=[
            pl.BlockSpec((loc_epochs, loc_rows, length), lambda i: (0, 0, 0)),
            pl.BlockSpec((length, BLOCK), lambda i: (0, i)),
        ],
        out_specs=pl.BlockSpec((dests, loc_epochs, loc_rows, width), lambda i: (i, 0, 0, 0)),
        out_shape=jax.ShapeDtypeStruct((devices, loc_epochs, loc_rows, width), jnp.bfloat16),
        compiler_params=pltpu.CompilerParams(vmem_limit_bytes=VMEM_LIMIT),
        cost_estimate=pl.CostEstimate(
            flops=2 * loc_epochs * loc_rows * length * length,
            bytes_accessed=2 * length * length + 4 * loc_epochs * loc_rows * length,
            transcendentals=0,
        ),
        name="row_transform",
    )(images, table_t)


def swap_halves(values):
    width = values.shape[1]
    if width % 128 == 0:
        return pltpu.roll(values, width // 2, axis=1)
    return jnp.concatenate([values[:, width // 2 :], values[:, : width // 2]], axis=1)


def column_kernel(
    epoch_count, rates, z_ref, table_ref, table_t_ref, coef_ref, lane_ref, out_ref, z_all, sums
):
    devices, loc_epochs, loc_rows, width = z_ref.shape
    row_count = devices // epoch_count
    epochs = epoch_count * loc_epochs
    cols = width // 2
    half_steps = pl.num_programs(0) // 2
    step = pl.program_id(0)
    pairs = rates * epochs

    @pl.when(step == 0)
    def _():
        for row in range(row_count):
            parts = [
                z_ref[row * epoch_count + core, loc]
                for core in range(epoch_count)
                for loc in range(loc_epochs)
            ]
            z_all[row * loc_rows : (row + 1) * loc_rows, :] = jnp.concatenate(parts, axis=1)

    @pl.when(step < half_steps)
    def _():
        products = jnp.dot(table_ref[...], z_all[...], preferred_element_type=jnp.float32)
        groups = BLOCK // width
        products = products.reshape(groups, 2, cols, epochs * width)
        even = products[:, 0].reshape(groups * cols, epochs * width)
        odd = products[:, 1].reshape(groups * cols, epochs * width)
        first = (step == 0) & (lax.broadcasted_iota(jnp.int32, (groups * cols, width), 0) == 0)
        results = []
        for rate in range(rates):
            straight = [0.0, 0.0]
            crossed = [0.0, 0.0]
            lead = [0.0, 0.0]
            for epoch in range(epochs):
                pair = rate * epochs + epoch
                even_part = even[:, epoch * width : (epoch + 1) * width]
                odd_part = odd[:, epoch * width : (epoch + 1) * width]
                cos_row = coef_ref[:, pair : pair + 1]
                sin_row = coef_ref[:, pairs + pair : pairs + pair + 1]
                turned = (
                    cos_row * even_part + sin_row * odd_part,
                    cos_row * odd_part - sin_row * even_part,
                )
                for which in range(2):
                    straight[which] += turned[which] * lane_ref[pair : pair + 1, :]
                    crossed[which] += turned[which] * lane_ref[pairs + pair : pairs + pair + 1, :]
                lead[0] += even_part[:8] * lane_ref[2 * pairs + pair : 2 * pairs + pair + 1, :]
                lead[1] += even_part[:8] * lane_ref[3 * pairs + pair : 3 * pairs + pair + 1, :]
            even_sum = straight[0] + swap_halves(crossed[0])
            odd_sum = straight[1] + swap_halves(crossed[1])
            lead_sum = lead[0] + swap_halves(lead[1])
            even_sum = jnp.where(first, lead_sum[0:1], even_sum)
            both = jnp.stack(
                [even_sum.reshape(groups, cols, width), odd_sum.reshape(groups, cols, width)], axis=1
            )
            results.append(both.reshape(BLOCK, width))
        start = pl.multiple_of(step * BLOCK, BLOCK)
        sums[pl.ds(start, BLOCK), :] = jnp.concatenate(results, axis=1).astype(jnp.bfloat16)

    @pl.when(step >= half_steps)
    def _():
        back = jnp.dot(table_t_ref[...], sums[...], preferred_element_type=jnp.float32)
        back = back.astype(jnp.bfloat16)
        dests, loc_rates = out_ref.shape[:2]
        for row in range(dests // epoch_count):
            for rate in range(rates):
                part = back[row * loc_rows : (row + 1) * loc_rows, rate * width : (rate + 1) * width]
                out_ref[row * epoch_count + rate // loc_rates, rate % loc_rates] = part


def column_stage(spectra, table, table_t, coefs, lanes, epoch_count, rates):
    devices, loc_epochs, loc_rows, width = spectra.shape
    length = table.shape[0]
    epochs = epoch_count * loc_epochs
    steps = length // BLOCK
    dests = BLOCK // loc_rows * epoch_count
    loc_rates = rates // epoch_count
    half_block = BLOCK // 2
    return pl.pallas_call(
        functools.partial(column_kernel, epoch_count, rates),
        grid=(2 * steps,),
        in_specs=[
            pl.BlockSpec(spectra.shape, lambda i: (0, 0, 0, 0)),
            pl.BlockSpec((BLOCK, length), lambda i: (jnp.minimum(i, steps - 1), 0)),
            pl.BlockSpec((BLOCK, length), lambda i: (jnp.maximum(i - steps, 0), 0)),
            pl.BlockSpec((half_block, coefs.shape[1]), lambda i: (jnp.minimum(i, steps - 1), 0)),
            pl.BlockSpec(lanes.shape, lambda i: (0, 0)),
        ],
        out_specs=pl.BlockSpec(
            (dests, loc_rates, loc_rows, width), lambda i: (jnp.maximum(i - steps, 0), 0, 0, 0)
        ),
        out_shape=jax.ShapeDtypeStruct((devices, loc_rates, loc_rows, width), jnp.bfloat16),
        scratch_shapes=[
            pltpu.VMEM((length, epochs * width), jnp.bfloat16),
            pltpu.VMEM((length, rates * width), jnp.bfloat16),
        ],
        compiler_params=pltpu.CompilerParams(vmem_limit_bytes=VMEM_LIMIT),
        cost_estimate=pl.CostEstimate(
            flops=2 * length * length * (epochs + rates) * width,
            bytes_accessed=4 * length * length,
            transcendentals=0,
        ),
        name="column_stage",
    )(spectra, table, table_t, coefs, lanes)


def image_kernel(back_ref, table_ref, out_ref, left):
    devices, loc_rates, loc_rows, width = back_ref.shape
    length = devices * width

    @pl.when(pl.program_id(0) == 0)
    def _():
        per_tile = 128 // width
        for rate in range(loc_rates):
            for tile in range(length // 128):
                parts = [back_ref[tile * per_tile + part, rate] for part in range(per_tile)]
                whole = parts[0] if per_tile == 1 else jnp.concatenate(parts, axis=1)
                left[rate * loc_rows : (rate + 1) * loc_rows, tile * 128 : (tile + 1) * 128] = whole

    pixels = jnp.dot(left[...], table_ref[...], preferred_element_type=jnp.float32)
    out_ref[...] = pixels.reshape(out_ref.shape)


def image_rows(back, table):
    devices, loc_rates, loc_rows, width = back.shape
    length = table.shape[0]
    return pl.pallas_call(
        image_kernel,
        grid=(length // BLOCK,),
        in_specs=[
            pl.BlockSpec(back.shape, lambda i: (0, 0, 0, 0)),
            pl.BlockSpec((length, BLOCK), lambda i: (0, i)),
        ],
        out_specs=pl.BlockSpec((loc_rates, loc_rows, BLOCK), lambda i: (0, 0, i)),
        out_shape=jax.ShapeDtypeStruct((loc_rates, loc_rows, length), jnp.float32),
        scratch_shapes=[pltpu.VMEM((loc_rates * loc_rows, length), jnp.bfloat16)],
        compiler_params=pltpu.CompilerParams(vmem_limit_bytes=VMEM_LIMIT),
        cost_estimate=pl.CostEstimate(
            flops=2 * loc_rates * loc_rows * length * length,
            bytes_accessed=2 * length * length + 6 * loc_rates * loc_rows * length,
            transcendentals=0,
        ),
        name="image_rows",
    )(back, table)


def ramp_factors(rate_vectors, epoch_times, device, cols, length):
    period = SUBPIX * length
    half = length // 2
    rates, epochs = rate_vectors.shape[0], epoch_times.shape[0]
    shift_y = (rate_vectors[:, 0:1] * epoch_times[None, :] % period).reshape(-1, 1)
    shift_x = (rate_vectors[:, 1:2] * epoch_times[None, :] % period).reshape(-1, 1)

    def angle(turns, whole):
        return (turns % whole).astype(jnp.float32) * (2.0 * math.pi / whole)

    freq_rows = jnp.arange(half, dtype=jnp.int32)[None, :]
    row_angle = angle(shift_y * (freq_rows - half), period)
    coefs = jnp.concatenate(
        [
            jnp.where(freq_rows == 0, 1.0, 2.0 * jnp.cos(row_angle)),
            jnp.where(freq_rows == 0, 0.0, 2.0 * jnp.sin(row_angle)),
        ]
    ).T
    lane = jnp.arange(2 * cols, dtype=jnp.int32)[None, :]
    freq_cols = device * cols + lane % cols
    is_sine = lane >= cols
    zero_col = (freq_cols == 0) & ~is_sine
    paired = freq_cols == 0
    col_angle = angle(shift_x * (freq_cols - half), period)
    scale = 1.0 / math.sqrt(epochs)
    ramp_cos = jnp.where(paired, scale, 2.0 * scale * jnp.cos(col_angle))
    ramp_sin = jnp.where(paired, 0.0, 2.0 * scale * jnp.sin(col_angle))
    ramp_sin = jnp.where(is_sine, ramp_sin, -ramp_sin)
    cos_x = jnp.cos(angle(shift_x, 2 * SUBPIX))
    cos_y = jnp.cos(angle(shift_y, 2 * SUBPIX))
    cos_xy = jnp.cos(angle(shift_x + shift_y, 2 * SUBPIX))
    main = jnp.where(zero_col, cos_y, cos_xy)
    lead = jnp.where(zero_col, 1.0, cos_x)
    lanes = jnp.concatenate([main * ramp_cos, main * ramp_sin, lead * ramp_cos, lead * ramp_sin])
    return coefs, lanes


def local(images, rate_vectors, epoch_times):
    loc_epochs, loc_rows, length = images.shape
    epoch_count = lax.axis_size("epoch")
    devices = lax.axis_size("row") * epoch_count
    device = lax.axis_index("row") * epoch_count + lax.axis_index("epoch")
    cols = length // 2 // devices
    table = packed_table(length, cols)
    table_t = jnp.asarray(np.ascontiguousarray(table.T))
    table = jnp.asarray(table)
    coefs, lanes = ramp_factors(rate_vectors, epoch_times, device, cols, length)
    rates = rate_vectors.shape[0]
    row_spectra = row_transform(images, table_t, devices, 2 * cols)
    spectra = lax.all_to_all(row_spectra, ("row", "epoch"), 0, 0, tiled=True)
    columns_back = column_stage(spectra, table, table_t, coefs, lanes, epoch_count, rates)
    back = lax.all_to_all(columns_back, ("row", "epoch"), 0, 0, tiled=True)
    return image_rows(back, table)


def solution(mesh):
    in_specs = (P(("group", "epoch"), "row", None), P(), P())
    out_specs = P(("group", "epoch"), "row", None)
    return jax.shard_map(local, mesh=mesh, in_specs=in_specs, out_specs=out_specs, check_vma=False)
```

time: 458 us -> 126 us (0.28); the launches traced: 450 us -> 125 us
  other arithmetic: 189 us -> 1.22 us
  local copies, waits for them, and re-layouts: 81.8 us -> 2.68 us
  matrix products: 58.5 us -> 0 us
  waiting for transfers between devices: 93.3 us -> 38.5 us
  Pallas kernels: 0 us -> 38.6 us
  blocking collectives: 14.7 us -> 36.2 us
    convert_element_type x4 -> x0, other arithmetic: 154 us -> none  [the longest x1 71.3 us: dft_tables(): (jnp.cos(angles) * factor).astype(jnp.bfloat16)]
    dot_general x4 -> x0, matrix products: 58.5 us -> none  [the longest x1 22.7 us: local(): jnp.einsum('vetr,wru->wvteu', gathered, stacked, preferred_element_type=j...]
    all_to_all x2 -> x1, waiting for transfers between devices: 93.3 us -> 38.5 us  [local(): spectra = lax.all_to_all(row_spectra, ('row', 'epoch'), 0, 0, tiled=True)]
    pallas_call x0 -> x3, Pallas kernels: none -> 38.6 us  [the longest x1 19 us: column_stage(): pl.pallas_call(functools.partial(column_kernel, epoch_count, rates), grid...]
    all_to_all x8 -> x0, local copies, waits for them, and re-layouts: 31.5 us -> none  [the longest x3 22.2 us: local(): lax.all_to_all(row_spectrum, 'row', split_axis=0, concat_axis=3, tiled=True)]
    reduce_sum x2 -> x0, other arithmetic: 24.9 us -> none  [one_rate(): summed_re = jnp.sum(real_part * ramp_re - imag_part * ramp_im, axis=1)]
    all_to_all x2 -> x1, blocking collectives: 14.7 us -> 36.2 us  [local(): back = lax.all_to_all(columns_back, ('row', 'epoch'), 0, 0, tiled=True)]
    convert_element_type x1 -> x0, local copies, waits for them, and re-layouts: 19.1 us -> none  [local(): row_spectrum = (row_terms * sign_wide).astype(jnp.bfloat16)]
  transfers between devices with their start and end apart: 2 -> 1, of which waited for: 1 -> 1; matrix products, arithmetic and copies ran while one was open for 16% -> 2% of each run, Pallas kernels for 0% -> 0%
where the time goes in v1:
time: 126 us; the launch traced here: 125 us
  Pallas kernels  38.6 us (31%)
  waiting for transfers between devices  38.5 us (31%)
  blocking collectives  36.2 us (29%)
  starting transfers between devices  7.49 us (6%)
  local copies, waits for them, and re-layouts  2.68 us (2%)
    all_to_all x1, waiting for transfers between devices, local(): spectra = lax.all_to_all(row_spectra, ('row', 'epoch'), 0, 0, tiled=True)  38.5 us
    all_to_all x1, blocking collectives, local(): back = lax.all_to_all(columns_back, ('row', 'epoch'), 0, 0, tiled=True)  36.2 us
    pallas_call x1, Pallas kernels, column_stage(): pl.pallas_call(functools.partial(column_kernel, epoch_count, rates), grid...  19 us
    pallas_call x1, Pallas kernels, row_transform(): pl.pallas_call(row_kernel, grid=(length // BLOCK,), in_specs=[pl.BlockSpe...  10.5 us
    pallas_call x1, Pallas kernels, image_rows(): pl.pallas_call(image_kernel, grid=(length // BLOCK,), in_specs=[pl.BlockS...  9.15 us
    all_to_all x1, starting transfers between devices, local(): spectra = lax.all_to_all(row_spectra, ('row', 'epoch'), 0, 0, tiled=True)  7.49 us
  transfers between devices with their start and end apart: 1, of which 1 were waited for; matrix products, arithmetic and copies ran while one was open for 2% of the time, Pallas kernels for 0%

profile of v1, /device:TPU:0, one launch (start us, length us, event | category | flops | bytes accessed | tf_op | source)
XLA Modules:
  0.0 124.7 jit_solution(1363699394909037709)
XLA Ops:
  0.0 10.5 %row_transform.1 = bf16[16,2,256,128]{3,2,1,0:T(8,128)(2,1)} custom-call(bf16[2,256,2048]{2,1,0:T(8,128)(2,1)} %images_ref.1, bf16[2048,2048]{1,0:T(8,128)(2,1)} %constant.110.clone.table_ref.table_t_ref), custom_call_target="tpu_custom_call" | custom-call | flops 4294967296 | bytes 12582912 | tf_op jit(solution)/shard_map/row_transform/pallas_call | solution.py:46
  10.5 0.0 copy-start.1
  10.5 0.0 copy-start.2
  10.5 7.5 %all-to-all-start = ((bf16[16,2,256,128]{3,2,1,0:T(8,128)(2,1)}), bf16[16,2,256,128]{3,2,1,0:T(8,128)(2,1)S(1)}, u32[]{:S(2)}, u32[]{:S(2)}) async-start(bf16[16,2,256,128]{3,2,1,0:T(8,128)(2,1)} %row_transform.1), calls=%async_computation | async-start | bytes 4194304 | tf_op jit(solution)/shard_map/all_to_all | solution.py:268
  18.0 0.0 copy-done.1
  18.0 0.2 slice_reduce_fusion
  18.2 0.0 copy-done.2
  18.2 0.1 broadcast_multiply_fusion
  18.2 0.1 mul.148
  18.3 0.1 fusion.9
  18.4 0.2 multiply_select_fusion.2
  18.6 1.0 copy.6
  19.6 0.1 mul.162
  19.7 0.1 fusion.12
  19.8 0.1 select_multiply_fusion.3
  20.0 0.6 pad_maximum_fusion.1.lane_ref
  20.6 38.5 %all-to-all-done.z_ref = bf16[16,2,256,128]{3,2,1,0:T(8,128)(2,1)S(1)} async-done(((bf16[16,2,256,128]{3,2,1,0:T(8,128)(2,1)}), bf16[16,2,256,128]{3,2,1,0:T(8,128)(2,1)S(1)}, u32[]{:S(2)}, u32[]{:S(2)}) %all-to-all-start) | async-done | bytes 2097184 | tf_op jit(solution)/shard_map/all_to_all | solution.py:268
  59.1 0.0 copy-start
  59.1 1.3 %copy-done = bf16[16,2,256,128]{3,2,1,0:T(8,128)(2,1)} copy-done((bf16[16,2,256,128]{3,2,1,0:T(8,128)(2,1)}, bf16[16,2,256,128]{3,2,1,0:T(8,128)(2,1)S(1)}, u32[]{:S(2)}) %copy-start) | copy-done | bytes 2097176
  60.4 19.0 %column_stage.1 = bf16[16,1,256,128]{3,2,1,0:T(8,128)(2,1)} custom-call(bf16[16,2,256,128]{3,2,1,0:T(8,128)(2,1)} %copy-done, bf16[2048,2048]{1,0:T(8,128)(2,1)} %constant.111.clone.table_ref, bf16[2048,2048]{1,0:T(8,128)(2,1)} %constant.110.clone.table_ref.table_t_ref, f32[1024,16]{1,0:T(8,128)} %bitcast.1, f32[32,128]{1,0:T(8,128)} %pad_maximum_fusion.1.lane_ref), custom_call_target="tpu_custom_call" | custom-call | flops 6442450944 | bytes 16777216 | tf_op jit(solution)/shard_map/column_stage/pallas_call | solution.py:151
  79.4 36.2 %all_to_all.10.back_ref = bf16[16,1,256,128]{3,2,1,0:T(8,128)(2,1)} all-to-all(bf16[16,1,256,128]{3,2,1,0:T(8,128)(2,1)} %column_stage.1), channel_id=1, replica_groups=mesh['group'=2,'row'=8,'epoch'=2] {'row','epoch'}, dimensions={0} | all-to-all | bytes 2097152 | tf_op jit(solution)/shard_map/all_to_all | solution.py:270
  115.5 9.1 %image_rows.1 = f32[1,256,2048]{2,1,0:T(8,128)} custom-call(bf16[16,1,256,128]{3,2,1,0:T(8,128)(2,1)} %all_to_all.10.back_ref, bf16[2048,2048]{1,0:T(8,128)(2,1)} %constant.111.clone.table_ref), custom_call_target="tpu_custom_call" | custom-call | flops 2147483648 | bytes 11534336 | tf_op jit(solution)/shard_map/image_rows/pallas_call | solution.py:199
  (7 shorter events, 0.1 us)
Async XLA Ops:
  10.5 7.5 %copy-start.1 = (s32[2,2]{1,0:T(2,128)S(1)}, s32[2,2]{1,0:T(2,128)}, u32[]{:S(2)}) copy-start(s32[2,2]{1,0:T(2,128)} %param.6) | copy-start | bytes 52
  10.5 7.7 %copy-start.2 = (s32[4]{0:T(128)S(1)}, s32[4]{0:T(128)}, u32[]{:S(2)}) copy-start(s32[4]{0:T(128)} %param.7) | copy-start | bytes 52
  10.5 48.6 %all-to-all-start = ((bf16[16,2,256,128]{3,2,1,0:T(8,128)(2,1)}), bf16[16,2,256,128]{3,2,1,0:T(8,128)(2,1)S(1)}, u32[]{:S(2)}, u32[]{:S(2)}) async-start(bf16[16,2,256,128]{3,2,1,0:T(8,128)(2,1)} %row_transform.1), calls=%async_computation | async-start | bytes 4194304 | tf_op jit(solution)/shard_map/all_to_all | solution.py:268
  59.1 1.3 %copy-start = (bf16[16,2,256,128]{3,2,1,0:T(8,128)(2,1)}, bf16[16,2,256,128]{3,2,1,0:T(8,128)(2,1)S(1)}, u32[]{:S(2)}) copy-start(bf16[16,2,256,128]{3,2,1,0:T(8,128)(2,1)S(1)} %all-to-all-done.z_ref) | copy-start | bytes 6291460

commit v2 on v1

v2 whole, which is shorter than its diff:
```python
import functools
import math

import jax
import jax.numpy as jnp
import ml_dtypes
import numpy as np
from jax import lax
from jax.experimental import pallas as pl
from jax.experimental.pallas import tpu as pltpu
from jax.sharding import PartitionSpec as P

SUBPIX = 16
CHUNKS = 2
MIN_COLS = 32
ROW_BLOCK = 512
COLUMN_BLOCK = 512
IMAGE_BLOCK = 512
VMEM_LIMIT = 44 * 1024 * 1024


def packed_table(length, cols):
    half = length // 2
    freqs = np.arange(half, dtype=np.int32)
    positions = np.arange(length, dtype=np.int32)
    turns = freqs[:, None] * positions[None, :] % length
    angles = turns.astype(np.float32) * np.float32(2.0 * math.pi / length)
    factor = np.float32(1.0 / math.sqrt(length))
    cosine = np.cos(angles) * factor
    sine = np.sin(angles) * factor
    sine[0] = np.where(positions % 2 == 0, factor, -factor)
    blocks = np.stack([cosine.reshape(-1, cols, length), sine.reshape(-1, cols, length)], axis=1)
    return blocks.reshape(length, length).astype(ml_dtypes.bfloat16)


def cost(flops, bytes_accessed):
    return pl.CostEstimate(flops=flops, bytes_accessed=bytes_accessed, transcendentals=0)


def is_low(shape, group):
    return lax.broadcasted_iota(jnp.int32, shape, 1) % (2 * group) < group


def pair_lanes(upper, lower, width):
    count = upper.shape[1] // width
    if 2 * width == 128:
        parts = []
        low = is_low((upper.shape[0], 128), width)
        for tile in range(count // 2):
            first = upper[:, tile * 128 : (tile + 1) * 128]
            second = lower[:, tile * 128 : (tile + 1) * 128]
            parts.append(jnp.where(low, first, pltpu.roll(second, width, axis=1)))
            parts.append(jnp.where(low, pltpu.roll(first, width, axis=1), second))
        return parts
    groups = [slice(group * width, (group + 1) * width) for group in range(count)]
    return [jnp.concatenate([upper[:, group], lower[:, group]], axis=1) for group in groups]


def row_kernel(images_ref, table_ref, out_ref):
    loc_epochs, loc_rows, length = images_ref.shape
    dests, _, width = out_ref.shape
    pixels = images_ref[...].reshape(loc_epochs * loc_rows, length)
    terms = jnp.dot(pixels, table_ref[...], preferred_element_type=jnp.float32)
    if loc_epochs == 2:
        parts = pair_lanes(terms[:loc_rows], terms[loc_rows:], width // 2)
    else:
        by_epoch = terms.reshape(loc_epochs, loc_rows, terms.shape[1])
        one = width // loc_epochs
        parts = [
            jnp.concatenate(
                [by_epoch[loc][:, dest * one : (dest + 1) * one] for loc in range(loc_epochs)],
                axis=1,
            )
            for dest in range(dests)
        ]
    for dest in range(dests):
        out_ref[dest] = parts[dest].astype(jnp.bfloat16)


def row_transform(images, table_t, chunk, chunks, devices):
    loc_epochs, loc_rows, length = images.shape
    columns = length // chunks
    width = columns // devices * loc_epochs
    block = min(ROW_BLOCK, columns)
    steps = columns // block
    dests = devices // steps
    return pl.pallas_call(
        row_kernel,
        grid=(steps,),
        in_specs=[
            pl.BlockSpec((loc_epochs, loc_rows, length), lambda i: (0, 0, 0)),
            pl.BlockSpec((length, block), lambda i: (0, chunk * steps + i)),
        ],
        out_specs=pl.BlockSpec((dests, loc_rows, width), lambda i: (i, 0, 0)),
        out_shape=jax.ShapeDtypeStruct((devices, loc_rows, width), jnp.bfloat16),
        compiler_params=pltpu.CompilerParams(vmem_limit_bytes=VMEM_LIMIT),
        cost_estimate=cost(
            2 * loc_epochs * loc_rows * length * columns,
            2 * length * columns + 4 * loc_epochs * loc_rows * length,
        ),
        name=f"row_transform_{chunk}",
    )(images, table_t)


def fold_epochs(sums, epochs, width):
    if len(sums) == 2 and epochs == 4 and width == 64:
        halves = [part[:, :128] + part[:, 128:] for part in sums]
        low = is_low(halves[0].shape, 64)
        kept = jnp.where(low, halves[0], halves[1])
        return kept + pltpu.roll(jnp.where(low, halves[1], halves[0]), 64, axis=1)
    folded = [
        sum(part[:, epoch * width : (epoch + 1) * width] for epoch in range(epochs))
        for part in sums
    ]
    return jnp.concatenate(folded, axis=1)


def swap_halves(values, cols):
    total = values.shape[1]
    if total == 128:
        low = is_low(values.shape, cols)
        ahead = pltpu.roll(values, 128 - cols, axis=1)
        return jnp.where(low, ahead, pltpu.roll(values, cols, axis=1))
    parts = [values[:, start : start + cols] for start in range(0, total, cols)]
    return jnp.concatenate([parts[index ^ 1] for index in range(len(parts))], axis=1)


def column_kernel(
    epoch_count, epochs, rates, z_ref, table_ref, table_t_ref, coef_ref, lane_ref, out_ref, z_all, sums
):
    devices, loc_rows, core_lanes = z_ref.shape
    row_count = devices // epoch_count
    lanes = core_lanes * epoch_count
    width = lanes // epochs
    cols = width // 2
    block = table_ref.shape[0]
    half_steps = pl.num_programs(0) // 2
    step = pl.program_id(0)

    @pl.when(step == 0)
    def _():
        for row in range(row_count):
            parts = [z_ref[row * epoch_count + core] for core in range(epoch_count)]
            z_all[row * loc_rows : (row + 1) * loc_rows, :] = jnp.concatenate(parts, axis=1)

    @pl.when(step < half_steps)
    def _():
        products = jnp.dot(table_ref[...], z_all[...], preferred_element_type=jnp.float32)
        groups = block // width
        products = products.reshape(groups, 2, cols, lanes)
        even = products[:, 0].reshape(groups * cols, lanes)
        odd = products[:, 1].reshape(groups * cols, lanes)
        straight, crossed, lead = ([], []), ([], []), ([], [])
        for rate in range(rates):
            cos_row = coef_ref[:, rate * lanes : (rate + 1) * lanes]
            sin_row = coef_ref[:, (rates + rate) * lanes : (rates + rate + 1) * lanes]
            turned = (cos_row * even + sin_row * odd, cos_row * odd - sin_row * even)
            for which in range(2):
                straight[which].append(turned[which] * lane_ref[rate : rate + 1, :])
                crossed[which].append(turned[which] * lane_ref[rates + rate : rates + rate + 1, :])
                at = (2 + which) * rates + rate
                lead[which].append(even[:8] * lane_ref[at : at + 1, :])

        def collect(plain, turned):
            summed = fold_epochs(plain, epochs, width)
            return summed + swap_halves(fold_epochs(turned, epochs, width), cols)

        even_sum = collect(straight[0], crossed[0])
        odd_sum = collect(straight[1], crossed[1])
        lead_sum = collect(lead[0], lead[1])
        first = lax.broadcasted_iota(jnp.int32, even_sum.shape, 0) == 0
        even_sum = jnp.where(first & (step == 0), lead_sum[0:1], even_sum)
        both = jnp.stack(
            [part.reshape(groups, cols, rates * width) for part in (even_sum, odd_sum)], axis=1
        )
        start = pl.multiple_of(step * block, block)
        sums[pl.ds(start, block), :] = both.reshape(block, rates * width).astype(jnp.bfloat16)

    @pl.when(step >= half_steps)
    def _():
        back = jnp.dot(table_t_ref[...], sums[...], preferred_element_type=jnp.float32)
        half_rows = loc_rows // 2
        for row in range(block // loc_rows):
            part = back[row * loc_rows : (row + 1) * loc_rows]
            pairs = pair_lanes(part[:half_rows], part[half_rows:], width)
            for rate in range(rates):
                out_ref[row * rates + rate] = pairs[rate].astype(jnp.bfloat16)


def column_stage(spectra, table, table_t, coefs, lane_factors, epoch_count, epochs, rates, chunk):
    devices, loc_rows, core_lanes = spectra.shape
    length = table.shape[0]
    lanes = core_lanes * epoch_count
    width = lanes // epochs
    block = COLUMN_BLOCK
    steps = length // block
    return pl.pallas_call(
        functools.partial(column_kernel, epoch_count, epochs, rates),
        grid=(2 * steps,),
        in_specs=[
            pl.BlockSpec(spectra.shape, lambda i: (0, 0, 0)),
            pl.BlockSpec((block, length), lambda i: (jnp.minimum(i, steps - 1), 0)),
            pl.BlockSpec((block, length), lambda i: (jnp.maximum(i - steps, 0), 0)),
            pl.BlockSpec((block // 2, coefs.shape[1]), lambda i: (jnp.minimum(i, steps - 1), 0)),
            pl.BlockSpec(lane_factors.shape, lambda i: (0, 0)),
        ],
        out_specs=pl.BlockSpec(
            (devices // steps, loc_rows // 2, 2 * width), lambda i: (jnp.maximum(i - steps, 0), 0, 0)
        ),
        out_shape=jax.ShapeDtypeStruct((devices, loc_rows // 2, 2 * width), jnp.bfloat16),
        scratch_shapes=[
            pltpu.VMEM((length, lanes), jnp.bfloat16),
            pltpu.VMEM((length, rates * width), jnp.bfloat16),
        ],
        compiler_params=pltpu.CompilerParams(vmem_limit_bytes=VMEM_LIMIT),
        cost_estimate=cost(
            2 * length * length * (epochs + rates) * width,
            4 * length * length + 4 * coefs.size + 4 * spectra.size,
        ),
        name=f"column_stage_{chunk}",
    )(spectra, table, table_t, coefs, lane_factors)


def image_kernel(has_partial, back_ref, table_ref, *refs):
    out_ref, left = refs[-2:]
    devices, half_rows, two_widths = back_ref.shape
    width = two_widths // 2

    @pl.when(pl.program_id(0) == 0)
    def _():
        per_tile = 128 // width
        for tile in range(devices * width // 128):
            blocks = [back_ref[tile * per_tile + part] for part in range(per_tile)]
            if per_tile == 2:
                blocks = [block.astype(jnp.float32) for block in blocks]
                sides = pair_lanes(blocks[0], blocks[1], width)
            else:
                sides = [
                    jnp.concatenate([block[:, :width] for block in blocks], axis=1),
                    jnp.concatenate([block[:, width:] for block in blocks], axis=1),
                ]
            for side in range(2):
                at = slice(side * half_rows, (side + 1) * half_rows)
                left[at, tile * 128 : (tile + 1) * 128] = sides[side].astype(jnp.bfloat16)

    pixels = jnp.dot(left[...], table_ref[...], preferred_element_type=jnp.float32)
    if has_partial:
        pixels = pixels + refs[0][...].reshape(pixels.shape)
    out_ref[...] = pixels.reshape(out_ref.shape)


def image_rows(back, table, partial, chunk, chunks):
    devices, half_rows, two_widths = back.shape
    length = table.shape[0]
    depth = devices * two_widths // 2
    rows = 2 * half_rows
    block = IMAGE_BLOCK
    image_spec = pl.BlockSpec((1, rows, block), lambda i: (0, 0, i))
    return pl.pallas_call(
        functools.partial(image_kernel, partial is not None),
        grid=(length // block,),
        in_specs=[
            pl.BlockSpec(back.shape, lambda i: (0, 0, 0)),
            pl.BlockSpec((depth, block), lambda i: (chunk, i)),
        ]
        + ([] if partial is None else [image_spec]),
        out_specs=image_spec,
        out_shape=jax.ShapeDtypeStruct((1, rows, length), jnp.float32),
        scratch_shapes=[pltpu.VMEM((rows, depth), jnp.bfloat16)],
        compiler_params=pltpu.CompilerParams(vmem_limit_bytes=VMEM_LIMIT),
        cost_estimate=cost(
            2 * rows * depth * length, 2 * depth * length + 8 * rows * length
        ),
        name=f"image_rows_{chunk}",
    )(back, table, *([] if partial is None else [partial]))


def turn_angle(turns, whole):
    return (turns % whole).astype(jnp.float32) * (2.0 * math.pi / whole)


def row_factors(shift_y, rates, width, length):
    half = length // 2
    freqs = jnp.arange(half, dtype=jnp.int32)[None, :]
    angles = turn_angle(shift_y * (freqs - half), SUBPIX * length)
    coefs = jnp.concatenate(
        [
            jnp.where(freqs == 0, 1.0, 2.0 * jnp.cos(angles)),
            jnp.where(freqs == 0, 0.0, 2.0 * jnp.sin(angles)),
        ]
    )
    spread = jnp.broadcast_to(coefs.T[:, :, None], (half, coefs.shape[0], width))
    return spread.reshape(half, coefs.shape[0] * width)


def column_factors(shift_y, shift_x, rates, epochs, first_freq, cols, length):
    half = length // 2
    lane = jnp.arange(2 * cols, dtype=jnp.int32)[None, :]
    freqs = first_freq + lane % cols
    is_sine = lane >= cols
    paired = freqs == 0
    zero_col = paired & ~is_sine
    angles = turn_angle(shift_x * (freqs - half), SUBPIX * length)
    scale = 1.0 / math.sqrt(epochs)
    ramp_cos = jnp.where(paired, scale, 2.0 * scale * jnp.cos(angles))
    ramp_sin = jnp.where(paired, 0.0, 2.0 * scale * jnp.sin(angles))
    ramp_sin = jnp.where(is_sine, ramp_sin, -ramp_sin)
    cos_x = jnp.cos(turn_angle(shift_x, 2 * SUBPIX))
    cos_y = jnp.cos(turn_angle(shift_y, 2 * SUBPIX))
    cos_xy = jnp.cos(turn_angle(shift_x + shift_y, 2 * SUBPIX))
    main = jnp.where(zero_col, cos_y, cos_xy)
    lead = jnp.where(zero_col, 1.0, cos_x)
    factors = jnp.stack([main * ramp_cos, main * ramp_sin, lead * ramp_cos, lead * ramp_sin])
    return factors.reshape(4 * rates, epochs * 2 * cols)


def local(images, rate_vectors, epoch_times):
    loc_epochs, loc_rows, length = images.shape
    epoch_count = lax.axis_size("epoch")
    devices = lax.axis_size("row") * epoch_count
    device = lax.axis_index("row") * epoch_count + lax.axis_index("epoch")
    rates, epochs = rate_vectors.shape[0], epoch_times.shape[0]
    chunks = max(1, min(CHUNKS, length // 2 // devices // MIN_COLS))
    cols = length // 2 // devices // chunks
    table = packed_table(length, cols)
    table_t = jnp.asarray(np.ascontiguousarray(table.T))
    table = jnp.asarray(table)
    period = SUBPIX * length
    shift_y = (rate_vectors[:, 0:1] * epoch_times[None, :] % period).reshape(-1, 1)
    shift_x = (rate_vectors[:, 1:2] * epoch_times[None, :] % period).reshape(-1, 1)
    coefs = row_factors(shift_y, rates, 2 * cols, length)

    def exchange(values):
        return lax.all_to_all(values, ("row", "epoch"), 0, 0, tiled=True)

    spectra = [
        exchange(row_transform(images, table_t, chunk, chunks, devices)) for chunk in range(chunks)
    ]
    backs = []
    for chunk in range(chunks):
        first_freq = (chunk * devices + device) * cols
        factors = column_factors(shift_y, shift_x, rates, epochs, first_freq, cols, length)
        backs.append(
            exchange(
                column_stage(
                    spectra[chunk], table, table_t, coefs, factors, epoch_count, epochs, rates, chunk
                )
            )
        )
    result = None
    for chunk in range(chunks):
        result = image_rows(backs[chunk], table, result, chunk, chunks)
    return result


def solution(mesh):
    in_specs = (P(("group", "epoch"), "row", None), P(), P())
    out_specs = P(("group", "epoch"), "row", None)
    return jax.shard_map(local, mesh=mesh, in_specs=in_specs, out_specs=out_specs, check_vma=False)
```

time: 126 us -> 116 us (0.921)
  blocking collectives: 36.2 us -> 0 us
  starting transfers between devices: 7.49 us -> 26.5 us
  local copies, waits for them, and re-layouts: 2.68 us -> 16.3 us
  waiting for transfers between devices: 38.5 us -> 27.4 us
  Pallas kernels: 38.6 us -> 43.8 us
    all_to_all x1 -> x0, blocking collectives: 36.2 us -> none  [local(): back = lax.all_to_all(columns_back, ('row', 'epoch'), 0, 0, tiled=True)]
    all_to_all x1 -> x4, starting transfers between devices: 7.49 us -> 26.5 us  [exchange(): return lax.all_to_all(values, ('row', 'epoch'), 0, 0, tiled=True)]
    all_to_all x1 -> x4, waiting for transfers between devices: 38.5 us -> 27.4 us  [exchange(): return lax.all_to_all(values, ('row', 'epoch'), 0, 0, tiled=True)]
    unnamed x6 -> x16, local copies, waits for them, and re-layouts: 1.33 us -> 7.91 us
    reshape x0 -> x3, local copies, waits for them, and re-layouts: none -> 5.51 us  [the longest x1 5.36 us: row_factors(): return spread.reshape(half, coefs.shape[0] * width)]
    pallas_call x3 -> x6, Pallas kernels: 38.6 us -> 43.8 us  [the longest x2 25.6 us: column_stage(): pl.pallas_call(functools.partial(column_kernel, epoch_count, epochs, rate...]
    broadcast_in_dim x0 -> x1, local copies, waits for them, and re-layouts: none -> 2.51 us  [row_factors(): jnp.broadcast_to(coefs.T[:, :, None], (half, coefs.shape[0], width))]
  transfers between devices with their start and end apart: 1 -> 4, of which waited for: 1 -> 2; matrix products, arithmetic and copies ran while one was open for 2% -> 8% of each run, Pallas kernels for 0% -> 30%
where the time goes in v2:
time: 116 us; the launch traced here: 115 us
  Pallas kernels  43.8 us (38%)
  waiting for transfers between devices  27.4 us (24%)
  starting transfers between devices  26.5 us (23%)
  local copies, waits for them, and re-layouts  16.3 us (14%)
    all_to_all x4, waiting for transfers between devices, exchange(): return lax.all_to_all(values, ('row', 'epoch'), 0, 0, tiled=True)  27.4 us
    all_to_all x4, starting transfers between devices, exchange(): return lax.all_to_all(values, ('row', 'epoch'), 0, 0, tiled=True)  26.5 us
    pallas_call x2, Pallas kernels, column_stage(): pl.pallas_call(functools.partial(column_kernel, epoch_count, epochs, rate...  25.6 us
    pallas_call x2, Pallas kernels, image_rows(): pl.pallas_call(functools.partial(image_kernel, partial is not None), grid...  9.47 us
    pallas_call x2, Pallas kernels, row_transform(): pl.pallas_call(row_kernel, grid=(steps,), in_specs=[pl.BlockSpec((loc_epo...  8.71 us
    unnamed x16, local copies, waits for them, and re-layouts  7.91 us
    reshape x1, local copies, waits for them, and re-layouts, row_factors(): return spread.reshape(half, coefs.shape[0] * width)  5.36 us
    broadcast_in_dim x1, local copies, waits for them, and re-layouts, row_factors(): jnp.broadcast_to(coefs.T[:, :, None], (half, coefs.shape[0], width))  2.51 us
  transfers between devices with their start and end apart: 4, of which 2 were waited for; matrix products, arithmetic and copies ran while one was open for 8% of the time, Pallas kernels for 30%

profile of v2, /device:TPU:0, one launch (start us, length us, event | category | flops | bytes accessed | tf_op | source)
XLA Modules:
  0.0 114.8 jit_solution(11573763283900044872)
XLA Ops:
  0.0 0.0 copy-start.2
  0.0 1.6 %copy-done.2 = bf16[2,256,2048]{2,1,0:T(8,128)(2,1)S(1)} copy-done((bf16[2,256,2048]{2,1,0:T(8,128)(2,1)S(1)}, bf16[2,256,2048]{2,1,0:T(8,128)(2,1)}, u32[]{:S(2)}) %copy-start.2) | copy-done | bytes 2097176
  1.6 0.0 copy-start.6
  1.6 0.0 copy-start.7
  1.6 0.0 copy-start.3
  1.6 4.4 %row_transform_0.1 = bf16[16,256,128]{2,1,0:T(8,128)(2,1)S(1)} custom-call(bf16[2,256,2048]{2,1,0:T(8,128)(2,1)S(1)} %copy-done.2, bf16[2048,2048]{1,0:T(8,128)(2,1)} %constant.124.clone.table_ref.table_t_ref), custom_call_target="tpu_custom_call" | custom-call | flops 2147483648 | bytes 8388608 | tf_op jit(solution)/shard_map/row_transform_0/pallas_call | solution.py:87
  6.0 0.0 copy-start.5
  6.0 1.0 copy-done.5
  7.0 7.4 %all-to-all-start.2 = ((bf16[16,256,128]{2,1,0:T(8,128)(2,1)}), bf16[16,256,128]{2,1,0:T(8,128)(2,1)S(1)}, u32[]{:S(2)}, u32[]{:S(2)}) async-start(bf16[16,256,128]{2,1,0:T(8,128)(2,1)} %copy-done.5), calls=%async_computation.2 | async-start | bytes 2097152 | tf_op jit(solution)/shard_map/all_to_all | solution.py:334
  14.4 0.0 copy-done.6
  14.4 0.2 slice_reduce_fusion
  14.6 0.0 copy-done.7
  14.6 0.1 broadcast_multiply_fusion
  14.6 0.1 mul.309
  14.7 0.1 mul.323
  14.8 0.0 copy-done.3
  14.9 4.3 %row_transform_1.1 = bf16[16,256,128]{2,1,0:T(8,128)(2,1)S(1)} custom-call(bf16[2,256,2048]{2,1,0:T(8,128)(2,1)S(1)} %copy-done.3, bf16[2048,2048]{1,0:T(8,128)(2,1)} %constant.124.clone.table_ref.table_t_ref), custom_call_target="tpu_custom_call" | custom-call | flops 2147483648 | bytes 8388608 | tf_op jit(solution)/shard_map/row_transform_1/pallas_call | solution.py:87
  19.2 0.0 copy-start.4
  19.2 1.0 copy-done.4
  20.1 17.2 %all-to-all-done.2.z_ref = bf16[16,256,128]{2,1,0:T(8,128)(2,1)S(1)} async-done(((bf16[16,256,128]{2,1,0:T(8,128)(2,1)}), bf16[16,256,128]{2,1,0:T(8,128)(2,1)S(1)}, u32[]{:S(2)}, u32[]{:S(2)}) %all-to-all-start.2) | async-done | bytes 1048608 | tf_op jit(solution)/shard_map/all_to_all | solution.py:334
  37.3 6.9 %all-to-all-start = ((bf16[16,256,128]{2,1,0:T(8,128)(2,1)}), bf16[16,256,128]{2,1,0:T(8,128)(2,1)S(1)}, u32[]{:S(2)}, u32[]{:S(2)}) async-start(bf16[16,256,128]{2,1,0:T(8,128)(2,1)} %copy-done.4), calls=%async_computation | async-start | bytes 2097152 | tf_op jit(solution)/shard_map/all_to_all | solution.py:334
  44.2 0.1 fusion.11
  44.3 0.1 fusion.14
  44.4 0.1 select_multiply_fusion.3
  44.5 0.1 reshape.1349.lane_ref
  44.6 0.2 multiply_select_fusion.2
  44.8 2.5 %broadcast_in_dim.135 = f32[1024,16,64]{0,2,1:T(8,128)} broadcast(f32[1024,16]{0,1:T(8,128)S(1)} %maximum_bitcast_fusion), dimensions={0,1} | broadcast | bytes 4259840 | tf_op jit(solution)/shard_map/broadcast_in_dim | solution.py:292
  47.4 5.4 %copy.6.coef_ref = f32[1024,1024]{1,0:T(8,128)} copy(f32[1024,1024]{0,1:T(8,128)} %bitcast.3) | data formatting | bytes 8388608 | tf_op jit(solution)/shard_map/reshape | solution.py:293
  52.7 0.0 copy-start
  52.7 2.2 %copy-done = f32[1024,1024]{1,0:T(8,128)S(1)} copy-done((f32[1024,1024]{1,0:T(8,128)S(1)}, f32[1024,1024]{1,0:T(8,128)}, u32[]{:S(2)}) %copy-start) | copy-done | bytes 4194328
  54.9 12.8 %column_stage_0.1 = bf16[16,128,128]{2,1,0:T(8,128)(2,1)} custom-call(bf16[16,256,128]{2,1,0:T(8,128)(2,1)S(1)} %all-to-all-done.2.z_ref, bf16[2048,2048]{1,0:T(8,128)(2,1)} %constant.125.clone.table_ref, bf16[2048,2048]{1,0:T(8,128)(2,1)} %constant.124.clone.table_ref.table_t_ref, f32[1024,1024]{1,0:T(8,128)S(1)} %copy-done, f32[8,256]{1,0:T(8,128)S(1)} %reshape.1349.lane_ref), custom_call_target="tpu_custom_call" | custom-call | flops 3221225472 | bytes 23068672 | tf_op jit(solution)/shard_map/column_stage_0/pallas_call | solution.py:197
  67.7 0.0 all-to-all-done.z_ref
  67.7 6.3 %all-to-all-start.3 = ((bf16[16,128,128]{2,1,0:T(8,128)(2,1)}), bf16[16,128,128]{2,1,0:T(8,128)(2,1)S(1)}, u32[]{:S(2)}, u32[]{:S(2)}) async-start(bf16[16,128,128]{2,1,0:T(8,128)(2,1)} %column_stage_0.1), calls=%async_computation.3 | async-start | bytes 1048576 | tf_op jit(solution)/shard_map/all_to_all | solution.py:334
  74.0 0.1 reshape.1348.lane_ref
  74.1 0.0 copy-start.1
  74.1 2.2 %copy-done.1 = f32[1024,1024]{1,0:T(8,128)S(1)} copy-done((f32[1024,1024]{1,0:T(8,128)S(1)}, f32[1024,1024]{1,0:T(8,128)}, u32[]{:S(2)}) %copy-start.1) | copy-done | bytes 4194328
  76.3 12.8 %column_stage_1.1 = bf16[16,128,128]{2,1,0:T(8,128)(2,1)} custom-call(bf16[16,256,128]{2,1,0:T(8,128)(2,1)S(1)} %all-to-all-done.z_ref, bf16[2048,2048]{1,0:T(8,128)(2,1)} %constant.125.clone.table_ref, bf16[2048,2048]{1,0:T(8,128)(2,1)} %constant.124.clone.table_ref.table_t_ref, f32[1024,1024]{1,0:T(8,128)S(1)} %copy-done.1, f32[8,256]{1,0:T(8,128)S(1)} %reshape.1348.lane_ref), custom_call_target="tpu_custom_call" | custom-call | flops 3221225472 | bytes 23068672 | tf_op jit(solution)/shard_map/column_stage_1/pallas_call | solution.py:197
  89.1 0.0 all-to-all-done.3.back_ref
  89.1 6.0 %all-to-all-start.1 = ((bf16[16,128,128]{2,1,0:T(8,128)(2,1)}), bf16[16,128,128]{2,1,0:T(8,128)(2,1)S(1)}, u32[]{:S(2)}, u32[]{:S(2)}) async-start(bf16[16,128,128]{2,1,0:T(8,128)(2,1)} %column_stage_1.1), calls=%async_computation.1 | async-start | bytes 1048576 | tf_op jit(solution)/shard_map/all_to_all | solution.py:334
  95.1 4.2 %image_rows_0.1.refs_0_ = f32[1,256,2048]{2,1,0:T(8,128)S(1)} custom-call(bf16[16,128,128]{2,1,0:T(8,128)(2,1)S(1)} %all-to-all-done.3.back_ref, bf16[2048,2048]{1,0:T(8,128)(2,1)} %constant.125.clone.table_ref), custom_call_target="tpu_custom_call" | custom-call | flops 1073741824 | bytes 8388608 | tf_op jit(solution)/shard_map/image_rows_0/pallas_call | solution.py:259
  99.4 10.2 %all-to-all-done.1.back_ref = bf16[16,128,128]{2,1,0:T(8,128)(2,1)S(1)} async-done(((bf16[16,128,128]{2,1,0:T(8,128)(2,1)}), bf16[16,128,128]{2,1,0:T(8,128)(2,1)S(1)}, u32[]{:S(2)}, u32[]{:S(2)}) %all-to-all-start.1) | async-done | bytes 524320 | tf_op jit(solution)/shard_map/all_to_all | solution.py:334
  109.6 5.2 %image_rows_1.1 = f32[1,256,2048]{2,1,0:T(8,128)} custom-call(bf16[16,128,128]{2,1,0:T(8,128)(2,1)S(1)} %all-to-all-done.1.back_ref, bf16[2048,2048]{1,0:T(8,128)(2,1)} %constant.125.clone.table_ref, f32[1,256,2048]{2,1,0:T(8,128)S(1)} %image_rows_0.1.refs_0_), custom_call_target="tpu_custom_call" | custom-call | flops 1073741824 | bytes 8388608 | tf_op jit(solution)/shard_map/image_rows_1/pallas_call | solution.py:259
  (10 shorter events, 0.1 us)
Async XLA Ops:
  0.0 1.6 %copy-start.2 = (bf16[2,256,2048]{2,1,0:T(8,128)(2,1)S(1)}, bf16[2,256,2048]{2,1,0:T(8,128)(2,1)}, u32[]{:S(2)}) copy-start(bf16[2,256,2048]{2,1,0:T(8,128)(2,1)} %images_ref.3) | copy-start | bytes 6291460
  1.6 12.8 %copy-start.6 = (s32[2,2]{1,0:T(2,128)S(1)}, s32[2,2]{1,0:T(2,128)}, u32[]{:S(2)}) copy-start(s32[2,2]{1,0:T(2,128)} %param.6) | copy-start | bytes 52
  1.6 13.0 %copy-start.7 = (s32[4]{0:T(128)S(1)}, s32[4]{0:T(128)}, u32[]{:S(2)}) copy-start(s32[4]{0:T(128)} %param.7) | copy-start | bytes 52
  1.6 13.3 %copy-start.3 = (bf16[2,256,2048]{2,1,0:T(8,128)(2,1)S(1)}, bf16[2,256,2048]{2,1,0:T(8,128)(2,1)}, u32[]{:S(2)}) copy-start(bf16[2,256,2048]{2,1,0:T(8,128)(2,1)} %images_ref.3) | copy-start | bytes 6291460
  6.0 1.0 copy-start.5
  7.0 30.3 %all-to-all-start.2 = ((bf16[16,256,128]{2,1,0:T(8,128)(2,1)}), bf16[16,256,128]{2,1,0:T(8,128)(2,1)S(1)}, u32[]{:S(2)}, u32[]{:S(2)}) async-start(bf16[16,256,128]{2,1,0:T(8,128)(2,1)} %copy-done.5), calls=%async_computation.2 | async-start | bytes 2097152 | tf_op jit(solution)/shard_map/all_to_all | solution.py:334
  19.2 1.0 copy-start.4
  37.3 30.4 %all-to-all-start = ((bf16[16,256,128]{2,1,0:T(8,128)(2,1)}), bf16[16,256,128]{2,1,0:T(8,128)(2,1)S(1)}, u32[]{:S(2)}, u32[]{:S(2)}) async-start(bf16[16,256,128]{2,1,0:T(8,128)(2,1)} %copy-done.4), calls=%async_computation | async-start | bytes 2097152 | tf_op jit(solution)/shard_map/all_to_all | solution.py:334
  52.7 2.2 %copy-start = (f32[1024,1024]{1,0:T(8,128)S(1)}, f32[1024,1024]{1,0:T(8,128)}, u32[]{:S(2)}) copy-start(f32[1024,1024]{1,0:T(8,128)} %copy.6.coef_ref) | copy-start | bytes 12582916
  67.7 21.4 %all-to-all-start.3 = ((bf16[16,128,128]{2,1,0:T(8,128)(2,1)}), bf16[16,128,128]{2,1,0:T(8,128)(2,1)S(1)}, u32[]{:S(2)}, u32[]{:S(2)}) async-start(bf16[16,128,128]{2,1,0:T(8,128)(2,1)} %column_stage_0.1), calls=%async_computation.3 | async-start | bytes 1048576 | tf_op jit(solution)/shard_map/all_to_all | solution.py:334
  74.1 2.2 %copy-start.1 = (f32[1024,1024]{1,0:T(8,128)S(1)}, f32[1024,1024]{1,0:T(8,128)}, u32[]{:S(2)}) copy-start(f32[1024,1024]{1,0:T(8,128)} %copy.6.coef_ref) | copy-start | bytes 12582916
  89.1 20.5 %all-to-all-start.1 = ((bf16[16,128,128]{2,1,0:T(8,128)(2,1)}), bf16[16,128,128]{2,1,0:T(8,128)(2,1)S(1)}, u32[]{:S(2)}, u32[]{:S(2)}) async-start(bf16[16,128,128]{2,1,0:T(8,128)(2,1)} %column_stage_1.1), calls=%async_computation.1 | async-start | bytes 1048576 | tf_op jit(solution)/shard_map/all_to_all | solution.py:334

commit v3 on v2

--- a/solution.py
+++ b/solution.py
@@ -13,6 +13,7 @@
 SUBPIX = 16
 CHUNKS = 2
 MIN_COLS = 32
+PAIRWISE_LIMIT = 16
 ROW_BLOCK = 512
 COLUMN_BLOCK = 512
 IMAGE_BLOCK = 512
@@ -331,7 +332,15 @@
     coefs = row_factors(shift_y, rates, 2 * cols, length)
 
     def exchange(values):
-        return lax.all_to_all(values, ("row", "epoch"), 0, 0, tiled=True)
+        if devices > PAIRWISE_LIMIT:
+            return lax.all_to_all(values, ("row", "epoch"), 0, 0, tiled=True)
+        received = values
+        for offset in range(1, devices):
+            sent = lax.dynamic_index_in_dim(values, device ^ offset, 0, keepdims=True)
+            pairs = [(index, index ^ offset) for index in range(devices)]
+            arrived = lax.ppermute(sent, ("row", "epoch"), pairs)
+            received = lax.dynamic_update_slice_in_dim(received, arrived, device ^ offset, 0)
+        return received
 
     spectra = [
         exchange(row_transform(images, table_t, chunk, chunks, devices)) for chunk in range(chunks)

time: 116 us -> 168 us (1.45)
  starting transfers between devices: 26.5 us -> 97.3 us
  waiting for transfers between devices: 27.4 us -> 13.7 us
  local copies, waits for them, and re-layouts: 16.3 us -> 13 us
    ppermute x0 -> x60, starting transfers between devices: none -> 97.3 us  [exchange(): arrived = lax.ppermute(sent, ('row', 'epoch'), pairs)]
    all_to_all x4 -> x0, waiting for transfers between devices: 27.4 us -> none  [exchange(): return lax.all_to_all(values, ('row', 'epoch'), 0, 0, tiled=True)]
    all_to_all x4 -> x0, starting transfers between devices: 26.5 us -> none  [exchange(): return lax.all_to_all(values, ('row', 'epoch'), 0, 0, tiled=True)]
    ppermute x0 -> x60, waiting for transfers between devices: none -> 13.7 us  [exchange(): arrived = lax.ppermute(sent, ('row', 'epoch'), pairs)]
    unnamed x16 -> x10, local copies, waits for them, and re-layouts: 7.91 us -> 3.19 us
  transfers between devices with their start and end apart: 4 -> 60, of which waited for: 2 -> 12; matrix products, arithmetic and copies ran while one was open for 8% -> 6% of each run, Pallas kernels for 30% -> 20%
where the time goes in v3:
time: 168 us
  starting transfers between devices  97.3 us (58%)
  Pallas kernels  42.5 us (25%)
  waiting for transfers between devices  13.7 us (8%)
  local copies, waits for them, and re-layouts  13 us (8%)
    ppermute x60, starting transfers between devices, exchange(): arrived = lax.ppermute(sent, ('row', 'epoch'), pairs)  97.3 us
    pallas_call x2, Pallas kernels, column_stage(): pl.pallas_call(functools.partial(column_kernel, epoch_count, epochs, rate...  24.4 us
    ppermute x60, waiting for transfers between devices, exchange(): arrived = lax.ppermute(sent, ('row', 'epoch'), pairs)  13.7 us
    pallas_call x2, Pallas kernels, image_rows(): pl.pallas_call(functools.partial(image_kernel, partial is not None), grid...  9.48 us
    pallas_call x2, Pallas kernels, row_transform(): pl.pallas_call(row_kernel, grid=(steps,), in_specs=[pl.BlockSpec((loc_epo...  8.57 us
    reshape x1, local copies, waits for them, and re-layouts, row_factors(): return spread.reshape(half, coefs.shape[0] * width)  5.41 us
  transfers between devices with their start and end apart: 60, of which 12 were waited for; matrix products, arithmetic and copies ran while one was open for 6% of the time, Pallas kernels for 20%

profile of v3, /device:TPU:0, one launch (start us, length us, event | category | flops | bytes accessed | tf_op | source)
XLA Modules:
  0.0 167.6 jit_solution(8350822825298107797)
XLA Ops:
  0.0 1.6 copy-done.1
  1.6 4.3 %row_transform_1.1 = bf16[16,256,128]{2,1,0:T(8,128)(2,1)S(1)} custom-call(bf16[2,256,2048]{2,1,0:T(8,128)(2,1)S(1)} %copy-done.1, bf16[2048,2048]{1,0:T(8,128)(2,1)} %constant.277.clone.table_ref.table_t_ref), custom_call_target="tpu_custom_call" | custom-call | flops 2147483648 | bytes 8388608 | tf_op jit(solution)/shard_map/row_transform_1/pallas_call | solution.py:88
  5.9 0.5 collective-permute-start
  6.4 1.6 copy-done.2
  8.0 4.3 %row_transform_0.1 = bf16[16,256,128]{2,1,0:T(8,128)(2,1)S(1)} custom-call(bf16[2,256,2048]{2,1,0:T(8,128)(2,1)S(1)} %copy-done.2, bf16[2048,2048]{1,0:T(8,128)(2,1)} %constant.277.clone.table_ref.table_t_ref), custom_call_target="tpu_custom_call" | custom-call | flops 2147483648 | bytes 8388608 | tf_op jit(solution)/shard_map/row_transform_0/pallas_call | solution.py:88
  13.2 2.5 %broadcast_in_dim.135 = f32[1024,16,64]{0,2,1:T(8,128)} broadcast(f32[1024,16]{0,1:T(8,128)S(1)} %maximum_bitcast_fusion), dimensions={0,1} | broadcast | bytes 4259840 | tf_op jit(solution)/shard_map/broadcast_in_dim | solution.py:293
  15.7 5.4 %copy.6.coef_ref = f32[1024,1024]{1,0:T(8,128)} copy(f32[1024,1024]{0,1:T(8,128)} %bitcast.3) | data formatting | bytes 8388608 | tf_op jit(solution)/shard_map/reshape | solution.py:294
  22.0 3.0 %collective-permute-start.1 = (bf16[1,256,128]{2,1,0:T(8,128)(2,1)S(1)}, bf16[1,256,128]{2,1,0:T(8,128)(2,1)S(1)}, u32[]{:S(2)}, u32[]{:S(2)}) collective-permute-start(bf16[1,256,128]{2,1,0:T(8,128)(2,1)S(1)} %get-tuple-element.39), channel_id=1, source_target_pairs={{0,2},{1,3},{2,0},{3,1},{4,6},{5,7},{6,4},{7,5},{8,10},{9,11},{10,... | collective-permute-start | bytes 196616 | tf_op jit(solution)/shard_map/ppermute | solution.py:341
  24.9 1.6 collective-permute-start.3
  26.8 2.7 %collective-permute-start.5 = (bf16[1,256,128]{2,1,0:T(8,128)(2,1)S(1)}, bf16[1,256,128]{2,1,0:T(8,128)(2,1)S(1)}, u32[]{:S(2)}, u32[]{:S(2)}) collective-permute-start(bf16[1,256,128]{2,1,0:T(8,128)(2,1)S(1)} %get-tuple-element.35), channel_id=1, source_target_pairs={{0,6},{1,7},{2,4},{3,5},{4,2},{5,3},{6,0},{7,1},{8,14},{9,15},{10,... | collective-permute-start | bytes 196616 | tf_op jit(solution)/shard_map/ppermute | solution.py:341
  29.8 2.7 %collective-permute-start.7 = (bf16[1,256,128]{2,1,0:T(8,128)(2,1)S(1)}, bf16[1,256,128]{2,1,0:T(8,128)(2,1)S(1)}, u32[]{:S(2)}, u32[]{:S(2)}) collective-permute-start(bf16[1,256,128]{2,1,0:T(8,128)(2,1)S(1)} %get-tuple-element.33), channel_id=1, source_target_pairs={{0,8},{1,9},{2,10},{3,11},{4,12},{5,13},{6,14},{7,15},{8,0},{9,1},... | collective-permute-start | bytes 196616 | tf_op jit(solution)/shard_map/ppermute | solution.py:341
  32.5 1.0 collective-permute-start.8
  33.4 2.9 %collective-permute-start.9 = (bf16[1,256,128]{2,1,0:T(8,128)(2,1)S(1)}, bf16[1,256,128]{2,1,0:T(8,128)(2,1)S(1)}, u32[]{:S(2)}, u32[]{:S(2)}) collective-permute-start(bf16[1,256,128]{2,1,0:T(8,128)(2,1)S(1)} %get-tuple-element.31), channel_id=1, source_target_pairs={{0,10},{1,11},{2,8},{3,9},{4,14},{5,15},{6,12},{7,13},{8,2},{9,3},... | collective-permute-start | bytes 196616 | tf_op jit(solution)/shard_map/ppermute | solution.py:341
  36.3 0.5 collective-permute-start.10
  36.9 3.0 %collective-permute-start.11 = (bf16[1,256,128]{2,1,0:T(8,128)(2,1)S(1)}, bf16[1,256,128]{2,1,0:T(8,128)(2,1)S(1)}, u32[]{:S(2)}, u32[]{:S(2)}) collective-permute-start(bf16[1,256,128]{2,1,0:T(8,128)(2,1)S(1)} %get-tuple-element.29), channel_id=1, source_target_pairs={{0,12},{1,13},{2,14},{3,15},{4,8},{5,9},{6,10},{7,11},{8,4},{9,5},... | collective-permute-start | bytes 196616 | tf_op jit(solution)/shard_map/ppermute | solution.py:341
  39.9 4.0 %collective-permute-start.12 = (bf16[1,256,128]{2,1,0:T(8,128)(2,1)S(1)}, bf16[1,256,128]{2,1,0:T(8,128)(2,1)S(1)}, u32[]{:S(2)}, u32[]{:S(2)}) collective-permute-start(bf16[1,256,128]{2,1,0:T(8,128)(2,1)S(1)} %get-tuple-element.28), channel_id=1, source_target_pairs={{0,13},{1,12},{2,15},{3,14},{4,9},{5,8},{6,11},{7,10},{8,5},{9,4},... | collective-permute-start | bytes 196616 | tf_op jit(solution)/shard_map/ppermute | solution.py:341
  43.9 0.6 collective-permute-done.8
  44.4 3.6 %collective-permute-start.13 = (bf16[1,256,128]{2,1,0:T(8,128)(2,1)S(1)}, bf16[1,256,128]{2,1,0:T(8,128)(2,1)S(1)}, u32[]{:S(2)}, u32[]{:S(2)}) collective-permute-start(bf16[1,256,128]{2,1,0:T(8,128)(2,1)S(1)} %get-tuple-element.27), channel_id=1, source_target_pairs={{0,14},{1,15},{2,12},{3,13},{4,10},{5,11},{6,8},{7,9},{8,6},{9,7},... | collective-permute-start | bytes 196616 | tf_op jit(solution)/shard_map/ppermute | solution.py:341
  48.3 0.8 collective-permute-start.14
  49.6 1.1 collective-permute-start.31
  50.8 0.8 collective-permute-start.32
  51.6 3.0 %collective-permute-start.33 = (bf16[1,256,128]{2,1,0:T(8,128)(2,1)S(1)}, bf16[1,256,128]{2,1,0:T(8,128)(2,1)S(1)}, u32[]{:S(2)}, u32[]{:S(2)}) collective-permute-start(bf16[1,256,128]{2,1,0:T(8,128)(2,1)S(1)} %get-tuple-element.22), channel_id=1, source_target_pairs={{0,4},{1,5},{2,6},{3,7},{4,0},{5,1},{6,2},{7,3},{8,12},{9,13},{10,... | collective-permute-start | bytes 196616 | tf_op jit(solution)/shard_map/ppermute | solution.py:341
  54.7 2.3 %collective-permute-start.34 = (bf16[1,256,128]{2,1,0:T(8,128)(2,1)S(1)}, bf16[1,256,128]{2,1,0:T(8,128)(2,1)S(1)}, u32[]{:S(2)}, u32[]{:S(2)}) collective-permute-start(bf16[1,256,128]{2,1,0:T(8,128)(2,1)S(1)} %get-tuple-element.21), channel_id=1, source_target_pairs={{0,5},{1,4},{2,7},{3,6},{4,1},{5,0},{6,3},{7,2},{8,13},{9,12},{10,... | collective-permute-start | bytes 196616 | tf_op jit(solution)/shard_map/ppermute | solution.py:341
  57.0 1.7 collective-permute-start.35
  58.7 12.1 %column_stage_1.1 = bf16[16,128,128]{2,1,0:T(8,128)(2,1)S(1)} custom-call(bf16[16,256,128]{2,1,0:T(8,128)(2,1)S(1)} %constant_dynamic-update-slice_fusion.45.z_ref, bf16[2048,2048]{1,0:T(8,128)(2,1)} %constant.278.clone.table_ref, bf16[2048,2048]{1,0:T(8,128)(2,1)} %constant.277.clone.table_ref.table_t_ref, f32[1024,1024]{1,0:T(8,128)S(1)} %copy-done, ...), custom_call_target="tpu_custom_call" | custom-call | flops 3221225472 | bytes 23068672 | tf_op jit(solution)/shard_map/column_stage_1/pallas_call | solution.py:198
  70.8 1.3 collective-permute-start.36
  72.1 2.4 %collective-permute-start.37 = (bf16[1,256,128]{2,1,0:T(8,128)(2,1)S(1)}, bf16[1,256,128]{2,1,0:T(8,128)(2,1)S(1)}, u32[]{:S(2)}, u32[]{:S(2)}) collective-permute-start(bf16[1,256,128]{2,1,0:T(8,128)(2,1)S(1)} %get-tuple-element.18), channel_id=1, source_target_pairs={{0,8},{1,9},{2,10},{3,11},{4,12},{5,13},{6,14},{7,15},{8,0},{9,1},... | collective-permute-start | bytes 196616 | tf_op jit(solution)/shard_map/ppermute | solution.py:341
  75.0 2.4 %collective-permute-start.39 = (bf16[1,256,128]{2,1,0:T(8,128)(2,1)S(1)}, bf16[1,256,128]{2,1,0:T(8,128)(2,1)S(1)}, u32[]{:S(2)}, u32[]{:S(2)}) collective-permute-start(bf16[1,256,128]{2,1,0:T(8,128)(2,1)S(1)} %get-tuple-element.16), channel_id=1, source_target_pairs={{0,10},{1,11},{2,8},{3,9},{4,14},{5,15},{6,12},{7,13},{8,2},{9,3},... | collective-permute-start | bytes 196616 | tf_op jit(solution)/shard_map/ppermute | solution.py:341
  77.5 1.2 collective-permute-start.40
  78.7 2.6 %collective-permute-start.41 = (bf16[1,256,128]{2,1,0:T(8,128)(2,1)S(1)}, bf16[1,256,128]{2,1,0:T(8,128)(2,1)S(1)}, u32[]{:S(2)}, u32[]{:S(2)}) collective-permute-start(bf16[1,256,128]{2,1,0:T(8,128)(2,1)S(1)} %get-tuple-element.14), channel_id=1, source_target_pairs={{0,12},{1,13},{2,14},{3,15},{4,8},{5,9},{6,10},{7,11},{8,4},{9,5},... | collective-permute-start | bytes 196616 | tf_op jit(solution)/shard_map/ppermute | solution.py:341
  81.3 0.7 collective-permute-done.37
  82.5 3.2 %collective-permute-done.38 = bf16[1,256,128]{2,1,0:T(8,128)(2,1)S(1)} collective-permute-done((bf16[1,256,128]{2,1,0:T(8,128)(2,1)S(1)}, bf16[1,256,128]{2,1,0:T(8,128)(2,1)S(1)}, u32[]{:S(2)}, u32[]{:S(2)}) %collective-permute-start.38) | collective-permute-done | bytes 65568 | tf_op jit(solution)/shard_map/ppermute | solution.py:341
  85.7 2.9 %collective-permute-start.43 = (bf16[1,256,128]{2,1,0:T(8,128)(2,1)S(1)}, bf16[1,256,128]{2,1,0:T(8,128)(2,1)S(1)}, u32[]{:S(2)}, u32[]{:S(2)}) collective-permute-start(bf16[1,256,128]{2,1,0:T(8,128)(2,1)S(1)} %get-tuple-element.12), channel_id=1, source_target_pairs={{0,14},{1,15},{2,12},{3,13},{4,10},{5,11},{6,8},{7,9},{8,6},{9,7},... | collective-permute-start | bytes 196616 | tf_op jit(solution)/shard_map/ppermute | solution.py:341
  88.7 2.1 %collective-permute-start.44 = (bf16[1,256,128]{2,1,0:T(8,128)(2,1)S(1)}, bf16[1,256,128]{2,1,0:T(8,128)(2,1)S(1)}, u32[]{:S(2)}, u32[]{:S(2)}) collective-permute-start(bf16[1,256,128]{2,1,0:T(8,128)(2,1)S(1)} %get-tuple-element.11), channel_id=1, source_target_pairs={{0,15},{1,14},{2,13},{3,12},{4,11},{5,10},{6,9},{7,8},{8,7},{9,6},... | collective-permute-start | bytes 196616 | tf_op jit(solution)/shard_map/ppermute | solution.py:341
  90.8 2.0 %collective-permute-start.15 = (bf16[1,128,128]{2,1,0:T(8,128)(2,1)S(1)}, bf16[1,128,128]{2,1,0:T(8,128)(2,1)S(1)}, u32[]{:S(2)}, u32[]{:S(2)}) collective-permute-start(bf16[1,128,128]{2,1,0:T(8,128)(2,1)S(1)} %constant_dynamic-slice_fusion.44), channel_id=1, source_target_pairs={{0,1},{1,0},{2,3},{3,2},{4,5},{5,4},{6,7},{7,6},{8,9},{9,8},{10,11... | collective-permute-start | bytes 98312 | tf_op jit(solution)/shard_map/ppermute | solution.py:341
  93.2 2.1 %collective-permute-done.44 = bf16[1,256,128]{2,1,0:T(8,128)(2,1)S(1)} collective-permute-done((bf16[1,256,128]{2,1,0:T(8,128)(2,1)S(1)}, bf16[1,256,128]{2,1,0:T(8,128)(2,1)S(1)}, u32[]{:S(2)}, u32[]{:S(2)}) %collective-permute-start.44) | collective-permute-done | bytes 65568 | tf_op jit(solution)/shard_map/ppermute | solution.py:341
  95.2 12.3 %column_stage_0.1 = bf16[16,128,128]{2,1,0:T(8,128)(2,1)S(1)} custom-call(bf16[16,256,128]{2,1,0:T(8,128)(2,1)S(1)} %constant_dynamic-update-slice_fusion.15.z_ref, bf16[2048,2048]{1,0:T(8,128)(2,1)} %constant.278.clone.table_ref, bf16[2048,2048]{1,0:T(8,128)(2,1)} %constant.277.clone.table_ref.table_t_ref, f32[1024,1024]{1,0:T(8,128)S(1)} %copy-done, ...), custom_call_target="tpu_custom_call" | custom-call | flops 3221225472 | bytes 23068672 | tf_op jit(solution)/shard_map/column_stage_0/pallas_call | solution.py:198
  107.6 0.8 collective-permute-start.45
  108.5 1.6 collective-permute-start.16
  110.2 3.3 %collective-permute-start.18 = (bf16[1,128,128]{2,1,0:T(8,128)(2,1)S(1)}, bf16[1,128,128]{2,1,0:T(8,128)(2,1)S(1)}, u32[]{:S(2)}, u32[]{:S(2)}) collective-permute-start(bf16[1,128,128]{2,1,0:T(8,128)(2,1)S(1)} %get-tuple-element.67), channel_id=1, source_target_pairs={{0,4},{1,5},{2,6},{3,7},{4,0},{5,1},{6,2},{7,3},{8,12},{9,13},{10,... | collective-permute-start | bytes 98312 | tf_op jit(solution)/shard_map/ppermute | solution.py:341
  113.5 2.5 %collective-permute-start.20 = (bf16[1,128,128]{2,1,0:T(8,128)(2,1)S(1)}, bf16[1,128,128]{2,1,0:T(8,128)(2,1)S(1)}, u32[]{:S(2)}, u32[]{:S(2)}) collective-permute-start(bf16[1,128,128]{2,1,0:T(8,128)(2,1)S(1)} %get-tuple-element.65), channel_id=1, source_target_pairs={{0,6},{1,7},{2,4},{3,5},{4,2},{5,3},{6,0},{7,1},{8,14},{9,15},{10,... | collective-permute-start | bytes 98312 | tf_op jit(solution)/shard_map/ppermute | solution.py:341
  116.3 2.5 %collective-permute-start.22 = (bf16[1,128,128]{2,1,0:T(8,128)(2,1)S(1)}, bf16[1,128,128]{2,1,0:T(8,128)(2,1)S(1)}, u32[]{:S(2)}, u32[]{:S(2)}) collective-permute-start(bf16[1,128,128]{2,1,0:T(8,128)(2,1)S(1)} %get-tuple-element.63), channel_id=1, source_target_pairs={{0,8},{1,9},{2,10},{3,11},{4,12},{5,13},{6,14},{7,15},{8,0},{9,1},... | collective-permute-start | bytes 98312 | tf_op jit(solution)/shard_map/ppermute | solution.py:341
  119.3 3.4 %collective-permute-start.24 = (bf16[1,128,128]{2,1,0:T(8,128)(2,1)S(1)}, bf16[1,128,128]{2,1,0:T(8,128)(2,1)S(1)}, u32[]{:S(2)}, u32[]{:S(2)}) collective-permute-start(bf16[1,128,128]{2,1,0:T(8,128)(2,1)S(1)} %get-tuple-element.61), channel_id=1, source_target_pairs={{0,10},{1,11},{2,8},{3,9},{4,14},{5,15},{6,12},{7,13},{8,2},{9,3},... | collective-permute-start | bytes 98312 | tf_op jit(solution)/shard_map/ppermute | solution.py:341
  122.8 2.4 %collective-permute-start.26 = (bf16[1,128,128]{2,1,0:T(8,128)(2,1)S(1)}, bf16[1,128,128]{2,1,0:T(8,128)(2,1)S(1)}, u32[]{:S(2)}, u32[]{:S(2)}) collective-permute-start(bf16[1,128,128]{2,1,0:T(8,128)(2,1)S(1)} %get-tuple-element.59), channel_id=1, source_target_pairs={{0,12},{1,13},{2,14},{3,15},{4,8},{5,9},{6,10},{7,11},{8,4},{9,5},... | collective-permute-start | bytes 98312 | tf_op jit(solution)/shard_map/ppermute | solution.py:341
  125.2 1.4 collective-permute-start.27
  126.7 3.2 %collective-permute-start.28 = (bf16[1,128,128]{2,1,0:T(8,128)(2,1)S(1)}, bf16[1,128,128]{2,1,0:T(8,128)(2,1)S(1)}, u32[]{:S(2)}, u32[]{:S(2)}) collective-permute-start(bf16[1,128,128]{2,1,0:T(8,128)(2,1)S(1)} %get-tuple-element.57), channel_id=1, source_target_pairs={{0,14},{1,15},{2,12},{3,13},{4,10},{5,11},{6,8},{7,9},{8,6},{9,7},... | collective-permute-start | bytes 98312 | tf_op jit(solution)/shard_map/ppermute | solution.py:341
  129.8 1.2 collective-permute-start.29
  131.1 1.2 collective-permute-start.46
  132.4 0.8 collective-permute-start.47
  133.3 1.5 collective-permute-start.49
  135.1 1.1 collective-permute-start.50
  136.5 1.3 collective-permute-start.51
  137.9 1.8 %collective-permute-start.52 = (bf16[1,128,128]{2,1,0:T(8,128)(2,1)S(1)}, bf16[1,128,128]{2,1,0:T(8,128)(2,1)S(1)}, u32[]{:S(2)}, u32[]{:S(2)}) collective-permute-start(bf16[1,128,128]{2,1,0:T(8,128)(2,1)S(1)} %get-tuple-element.48), channel_id=1, source_target_pairs={{0,8},{1,9},{2,10},{3,11},{4,12},{5,13},{6,14},{7,15},{8,0},{9,1},... | collective-permute-start | bytes 98312 | tf_op jit(solution)/shard_map/ppermute | solution.py:341
  139.7 0.9 collective-permute-start.53
  140.6 2.1 %collective-permute-start.54 = (bf16[1,128,128]{2,1,0:T(8,128)(2,1)S(1)}, bf16[1,128,128]{2,1,0:T(8,128)(2,1)S(1)}, u32[]{:S(2)}, u32[]{:S(2)}) collective-permute-start(bf16[1,128,128]{2,1,0:T(8,128)(2,1)S(1)} %get-tuple-element.46), channel_id=1, source_target_pairs={{0,10},{1,11},{2,8},{3,9},{4,14},{5,15},{6,12},{7,13},{8,2},{9,3},... | collective-permute-start | bytes 98312 | tf_op jit(solution)/shard_map/ppermute | solution.py:341
  142.7 1.7 collective-permute-start.55
  144.4 2.4 %collective-permute-start.56 = (bf16[1,128,128]{2,1,0:T(8,128)(2,1)S(1)}, bf16[1,128,128]{2,1,0:T(8,128)(2,1)S(1)}, u32[]{:S(2)}, u32[]{:S(2)}) collective-permute-start(bf16[1,128,128]{2,1,0:T(8,128)(2,1)S(1)} %get-tuple-element.44), channel_id=1, source_target_pairs={{0,12},{1,13},{2,14},{3,15},{4,8},{5,9},{6,10},{7,11},{8,4},{9,5},... | collective-permute-start | bytes 98312 | tf_op jit(solution)/shard_map/ppermute | solution.py:341
  146.8 1.2 collective-permute-start.57
  148.0 3.6 %collective-permute-start.58 = (bf16[1,128,128]{2,1,0:T(8,128)(2,1)S(1)}, bf16[1,128,128]{2,1,0:T(8,128)(2,1)S(1)}, u32[]{:S(2)}, u32[]{:S(2)}) collective-permute-start(bf16[1,128,128]{2,1,0:T(8,128)(2,1)S(1)} %get-tuple-element.42), channel_id=1, source_target_pairs={{0,14},{1,15},{2,12},{3,13},{4,10},{5,11},{6,8},{7,9},{8,6},{9,7},... | collective-permute-start | bytes 98312 | tf_op jit(solution)/shard_map/ppermute | solution.py:341
  151.7 1.0 collective-permute-start.59
  152.7 2.0 %collective-permute-done.58 = bf16[1,128,128]{2,1,0:T(8,128)(2,1)S(1)} collective-permute-done((bf16[1,128,128]{2,1,0:T(8,128)(2,1)S(1)}, bf16[1,128,128]{2,1,0:T(8,128)(2,1)S(1)}, u32[]{:S(2)}, u32[]{:S(2)}) %collective-permute-start.58) | collective-permute-done | bytes 32800 | tf_op jit(solution)/shard_map/ppermute | solution.py:341
  154.7 3.4 %collective-permute-done.59 = bf16[1,128,128]{2,1,0:T(8,128)(2,1)S(1)} collective-permute-done((bf16[1,128,128]{2,1,0:T(8,128)(2,1)S(1)}, bf16[1,128,128]{2,1,0:T(8,128)(2,1)S(1)}, u32[]{:S(2)}, u32[]{:S(2)}) %collective-permute-start.59) | collective-permute-done | bytes 32800 | tf_op jit(solution)/shard_map/ppermute | solution.py:341
  158.1 4.2 %image_rows_0.1.refs_0_ = f32[1,256,2048]{2,1,0:T(8,128)S(1)} custom-call(bf16[16,128,128]{2,1,0:T(8,128)(2,1)S(1)} %constant_dynamic-update-slice_fusion.back_ref, bf16[2048,2048]{1,0:T(8,128)(2,1)} %constant.278.clone.table_ref), custom_call_target="tpu_custom_call" | custom-call | flops 1073741824 | bytes 8388608 | tf_op jit(solution)/shard_map/image_rows_0/pallas_call | solution.py:260
  162.4 5.2 %image_rows_1.1 = f32[1,256,2048]{2,1,0:T(8,128)} custom-call(bf16[16,128,128]{2,1,0:T(8,128)(2,1)S(1)} %constant_dynamic-update-slice_fusion.30.back_ref, bf16[2048,2048]{1,0:T(8,128)(2,1)} %constant.278.clone.table_ref, f32[1,256,2048]{2,1,0:T(8,128)S(1)} %image_rows_0.1.refs_0_), custom_call_target="tpu_custom_call" | custom-call | flops 1073741824 | bytes 8388608 | tf_op jit(solution)/shard_map/image_rows_1/pallas_call | solution.py:260
  (159 shorter events, 6.4 us)
Async XLA Ops:
  0.0 1.6 copy-start.1
  5.9 15.8 %collective-permute-start = (bf16[1,256,128]{2,1,0:T(8,128)(2,1)S(1)}, bf16[1,256,128]{2,1,0:T(8,128)(2,1)S(1)}, u32[]{:S(2)}, u32[]{:S(2)}) collective-permute-start(bf16[1,256,128]{2,1,0:T(8,128)(2,1)S(1)} %constant_dynamic-slice_fusion.59), channel_id=1, source_target_pairs={{0,1},{1,0},{2,3},{3,2},{4,5},{5,4},{6,7},{7,6},{8,9},{9,8},{10,11... | collective-permute-start | bytes 196616 | tf_op jit(solution)/shard_map/ppermute | solution.py:341
  8.0 4.6 %copy-start.3 = (s32[2,2]{1,0:T(2,128)S(1)}, s32[2,2]{1,0:T(2,128)}, u32[]{:S(2)}) copy-start(s32[2,2]{1,0:T(2,128)} %param.6) | copy-start | bytes 52
  8.0 4.8 %copy-start.4 = (s32[4]{0:T(128)S(1)}, s32[4]{0:T(128)}, u32[]{:S(2)}) copy-start(s32[4]{0:T(128)} %param.7) | copy-start | bytes 52
  12.3 14.5 %collective-permute-start.30 = (bf16[1,256,128]{2,1,0:T(8,128)(2,1)S(1)}, bf16[1,256,128]{2,1,0:T(8,128)(2,1)S(1)}, u32[]{:S(2)}, u32[]{:S(2)}) collective-permute-start(bf16[1,256,128]{2,1,0:T(8,128)(2,1)S(1)} %constant_dynamic-slice_fusion.29), channel_id=1, source_target_pairs={{0,1},{1,0},{2,3},{3,2},{4,5},{5,4},{6,7},{7,6},{8,9},{9,8},{10,11... | collective-permute-start | bytes 196616 | tf_op jit(solution)/shard_map/ppermute | solution.py:341
  21.7 37.0 %copy-start = (f32[1024,1024]{1,0:T(8,128)S(1)}, f32[1024,1024]{1,0:T(8,128)}, u32[]{:S(2)}) copy-start(f32[1024,1024]{1,0:T(8,128)} %copy.6.coef_ref) | copy-start | bytes 12582916
  22.0 7.7 %collective-permute-start.1 = (bf16[1,256,128]{2,1,0:T(8,128)(2,1)S(1)}, bf16[1,256,128]{2,1,0:T(8,128)(2,1)S(1)}, u32[]{:S(2)}, u32[]{:S(2)}) collective-permute-start(bf16[1,256,128]{2,1,0:T(8,128)(2,1)S(1)} %get-tuple-element.39), channel_id=1, source_target_pairs={{0,2},{1,3},{2,0},{3,1},{4,6},{5,7},{6,4},{7,5},{8,10},{9,11},{10,... | collective-permute-start | bytes 196616 | tf_op jit(solution)/shard_map/ppermute | solution.py:341
  24.9 4.8 %collective-permute-start.2 = (bf16[1,256,128]{2,1,0:T(8,128)(2,1)S(1)}, bf16[1,256,128]{2,1,0:T(8,128)(2,1)S(1)}, u32[]{:S(2)}, u32[]{:S(2)}) collective-permute-start(bf16[1,256,128]{2,1,0:T(8,128)(2,1)S(1)} %get-tuple-element.38), channel_id=1, source_target_pairs={{0,3},{1,2},{2,1},{3,0},{4,7},{5,6},{6,5},{7,4},{8,11},{9,10},{10,... | collective-permute-start | bytes 196616 | tf_op jit(solution)/shard_map/ppermute | solution.py:341
  24.9 7.5 %collective-permute-start.3 = (bf16[1,256,128]{2,1,0:T(8,128)(2,1)S(1)}, bf16[1,256,128]{2,1,0:T(8,128)(2,1)S(1)}, u32[]{:S(2)}, u32[]{:S(2)}) collective-permute-start(bf16[1,256,128]{2,1,0:T(8,128)(2,1)S(1)} %get-tuple-element.37), channel_id=1, source_target_pairs={{0,4},{1,5},{2,6},{3,7},{4,0},{5,1},{6,2},{7,3},{8,12},{9,13},{10,... | collective-permute-start | bytes 196616 | tf_op jit(solution)/shard_map/ppermute | solution.py:341
  26.5 6.9 %collective-permute-start.4 = (bf16[1,256,128]{2,1,0:T(8,128)(2,1)S(1)}, bf16[1,256,128]{2,1,0:T(8,128)(2,1)S(1)}, u32[]{:S(2)}, u32[]{:S(2)}) collective-permute-start(bf16[1,256,128]{2,1,0:T(8,128)(2,1)S(1)} %get-tuple-element.36), channel_id=1, source_target_pairs={{0,5},{1,4},{2,7},{3,6},{4,1},{5,0},{6,3},{7,2},{8,13},{9,12},{10,... | collective-permute-start | bytes 196616 | tf_op jit(solution)/shard_map/ppermute | solution.py:341
  26.8 9.5 %collective-permute-start.5 = (bf16[1,256,128]{2,1,0:T(8,128)(2,1)S(1)}, bf16[1,256,128]{2,1,0:T(8,128)(2,1)S(1)}, u32[]{:S(2)}, u32[]{:S(2)}) collective-permute-start(bf16[1,256,128]{2,1,0:T(8,128)(2,1)S(1)} %get-tuple-element.35), channel_id=1, source_target_pairs={{0,6},{1,7},{2,4},{3,5},{4,2},{5,3},{6,0},{7,1},{8,14},{9,15},{10,... | collective-permute-start | bytes 196616 | tf_op jit(solution)/shard_map/ppermute | solution.py:341
  29.7 7.2 %collective-permute-start.6 = (bf16[1,256,128]{2,1,0:T(8,128)(2,1)S(1)}, bf16[1,256,128]{2,1,0:T(8,128)(2,1)S(1)}, u32[]{:S(2)}, u32[]{:S(2)}) collective-permute-start(bf16[1,256,128]{2,1,0:T(8,128)(2,1)S(1)} %get-tuple-element.34), channel_id=1, source_target_pairs={{0,7},{1,6},{2,5},{3,4},{4,3},{5,2},{6,1},{7,0},{8,15},{9,14},{10,... | collective-permute-start | bytes 196616 | tf_op jit(solution)/shard_map/ppermute | solution.py:341
  29.8 10.1 %collective-permute-start.7 = (bf16[1,256,128]{2,1,0:T(8,128)(2,1)S(1)}, bf16[1,256,128]{2,1,0:T(8,128)(2,1)S(1)}, u32[]{:S(2)}, u32[]{:S(2)}) collective-permute-start(bf16[1,256,128]{2,1,0:T(8,128)(2,1)S(1)} %get-tuple-element.33), channel_id=1, source_target_pairs={{0,8},{1,9},{2,10},{3,11},{4,12},{5,13},{6,14},{7,15},{8,0},{9,1},... | collective-permute-start | bytes 196616 | tf_op jit(solution)/shard_map/ppermute | solution.py:341
  32.5 12.0 %collective-permute-start.8 = (bf16[1,256,128]{2,1,0:T(8,128)(2,1)S(1)}, bf16[1,256,128]{2,1,0:T(8,128)(2,1)S(1)}, u32[]{:S(2)}, u32[]{:S(2)}) collective-permute-start(bf16[1,256,128]{2,1,0:T(8,128)(2,1)S(1)} %get-tuple-element.32), channel_id=1, source_target_pairs={{0,9},{1,8},{2,11},{3,10},{4,13},{5,12},{6,15},{7,14},{8,1},{9,0},... | collective-permute-start | bytes 196616 | tf_op jit(solution)/shard_map/ppermute | solution.py:341
  33.4 14.9 %collective-permute-start.9 = (bf16[1,256,128]{2,1,0:T(8,128)(2,1)S(1)}, bf16[1,256,128]{2,1,0:T(8,128)(2,1)S(1)}, u32[]{:S(2)}, u32[]{:S(2)}) collective-permute-start(bf16[1,256,128]{2,1,0:T(8,128)(2,1)S(1)} %get-tuple-element.31), channel_id=1, source_target_pairs={{0,10},{1,11},{2,8},{3,9},{4,14},{5,15},{6,12},{7,13},{8,2},{9,3},... | collective-permute-start | bytes 196616 | tf_op jit(solution)/shard_map/ppermute | solution.py:341
  36.3 13.3 %collective-permute-start.10 = (bf16[1,256,128]{2,1,0:T(8,128)(2,1)S(1)}, bf16[1,256,128]{2,1,0:T(8,128)(2,1)S(1)}, u32[]{:S(2)}, u32[]{:S(2)}) collective-permute-start(bf16[1,256,128]{2,1,0:T(8,128)(2,1)S(1)} %get-tuple-element.30), channel_id=1, source_target_pairs={{0,11},{1,10},{2,9},{3,8},{4,15},{5,14},{6,13},{7,12},{8,3},{9,2},... | collective-permute-start | bytes 196616 | tf_op jit(solution)/shard_map/ppermute | solution.py:341
  36.9 13.9 %collective-permute-start.11 = (bf16[1,256,128]{2,1,0:T(8,128)(2,1)S(1)}, bf16[1,256,128]{2,1,0:T(8,128)(2,1)S(1)}, u32[]{:S(2)}, u32[]{:S(2)}) collective-permute-start(bf16[1,256,128]{2,1,0:T(8,128)(2,1)S(1)} %get-tuple-element.29), channel_id=1, source_target_pairs={{0,12},{1,13},{2,14},{3,15},{4,8},{5,9},{6,10},{7,11},{8,4},{9,5},... | collective-permute-start | bytes 196616 | tf_op jit(solution)/shard_map/ppermute | solution.py:341
  39.9 11.7 %collective-permute-start.12 = (bf16[1,256,128]{2,1,0:T(8,128)(2,1)S(1)}, bf16[1,256,128]{2,1,0:T(8,128)(2,1)S(1)}, u32[]{:S(2)}, u32[]{:S(2)}) collective-permute-start(bf16[1,256,128]{2,1,0:T(8,128)(2,1)S(1)} %get-tuple-element.28), channel_id=1, source_target_pairs={{0,13},{1,12},{2,15},{3,14},{4,9},{5,8},{6,11},{7,10},{8,5},{9,4},... | collective-permute-start | bytes 196616 | tf_op jit(solution)/shard_map/ppermute | solution.py:341
  44.4 10.2 %collective-permute-start.13 = (bf16[1,256,128]{2,1,0:T(8,128)(2,1)S(1)}, bf16[1,256,128]{2,1,0:T(8,128)(2,1)S(1)}, u32[]{:S(2)}, u32[]{:S(2)}) collective-permute-start(bf16[1,256,128]{2,1,0:T(8,128)(2,1)S(1)} %get-tuple-element.27), channel_id=1, source_target_pairs={{0,14},{1,15},{2,12},{3,13},{4,10},{5,11},{6,8},{7,9},{8,6},{9,7},... | collective-permute-start | bytes 196616 | tf_op jit(solution)/shard_map/ppermute | solution.py:341
  48.3 8.7 %collective-permute-start.14 = (bf16[1,256,128]{2,1,0:T(8,128)(2,1)S(1)}, bf16[1,256,128]{2,1,0:T(8,128)(2,1)S(1)}, u32[]{:S(2)}, u32[]{:S(2)}) collective-permute-start(bf16[1,256,128]{2,1,0:T(8,128)(2,1)S(1)} %get-tuple-element.26), channel_id=1, source_target_pairs={{0,15},{1,14},{2,13},{3,12},{4,11},{5,10},{6,9},{7,8},{8,7},{9,6},... | collective-permute-start | bytes 196616 | tf_op jit(solution)/shard_map/ppermute | solution.py:341
  49.6 21.2 %collective-permute-start.31 = (bf16[1,256,128]{2,1,0:T(8,128)(2,1)S(1)}, bf16[1,256,128]{2,1,0:T(8,128)(2,1)S(1)}, u32[]{:S(2)}, u32[]{:S(2)}) collective-permute-start(bf16[1,256,128]{2,1,0:T(8,128)(2,1)S(1)} %get-tuple-element.24), channel_id=1, source_target_pairs={{0,2},{1,3},{2,0},{3,1},{4,6},{5,7},{6,4},{7,5},{8,10},{9,11},{10,... | collective-permute-start | bytes 196616 | tf_op jit(solution)/shard_map/ppermute | solution.py:341
  50.8 21.3 %collective-permute-start.32 = (bf16[1,256,128]{2,1,0:T(8,128)(2,1)S(1)}, bf16[1,256,128]{2,1,0:T(8,128)(2,1)S(1)}, u32[]{:S(2)}, u32[]{:S(2)}) collective-permute-start(bf16[1,256,128]{2,1,0:T(8,128)(2,1)S(1)} %get-tuple-element.23), channel_id=1, source_target_pairs={{0,3},{1,2},{2,1},{3,0},{4,7},{5,6},{6,5},{7,4},{8,11},{9,10},{10,... | collective-permute-start | bytes 196616 | tf_op jit(solution)/shard_map/ppermute | solution.py:341
  51.6 23.0 %collective-permute-start.33 = (bf16[1,256,128]{2,1,0:T(8,128)(2,1)S(1)}, bf16[1,256,128]{2,1,0:T(8,128)(2,1)S(1)}, u32[]{:S(2)}, u32[]{:S(2)}) collective-permute-start(bf16[1,256,128]{2,1,0:T(8,128)(2,1)S(1)} %get-tuple-element.22), channel_id=1, source_target_pairs={{0,4},{1,5},{2,6},{3,7},{4,0},{5,1},{6,2},{7,3},{8,12},{9,13},{10,... | collective-permute-start | bytes 196616 | tf_op jit(solution)/shard_map/ppermute | solution.py:341
  54.7 20.4 %collective-permute-start.34 = (bf16[1,256,128]{2,1,0:T(8,128)(2,1)S(1)}, bf16[1,256,128]{2,1,0:T(8,128)(2,1)S(1)}, u32[]{:S(2)}, u32[]{:S(2)}) collective-permute-start(bf16[1,256,128]{2,1,0:T(8,128)(2,1)S(1)} %get-tuple-element.21), channel_id=1, source_target_pairs={{0,5},{1,4},{2,7},{3,6},{4,1},{5,0},{6,3},{7,2},{8,13},{9,12},{10,... | collective-permute-start | bytes 196616 | tf_op jit(solution)/shard_map/ppermute | solution.py:341
  57.0 20.5 %collective-permute-start.35 = (bf16[1,256,128]{2,1,0:T(8,128)(2,1)S(1)}, bf16[1,256,128]{2,1,0:T(8,128)(2,1)S(1)}, u32[]{:S(2)}, u32[]{:S(2)}) collective-permute-start(bf16[1,256,128]{2,1,0:T(8,128)(2,1)S(1)} %get-tuple-element.20), channel_id=1, source_target_pairs={{0,6},{1,7},{2,4},{3,5},{4,2},{5,3},{6,0},{7,1},{8,14},{9,15},{10,... | collective-permute-start | bytes 196616 | tf_op jit(solution)/shard_map/ppermute | solution.py:341
  70.8 7.8 %collective-permute-start.36 = (bf16[1,256,128]{2,1,0:T(8,128)(2,1)S(1)}, bf16[1,256,128]{2,1,0:T(8,128)(2,1)S(1)}, u32[]{:S(2)}, u32[]{:S(2)}) collective-permute-start(bf16[1,256,128]{2,1,0:T(8,128)(2,1)S(1)} %get-tuple-element.19), channel_id=1, source_target_pairs={{0,7},{1,6},{2,5},{3,4},{4,3},{5,2},{6,1},{7,0},{8,15},{9,14},{10,... | collective-permute-start | bytes 196616 | tf_op jit(solution)/shard_map/ppermute | solution.py:341
  72.1 9.9 %collective-permute-start.37 = (bf16[1,256,128]{2,1,0:T(8,128)(2,1)S(1)}, bf16[1,256,128]{2,1,0:T(8,128)(2,1)S(1)}, u32[]{:S(2)}, u32[]{:S(2)}) collective-permute-start(bf16[1,256,128]{2,1,0:T(8,128)(2,1)S(1)} %get-tuple-element.18), channel_id=1, source_target_pairs={{0,8},{1,9},{2,10},{3,11},{4,12},{5,13},{6,14},{7,15},{8,0},{9,1},... | collective-permute-start | bytes 196616 | tf_op jit(solution)/shard_map/ppermute | solution.py:341
  74.6 11.1 %collective-permute-start.38 = (bf16[1,256,128]{2,1,0:T(8,128)(2,1)S(1)}, bf16[1,256,128]{2,1,0:T(8,128)(2,1)S(1)}, u32[]{:S(2)}, u32[]{:S(2)}) collective-permute-start(bf16[1,256,128]{2,1,0:T(8,128)(2,1)S(1)} %get-tuple-element.17), channel_id=1, source_target_pairs={{0,9},{1,8},{2,11},{3,10},{4,13},{5,12},{6,15},{7,14},{8,1},{9,0},... | collective-permute-start | bytes 196616 | tf_op jit(solution)/shard_map/ppermute | solution.py:341
  75.0 13.6 %collective-permute-start.39 = (bf16[1,256,128]{2,1,0:T(8,128)(2,1)S(1)}, bf16[1,256,128]{2,1,0:T(8,128)(2,1)S(1)}, u32[]{:S(2)}, u32[]{:S(2)}) collective-permute-start(bf16[1,256,128]{2,1,0:T(8,128)(2,1)S(1)} %get-tuple-element.16), channel_id=1, source_target_pairs={{0,10},{1,11},{2,8},{3,9},{4,14},{5,15},{6,12},{7,13},{8,2},{9,3},... | collective-permute-start | bytes 196616 | tf_op jit(solution)/shard_map/ppermute | solution.py:341
  77.5 13.3 %collective-permute-start.40 = (bf16[1,256,128]{2,1,0:T(8,128)(2,1)S(1)}, bf16[1,256,128]{2,1,0:T(8,128)(2,1)S(1)}, u32[]{:S(2)}, u32[]{:S(2)}) collective-permute-start(bf16[1,256,128]{2,1,0:T(8,128)(2,1)S(1)} %get-tuple-element.15), channel_id=1, source_target_pairs={{0,11},{1,10},{2,9},{3,8},{4,15},{5,14},{6,13},{7,12},{8,3},{9,2},... | collective-permute-start | bytes 196616 | tf_op jit(solution)/shard_map/ppermute | solution.py:341
  78.7 14.1 %collective-permute-start.41 = (bf16[1,256,128]{2,1,0:T(8,128)(2,1)S(1)}, bf16[1,256,128]{2,1,0:T(8,128)(2,1)S(1)}, u32[]{:S(2)}, u32[]{:S(2)}) collective-permute-start(bf16[1,256,128]{2,1,0:T(8,128)(2,1)S(1)} %get-tuple-element.14), channel_id=1, source_target_pairs={{0,12},{1,13},{2,14},{3,15},{4,8},{5,9},{6,10},{7,11},{8,4},{9,5},... | collective-permute-start | bytes 196616 | tf_op jit(solution)/shard_map/ppermute | solution.py:341
  82.0 10.8 %collective-permute-start.42 = (bf16[1,256,128]{2,1,0:T(8,128)(2,1)S(1)}, bf16[1,256,128]{2,1,0:T(8,128)(2,1)S(1)}, u32[]{:S(2)}, u32[]{:S(2)}) collective-permute-start(bf16[1,256,128]{2,1,0:T(8,128)(2,1)S(1)} %get-tuple-element.13), channel_id=1, source_target_pairs={{0,13},{1,12},{2,15},{3,14},{4,9},{5,8},{6,11},{7,10},{8,5},{9,4},... | collective-permute-start | bytes 196616 | tf_op jit(solution)/shard_map/ppermute | solution.py:341
  85.7 7.4 %collective-permute-start.43 = (bf16[1,256,128]{2,1,0:T(8,128)(2,1)S(1)}, bf16[1,256,128]{2,1,0:T(8,128)(2,1)S(1)}, u32[]{:S(2)}, u32[]{:S(2)}) collective-permute-start(bf16[1,256,128]{2,1,0:T(8,128)(2,1)S(1)} %get-tuple-element.12), channel_id=1, source_target_pairs={{0,14},{1,15},{2,12},{3,13},{4,10},{5,11},{6,8},{7,9},{8,6},{9,7},... | collective-permute-start | bytes 196616 | tf_op jit(solution)/shard_map/ppermute | solution.py:341
  88.7 6.6 %collective-permute-start.44 = (bf16[1,256,128]{2,1,0:T(8,128)(2,1)S(1)}, bf16[1,256,128]{2,1,0:T(8,128)(2,1)S(1)}, u32[]{:S(2)}, u32[]{:S(2)}) collective-permute-start(bf16[1,256,128]{2,1,0:T(8,128)(2,1)S(1)} %get-tuple-element.11), channel_id=1, source_target_pairs={{0,15},{1,14},{2,13},{3,12},{4,11},{5,10},{6,9},{7,8},{8,7},{9,6},... | collective-permute-start | bytes 196616 | tf_op jit(solution)/shard_map/ppermute | solution.py:341
  90.8 17.6 %collective-permute-start.15 = (bf16[1,128,128]{2,1,0:T(8,128)(2,1)S(1)}, bf16[1,128,128]{2,1,0:T(8,128)(2,1)S(1)}, u32[]{:S(2)}, u32[]{:S(2)}) collective-permute-start(bf16[1,128,128]{2,1,0:T(8,128)(2,1)S(1)} %constant_dynamic-slice_fusion.44), channel_id=1, source_target_pairs={{0,1},{1,0},{2,3},{3,2},{4,5},{5,4},{6,7},{7,6},{8,9},{9,8},{10,11... | collective-permute-start | bytes 98312 | tf_op jit(solution)/shard_map/ppermute | solution.py:341
  107.6 5.9 %collective-permute-start.45 = (bf16[1,128,128]{2,1,0:T(8,128)(2,1)S(1)}, bf16[1,128,128]{2,1,0:T(8,128)(2,1)S(1)}, u32[]{:S(2)}, u32[]{:S(2)}) collective-permute-start(bf16[1,128,128]{2,1,0:T(8,128)(2,1)S(1)} %constant_dynamic-slice_fusion.14), channel_id=1, source_target_pairs={{0,1},{1,0},{2,3},{3,2},{4,5},{5,4},{6,7},{7,6},{8,9},{9,8},{10,11... | collective-permute-start | bytes 98312 | tf_op jit(solution)/shard_map/ppermute | solution.py:341
  108.5 7.6 %collective-permute-start.16 = (bf16[1,128,128]{2,1,0:T(8,128)(2,1)S(1)}, bf16[1,128,128]{2,1,0:T(8,128)(2,1)S(1)}, u32[]{:S(2)}, u32[]{:S(2)}) collective-permute-start(bf16[1,128,128]{2,1,0:T(8,128)(2,1)S(1)} %get-tuple-element.69), channel_id=1, source_target_pairs={{0,2},{1,3},{2,0},{3,1},{4,6},{5,7},{6,4},{7,5},{8,10},{9,11},{10,... | collective-permute-start | bytes 98312 | tf_op jit(solution)/shard_map/ppermute | solution.py:341
  110.1 6.1 %collective-permute-start.17 = (bf16[1,128,128]{2,1,0:T(8,128)(2,1)S(1)}, bf16[1,128,128]{2,1,0:T(8,128)(2,1)S(1)}, u32[]{:S(2)}, u32[]{:S(2)}) collective-permute-start(bf16[1,128,128]{2,1,0:T(8,128)(2,1)S(1)} %get-tuple-element.68), channel_id=1, source_target_pairs={{0,3},{1,2},{2,1},{3,0},{4,7},{5,6},{6,5},{7,4},{8,11},{9,10},{10,... | collective-permute-start | bytes 98312 | tf_op jit(solution)/shard_map/ppermute | solution.py:341
  110.2 8.6 %collective-permute-start.18 = (bf16[1,128,128]{2,1,0:T(8,128)(2,1)S(1)}, bf16[1,128,128]{2,1,0:T(8,128)(2,1)S(1)}, u32[]{:S(2)}, u32[]{:S(2)}) collective-permute-start(bf16[1,128,128]{2,1,0:T(8,128)(2,1)S(1)} %get-tuple-element.67), channel_id=1, source_target_pairs={{0,4},{1,5},{2,6},{3,7},{4,0},{5,1},{6,2},{7,3},{8,12},{9,13},{10,... | collective-permute-start | bytes 98312 | tf_op jit(solution)/shard_map/ppermute | solution.py:341
  113.5 5.8 %collective-permute-start.19 = (bf16[1,128,128]{2,1,0:T(8,128)(2,1)S(1)}, bf16[1,128,128]{2,1,0:T(8,128)(2,1)S(1)}, u32[]{:S(2)}, u32[]{:S(2)}) collective-permute-start(bf16[1,128,128]{2,1,0:T(8,128)(2,1)S(1)} %get-tuple-element.66), channel_id=1, source_target_pairs={{0,5},{1,4},{2,7},{3,6},{4,1},{5,0},{6,3},{7,2},{8,13},{9,12},{10,... | collective-permute-start | bytes 98312 | tf_op jit(solution)/shard_map/ppermute | solution.py:341
  113.5 9.2 %collective-permute-start.20 = (bf16[1,128,128]{2,1,0:T(8,128)(2,1)S(1)}, bf16[1,128,128]{2,1,0:T(8,128)(2,1)S(1)}, u32[]{:S(2)}, u32[]{:S(2)}) collective-permute-start(bf16[1,128,128]{2,1,0:T(8,128)(2,1)S(1)} %get-tuple-element.65), channel_id=1, source_target_pairs={{0,6},{1,7},{2,4},{3,5},{4,2},{5,3},{6,0},{7,1},{8,14},{9,15},{10,... | collective-permute-start | bytes 98312 | tf_op jit(solution)/shard_map/ppermute | solution.py:341
  116.1 6.7 %collective-permute-start.21 = (bf16[1,128,128]{2,1,0:T(8,128)(2,1)S(1)}, bf16[1,128,128]{2,1,0:T(8,128)(2,1)S(1)}, u32[]{:S(2)}, u32[]{:S(2)}) collective-permute-start(bf16[1,128,128]{2,1,0:T(8,128)(2,1)S(1)} %get-tuple-element.64), channel_id=1, source_target_pairs={{0,7},{1,6},{2,5},{3,4},{4,3},{5,2},{6,1},{7,0},{8,15},{9,14},{10,... | collective-permute-start | bytes 98312 | tf_op jit(solution)/shard_map/ppermute | solution.py:341
  116.3 9.0 %collective-permute-start.22 = (bf16[1,128,128]{2,1,0:T(8,128)(2,1)S(1)}, bf16[1,128,128]{2,1,0:T(8,128)(2,1)S(1)}, u32[]{:S(2)}, u32[]{:S(2)}) collective-permute-start(bf16[1,128,128]{2,1,0:T(8,128)(2,1)S(1)} %get-tuple-element.63), channel_id=1, source_target_pairs={{0,8},{1,9},{2,10},{3,11},{4,12},{5,13},{6,14},{7,15},{8,0},{9,1},... | collective-permute-start | bytes 98312 | tf_op jit(solution)/shard_map/ppermute | solution.py:341
  118.8 7.9 %collective-permute-start.23 = (bf16[1,128,128]{2,1,0:T(8,128)(2,1)S(1)}, bf16[1,128,128]{2,1,0:T(8,128)(2,1)S(1)}, u32[]{:S(2)}, u32[]{:S(2)}) collective-permute-start(bf16[1,128,128]{2,1,0:T(8,128)(2,1)S(1)} %get-tuple-element.62), channel_id=1, source_target_pairs={{0,9},{1,8},{2,11},{3,10},{4,13},{5,12},{6,15},{7,14},{8,1},{9,0},... | collective-permute-start | bytes 98312 | tf_op jit(solution)/shard_map/ppermute | solution.py:341
  119.3 10.6 %collective-permute-start.24 = (bf16[1,128,128]{2,1,0:T(8,128)(2,1)S(1)}, bf16[1,128,128]{2,1,0:T(8,128)(2,1)S(1)}, u32[]{:S(2)}, u32[]{:S(2)}) collective-permute-start(bf16[1,128,128]{2,1,0:T(8,128)(2,1)S(1)} %get-tuple-element.61), channel_id=1, source_target_pairs={{0,10},{1,11},{2,8},{3,9},{4,14},{5,15},{6,12},{7,13},{8,2},{9,3},... | collective-permute-start | bytes 98312 | tf_op jit(solution)/shard_map/ppermute | solution.py:341
  122.7 8.4 %collective-permute-start.25 = (bf16[1,128,128]{2,1,0:T(8,128)(2,1)S(1)}, bf16[1,128,128]{2,1,0:T(8,128)(2,1)S(1)}, u32[]{:S(2)}, u32[]{:S(2)}) collective-permute-start(bf16[1,128,128]{2,1,0:T(8,128)(2,1)S(1)} %get-tuple-element.60), channel_id=1, source_target_pairs={{0,11},{1,10},{2,9},{3,8},{4,15},{5,14},{6,13},{7,12},{8,3},{9,2},... | collective-permute-start | bytes 98312 | tf_op jit(solution)/shard_map/ppermute | solution.py:341
  122.8 9.6 %collective-permute-start.26 = (bf16[1,128,128]{2,1,0:T(8,128)(2,1)S(1)}, bf16[1,128,128]{2,1,0:T(8,128)(2,1)S(1)}, u32[]{:S(2)}, u32[]{:S(2)}) collective-permute-start(bf16[1,128,128]{2,1,0:T(8,128)(2,1)S(1)} %get-tuple-element.59), channel_id=1, source_target_pairs={{0,12},{1,13},{2,14},{3,15},{4,8},{5,9},{6,10},{7,11},{8,4},{9,5},... | collective-permute-start | bytes 98312 | tf_op jit(solution)/shard_map/ppermute | solution.py:341
  125.2 7.9 %collective-permute-start.27 = (bf16[1,128,128]{2,1,0:T(8,128)(2,1)S(1)}, bf16[1,128,128]{2,1,0:T(8,128)(2,1)S(1)}, u32[]{:S(2)}, u32[]{:S(2)}) collective-permute-start(bf16[1,128,128]{2,1,0:T(8,128)(2,1)S(1)} %get-tuple-element.58), channel_id=1, source_target_pairs={{0,13},{1,12},{2,15},{3,14},{4,9},{5,8},{6,11},{7,10},{8,5},{9,4},... | collective-permute-start | bytes 98312 | tf_op jit(solution)/shard_map/ppermute | solution.py:341
  126.7 6.7 %collective-permute-start.28 = (bf16[1,128,128]{2,1,0:T(8,128)(2,1)S(1)}, bf16[1,128,128]{2,1,0:T(8,128)(2,1)S(1)}, u32[]{:S(2)}, u32[]{:S(2)}) collective-permute-start(bf16[1,128,128]{2,1,0:T(8,128)(2,1)S(1)} %get-tuple-element.57), channel_id=1, source_target_pairs={{0,14},{1,15},{2,12},{3,13},{4,10},{5,11},{6,8},{7,9},{8,6},{9,7},... | collective-permute-start | bytes 98312 | tf_op jit(solution)/shard_map/ppermute | solution.py:341
  129.8 32.5 %collective-permute-start.29 = (bf16[1,128,128]{2,1,0:T(8,128)(2,1)S(1)}, bf16[1,128,128]{2,1,0:T(8,128)(2,1)S(1)}, u32[]{:S(2)}, u32[]{:S(2)}) collective-permute-start(bf16[1,128,128]{2,1,0:T(8,128)(2,1)S(1)} %get-tuple-element.56), channel_id=1, source_target_pairs={{0,15},{1,14},{2,13},{3,12},{4,11},{5,10},{6,9},{7,8},{8,7},{9,6},... | collective-permute-start | bytes 98312 | tf_op jit(solution)/shard_map/ppermute | solution.py:341
  131.1 4.0 %collective-permute-start.46 = (bf16[1,128,128]{2,1,0:T(8,128)(2,1)S(1)}, bf16[1,128,128]{2,1,0:T(8,128)(2,1)S(1)}, u32[]{:S(2)}, u32[]{:S(2)}) collective-permute-start(bf16[1,128,128]{2,1,0:T(8,128)(2,1)S(1)} %get-tuple-element.54), channel_id=1, source_target_pairs={{0,2},{1,3},{2,0},{3,1},{4,6},{5,7},{6,4},{7,5},{8,10},{9,11},{10,... | collective-permute-start | bytes 98312 | tf_op jit(solution)/shard_map/ppermute | solution.py:341
  132.4 4.2 %collective-permute-start.47 = (bf16[1,128,128]{2,1,0:T(8,128)(2,1)S(1)}, bf16[1,128,128]{2,1,0:T(8,128)(2,1)S(1)}, u32[]{:S(2)}, u32[]{:S(2)}) collective-permute-start(bf16[1,128,128]{2,1,0:T(8,128)(2,1)S(1)} %get-tuple-element.53), channel_id=1, source_target_pairs={{0,3},{1,2},{2,1},{3,0},{4,7},{5,6},{6,5},{7,4},{8,11},{9,10},{10,... | collective-permute-start | bytes 98312 | tf_op jit(solution)/shard_map/ppermute | solution.py:341
  133.2 4.7 %collective-permute-start.48 = (bf16[1,128,128]{2,1,0:T(8,128)(2,1)S(1)}, bf16[1,128,128]{2,1,0:T(8,128)(2,1)S(1)}, u32[]{:S(2)}, u32[]{:S(2)}) collective-permute-start(bf16[1,128,128]{2,1,0:T(8,128)(2,1)S(1)} %get-tuple-element.52), channel_id=1, source_target_pairs={{0,4},{1,5},{2,6},{3,7},{4,0},{5,1},{6,2},{7,3},{8,12},{9,13},{10,... | collective-permute-start | bytes 98312 | tf_op jit(solution)/shard_map/ppermute | solution.py:341
  133.3 6.3 %collective-permute-start.49 = (bf16[1,128,128]{2,1,0:T(8,128)(2,1)S(1)}, bf16[1,128,128]{2,1,0:T(8,128)(2,1)S(1)}, u32[]{:S(2)}, u32[]{:S(2)}) collective-permute-start(bf16[1,128,128]{2,1,0:T(8,128)(2,1)S(1)} %get-tuple-element.51), channel_id=1, source_target_pairs={{0,5},{1,4},{2,7},{3,6},{4,1},{5,0},{6,3},{7,2},{8,13},{9,12},{10,... | collective-permute-start | bytes 98312 | tf_op jit(solution)/shard_map/ppermute | solution.py:341
  135.1 5.5 %collective-permute-start.50 = (bf16[1,128,128]{2,1,0:T(8,128)(2,1)S(1)}, bf16[1,128,128]{2,1,0:T(8,128)(2,1)S(1)}, u32[]{:S(2)}, u32[]{:S(2)}) collective-permute-start(bf16[1,128,128]{2,1,0:T(8,128)(2,1)S(1)} %get-tuple-element.50), channel_id=1, source_target_pairs={{0,6},{1,7},{2,4},{3,5},{4,2},{5,3},{6,0},{7,1},{8,14},{9,15},{10,... | collective-permute-start | bytes 98312 | tf_op jit(solution)/shard_map/ppermute | solution.py:341
  136.5 6.2 %collective-permute-start.51 = (bf16[1,128,128]{2,1,0:T(8,128)(2,1)S(1)}, bf16[1,128,128]{2,1,0:T(8,128)(2,1)S(1)}, u32[]{:S(2)}, u32[]{:S(2)}) collective-permute-start(bf16[1,128,128]{2,1,0:T(8,128)(2,1)S(1)} %get-tuple-element.49), channel_id=1, source_target_pairs={{0,7},{1,6},{2,5},{3,4},{4,3},{5,2},{6,1},{7,0},{8,15},{9,14},{10,... | collective-permute-start | bytes 98312 | tf_op jit(solution)/shard_map/ppermute | solution.py:341
  137.9 6.5 %collective-permute-start.52 = (bf16[1,128,128]{2,1,0:T(8,128)(2,1)S(1)}, bf16[1,128,128]{2,1,0:T(8,128)(2,1)S(1)}, u32[]{:S(2)}, u32[]{:S(2)}) collective-permute-start(bf16[1,128,128]{2,1,0:T(8,128)(2,1)S(1)} %get-tuple-element.48), channel_id=1, source_target_pairs={{0,8},{1,9},{2,10},{3,11},{4,12},{5,13},{6,14},{7,15},{8,0},{9,1},... | collective-permute-start | bytes 98312 | tf_op jit(solution)/shard_map/ppermute | solution.py:341
  139.7 7.1 %collective-permute-start.53 = (bf16[1,128,128]{2,1,0:T(8,128)(2,1)S(1)}, bf16[1,128,128]{2,1,0:T(8,128)(2,1)S(1)}, u32[]{:S(2)}, u32[]{:S(2)}) collective-permute-start(bf16[1,128,128]{2,1,0:T(8,128)(2,1)S(1)} %get-tuple-element.47), channel_id=1, source_target_pairs={{0,9},{1,8},{2,11},{3,10},{4,13},{5,12},{6,15},{7,14},{8,1},{9,0},... | collective-permute-start | bytes 98312 | tf_op jit(solution)/shard_map/ppermute | solution.py:341
  140.6 7.4 %collective-permute-start.54 = (bf16[1,128,128]{2,1,0:T(8,128)(2,1)S(1)}, bf16[1,128,128]{2,1,0:T(8,128)(2,1)S(1)}, u32[]{:S(2)}, u32[]{:S(2)}) collective-permute-start(bf16[1,128,128]{2,1,0:T(8,128)(2,1)S(1)} %get-tuple-element.46), channel_id=1, source_target_pairs={{0,10},{1,11},{2,8},{3,9},{4,14},{5,15},{6,12},{7,13},{8,2},{9,3},... | collective-permute-start | bytes 98312 | tf_op jit(solution)/shard_map/ppermute | solution.py:341
  142.7 9.0 %collective-permute-start.55 = (bf16[1,128,128]{2,1,0:T(8,128)(2,1)S(1)}, bf16[1,128,128]{2,1,0:T(8,128)(2,1)S(1)}, u32[]{:S(2)}, u32[]{:S(2)}) collective-permute-start(bf16[1,128,128]{2,1,0:T(8,128)(2,1)S(1)} %get-tuple-element.45), channel_id=1, source_target_pairs={{0,11},{1,10},{2,9},{3,8},{4,15},{5,14},{6,13},{7,12},{8,3},{9,2},... | collective-permute-start | bytes 98312 | tf_op jit(solution)/shard_map/ppermute | solution.py:341
  144.4 8.3 %collective-permute-start.56 = (bf16[1,128,128]{2,1,0:T(8,128)(2,1)S(1)}, bf16[1,128,128]{2,1,0:T(8,128)(2,1)S(1)}, u32[]{:S(2)}, u32[]{:S(2)}) collective-permute-start(bf16[1,128,128]{2,1,0:T(8,128)(2,1)S(1)} %get-tuple-element.44), channel_id=1, source_target_pairs={{0,12},{1,13},{2,14},{3,15},{4,8},{5,9},{6,10},{7,11},{8,4},{9,5},... | collective-permute-start | bytes 98312 | tf_op jit(solution)/shard_map/ppermute | solution.py:341
  146.8 5.9 %collective-permute-start.57 = (bf16[1,128,128]{2,1,0:T(8,128)(2,1)S(1)}, bf16[1,128,128]{2,1,0:T(8,128)(2,1)S(1)}, u32[]{:S(2)}, u32[]{:S(2)}) collective-permute-start(bf16[1,128,128]{2,1,0:T(8,128)(2,1)S(1)} %get-tuple-element.43), channel_id=1, source_target_pairs={{0,13},{1,12},{2,15},{3,14},{4,9},{5,8},{6,11},{7,10},{8,5},{9,4},... | collective-permute-start | bytes 98312 | tf_op jit(solution)/shard_map/ppermute | solution.py:341
  148.0 6.7 %collective-permute-start.58 = (bf16[1,128,128]{2,1,0:T(8,128)(2,1)S(1)}, bf16[1,128,128]{2,1,0:T(8,128)(2,1)S(1)}, u32[]{:S(2)}, u32[]{:S(2)}) collective-permute-start(bf16[1,128,128]{2,1,0:T(8,128)(2,1)S(1)} %get-tuple-element.42), channel_id=1, source_target_pairs={{0,14},{1,15},{2,12},{3,13},{4,10},{5,11},{6,8},{7,9},{8,6},{9,7},... | collective-permute-start | bytes 98312 | tf_op jit(solution)/shard_map/ppermute | solution.py:341
  151.7 6.4 %collective-permute-start.59 = (bf16[1,128,128]{2,1,0:T(8,128)(2,1)S(1)}, bf16[1,128,128]{2,1,0:T(8,128)(2,1)S(1)}, u32[]{:S(2)}, u32[]{:S(2)}) collective-permute-start(bf16[1,128,128]{2,1,0:T(8,128)(2,1)S(1)} %get-tuple-element.41), channel_id=1, source_target_pairs={{0,15},{1,14},{2,13},{3,12},{4,11},{5,10},{6,9},{7,8},{8,7},{9,6},... | collective-permute-start | bytes 98312 | tf_op jit(solution)/shard_map/ppermute | solution.py:341
  (1 other events, 1.6 us)

commit v4 on v0

v4 whole, which is shorter than its diff:
```python
import functools
import math

import jax
import jax.numpy as jnp
import ml_dtypes
import numpy as np
from jax import lax
from jax.experimental import pallas as pl
from jax.experimental.pallas import tpu as pltpu
from jax.sharding import PartitionSpec as P

SUBPIX = 16
CHUNKS = 2
MIN_COLS = 64
BLOCK = 512
VMEM_LIMIT = 40 * 1024 * 1024


def packed_table(length, cols):
    half = length // 2
    freqs = np.arange(half, dtype=np.int32)
    positions = np.arange(length, dtype=np.int32)
    turns = freqs[:, None] * positions[None, :] % length
    angles = turns.astype(np.float32) * np.float32(2.0 * math.pi / length)
    factor = np.float32(1.0 / math.sqrt(length))
    cosine = np.cos(angles) * factor
    sine = np.sin(angles) * factor
    sine[0] = np.where(positions % 2 == 0, factor, -factor)
    blocks = np.stack([cosine.reshape(-1, cols, length), sine.reshape(-1, cols, length)], axis=1)
    return blocks.reshape(length, length).astype(ml_dtypes.bfloat16)


def cost(flops, bytes_accessed):
    return pl.CostEstimate(flops=flops, bytes_accessed=bytes_accessed, transcendentals=0)


def row_kernel(images_ref, table_ref, out_ref, total):
    loc_epochs, loc_rows, depth = images_ref.shape
    dests, _, lanes = out_ref.shape
    width = lanes // loc_epochs
    step = pl.program_id(0)
    pixels = images_ref[...].reshape(loc_epochs * loc_rows, depth)
    terms = jnp.dot(pixels, table_ref[...], preferred_element_type=jnp.float32)

    @pl.when(step == 0)
    def _():
        total[...] = terms

    @pl.when(step > 0)
    def _():
        total[...] += terms

    @pl.when(step == pl.num_programs(0) - 1)
    def _():
        for dest in range(dests):
            for loc in range(loc_epochs):
                part = total[loc * loc_rows : (loc + 1) * loc_rows, dest * width : (dest + 1) * width]
                out_ref[dest, :, loc * width : (loc + 1) * width] = part.astype(jnp.bfloat16)


def row_transform(images, table_t, chunk, chunks, row_count):
    loc_epochs, loc_rows, length = images.shape
    columns = length // chunks
    lanes = columns // row_count * loc_epochs
    steps = length // BLOCK
    rows = loc_epochs * loc_rows
    return pl.pallas_call(
        row_kernel,
        grid=(steps,),
        in_specs=[
            pl.BlockSpec((loc_epochs, loc_rows, BLOCK), lambda i: (0, 0, i)),
            pl.BlockSpec((BLOCK, columns), lambda i: (i, chunk)),
        ],
        out_specs=pl.BlockSpec((row_count, loc_rows, lanes), lambda i: (0, 0, 0)),
        out_shape=jax.ShapeDtypeStruct((row_count, loc_rows, lanes), jnp.bfloat16),
        scratch_shapes=[pltpu.VMEM((rows, columns), jnp.float32)],
        compiler_params=pltpu.CompilerParams(vmem_limit_bytes=VMEM_LIMIT),
        cost_estimate=cost(2 * rows * length * columns, 2 * length * columns + 4 * rows * length),
        name=f"row_transform_{chunk}",
    )(images, table_t)


def swap_halves(values):
    width = values.shape[1]
    if width % 128 == 0:
        return pltpu.roll(values, width // 2, axis=1)
    return jnp.concatenate([values[:, width // 2 :], values[:, : width // 2]], axis=1)


def stack_kernel(rates, loc_epochs, z_ref, table_ref, coef_ref, lane_ref, *out_refs):
    width = z_ref.shape[1] // loc_epochs
    cols = width // 2
    block = table_ref.shape[0]
    groups = block // width
    pairs = rates * loc_epochs
    step = pl.program_id(0)
    products = jnp.dot(table_ref[...], z_ref[...], preferred_element_type=jnp.float32)
    products = products.reshape(groups, 2, cols, loc_epochs * width)
    even = products[:, 0].reshape(groups * cols, loc_epochs * width)
    odd = products[:, 1].reshape(groups * cols, loc_epochs * width)
    first = lax.broadcasted_iota(jnp.int32, (groups * cols, width), 0) == 0
    for rate in range(rates):
        straight, crossed, lead = [0.0, 0.0], [0.0, 0.0], [0.0, 0.0]
        for epoch in range(loc_epochs):
            pair = rate * loc_epochs + epoch
            even_part = even[:, epoch * width : (epoch + 1) * width]
            odd_part = odd[:, epoch * width : (epoch + 1) * width]
            cos_row = coef_ref[:, pair : pair + 1]
            sin_row = coef_ref[:, pairs + pair : pairs + pair + 1]
            turned = (
                cos_row * even_part + sin_row * odd_part,
                cos_row * odd_part - sin_row * even_part,
            )
            factors = [lane_ref[kind * pairs + pair : kind * pairs + pair + 1, :] for kind in range(4)]
            for which in range(2):
                straight[which] += turned[which] * factors[0]
                crossed[which] += turned[which] * factors[1]
                lead[which] += even_part[:8] * factors[2 + which]
        even_sum = straight[0] + swap_halves(crossed[0])
        odd_sum = straight[1] + swap_halves(crossed[1])
        lead_sum = lead[0] + swap_halves(lead[1])
        even_sum = jnp.where(first & (step == 0), lead_sum[0:1], even_sum)
        both = jnp.stack(
            [part.reshape(groups, cols, width) for part in (even_sum, odd_sum)], axis=1
        )
        out_refs[rate][...] = both.reshape(block, width).astype(jnp.bfloat16)


def stack_rates(spectra, table, coefs, lane_factors, rates, loc_epochs, chunk):
    length, lanes = spectra.shape
    width = lanes // loc_epochs
    return pl.pallas_call(
        functools.partial(stack_kernel, rates, loc_epochs),
        grid=(length // BLOCK,),
        in_specs=[
            pl.BlockSpec(spectra.shape, lambda i: (0, 0)),
            pl.BlockSpec((BLOCK, length), lambda i: (i, 0)),
            pl.BlockSpec((BLOCK // 2, coefs.shape[1]), lambda i: (i, 0)),
            pl.BlockSpec(lane_factors.shape, lambda i: (0, 0)),
        ],
        out_specs=[pl.BlockSpec((BLOCK, width), lambda i: (i, 0))] * rates,
        out_shape=[jax.ShapeDtypeStruct((length, width), jnp.bfloat16)] * rates,
        compiler_params=pltpu.CompilerParams(vmem_limit_bytes=VMEM_LIMIT),
        cost_estimate=cost(2 * length * length * lanes, 2 * length * length + 4 * length * lanes),
        name=f"stack_rates_{chunk}",
    )(spectra, table, coefs, lane_factors)


CONTRACT_FIRST = (((0,), (0,)), ((), ()))


def inverse_kernel(own_ref, other_ref, table_ref, out_ref, sums):
    dests, _, loc_rows = out_ref.shape

    @pl.when(pl.program_id(0) == 0)
    def _():
        total = own_ref[...].astype(jnp.float32) + other_ref[...].astype(jnp.float32)
        sums[...] = total.T.astype(jnp.bfloat16)

    back = jnp.dot(sums[...], table_ref[...], preferred_element_type=jnp.float32)
    back = back.astype(jnp.bfloat16)
    for dest in range(dests):
        out_ref[dest] = back[:, dest * loc_rows : (dest + 1) * loc_rows]


def inverse_columns(own, other, table, row_count, chunk):
    length, width = own.shape
    loc_rows = length // row_count
    dests = BLOCK // loc_rows
    return pl.pallas_call(
        inverse_kernel,
        grid=(length // BLOCK,),
        in_specs=[
            pl.BlockSpec(own.shape, lambda i: (0, 0)),
            pl.BlockSpec(own.shape, lambda i: (0, 0)),
            pl.BlockSpec((length, BLOCK), lambda i: (0, i)),
        ],
        out_specs=pl.BlockSpec((dests, width, loc_rows), lambda i: (i, 0, 0)),
        out_shape=jax.ShapeDtypeStruct((row_count, width, loc_rows), jnp.bfloat16),
        scratch_shapes=[pltpu.VMEM((width, length), jnp.bfloat16)],
        compiler_params=pltpu.CompilerParams(vmem_limit_bytes=VMEM_LIMIT),
        cost_estimate=cost(2 * length * length * width, 2 * length * length + 6 * length * width),
        name=f"inverse_columns_{chunk}",
    )(own, other, table)


def image_kernel(has_partial, back_ref, table_ref, *refs):
    out_ref, left = refs[-2:]

    @pl.when(pl.program_id(0) == 0)
    def _():
        left[...] = back_ref[...].T

    pixels = jnp.dot(left[...], table_ref[...], preferred_element_type=jnp.float32)
    if has_partial:
        pixels = pixels + refs[0][0]
    out_ref[0] = pixels


def image_rows(back, table, partial, chunk):
    depth, rows = back.shape
    length = table.shape[0]
    image_spec = pl.BlockSpec((1, rows, BLOCK), lambda i: (0, 0, i))
    partials = [] if partial is None else [partial]
    return pl.pallas_call(
        functools.partial(image_kernel, partial is not None),
        grid=(length // BLOCK,),
        in_specs=[
            pl.BlockSpec(back.shape, lambda i: (0, 0)),
            pl.BlockSpec((depth, BLOCK), lambda i: (chunk, i)),
        ]
        + [image_spec] * len(partials),
        out_specs=image_spec,
        out_shape=jax.ShapeDtypeStruct((1, rows, length), jnp.float32),
        scratch_shapes=[pltpu.VMEM((rows, depth), jnp.bfloat16)],
        compiler_params=pltpu.CompilerParams(vmem_limit_bytes=VMEM_LIMIT),
        cost_estimate=cost(2 * rows * depth * length, 2 * depth * length + 8 * rows * length),
        name=f"image_rows_{chunk}",
    )(back, table, *partials)


def turn_angle(turns, whole):
    return (turns % whole).astype(jnp.float32) * (2.0 * math.pi / whole)


def row_factors(shift_y, length):
    half = length // 2
    freqs = jnp.arange(half, dtype=jnp.int32)[:, None]
    angles = turn_angle((freqs - half) * shift_y[None, :], SUBPIX * length)
    return jnp.concatenate(
        [
            jnp.where(freqs == 0, 1.0, 2.0 * jnp.cos(angles)),
            jnp.where(freqs == 0, 0.0, 2.0 * jnp.sin(angles)),
        ],
        axis=1,
    )


def column_factors(shift_y, shift_x, scale, first_freq, cols, length):
    half = length // 2
    shift_y, shift_x = shift_y[:, None], shift_x[:, None]
    lane = jnp.arange(2 * cols, dtype=jnp.int32)[None, :]
    freqs = first_freq + lane % cols
    is_sine = lane >= cols
    paired = freqs == 0
    zero_col = paired & ~is_sine
    angles = turn_angle(shift_x * (freqs - half), SUBPIX * length)
    ramp_cos = jnp.where(paired, scale, 2.0 * scale * jnp.cos(angles))
    ramp_sin = jnp.where(paired, 0.0, 2.0 * scale * jnp.sin(angles))
    ramp_sin = jnp.where(is_sine, ramp_sin, -ramp_sin)
    cos_x = jnp.cos(turn_angle(shift_x, 2 * SUBPIX))
    cos_y = jnp.cos(turn_angle(shift_y, 2 * SUBPIX))
    cos_xy = jnp.cos(turn_angle(shift_x + shift_y, 2 * SUBPIX))
    main = jnp.where(zero_col, cos_y, cos_xy)
    lead = jnp.where(zero_col, 1.0, cos_x)
    return jnp.concatenate([main * ramp_cos, main * ramp_sin, lead * ramp_cos, lead * ramp_sin])


def local(images, rate_vectors, epoch_times):
    loc_epochs, loc_rows, length = images.shape
    row_count = lax.axis_size("row")
    row_pos, core = lax.axis_index("row"), lax.axis_index("epoch")
    rates, epochs = rate_vectors.shape[0], epoch_times.shape[0]
    chunks = max(1, min(CHUNKS, length // 2 // row_count // MIN_COLS))
    cols = length // 2 // row_count // chunks
    table = packed_table(length, cols)
    table_t = jnp.asarray(np.ascontiguousarray(table.T))
    table = jnp.asarray(table)
    period = SUBPIX * length
    own_times = lax.dynamic_slice_in_dim(epoch_times, core * loc_epochs, loc_epochs)
    own_first = jnp.where(core == 0, rate_vectors, rate_vectors[::-1])
    shift_y = (own_first[:, 0:1] * own_times[None, :] % period).reshape(-1)
    shift_x = (own_first[:, 1:2] * own_times[None, :] % period).reshape(-1)
    coefs = row_factors(shift_y, length)
    scale = 1.0 / math.sqrt(epochs)

    def exchange(values):
        return lax.all_to_all(values, "row", 0, 0, tiled=True)

    spectra = [
        exchange(row_transform(images, table_t, chunk, chunks, row_count))
        for chunk in range(chunks)
    ]
    backs = []
    for chunk in range(chunks):
        first_freq = (chunk * row_count + row_pos) * cols
        factors = column_factors(shift_y, shift_x, scale, first_freq, cols, length)
        own, other = stack_rates(
            spectra[chunk].reshape(length, -1), table, coefs, factors, rates, loc_epochs, chunk
        )
        other = lax.ppermute(other, "epoch", [(0, 1), (1, 0)])
        backs.append(exchange(inverse_columns(own, other, table, row_count, chunk)))
    result = None
    for chunk in range(chunks):
        result = image_rows(backs[chunk].reshape(-1, loc_rows), table, result, chunk)
    return result


def solution(mesh):
    in_specs = (P(("group", "epoch"), "row", None), P(), P())
    out_specs = P(("group", "epoch"), "row", None)
    return jax.shard_map(local, mesh=mesh, in_specs=in_specs, out_specs=out_specs, check_vma=False)
```

time: 458 us -> 121 us (0.26); the launches traced: 450 us -> 120 us
  other arithmetic: 189 us -> 0.67 us
  matrix products: 58.5 us -> 0 us
  local copies, waits for them, and re-layouts: 81.8 us -> 26.9 us
  waiting for transfers between devices: 93.3 us -> 40.9 us
  Pallas kernels: 0 us -> 30.7 us
  blocking collectives: 14.7 us -> 0 us
  starting transfers between devices: 10.9 us -> 20.8 us
    convert_element_type x4 -> x0, other arithmetic: 154 us -> none  [the longest x1 71.3 us: dft_tables(): (jnp.cos(angles) * factor).astype(jnp.bfloat16)]
    dot_general x4 -> x0, matrix products: 58.5 us -> none  [the longest x1 22.7 us: local(): jnp.einsum('vetr,wru->wvteu', gathered, stacked, preferred_element_type=j...]
    all_to_all x2 -> x4, waiting for transfers between devices: 93.3 us -> 37.1 us  [exchange(): return lax.all_to_all(values, 'row', 0, 0, tiled=True)]
    all_to_all x8 -> x0, local copies, waits for them, and re-layouts: 31.5 us -> none  [the longest x3 22.2 us: local(): lax.all_to_all(row_spectrum, 'row', split_axis=0, concat_axis=3, tiled=True)]
    pallas_call x0 -> x8, Pallas kernels: none -> 30.7 us  [the longest x2 9.29 us: row_transform(): pl.pallas_call(row_kernel, grid=(steps,), in_specs=[pl.BlockSpec((loc_epo...]
    reduce_sum x2 -> x0, other arithmetic: 24.9 us -> none  [one_rate(): summed_re = jnp.sum(real_part * ramp_re - imag_part * ramp_im, axis=1)]
    convert_element_type x1 -> x0, local copies, waits for them, and re-layouts: 19.1 us -> none  [local(): row_spectrum = (row_terms * sign_wide).astype(jnp.bfloat16)]
    another operation x5 -> x0, local copies, waits for them, and re-layouts: 16.9 us -> none  [the longest x1 14 us: local(): jnp.stack([real_part, imag_part], axis=2).astype(jnp.bfloat16)]
  transfers between devices with their start and end apart: 2 -> 6, of which waited for: 1 -> 5; matrix products, arithmetic and copies ran while one was open for 16% -> 1% of each run, Pallas kernels for 0% -> 18%
where the time goes in v4:
time: 121 us; the launch traced here: 120 us
  waiting for transfers between devices  40.9 us (34%)
  Pallas kernels  30.7 us (25%)
  local copies, waits for them, and re-layouts  26.9 us (22%)
  starting transfers between devices  20.8 us (17%)
    all_to_all x4, waiting for transfers between devices, exchange(): return lax.all_to_all(values, 'row', 0, 0, tiled=True)  37.1 us
    unnamed x24, local copies, waits for them, and re-layouts  26.2 us
    all_to_all x4, starting transfers between devices, exchange(): return lax.all_to_all(values, 'row', 0, 0, tiled=True)  20.6 us
    pallas_call x2, Pallas kernels, row_transform(): pl.pallas_call(row_kernel, grid=(steps,), in_specs=[pl.BlockSpec((loc_epo...  9.29 us
    pallas_call x2, Pallas kernels, stack_rates(): pl.pallas_call(functools.partial(stack_kernel, rates, loc_epochs), grid=(...  8.66 us
    pallas_call x2, Pallas kernels, inverse_columns(): pl.pallas_call(inverse_kernel, grid=(length // BLOCK,), in_specs=[pl.Bloc...  6.8 us
    pallas_call x2, Pallas kernels, image_rows(): pl.pallas_call(functools.partial(image_kernel, partial is not None), grid...  5.95 us
    ppermute x2, waiting for transfers between devices, local(): other = lax.ppermute(other, 'epoch', [(0, 1), (1, 0)])  3.79 us
  transfers between devices with their start and end apart: 6, of which 5 were waited for; matrix products, arithmetic and copies ran while one was open for 1% of the time, Pallas kernels for 18%

profile of v4, /device:TPU:0, one launch (start us, length us, event | category | flops | bytes accessed | tf_op | source)
XLA Modules:
  0.0 120.1 jit_solution(3625565924360843782)
XLA Ops:
  0.0 0.0 copy-start.5
  0.0 3.4 %copy-done.5 = bf16[2048,2048]{1,0:T(8,128)(2,1)S(1)} copy-done((bf16[2048,2048]{1,0:T(8,128)(2,1)S(1)}, bf16[2048,2048]{1,0:T(8,128)(2,1)}, u32[]{:S(2)}) %copy-start.5) | copy-done | bytes 8388632
  3.4 0.0 copy-start.7
  3.4 1.6 %copy-done.7 = bf16[2,256,2048]{2,1,0:T(8,128)(2,1)S(1)} copy-done((bf16[2,256,2048]{2,1,0:T(8,128)(2,1)S(1)}, bf16[2,256,2048]{2,1,0:T(8,128)(2,1)}, u32[]{:S(2)}) %copy-start.7) | copy-done | bytes 2097176
  5.0 5.1 %row_transform_0.1 = bf16[8,256,256]{2,1,0:T(8,128)(2,1)} custom-call(bf16[2,256,2048]{2,1,0:T(8,128)(2,1)S(1)} %copy-done.7, bf16[2048,2048]{1,0:T(8,128)(2,1)S(1)} %copy-done.5), custom_call_target="tpu_custom_call" | custom-call | flops 2147483648 | bytes 8388608 | tf_op jit(solution)/shard_map/row_transform_0/pallas_call | solution.py:68
  10.1 0.0 copy-start.10
  10.1 0.0 copy-start.11
  10.1 0.0 copy-start.8
  10.1 7.4 %all-to-all-start.2 = ((bf16[8,256,256]{2,1,0:T(8,128)(2,1)}), bf16[8,256,256]{2,1,0:T(8,128)(2,1)}, u32[]{:S(2)}, u32[]{:S(2)}) async-start(bf16[8,256,256]{2,1,0:T(8,128)(2,1)} %row_transform_0.1), calls=%async_computation.2 | async-start | bytes 2097152 | tf_op jit(solution)/shard_map/all_to_all | solution.py:279
  17.5 0.0 copy-done.10
  17.5 0.0 copy-done.11
  17.5 0.1 dynamic_slice.3
  17.6 0.2 slice_reduce_fusion
  17.8 0.1 broadcast_multiply_fusion
  17.9 0.1 mul.192
  17.9 0.1 mul.180
  18.0 0.1 fusion.11
  18.1 0.2 multiply_select_fusion.2
  18.3 0.2 copy.6.coef_ref
  18.6 0.0 copy-done.8
  18.6 0.0 copy-start.6
  18.6 3.4 %copy-done.6 = bf16[2048,2048]{1,0:T(8,128)(2,1)S(1)} copy-done((bf16[2048,2048]{1,0:T(8,128)(2,1)S(1)}, bf16[2048,2048]{1,0:T(8,128)(2,1)}, u32[]{:S(2)}) %copy-start.6) | copy-done | bytes 8388632
  22.0 4.2 %row_transform_1.1 = bf16[8,256,256]{2,1,0:T(8,128)(2,1)S(1)} custom-call(bf16[2,256,2048]{2,1,0:T(8,128)(2,1)S(1)} %copy-done.8, bf16[2048,2048]{1,0:T(8,128)(2,1)S(1)} %copy-done.6), custom_call_target="tpu_custom_call" | custom-call | flops 2147483648 | bytes 8388608 | tf_op jit(solution)/shard_map/row_transform_1/pallas_call | solution.py:68
  26.2 0.0 copy-start.9
  26.2 1.0 copy-done.9
  27.1 16.2 %all-to-all-done.2 = bf16[8,256,256]{2,1,0:T(8,128)(2,1)} async-done(((bf16[8,256,256]{2,1,0:T(8,128)(2,1)}), bf16[8,256,256]{2,1,0:T(8,128)(2,1)}, u32[]{:S(2)}, u32[]{:S(2)}) %all-to-all-start.2) | async-done | bytes 1048608 | tf_op jit(solution)/shard_map/all_to_all | solution.py:279
  43.4 3.6 %all-to-all-start = ((bf16[8,256,256]{2,1,0:T(8,128)(2,1)}), bf16[8,256,256]{2,1,0:T(8,128)(2,1)S(1)}, u32[]{:S(2)}, u32[]{:S(2)}) async-start(bf16[8,256,256]{2,1,0:T(8,128)(2,1)} %copy-done.9), calls=%async_computation | async-start | bytes 2097152 | tf_op jit(solution)/shard_map/all_to_all | solution.py:279
  47.0 0.1 fusion.14
  47.1 0.1 select_multiply_fusion.3
  47.2 0.0 copy-start
  47.2 3.4 %copy-done = bf16[2048,2048]{1,0:T(8,128)(2,1)S(1)} copy-done((bf16[2048,2048]{1,0:T(8,128)(2,1)S(1)}, bf16[2048,2048]{1,0:T(8,128)(2,1)}, u32[]{:S(2)}) %copy-start) | copy-done | bytes 8388632
  50.6 4.9 %stack_rates_0.1 = (bf16[2048,128]{1,0:T(8,128)(2,1)S(1)}, bf16[2048,128]{1,0:T(8,128)(2,1)S(1)}) custom-call(bf16[2048,256]{1,0:T(8,128)(2,1)} %bitcast.2.z_ref, bf16[2048,2048]{1,0:T(8,128)(2,1)S(1)} %copy-done, f32[1024,8]{1,0:T(8,128)S(1)} %copy.6.coef_ref, f32[16,128]{1,0:T(8,128)S(1)} %pad_maximum_fusion.2.lane_ref), custom_call_target="tpu_custom_call" | custom-call | flops 2147483648 | bytes 10485760 | tf_op jit(solution)/shard_map/stack_rates_0/pallas_call | solution.py:133
  55.6 0.1 collective-permute-start.1
  55.7 1.9 %collective-permute-done.1.other_ref = bf16[2048,128]{1,0:T(8,128)(2,1)S(1)} collective-permute-done((bf16[2048,128]{1,0:T(8,128)(2,1)S(1)}, bf16[2048,128]{1,0:T(8,128)(2,1)S(1)}, u32[]{:S(2)}, u32[]{:S(2)}) %collective-permute-start.1) | collective-permute-done | bytes 524320 | tf_op jit(solution)/shard_map/ppermute | solution.py:292
  57.5 3.4 %inverse_columns_0.1 = bf16[8,128,256]{2,1,0:T(8,128)(2,1)} custom-call(bf16[2048,128]{1,0:T(8,128)(2,1)S(1)} %get-tuple-element.11.own_ref, bf16[2048,128]{1,0:T(8,128)(2,1)S(1)} %collective-permute-done.1.other_ref, bf16[2048,2048]{1,0:T(8,128)(2,1)S(1)} %copy-done), custom_call_target="tpu_custom_call" | custom-call | flops 1073741824 | bytes 9961472 | tf_op jit(solution)/shard_map/inverse_columns_0/pallas_call | solution.py:171
  60.9 12.0 %all-to-all-done = bf16[8,256,256]{2,1,0:T(8,128)(2,1)S(1)} async-done(((bf16[8,256,256]{2,1,0:T(8,128)(2,1)}), bf16[8,256,256]{2,1,0:T(8,128)(2,1)S(1)}, u32[]{:S(2)}, u32[]{:S(2)}) %all-to-all-start) | async-done | bytes 1048608 | tf_op jit(solution)/shard_map/all_to_all | solution.py:279
  72.9 3.6 %all-to-all-start.3 = ((bf16[8,128,256]{2,1,0:T(8,128)(2,1)}), bf16[8,128,256]{2,1,0:T(8,128)(2,1)S(1)}, u32[]{:S(2)}, u32[]{:S(2)}) async-start(bf16[8,128,256]{2,1,0:T(8,128)(2,1)} %inverse_columns_0.1), calls=%async_computation.3 | async-start | bytes 1048576 | tf_op jit(solution)/shard_map/all_to_all | solution.py:279
  76.5 0.0 copy-start.1
  76.6 3.4 %copy-done.1 = bf16[2048,2048]{1,0:T(8,128)(2,1)S(1)} copy-done((bf16[2048,2048]{1,0:T(8,128)(2,1)S(1)}, bf16[2048,2048]{1,0:T(8,128)(2,1)}, u32[]{:S(2)}) %copy-start.1) | copy-done | bytes 8388632
  79.9 3.7 %stack_rates_1.1 = (bf16[2048,128]{1,0:T(8,128)(2,1)S(1)}, bf16[2048,128]{1,0:T(8,128)(2,1)S(1)}) custom-call(bf16[2048,256]{1,0:T(8,128)(2,1)S(1)} %bitcast.4, bf16[2048,2048]{1,0:T(8,128)(2,1)S(1)} %copy-done.1, f32[1024,8]{1,0:T(8,128)S(1)} %copy.6.coef_ref, f32[16,128]{1,0:T(8,128)S(1)} %pad_maximum_fusion.1.lane_ref), custom_call_target="tpu_custom_call" | custom-call | flops 2147483648 | bytes 10485760 | tf_op jit(solution)/shard_map/stack_rates_1/pallas_call | solution.py:133
  83.7 0.1 collective-permute-start
  83.7 1.9 %collective-permute-done.other_ref = bf16[2048,128]{1,0:T(8,128)(2,1)S(1)} collective-permute-done((bf16[2048,128]{1,0:T(8,128)(2,1)S(1)}, bf16[2048,128]{1,0:T(8,128)(2,1)S(1)}, u32[]{:S(2)}, u32[]{:S(2)}) %collective-permute-start) | collective-permute-done | bytes 524320 | tf_op jit(solution)/shard_map/ppermute | solution.py:292
  85.6 0.0 copy-start.2
  85.6 3.4 %copy-done.2 = bf16[2048,2048]{1,0:T(8,128)(2,1)S(1)} copy-done((bf16[2048,2048]{1,0:T(8,128)(2,1)S(1)}, bf16[2048,2048]{1,0:T(8,128)(2,1)}, u32[]{:S(2)}) %copy-start.2) | copy-done | bytes 8388632
  89.0 3.4 %inverse_columns_1.1 = bf16[8,128,256]{2,1,0:T(8,128)(2,1)} custom-call(bf16[2048,128]{1,0:T(8,128)(2,1)S(1)} %get-tuple-element.9.own_ref, bf16[2048,128]{1,0:T(8,128)(2,1)S(1)} %collective-permute-done.other_ref, bf16[2048,2048]{1,0:T(8,128)(2,1)S(1)} %copy-done.2), custom_call_target="tpu_custom_call" | custom-call | flops 1073741824 | bytes 9961472 | tf_op jit(solution)/shard_map/inverse_columns_1/pallas_call | solution.py:171
  92.4 0.0 all-to-all-done.3
  92.4 6.0 %all-to-all-start.1 = ((bf16[8,128,256]{2,1,0:T(8,128)(2,1)}), bf16[8,128,256]{2,1,0:T(8,128)(2,1)S(1)}, u32[]{:S(2)}, u32[]{:S(2)}) async-start(bf16[8,128,256]{2,1,0:T(8,128)(2,1)} %inverse_columns_1.1), calls=%async_computation.1 | async-start | bytes 1048576 | tf_op jit(solution)/shard_map/all_to_all | solution.py:279
  98.4 0.0 copy-start.3
  98.4 3.4 %copy-done.3 = bf16[2048,2048]{1,0:T(8,128)(2,1)S(1)} copy-done((bf16[2048,2048]{1,0:T(8,128)(2,1)S(1)}, bf16[2048,2048]{1,0:T(8,128)(2,1)}, u32[]{:S(2)}) %copy-start.3) | copy-done | bytes 8388632
  101.8 2.5 %image_rows_0.1.refs_0_ = f32[1,256,2048]{2,1,0:T(8,128)S(1)} custom-call(bf16[1024,256]{1,0:T(8,128)(2,1)S(1)} %bitcast.6, bf16[2048,2048]{1,0:T(8,128)(2,1)S(1)} %copy-done.3), custom_call_target="tpu_custom_call" | custom-call | flops 1073741824 | bytes 8388608 | tf_op jit(solution)/shard_map/image_rows_0/pallas_call | solution.py:206
  104.3 8.9 %all-to-all-done.1 = bf16[8,128,256]{2,1,0:T(8,128)(2,1)S(1)} async-done(((bf16[8,128,256]{2,1,0:T(8,128)(2,1)}), bf16[8,128,256]{2,1,0:T(8,128)(2,1)S(1)}, u32[]{:S(2)}, u32[]{:S(2)}) %all-to-all-start.1) | async-done | bytes 524320 | tf_op jit(solution)/shard_map/all_to_all | solution.py:279
  113.2 0.0 copy-start.4
  113.2 3.4 %copy-done.4 = bf16[2048,2048]{1,0:T(8,128)(2,1)S(1)} copy-done((bf16[2048,2048]{1,0:T(8,128)(2,1)S(1)}, bf16[2048,2048]{1,0:T(8,128)(2,1)}, u32[]{:S(2)}) %copy-start.4) | copy-done | bytes 8388632
  116.6 3.5 %image_rows_1.1 = f32[1,256,2048]{2,1,0:T(8,128)} custom-call(bf16[1024,256]{1,0:T(8,128)(2,1)S(1)} %bitcast.5, bf16[2048,2048]{1,0:T(8,128)(2,1)S(1)} %copy-done.4, f32[1,256,2048]{2,1,0:T(8,128)S(1)} %image_rows_0.1.refs_0_), custom_call_target="tpu_custom_call" | custom-call | flops 1073741824 | bytes 8388608 | tf_op jit(solution)/shard_map/image_rows_1/pallas_call | solution.py:206
  (12 shorter events, 0.2 us)
Async XLA Ops:
  0.0 3.4 %copy-start.5 = (bf16[2048,2048]{1,0:T(8,128)(2,1)S(1)}, bf16[2048,2048]{1,0:T(8,128)(2,1)}, u32[]{:S(2)}) copy-start(bf16[2048,2048]{1,0:T(8,128)(2,1)} %constant.135.clone.table_ref) | copy-start | bytes 25165828
  3.4 1.6 %copy-start.7 = (bf16[2,256,2048]{2,1,0:T(8,128)(2,1)S(1)}, bf16[2,256,2048]{2,1,0:T(8,128)(2,1)}, u32[]{:S(2)}) copy-start(bf16[2,256,2048]{2,1,0:T(8,128)(2,1)} %images_ref.3) | copy-start | bytes 6291460
  10.1 7.4 %copy-start.10 = (s32[2,2]{1,0:T(2,128)S(1)}, s32[2,2]{1,0:T(2,128)}, u32[]{:S(2)}) copy-start(s32[2,2]{1,0:T(2,128)} %param.6) | copy-start | bytes 52
  10.1 7.4 %copy-start.11 = (s32[4]{0:T(128)S(1)}, s32[4]{0:T(128)}, u32[]{:S(2)}) copy-start(s32[4]{0:T(128)} %param.7) | copy-start | bytes 52
  10.1 8.5 %copy-start.8 = (bf16[2,256,2048]{2,1,0:T(8,128)(2,1)S(1)}, bf16[2,256,2048]{2,1,0:T(8,128)(2,1)}, u32[]{:S(2)}) copy-start(bf16[2,256,2048]{2,1,0:T(8,128)(2,1)} %images_ref.3) | copy-start | bytes 6291460
  10.1 33.3 %all-to-all-start.2 = ((bf16[8,256,256]{2,1,0:T(8,128)(2,1)}), bf16[8,256,256]{2,1,0:T(8,128)(2,1)}, u32[]{:S(2)}, u32[]{:S(2)}) async-start(bf16[8,256,256]{2,1,0:T(8,128)(2,1)} %row_transform_0.1), calls=%async_computation.2 | async-start | bytes 2097152 | tf_op jit(solution)/shard_map/all_to_all | solution.py:279
  18.6 3.4 %copy-start.6 = (bf16[2048,2048]{1,0:T(8,128)(2,1)S(1)}, bf16[2048,2048]{1,0:T(8,128)(2,1)}, u32[]{:S(2)}) copy-start(bf16[2048,2048]{1,0:T(8,128)(2,1)} %constant.135.clone.table_ref) | copy-start | bytes 25165828
  26.2 1.0 copy-start.9
  43.4 29.5 %all-to-all-start = ((bf16[8,256,256]{2,1,0:T(8,128)(2,1)}), bf16[8,256,256]{2,1,0:T(8,128)(2,1)S(1)}, u32[]{:S(2)}, u32[]{:S(2)}) async-start(bf16[8,256,256]{2,1,0:T(8,128)(2,1)} %copy-done.9), calls=%async_computation | async-start | bytes 2097152 | tf_op jit(solution)/shard_map/all_to_all | solution.py:279
  47.2 3.4 %copy-start = (bf16[2048,2048]{1,0:T(8,128)(2,1)S(1)}, bf16[2048,2048]{1,0:T(8,128)(2,1)}, u32[]{:S(2)}) copy-start(bf16[2048,2048]{1,0:T(8,128)(2,1)} %constant.136.clone.table_ref) | copy-start | bytes 25165828
  55.6 2.0 %collective-permute-start.1 = (bf16[2048,128]{1,0:T(8,128)(2,1)S(1)}, bf16[2048,128]{1,0:T(8,128)(2,1)S(1)}, u32[]{:S(2)}, u32[]{:S(2)}) collective-permute-start(bf16[2048,128]{1,0:T(8,128)(2,1)S(1)} %get-tuple-element.12), channel_id=1, source_target_pairs={{0,1},{1,0},{2,3},{3,2},{4,5},{5,4},{6,7},{7,6},{8,9},{9,8},{10,11... | collective-permute-start | bytes 1572872 | tf_op jit(solution)/shard_map/ppermute | solution.py:292
  72.9 19.5 %all-to-all-start.3 = ((bf16[8,128,256]{2,1,0:T(8,128)(2,1)}), bf16[8,128,256]{2,1,0:T(8,128)(2,1)S(1)}, u32[]{:S(2)}, u32[]{:S(2)}) async-start(bf16[8,128,256]{2,1,0:T(8,128)(2,1)} %inverse_columns_0.1), calls=%async_computation.3 | async-start | bytes 1048576 | tf_op jit(solution)/shard_map/all_to_all | solution.py:279
  76.5 3.4 %copy-start.1 = (bf16[2048,2048]{1,0:T(8,128)(2,1)S(1)}, bf16[2048,2048]{1,0:T(8,128)(2,1)}, u32[]{:S(2)}) copy-start(bf16[2048,2048]{1,0:T(8,128)(2,1)} %constant.136.clone.table_ref) | copy-start | bytes 25165828
  83.7 2.0 %collective-permute-start = (bf16[2048,128]{1,0:T(8,128)(2,1)S(1)}, bf16[2048,128]{1,0:T(8,128)(2,1)S(1)}, u32[]{:S(2)}, u32[]{:S(2)}) collective-permute-start(bf16[2048,128]{1,0:T(8,128)(2,1)S(1)} %get-tuple-element.10), channel_id=1, source_target_pairs={{0,1},{1,0},{2,3},{3,2},{4,5},{5,4},{6,7},{7,6},{8,9},{9,8},{10,11... | collective-permute-start | bytes 1572872 | tf_op jit(solution)/shard_map/ppermute | solution.py:292
  85.6 3.4 %copy-start.2 = (bf16[2048,2048]{1,0:T(8,128)(2,1)S(1)}, bf16[2048,2048]{1,0:T(8,128)(2,1)}, u32[]{:S(2)}) copy-start(bf16[2048,2048]{1,0:T(8,128)(2,1)} %constant.136.clone.table_ref) | copy-start | bytes 25165828
  92.4 20.8 %all-to-all-start.1 = ((bf16[8,128,256]{2,1,0:T(8,128)(2,1)}), bf16[8,128,256]{2,1,0:T(8,128)(2,1)S(1)}, u32[]{:S(2)}, u32[]{:S(2)}) async-start(bf16[8,128,256]{2,1,0:T(8,128)(2,1)} %inverse_columns_1.1), calls=%async_computation.1 | async-start | bytes 1048576 | tf_op jit(solution)/shard_map/all_to_all | solution.py:279
  98.4 3.4 %copy-start.3 = (bf16[2048,2048]{1,0:T(8,128)(2,1)S(1)}, bf16[2048,2048]{1,0:T(8,128)(2,1)}, u32[]{:S(2)}) copy-start(bf16[2048,2048]{1,0:T(8,128)(2,1)} %constant.136.clone.table_ref) | copy-start | bytes 25165828
  113.2 3.4 %copy-start.4 = (bf16[2048,2048]{1,0:T(8,128)(2,1)S(1)}, bf16[2048,2048]{1,0:T(8,128)(2,1)}, u32[]{:S(2)}) copy-start(bf16[2048,2048]{1,0:T(8,128)(2,1)} %constant.136.clone.table_ref) | copy-start | bytes 25165828

commit v5 on v4

--- a/solution.py
+++ b/solution.py
@@ -14,7 +14,7 @@
 CHUNKS = 2
 MIN_COLS = 64
 BLOCK = 512
-VMEM_LIMIT = 40 * 1024 * 1024
+VMEM_LIMIT = 58 * 1024 * 1024
 
 
 def packed_table(length, cols):

time: 121 us -> 118 us (0.975)
  local copies, waits for them, and re-layouts: 26.9 us -> 3.85 us
  Pallas kernels: 30.7 us -> 51.3 us
  waiting for transfers between devices: 40.9 us -> 39.6 us
    unnamed x24 -> x16, local copies, waits for them, and re-layouts: 26.2 us -> 2.39 us
    pallas_call x2, Pallas kernels: 8.66 us -> 14.6 us  [stack_rates(): pl.pallas_call(functools.partial(stack_kernel, rates, loc_epochs), grid=(...]
    pallas_call x2, Pallas kernels: 6.8 us -> 12.2 us  [inverse_columns(): pl.pallas_call(inverse_kernel, grid=(length // BLOCK,), in_specs=[pl.Bloc...]
    pallas_call x2, Pallas kernels: 5.95 us -> 11.1 us  [image_rows(): pl.pallas_call(functools.partial(image_kernel, partial is not None), grid...]
    pallas_call x2, Pallas kernels: 9.29 us -> 13.4 us  [row_transform(): pl.pallas_call(row_kernel, grid=(steps,), in_specs=[pl.BlockSpec((loc_epo...]
    all_to_all x4, waiting for transfers between devices: 37.1 us -> 35.4 us  [exchange(): return lax.all_to_all(values, 'row', 0, 0, tiled=True)]
  transfers between devices with their start and end apart: 6 -> 6, of which waited for: 5 -> 5; matrix products, arithmetic and copies ran while one was open for 1% -> 3% of each run, Pallas kernels for 18% -> 33%
where the time goes in v5:
time: 118 us; the launch traced here: 117 us
  Pallas kernels  51.3 us (43%)
  waiting for transfers between devices  39.6 us (34%)
  starting transfers between devices  20.6 us (17%)
  local copies, waits for them, and re-layouts  3.85 us (3%)
  other arithmetic  1.85 us (2%)
    all_to_all x4, waiting for transfers between devices, exchange(): return lax.all_to_all(values, 'row', 0, 0, tiled=True)  35.4 us
    all_to_all x4, starting transfers between devices, exchange(): return lax.all_to_all(values, 'row', 0, 0, tiled=True)  20.6 us
    pallas_call x2, Pallas kernels, stack_rates(): pl.pallas_call(functools.partial(stack_kernel, rates, loc_epochs), grid=(...  14.6 us
    pallas_call x2, Pallas kernels, row_transform(): pl.pallas_call(row_kernel, grid=(steps,), in_specs=[pl.BlockSpec((loc_epo...  13.4 us
    pallas_call x2, Pallas kernels, inverse_columns(): pl.pallas_call(inverse_kernel, grid=(length // BLOCK,), in_specs=[pl.Bloc...  12.2 us
    pallas_call x2, Pallas kernels, image_rows(): pl.pallas_call(functools.partial(image_kernel, partial is not None), grid...  11.1 us
    ppermute x2, waiting for transfers between devices, local(): other = lax.ppermute(other, 'epoch', [(0, 1), (1, 0)])  4.24 us
    unnamed x16, local copies, waits for them, and re-layouts  2.39 us
  transfers between devices with their start and end apart: 6, of which 5 were waited for; matrix products, arithmetic and copies ran while one was open for 3% of the time, Pallas kernels for 33%

profile of v5, /device:TPU:0, one launch (start us, length us, event | category | flops | bytes accessed | tf_op | source)
XLA Modules:
  0.0 117.2 jit_solution(462258330007955012)
XLA Ops:
  0.0 6.7 %row_transform_0.1 = bf16[8,256,256]{2,1,0:T(8,128)(2,1)} custom-call(bf16[2,256,2048]{2,1,0:T(8,128)(2,1)} %images_ref.3, bf16[2048,2048]{1,0:T(8,128)(2,1)} %constant.135.clone.table_ref), custom_call_target="tpu_custom_call" | custom-call | flops 2147483648 | bytes 8388608 | tf_op jit(solution)/shard_map/row_transform_0/pallas_call | solution.py:68
  6.7 0.0 copy-start.6
  6.7 0.0 copy-start.7
  6.7 7.4 %all-to-all-start.2 = ((bf16[8,256,256]{2,1,0:T(8,128)(2,1)}), bf16[8,256,256]{2,1,0:T(8,128)(2,1)S(1)}, u32[]{:S(2)}, u32[]{:S(2)}) async-start(bf16[8,256,256]{2,1,0:T(8,128)(2,1)} %row_transform_0.1), calls=%async_computation.2 | async-start | bytes 2097152 | tf_op jit(solution)/shard_map/all_to_all | solution.py:279
  14.1 0.0 copy-done.6
  14.1 0.0 copy-done.7
  14.1 0.1 dynamic_slice.3
  14.2 0.2 slice_reduce_fusion
  14.4 0.1 broadcast_multiply_fusion
  14.5 0.1 mul.192
  14.5 0.1 mul.180
  14.6 0.1 fusion.11
  14.7 0.2 multiply_select_fusion.2
  14.9 1.0 copy.6.coef_ref
  16.0 6.7 %row_transform_1.1 = bf16[8,256,256]{2,1,0:T(8,128)(2,1)} custom-call(bf16[2,256,2048]{2,1,0:T(8,128)(2,1)} %images_ref.3, bf16[2048,2048]{1,0:T(8,128)(2,1)} %constant.135.clone.table_ref), custom_call_target="tpu_custom_call" | custom-call | flops 2147483648 | bytes 8388608 | tf_op jit(solution)/shard_map/row_transform_1/pallas_call | solution.py:68
  22.6 17.2 %all-to-all-done.2 = bf16[8,256,256]{2,1,0:T(8,128)(2,1)S(1)} async-done(((bf16[8,256,256]{2,1,0:T(8,128)(2,1)}), bf16[8,256,256]{2,1,0:T(8,128)(2,1)S(1)}, u32[]{:S(2)}, u32[]{:S(2)}) %all-to-all-start.2) | async-done | bytes 1048608 | tf_op jit(solution)/shard_map/all_to_all | solution.py:279
  39.8 0.0 copy-start
  39.8 3.6 %all-to-all-start = ((bf16[8,256,256]{2,1,0:T(8,128)(2,1)}), bf16[8,256,256]{2,1,0:T(8,128)(2,1)S(1)}, u32[]{:S(2)}, u32[]{:S(2)}) async-start(bf16[8,256,256]{2,1,0:T(8,128)(2,1)} %row_transform_1.1), calls=%async_computation | async-start | bytes 2097152 | tf_op jit(solution)/shard_map/all_to_all | solution.py:279
  43.5 0.1 fusion.14
  43.6 0.1 select_multiply_fusion.3
  43.7 0.6 pad_maximum_fusion.2.lane_ref
  44.3 0.0 copy-done
  44.3 7.3 %stack_rates_0.1 = (bf16[2048,128]{1,0:T(8,128)(2,1)}, bf16[2048,128]{1,0:T(8,128)(2,1)}) custom-call(bf16[2048,256]{1,0:T(8,128)(2,1)} %bitcast.4, bf16[2048,2048]{1,0:T(8,128)(2,1)} %constant.136.clone.table_ref, f32[1024,8]{1,0:T(8,128)} %copy.6.coef_ref, f32[16,128]{1,0:T(8,128)} %pad_maximum_fusion.2.lane_ref), custom_call_target="tpu_custom_call" | custom-call | flops 2147483648 | bytes 10485760 | tf_op jit(solution)/shard_map/stack_rates_0/pallas_call | solution.py:133
  51.6 0.0 collective-permute-start.1
  51.6 2.1 %collective-permute-done.1.other_ref = bf16[2048,128]{1,0:T(8,128)(2,1)S(1)} collective-permute-done((bf16[2048,128]{1,0:T(8,128)(2,1)}, bf16[2048,128]{1,0:T(8,128)(2,1)S(1)}, u32[]{:S(2)}, u32[]{:S(2)}) %collective-permute-start.1) | collective-permute-done | bytes 524320 | tf_op jit(solution)/shard_map/ppermute | solution.py:292
  53.7 0.0 copy-start.4
  53.7 0.8 copy-done.4
  54.5 6.1 %inverse_columns_0.1 = bf16[8,128,256]{2,1,0:T(8,128)(2,1)} custom-call(bf16[2048,128]{1,0:T(8,128)(2,1)} %get-tuple-element.11.own_ref, bf16[2048,128]{1,0:T(8,128)(2,1)} %copy-done.4, bf16[2048,2048]{1,0:T(8,128)(2,1)} %constant.136.clone.table_ref), custom_call_target="tpu_custom_call" | custom-call | flops 1073741824 | bytes 9961472 | tf_op jit(solution)/shard_map/inverse_columns_0/pallas_call | solution.py:171
  60.6 8.8 %all-to-all-done = bf16[8,256,256]{2,1,0:T(8,128)(2,1)S(1)} async-done(((bf16[8,256,256]{2,1,0:T(8,128)(2,1)}), bf16[8,256,256]{2,1,0:T(8,128)(2,1)S(1)}, u32[]{:S(2)}, u32[]{:S(2)}) %all-to-all-start) | async-done | bytes 1048608 | tf_op jit(solution)/shard_map/all_to_all | solution.py:279
  69.4 0.0 copy-start.1
  69.4 3.6 %all-to-all-start.3 = ((bf16[8,128,256]{2,1,0:T(8,128)(2,1)}), bf16[8,128,256]{2,1,0:T(8,128)(2,1)S(1)}, u32[]{:S(2)}, u32[]{:S(2)}) async-start(bf16[8,128,256]{2,1,0:T(8,128)(2,1)} %inverse_columns_0.1), calls=%async_computation.3 | async-start | bytes 1048576 | tf_op jit(solution)/shard_map/all_to_all | solution.py:279
  73.0 0.6 pad_maximum_fusion.1.lane_ref
  73.6 0.0 copy-done.1
  73.6 7.3 %stack_rates_1.1 = (bf16[2048,128]{1,0:T(8,128)(2,1)}, bf16[2048,128]{1,0:T(8,128)(2,1)}) custom-call(bf16[2048,256]{1,0:T(8,128)(2,1)} %bitcast.5, bf16[2048,2048]{1,0:T(8,128)(2,1)} %constant.136.clone.table_ref, f32[1024,8]{1,0:T(8,128)} %copy.6.coef_ref, f32[16,128]{1,0:T(8,128)} %pad_maximum_fusion.1.lane_ref), custom_call_target="tpu_custom_call" | custom-call | flops 2147483648 | bytes 10485760 | tf_op jit(solution)/shard_map/stack_rates_1/pallas_call | solution.py:133
  80.9 0.0 collective-permute-start
  80.9 2.1 %collective-permute-done.other_ref = bf16[2048,128]{1,0:T(8,128)(2,1)S(1)} collective-permute-done((bf16[2048,128]{1,0:T(8,128)(2,1)}, bf16[2048,128]{1,0:T(8,128)(2,1)S(1)}, u32[]{:S(2)}, u32[]{:S(2)}) %collective-permute-start) | collective-permute-done | bytes 524320 | tf_op jit(solution)/shard_map/ppermute | solution.py:292
  83.0 0.0 copy-start.5
  83.0 0.8 copy-done.5
  83.8 6.1 %inverse_columns_1.1 = bf16[8,128,256]{2,1,0:T(8,128)(2,1)} custom-call(bf16[2048,128]{1,0:T(8,128)(2,1)} %get-tuple-element.9.own_ref, bf16[2048,128]{1,0:T(8,128)(2,1)} %copy-done.5, bf16[2048,2048]{1,0:T(8,128)(2,1)} %constant.136.clone.table_ref), custom_call_target="tpu_custom_call" | custom-call | flops 1073741824 | bytes 9961472 | tf_op jit(solution)/shard_map/inverse_columns_1/pallas_call | solution.py:171
  89.9 0.0 all-to-all-done.3
  89.9 0.0 copy-start.3
  89.9 6.0 %all-to-all-start.1 = ((bf16[8,128,256]{2,1,0:T(8,128)(2,1)}), bf16[8,128,256]{2,1,0:T(8,128)(2,1)S(1)}, u32[]{:S(2)}, u32[]{:S(2)}) async-start(bf16[8,128,256]{2,1,0:T(8,128)(2,1)} %inverse_columns_1.1), calls=%async_computation.1 | async-start | bytes 1048576 | tf_op jit(solution)/shard_map/all_to_all | solution.py:279
  95.9 0.0 copy-done.3
  95.9 5.4 %image_rows_0.1.refs_0_ = f32[1,256,2048]{2,1,0:T(8,128)} custom-call(bf16[1024,256]{1,0:T(8,128)(2,1)} %bitcast.7, bf16[2048,2048]{1,0:T(8,128)(2,1)} %constant.136.clone.table_ref), custom_call_target="tpu_custom_call" | custom-call | flops 1073741824 | bytes 8388608 | tf_op jit(solution)/shard_map/image_rows_0/pallas_call | solution.py:206
  101.3 9.4 %all-to-all-done.1 = bf16[8,128,256]{2,1,0:T(8,128)(2,1)S(1)} async-done(((bf16[8,128,256]{2,1,0:T(8,128)(2,1)}), bf16[8,128,256]{2,1,0:T(8,128)(2,1)S(1)}, u32[]{:S(2)}, u32[]{:S(2)}) %all-to-all-start.1) | async-done | bytes 524320 | tf_op jit(solution)/shard_map/all_to_all | solution.py:279
  110.7 0.0 copy-start.2
  110.7 0.8 copy-done.2
  111.5 5.7 %image_rows_1.1 = f32[1,256,2048]{2,1,0:T(8,128)} custom-call(bf16[1024,256]{1,0:T(8,128)(2,1)} %bitcast.6, bf16[2048,2048]{1,0:T(8,128)(2,1)} %constant.136.clone.table_ref, f32[1,256,2048]{2,1,0:T(8,128)} %image_rows_0.1.refs_0_), custom_call_target="tpu_custom_call" | custom-call | flops 1073741824 | bytes 8388608 | tf_op jit(solution)/shard_map/image_rows_1/pallas_call | solution.py:206
  (10 shorter events, 0.1 us)
Async XLA Ops:
  6.7 7.4 %copy-start.6 = (s32[2,2]{1,0:T(2,128)S(1)}, s32[2,2]{1,0:T(2,128)}, u32[]{:S(2)}) copy-start(s32[2,2]{1,0:T(2,128)} %param.6) | copy-start | bytes 52
  6.7 7.4 %copy-start.7 = (s32[4]{0:T(128)S(1)}, s32[4]{0:T(128)}, u32[]{:S(2)}) copy-start(s32[4]{0:T(128)} %param.7) | copy-start | bytes 52
  6.7 33.2 %all-to-all-start.2 = ((bf16[8,256,256]{2,1,0:T(8,128)(2,1)}), bf16[8,256,256]{2,1,0:T(8,128)(2,1)S(1)}, u32[]{:S(2)}, u32[]{:S(2)}) async-start(bf16[8,256,256]{2,1,0:T(8,128)(2,1)} %row_transform_0.1), calls=%async_computation.2 | async-start | bytes 2097152 | tf_op jit(solution)/shard_map/all_to_all | solution.py:279
  39.8 4.5 %copy-start = (bf16[8,256,256]{2,1,0:T(8,128)(2,1)}, bf16[8,256,256]{2,1,0:T(8,128)(2,1)S(1)}, u32[]{:S(2)}) copy-start(bf16[8,256,256]{2,1,0:T(8,128)(2,1)S(1)} %all-to-all-done.2) | copy-start | bytes 3145732
  39.8 29.5 %all-to-all-start = ((bf16[8,256,256]{2,1,0:T(8,128)(2,1)}), bf16[8,256,256]{2,1,0:T(8,128)(2,1)S(1)}, u32[]{:S(2)}, u32[]{:S(2)}) async-start(bf16[8,256,256]{2,1,0:T(8,128)(2,1)} %row_transform_1.1), calls=%async_computation | async-start | bytes 2097152 | tf_op jit(solution)/shard_map/all_to_all | solution.py:279
  51.6 2.1 %collective-permute-start.1 = (bf16[2048,128]{1,0:T(8,128)(2,1)}, bf16[2048,128]{1,0:T(8,128)(2,1)S(1)}, u32[]{:S(2)}, u32[]{:S(2)}) collective-permute-start(bf16[2048,128]{1,0:T(8,128)(2,1)} %get-tuple-element.12), channel_id=1, source_target_pairs={{0,1},{1,0},{2,3},{3,2},{4,5},{5,4},{6,7},{7,6},{8,9},{9,8},{10,11... | collective-permute-start | bytes 1572872 | tf_op jit(solution)/shard_map/ppermute | solution.py:292
  53.7 0.8 copy-start.4
  69.4 4.2 %copy-start.1 = (bf16[8,256,256]{2,1,0:T(8,128)(2,1)}, bf16[8,256,256]{2,1,0:T(8,128)(2,1)S(1)}, u32[]{:S(2)}) copy-start(bf16[8,256,256]{2,1,0:T(8,128)(2,1)S(1)} %all-to-all-done) | copy-start | bytes 3145732
  69.4 20.5 %all-to-all-start.3 = ((bf16[8,128,256]{2,1,0:T(8,128)(2,1)}), bf16[8,128,256]{2,1,0:T(8,128)(2,1)S(1)}, u32[]{:S(2)}, u32[]{:S(2)}) async-start(bf16[8,128,256]{2,1,0:T(8,128)(2,1)} %inverse_columns_0.1), calls=%async_computation.3 | async-start | bytes 1048576 | tf_op jit(solution)/shard_map/all_to_all | solution.py:279
  80.9 2.1 %collective-permute-start = (bf16[2048,128]{1,0:T(8,128)(2,1)}, bf16[2048,128]{1,0:T(8,128)(2,1)S(1)}, u32[]{:S(2)}, u32[]{:S(2)}) collective-permute-start(bf16[2048,128]{1,0:T(8,128)(2,1)} %get-tuple-element.10), channel_id=1, source_target_pairs={{0,1},{1,0},{2,3},{3,2},{4,5},{5,4},{6,7},{7,6},{8,9},{9,8},{10,11... | collective-permute-start | bytes 1572872 | tf_op jit(solution)/shard_map/ppermute | solution.py:292
  83.0 0.8 copy-start.5
  89.9 6.0 %copy-start.3 = (bf16[8,128,256]{2,1,0:T(8,128)(2,1)}, bf16[8,128,256]{2,1,0:T(8,128)(2,1)S(1)}, u32[]{:S(2)}) copy-start(bf16[8,128,256]{2,1,0:T(8,128)(2,1)S(1)} %all-to-all-done.3) | copy-start | bytes 1572868
  89.9 20.8 %all-to-all-start.1 = ((bf16[8,128,256]{2,1,0:T(8,128)(2,1)}), bf16[8,128,256]{2,1,0:T(8,128)(2,1)S(1)}, u32[]{:S(2)}, u32[]{:S(2)}) async-start(bf16[8,128,256]{2,1,0:T(8,128)(2,1)} %inverse_columns_1.1), calls=%async_computation.1 | async-start | bytes 1048576 | tf_op jit(solution)/shard_map/all_to_all | solution.py:279
  110.7 0.8 copy-start.2

commit v6 on v5

--- a/solution.py
+++ b/solution.py
@@ -13,6 +13,8 @@
 SUBPIX = 16
 CHUNKS = 2
 MIN_COLS = 64
+PAIRWISE_LIMIT = 8
+PAIR_ORDER = (7, 4, 1, 6, 5, 2, 3)
 BLOCK = 512
 VMEM_LIMIT = 58 * 1024 * 1024
 
@@ -276,7 +278,15 @@
     scale = 1.0 / math.sqrt(epochs)
 
     def exchange(values):
-        return lax.all_to_all(values, "row", 0, 0, tiled=True)
+        if row_count > PAIRWISE_LIMIT:
+            return lax.all_to_all(values, "row", 0, 0, tiled=True)
+        received = values
+        for offset in PAIR_ORDER:
+            sent = lax.dynamic_index_in_dim(values, row_pos ^ offset, 0, keepdims=True)
+            pairs = [(index, index ^ offset) for index in range(row_count)]
+            arrived = lax.ppermute(sent, "row", pairs)
+            received = lax.dynamic_update_slice_in_dim(received, arrived, row_pos ^ offset, 0)
+        return received
 
     spectra = [
         exchange(row_transform(images, table_t, chunk, chunks, row_count))

time: 118 us -> 150 us (1.27)
  starting transfers between devices: 20.6 us -> 45.4 us
  local copies, waits for them, and re-layouts: 3.85 us -> 14.5 us
  waiting for transfers between devices: 39.6 us -> 36 us
    ppermute x0 -> x28, starting transfers between devices: none -> 45.3 us  [exchange(): arrived = lax.ppermute(sent, 'row', pairs)]
    ppermute x0 -> x28, waiting for transfers between devices: none -> 36 us  [exchange(): arrived = lax.ppermute(sent, 'row', pairs)]
    all_to_all x4 -> x0, waiting for transfers between devices: 35.4 us -> none  [exchange(): return lax.all_to_all(values, 'row', 0, 0, tiled=True)]
    all_to_all x4 -> x0, starting transfers between devices: 20.6 us -> none  [exchange(): return lax.all_to_all(values, 'row', 0, 0, tiled=True)]
    dynamic_slice x0 -> x8, local copies, waits for them, and re-layouts: none -> 5.42 us  [exchange(): sent = lax.dynamic_index_in_dim(values, row_pos ^ offset, 0, keepdims=True)]
    ppermute x2, waiting for transfers between devices: 4.24 us -> 0.01 us  [local(): other = lax.ppermute(other, 'epoch', [(0, 1), (1, 0)])]
    dynamic_update_slice x0 -> x24, local copies, waits for them, and re-layouts: none -> 4.01 us  [exchange(): lax.dynamic_update_slice_in_dim(received, arrived, row_pos ^ offset, 0)]
    unnamed x16 -> x20, local copies, waits for them, and re-layouts: 2.39 us -> 3.54 us
  transfers between devices with their start and end apart: 6 -> 30, of which waited for: 5 -> 8; matrix products, arithmetic and copies ran while one was open for 3% -> 8% of each run, Pallas kernels for 33% -> 26%
where the time goes in v6:
time: 150 us; the launch traced here: 149 us
  Pallas kernels  51.3 us (34%)
  starting transfers between devices  45.4 us (30%)
  waiting for transfers between devices  36 us (24%)
  local copies, waits for them, and re-layouts  14.5 us (10%)
  other arithmetic  1.86 us (1%)
    ppermute x28, starting transfers between devices, exchange(): arrived = lax.ppermute(sent, 'row', pairs)  45.3 us
    ppermute x28, waiting for transfers between devices, exchange(): arrived = lax.ppermute(sent, 'row', pairs)  36 us
    pallas_call x2, Pallas kernels, stack_rates(): pl.pallas_call(functools.partial(stack_kernel, rates, loc_epochs), grid=(...  14.6 us
    pallas_call x2, Pallas kernels, row_transform(): pl.pallas_call(row_kernel, grid=(steps,), in_specs=[pl.BlockSpec((loc_epo...  13.4 us
    pallas_call x2, Pallas kernels, inverse_columns(): pl.pallas_call(inverse_kernel, grid=(length // BLOCK,), in_specs=[pl.Bloc...  12.2 us
    pallas_call x2, Pallas kernels, image_rows(): pl.pallas_call(functools.partial(image_kernel, partial is not None), grid...  11.1 us
    dynamic_slice x8, local copies, waits for them, and re-layouts, exchange(): sent = lax.dynamic_index_in_dim(values, row_pos ^ offset, 0, keepdims=True)  5.42 us
    dynamic_update_slice x24, local copies, waits for them, and re-layouts, exchange(): lax.dynamic_update_slice_in_dim(received, arrived, row_pos ^ offset, 0)  4.01 us
  transfers between devices with their start and end apart: 30, of which 8 were waited for; matrix products, arithmetic and copies ran while one was open for 8% of the time, Pallas kernels for 26%

profile of v6, /device:TPU:0, one launch (start us, length us, event | category | flops | bytes accessed | tf_op | source)
XLA Modules:
  0.0 149.4 jit_solution(17429075211860588221)
XLA Ops:
  0.0 6.7 %row_transform_0.1 = bf16[8,256,256]{2,1,0:T(8,128)(2,1)} custom-call(bf16[2,256,2048]{2,1,0:T(8,128)(2,1)} %images_ref.3, bf16[2048,2048]{1,0:T(8,128)(2,1)} %constant.205.clone.table_ref), custom_call_target="tpu_custom_call" | custom-call | flops 2147483648 | bytes 8388608 | tf_op jit(solution)/shard_map/row_transform_0/pallas_call | solution.py:70
  6.7 0.9 constant_dynamic-slice_fusion.13
  7.6 6.0 %collective-permute-start.15 = (bf16[1,256,256]{2,1,0:T(8,128)(2,1)S(1)}, bf16[1,256,256]{2,1,0:T(8,128)(2,1)S(1)}, u32[]{:S(2)}, u32[]{:S(2)}) collective-permute-start(bf16[1,256,256]{2,1,0:T(8,128)(2,1)S(1)} %constant_dynamic-slice_fusion.13), channel_id=1, source_target_pairs={{0,14},{2,12},{4,10},{6,8},{8,6},{10,4},{12,2},{14,0},{1,15},{3,13... | collective-permute-start | bytes 393224 | tf_op jit(solution)/shard_map/ppermute | solution.py:287
  13.7 6.7 %row_transform_1.1 = bf16[8,256,256]{2,1,0:T(8,128)(2,1)} custom-call(bf16[2,256,2048]{2,1,0:T(8,128)(2,1)} %images_ref.3, bf16[2048,2048]{1,0:T(8,128)(2,1)} %constant.205.clone.table_ref), custom_call_target="tpu_custom_call" | custom-call | flops 2147483648 | bytes 8388608 | tf_op jit(solution)/shard_map/row_transform_1/pallas_call | solution.py:70
  20.4 1.0 constant_dynamic-slice_fusion.27
  21.4 0.2 collective-permute-start
  21.7 0.2 slice_reduce_fusion
  22.0 0.1 mul.192
  22.1 0.1 mul.180
  22.3 0.2 multiply_select_fusion.2
  22.6 0.1 select_multiply_fusion.3
  22.7 0.6 pad_maximum_fusion.2.lane_ref
  23.3 1.0 copy.6.coef_ref
  24.3 0.6 pad_maximum_fusion.1.lane_ref
  25.0 0.9 collective-permute-start.21
  25.9 2.2 %collective-permute-start.20 = (bf16[1,256,256]{2,1,0:T(8,128)(2,1)S(1)}, bf16[1,256,256]{2,1,0:T(8,128)(2,1)S(1)}, u32[]{:S(2)}, u32[]{:S(2)}) collective-permute-start(bf16[1,256,256]{2,1,0:T(8,128)(2,1)S(1)} %get-tuple-element.20), channel_id=1, source_target_pairs={{0,4},{2,6},{4,0},{6,2},{8,12},{10,14},{12,8},{14,10},{1,5},{3,7},... | collective-permute-start | bytes 393224 | tf_op jit(solution)/shard_map/ppermute | solution.py:287
  28.1 2.2 %collective-permute-start.19 = (bf16[1,256,256]{2,1,0:T(8,128)(2,1)S(1)}, bf16[1,256,256]{2,1,0:T(8,128)(2,1)S(1)}, u32[]{:S(2)}, u32[]{:S(2)}) collective-permute-start(bf16[1,256,256]{2,1,0:T(8,128)(2,1)S(1)} %get-tuple-element.21), channel_id=1, source_target_pairs={{0,10},{2,8},{4,14},{6,12},{8,2},{10,0},{12,6},{14,4},{1,11},{3,9}... | collective-permute-start | bytes 393224 | tf_op jit(solution)/shard_map/ppermute | solution.py:287
  30.4 1.4 collective-permute-start.17
  31.7 0.8 collective-permute-start.16
  32.6 9.7 %collective-permute-done.16 = bf16[1,256,256]{2,1,0:T(8,128)(2,1)S(1)} collective-permute-done((bf16[1,256,256]{2,1,0:T(8,128)(2,1)S(1)}, bf16[1,256,256]{2,1,0:T(8,128)(2,1)S(1)}, u32[]{:S(2)}, u32[]{:S(2)}) %collective-permute-start.16) | collective-permute-done | bytes 131104 | tf_op jit(solution)/shard_map/ppermute | solution.py:287
  42.3 3.2 %collective-permute-start.18 = (bf16[1,256,256]{2,1,0:T(8,128)(2,1)S(1)}, bf16[1,256,256]{2,1,0:T(8,128)(2,1)S(1)}, u32[]{:S(2)}, u32[]{:S(2)}) collective-permute-start(bf16[1,256,256]{2,1,0:T(8,128)(2,1)S(1)} %get-tuple-element.22), channel_id=1, source_target_pairs={{0,12},{2,14},{4,8},{6,10},{8,4},{10,6},{12,0},{14,2},{1,13},{3,15... | collective-permute-start | bytes 393224 | tf_op jit(solution)/shard_map/ppermute | solution.py:287
  45.7 4.7 %collective-permute-done.18 = bf16[1,256,256]{2,1,0:T(8,128)(2,1)S(1)} collective-permute-done((bf16[1,256,256]{2,1,0:T(8,128)(2,1)S(1)}, bf16[1,256,256]{2,1,0:T(8,128)(2,1)S(1)}, u32[]{:S(2)}, u32[]{:S(2)}) %collective-permute-start.18) | collective-permute-done | bytes 131104 | tf_op jit(solution)/shard_map/ppermute | solution.py:287
  50.4 4.8 %collective-permute-start.4 = (bf16[1,256,256]{2,1,0:T(8,128)(2,1)S(1)}, bf16[1,256,256]{2,1,0:T(8,128)(2,1)S(1)}, u32[]{:S(2)}, u32[]{:S(2)}) collective-permute-start(bf16[1,256,256]{2,1,0:T(8,128)(2,1)S(1)} %get-tuple-element.28), channel_id=1, source_target_pairs={{0,10},{2,8},{4,14},{6,12},{8,2},{10,0},{12,6},{14,4},{1,11},{3,9}... | collective-permute-start | bytes 393224 | tf_op jit(solution)/shard_map/ppermute | solution.py:287
  55.2 0.6 collective-permute-start.1
  55.9 1.0 copy-done.3
  56.9 7.3 %stack_rates_0.1 = (bf16[2048,128]{1,0:T(8,128)(2,1)}, bf16[2048,128]{1,0:T(8,128)(2,1)}) custom-call(bf16[2048,256]{1,0:T(8,128)(2,1)} %bitcast.5, bf16[2048,2048]{1,0:T(8,128)(2,1)} %constant.206.clone.table_ref, f32[1024,8]{1,0:T(8,128)} %copy.6.coef_ref, f32[16,128]{1,0:T(8,128)} %pad_maximum_fusion.2.lane_ref), custom_call_target="tpu_custom_call" | custom-call | flops 2147483648 | bytes 10485760 | tf_op jit(solution)/shard_map/stack_rates_0/pallas_call | solution.py:135
  64.2 1.9 %collective-permute-start.3 = (bf16[1,256,256]{2,1,0:T(8,128)(2,1)S(1)}, bf16[1,256,256]{2,1,0:T(8,128)(2,1)S(1)}, u32[]{:S(2)}, u32[]{:S(2)}) collective-permute-start(bf16[1,256,256]{2,1,0:T(8,128)(2,1)S(1)} %get-tuple-element.29), channel_id=1, source_target_pairs={{0,12},{2,14},{4,8},{6,10},{8,4},{10,6},{12,0},{14,2},{1,13},{3,15... | collective-permute-start | bytes 393224 | tf_op jit(solution)/shard_map/ppermute | solution.py:287
  66.1 4.9 %collective-permute-done.3 = bf16[1,256,256]{2,1,0:T(8,128)(2,1)S(1)} collective-permute-done((bf16[1,256,256]{2,1,0:T(8,128)(2,1)S(1)}, bf16[1,256,256]{2,1,0:T(8,128)(2,1)S(1)}, u32[]{:S(2)}, u32[]{:S(2)}) %collective-permute-start.3) | collective-permute-done | bytes 131104 | tf_op jit(solution)/shard_map/ppermute | solution.py:287
  71.2 1.0 copy-done.1
  72.2 7.3 %stack_rates_1.1 = (bf16[2048,128]{1,0:T(8,128)(2,1)}, bf16[2048,128]{1,0:T(8,128)(2,1)}) custom-call(bf16[2048,256]{1,0:T(8,128)(2,1)} %bitcast.4, bf16[2048,2048]{1,0:T(8,128)(2,1)} %constant.206.clone.table_ref, f32[1024,8]{1,0:T(8,128)} %copy.6.coef_ref, f32[16,128]{1,0:T(8,128)} %pad_maximum_fusion.1.lane_ref), custom_call_target="tpu_custom_call" | custom-call | flops 2147483648 | bytes 10485760 | tf_op jit(solution)/shard_map/stack_rates_1/pallas_call | solution.py:135
  79.5 0.8 copy-done.6
  80.3 6.1 %inverse_columns_0.1 = bf16[8,128,256]{2,1,0:T(8,128)(2,1)} custom-call(bf16[2048,128]{1,0:T(8,128)(2,1)} %get-tuple-element.11.own_ref, bf16[2048,128]{1,0:T(8,128)(2,1)} %copy-done.6, bf16[2048,2048]{1,0:T(8,128)(2,1)} %constant.206.clone.table_ref), custom_call_target="tpu_custom_call" | custom-call | flops 1073741824 | bytes 9961472 | tf_op jit(solution)/shard_map/inverse_columns_0/pallas_call | solution.py:173
  86.4 0.8 constant_dynamic-slice_fusion.6
  87.2 3.3 %collective-permute-start.23 = (bf16[1,128,256]{2,1,0:T(8,128)(2,1)S(1)}, bf16[1,128,256]{2,1,0:T(8,128)(2,1)S(1)}, u32[]{:S(2)}, u32[]{:S(2)}) collective-permute-start(bf16[1,128,256]{2,1,0:T(8,128)(2,1)S(1)} %constant_dynamic-slice_fusion.6), channel_id=1, source_target_pairs={{0,14},{2,12},{4,10},{6,8},{8,6},{10,4},{12,2},{14,0},{1,15},{3,13... | collective-permute-start | bytes 196616 | tf_op jit(solution)/shard_map/ppermute | solution.py:287
  90.5 0.8 copy-done.7
  91.3 6.2 %inverse_columns_1.1 = bf16[8,128,256]{2,1,0:T(8,128)(2,1)} custom-call(bf16[2048,128]{1,0:T(8,128)(2,1)} %get-tuple-element.9.own_ref, bf16[2048,128]{1,0:T(8,128)(2,1)} %copy-done.7, bf16[2048,2048]{1,0:T(8,128)(2,1)} %constant.206.clone.table_ref), custom_call_target="tpu_custom_call" | custom-call | flops 1073741824 | bytes 9961472 | tf_op jit(solution)/shard_map/inverse_columns_1/pallas_call | solution.py:173
  97.4 0.8 constant_dynamic-slice_fusion.20
  98.3 1.5 collective-permute-start.8
  99.8 0.1 collective-permute-start.29
  99.9 2.9 %collective-permute-start.28 = (bf16[1,128,256]{2,1,0:T(8,128)(2,1)S(1)}, bf16[1,128,256]{2,1,0:T(8,128)(2,1)S(1)}, u32[]{:S(2)}, u32[]{:S(2)}) collective-permute-start(bf16[1,128,256]{2,1,0:T(8,128)(2,1)S(1)} %get-tuple-element.34), channel_id=1, source_target_pairs={{0,4},{2,6},{4,0},{6,2},{8,12},{10,14},{12,8},{14,10},{1,5},{3,7},... | collective-permute-start | bytes 196616 | tf_op jit(solution)/shard_map/ppermute | solution.py:287
  102.8 1.0 collective-permute-start.27
  103.7 1.5 collective-permute-start.26
  105.2 0.7 collective-permute-done.8
  105.9 0.7 collective-permute-start.24
  106.6 1.7 %constant_dynamic-slice_fusion.14 = (bf16[1,128,256]{2,1,0:T(8,128)(2,1)S(1)}, bf16[1,128,256]{2,1,0:T(8,128)(2,1)S(1)}, bf16[1,128,256]{2,1,0:T(8,128)(2,1)S(1)...) fusion(bf16[8,128,256]{2,1,0:T(8,128)(2,1)} %inverse_columns_1., ...), kind=kLoop, calls=%fused_computation.40 | loop fusion | bytes 917532 | tf_op jit(solution)/shard_map/jit(dynamic_index_in_dim)/dynamic_slice | solution.py:285
  108.3 5.8 %collective-permute-done.24 = bf16[1,128,256]{2,1,0:T(8,128)(2,1)S(1)} collective-permute-done((bf16[1,128,256]{2,1,0:T(8,128)(2,1)S(1)}, bf16[1,128,256]{2,1,0:T(8,128)(2,1)S(1)}, u32[]{:S(2)}, u32[]{:S(2)}) %collective-permute-start.24) | collective-permute-done | bytes 65568 | tf_op jit(solution)/shard_map/ppermute | solution.py:287
  114.1 1.7 %collective-permute-start.25 = (bf16[1,128,256]{2,1,0:T(8,128)(2,1)S(1)}, bf16[1,128,256]{2,1,0:T(8,128)(2,1)S(1)}, u32[]{:S(2)}, u32[]{:S(2)}) collective-permute-start(bf16[1,128,256]{2,1,0:T(8,128)(2,1)S(1)} %get-tuple-element.37), channel_id=1, source_target_pairs={{0,2},{2,0},{4,6},{6,4},{8,10},{10,8},{12,14},{14,12},{1,3},{3,1},... | collective-permute-start | bytes 196616 | tf_op jit(solution)/shard_map/ppermute | solution.py:287
  115.8 2.5 %collective-permute-done.25 = bf16[1,128,256]{2,1,0:T(8,128)(2,1)S(1)} collective-permute-done((bf16[1,128,256]{2,1,0:T(8,128)(2,1)S(1)}, bf16[1,128,256]{2,1,0:T(8,128)(2,1)S(1)}, u32[]{:S(2)}, u32[]{:S(2)}) %collective-permute-start.25) | collective-permute-done | bytes 65568 | tf_op jit(solution)/shard_map/ppermute | solution.py:287
  118.3 0.4 collective-permute-start.14
  118.7 2.9 %collective-permute-start.13 = (bf16[1,128,256]{2,1,0:T(8,128)(2,1)S(1)}, bf16[1,128,256]{2,1,0:T(8,128)(2,1)S(1)}, u32[]{:S(2)}, u32[]{:S(2)}) collective-permute-start(bf16[1,128,256]{2,1,0:T(8,128)(2,1)S(1)} %get-tuple-element.41), channel_id=1, source_target_pairs={{0,4},{2,6},{4,0},{6,2},{8,12},{10,14},{12,8},{14,10},{1,5},{3,7},... | collective-permute-start | bytes 196616 | tf_op jit(solution)/shard_map/ppermute | solution.py:287
  121.6 0.6 collective-permute-start.12
  122.3 1.9 %collective-permute-start.11 = (bf16[1,128,256]{2,1,0:T(8,128)(2,1)S(1)}, bf16[1,128,256]{2,1,0:T(8,128)(2,1)S(1)}, u32[]{:S(2)}, u32[]{:S(2)}) collective-permute-start(bf16[1,128,256]{2,1,0:T(8,128)(2,1)S(1)} %get-tuple-element.43), channel_id=1, source_target_pairs={{0,12},{2,14},{4,8},{6,10},{8,4},{10,6},{12,0},{14,2},{1,13},{3,15... | collective-permute-start | bytes 196616 | tf_op jit(solution)/shard_map/ppermute | solution.py:287
  124.2 1.3 collective-permute-start.9
  125.5 5.3 %collective-permute-done.9 = bf16[1,128,256]{2,1,0:T(8,128)(2,1)S(1)} collective-permute-done((bf16[1,128,256]{2,1,0:T(8,128)(2,1)S(1)}, bf16[1,128,256]{2,1,0:T(8,128)(2,1)S(1)}, u32[]{:S(2)}, u32[]{:S(2)}) %collective-permute-start.9) | collective-permute-done | bytes 65568 | tf_op jit(solution)/shard_map/ppermute | solution.py:287
  130.8 1.3 collective-permute-start.10
  132.1 0.6 constant_dynamic-update-slice_fusion.19
  132.8 2.3 %collective-permute-done.10 = bf16[1,128,256]{2,1,0:T(8,128)(2,1)S(1)} collective-permute-done((bf16[1,128,256]{2,1,0:T(8,128)(2,1)S(1)}, bf16[1,128,256]{2,1,0:T(8,128)(2,1)S(1)}, u32[]{:S(2)}, u32[]{:S(2)}) %collective-permute-start.10) | collective-permute-done | bytes 65568 | tf_op jit(solution)/shard_map/ppermute | solution.py:287
  135.1 0.6 constant_dynamic-update-slice_fusion.18
  135.7 0.6 constant_dynamic-update-slice_fusion.17
  136.3 0.6 constant_dynamic-update-slice_fusion.16
  137.0 0.6 constant_dynamic-update-slice_fusion.15
  137.6 5.4 %image_rows_0.1.refs_0_ = f32[1,256,2048]{2,1,0:T(8,128)} custom-call(bf16[1024,256]{1,0:T(8,128)(2,1)} %bitcast.7, bf16[2048,2048]{1,0:T(8,128)(2,1)} %constant.206.clone.table_ref), custom_call_target="tpu_custom_call" | custom-call | flops 1073741824 | bytes 8388608 | tf_op jit(solution)/shard_map/image_rows_0/pallas_call | solution.py:208
  143.0 0.6 constant_dynamic-update-slice_fusion.14
  143.6 5.7 %image_rows_1.1 = f32[1,256,2048]{2,1,0:T(8,128)} custom-call(bf16[1024,256]{1,0:T(8,128)(2,1)} %bitcast.6, bf16[2048,2048]{1,0:T(8,128)(2,1)} %constant.206.clone.table_ref, f32[1,256,2048]{2,1,0:T(8,128)} %image_rows_0.1.refs_0_), custom_call_target="tpu_custom_call" | custom-call | flops 1073741824 | bytes 8388608 | tf_op jit(solution)/shard_map/image_rows_1/pallas_call | solution.py:208
  (79 shorter events, 1.1 us)
Async XLA Ops:
  7.6 14.0 %copy-start.8 = (s32[2,2]{1,0:T(2,128)S(1)}, s32[2,2]{1,0:T(2,128)}, u32[]{:S(2)}) copy-start(s32[2,2]{1,0:T(2,128)} %param.6) | copy-start | bytes 52
  7.6 14.2 %copy-start.9 = (s32[4]{0:T(128)S(1)}, s32[4]{0:T(128)}, u32[]{:S(2)}) copy-start(s32[4]{0:T(128)} %param.7) | copy-start | bytes 52
  7.6 17.3 %copy-start.2 = (bf16[8,256,256]{2,1,0:T(8,128)(2,1)S(1)}, bf16[8,256,256]{2,1,0:T(8,128)(2,1)}, u32[]{:S(2)}) copy-start(bf16[8,256,256]{2,1,0:T(8,128)(2,1)} %row_transform_0.1) | copy-start | bytes 3145732
  7.6 17.3 %collective-permute-start.15 = (bf16[1,256,256]{2,1,0:T(8,128)(2,1)S(1)}, bf16[1,256,256]{2,1,0:T(8,128)(2,1)S(1)}, u32[]{:S(2)}, u32[]{:S(2)}) collective-permute-start(bf16[1,256,256]{2,1,0:T(8,128)(2,1)S(1)} %constant_dynamic-slice_fusion.13), channel_id=1, source_target_pairs={{0,14},{2,12},{4,10},{6,8},{8,6},{10,4},{12,2},{14,0},{1,15},{3,13... | collective-permute-start | bytes 393224 | tf_op jit(solution)/shard_map/ppermute | solution.py:287
  20.4 12.2 %copy-start = (bf16[8,256,256]{2,1,0:T(8,128)(2,1)S(1)}, bf16[8,256,256]{2,1,0:T(8,128)(2,1)}, u32[]{:S(2)}) copy-start(bf16[8,256,256]{2,1,0:T(8,128)(2,1)} %row_transform_1.1) | copy-start | bytes 3145732
  21.4 10.4 %collective-permute-start = (bf16[1,256,256]{2,1,0:T(8,128)(2,1)S(1)}, bf16[1,256,256]{2,1,0:T(8,128)(2,1)S(1)}, u32[]{:S(2)}, u32[]{:S(2)}) collective-permute-start(bf16[1,256,256]{2,1,0:T(8,128)(2,1)S(1)} %constant_dynamic-slice_fusion.27), channel_id=1, source_target_pairs={{0,14},{2,12},{4,10},{6,8},{8,6},{10,4},{12,2},{14,0},{1,15},{3,13... | collective-permute-start | bytes 393224 | tf_op jit(solution)/shard_map/ppermute | solution.py:287
  25.0 30.2 %collective-permute-start.21 = (bf16[1,256,256]{2,1,0:T(8,128)(2,1)S(1)}, bf16[1,256,256]{2,1,0:T(8,128)(2,1)S(1)}, u32[]{:S(2)}, u32[]{:S(2)}) collective-permute-start(bf16[1,256,256]{2,1,0:T(8,128)(2,1)S(1)} %get-tuple-element.19), channel_id=1, source_target_pairs={{0,6},{2,4},{4,2},{6,0},{8,14},{10,12},{12,10},{14,8},{1,7},{3,5},... | collective-permute-start | bytes 393224 | tf_op jit(solution)/shard_map/ppermute | solution.py:287
  25.9 29.2 %collective-permute-start.20 = (bf16[1,256,256]{2,1,0:T(8,128)(2,1)S(1)}, bf16[1,256,256]{2,1,0:T(8,128)(2,1)S(1)}, u32[]{:S(2)}, u32[]{:S(2)}) collective-permute-start(bf16[1,256,256]{2,1,0:T(8,128)(2,1)S(1)} %get-tuple-element.20), channel_id=1, source_target_pairs={{0,4},{2,6},{4,0},{6,2},{8,12},{10,14},{12,8},{14,10},{1,5},{3,7},... | collective-permute-start | bytes 393224 | tf_op jit(solution)/shard_map/ppermute | solution.py:287
  28.1 22.2 %collective-permute-start.19 = (bf16[1,256,256]{2,1,0:T(8,128)(2,1)S(1)}, bf16[1,256,256]{2,1,0:T(8,128)(2,1)S(1)}, u32[]{:S(2)}, u32[]{:S(2)}) collective-permute-start(bf16[1,256,256]{2,1,0:T(8,128)(2,1)S(1)} %get-tuple-element.21), channel_id=1, source_target_pairs={{0,10},{2,8},{4,14},{6,12},{8,2},{10,0},{12,6},{14,4},{1,11},{3,9}... | collective-permute-start | bytes 393224 | tf_op jit(solution)/shard_map/ppermute | solution.py:287
  30.4 15.2 %collective-permute-start.17 = (bf16[1,256,256]{2,1,0:T(8,128)(2,1)S(1)}, bf16[1,256,256]{2,1,0:T(8,128)(2,1)S(1)}, u32[]{:S(2)}, u32[]{:S(2)}) collective-permute-start(bf16[1,256,256]{2,1,0:T(8,128)(2,1)S(1)} %get-tuple-element.23), channel_id=1, source_target_pairs={{0,2},{2,0},{4,6},{6,4},{8,10},{10,8},{12,14},{14,12},{1,3},{3,1},... | collective-permute-start | bytes 393224 | tf_op jit(solution)/shard_map/ppermute | solution.py:287
  31.7 10.6 %collective-permute-start.16 = (bf16[1,256,256]{2,1,0:T(8,128)(2,1)S(1)}, bf16[1,256,256]{2,1,0:T(8,128)(2,1)S(1)}, u32[]{:S(2)}, u32[]{:S(2)}) collective-permute-start(bf16[1,256,256]{2,1,0:T(8,128)(2,1)S(1)} %get-tuple-element.24), channel_id=1, source_target_pairs={{0,8},{2,10},{4,12},{6,14},{8,0},{10,2},{12,4},{14,6},{1,9},{3,11}... | collective-permute-start | bytes 393224 | tf_op jit(solution)/shard_map/ppermute | solution.py:287
  42.3 8.0 %collective-permute-start.18 = (bf16[1,256,256]{2,1,0:T(8,128)(2,1)S(1)}, bf16[1,256,256]{2,1,0:T(8,128)(2,1)S(1)}, u32[]{:S(2)}, u32[]{:S(2)}) collective-permute-start(bf16[1,256,256]{2,1,0:T(8,128)(2,1)S(1)} %get-tuple-element.22), channel_id=1, source_target_pairs={{0,12},{2,14},{4,8},{6,10},{8,4},{10,6},{12,0},{14,2},{1,13},{3,15... | collective-permute-start | bytes 393224 | tf_op jit(solution)/shard_map/ppermute | solution.py:287
  45.6 25.6 %collective-permute-start.6 = (bf16[1,256,256]{2,1,0:T(8,128)(2,1)S(1)}, bf16[1,256,256]{2,1,0:T(8,128)(2,1)S(1)}, u32[]{:S(2)}, u32[]{:S(2)}) collective-permute-start(bf16[1,256,256]{2,1,0:T(8,128)(2,1)S(1)} %get-tuple-element.26), channel_id=1, source_target_pairs={{0,6},{2,4},{4,2},{6,0},{8,14},{10,12},{12,10},{14,8},{1,7},{3,5},... | collective-permute-start | bytes 393224 | tf_op jit(solution)/shard_map/ppermute | solution.py:287
  50.3 20.8 %collective-permute-start.5 = (bf16[1,256,256]{2,1,0:T(8,128)(2,1)S(1)}, bf16[1,256,256]{2,1,0:T(8,128)(2,1)S(1)}, u32[]{:S(2)}, u32[]{:S(2)}) collective-permute-start(bf16[1,256,256]{2,1,0:T(8,128)(2,1)S(1)} %get-tuple-element.27), channel_id=1, source_target_pairs={{0,4},{2,6},{4,0},{6,2},{8,12},{10,14},{12,8},{14,10},{1,5},{3,7},... | collective-permute-start | bytes 393224 | tf_op jit(solution)/shard_map/ppermute | solution.py:287
  50.4 20.7 %collective-permute-start.4 = (bf16[1,256,256]{2,1,0:T(8,128)(2,1)S(1)}, bf16[1,256,256]{2,1,0:T(8,128)(2,1)S(1)}, u32[]{:S(2)}, u32[]{:S(2)}) collective-permute-start(bf16[1,256,256]{2,1,0:T(8,128)(2,1)S(1)} %get-tuple-element.28), channel_id=1, source_target_pairs={{0,10},{2,8},{4,14},{6,12},{8,2},{10,0},{12,6},{14,4},{1,11},{3,9}... | collective-permute-start | bytes 393224 | tf_op jit(solution)/shard_map/ppermute | solution.py:287
  55.1 10.9 %collective-permute-start.2 = (bf16[1,256,256]{2,1,0:T(8,128)(2,1)S(1)}, bf16[1,256,256]{2,1,0:T(8,128)(2,1)S(1)}, u32[]{:S(2)}, u32[]{:S(2)}) collective-permute-start(bf16[1,256,256]{2,1,0:T(8,128)(2,1)S(1)} %get-tuple-element.30), channel_id=1, source_target_pairs={{0,2},{2,0},{4,6},{6,4},{8,10},{10,8},{12,14},{14,12},{1,3},{3,1},... | collective-permute-start | bytes 393224 | tf_op jit(solution)/shard_map/ppermute | solution.py:287
  55.2 8.9 %collective-permute-start.1 = (bf16[1,256,256]{2,1,0:T(8,128)(2,1)S(1)}, bf16[1,256,256]{2,1,0:T(8,128)(2,1)S(1)}, u32[]{:S(2)}, u32[]{:S(2)}) collective-permute-start(bf16[1,256,256]{2,1,0:T(8,128)(2,1)S(1)} %get-tuple-element.31), channel_id=1, source_target_pairs={{0,8},{2,10},{4,12},{6,14},{8,0},{10,2},{12,4},{14,6},{1,9},{3,11}... | collective-permute-start | bytes 393224 | tf_op jit(solution)/shard_map/ppermute | solution.py:287
  55.9 1.0 copy-start.3
  64.2 6.9 %collective-permute-start.3 = (bf16[1,256,256]{2,1,0:T(8,128)(2,1)S(1)}, bf16[1,256,256]{2,1,0:T(8,128)(2,1)S(1)}, u32[]{:S(2)}, u32[]{:S(2)}) collective-permute-start(bf16[1,256,256]{2,1,0:T(8,128)(2,1)S(1)} %get-tuple-element.29), channel_id=1, source_target_pairs={{0,12},{2,14},{4,8},{6,10},{8,4},{10,6},{12,0},{14,2},{1,13},{3,15... | collective-permute-start | bytes 393224 | tf_op jit(solution)/shard_map/ppermute | solution.py:287
  66.0 13.4 %collective-permute-start.22 = (bf16[2048,128]{1,0:T(8,128)(2,1)}, bf16[2048,128]{1,0:T(8,128)(2,1)S(1)}, u32[]{:S(2)}, u32[]{:S(2)}) collective-permute-start(bf16[2048,128]{1,0:T(8,128)(2,1)} %get-tuple-element.12), channel_id=1, source_target_pairs={{0,1},{1,0},{2,3},{3,2},{4,5},{5,4},{6,7},{7,6},{8,9},{9,8},{10,11... | collective-permute-start | bytes 1572872 | tf_op jit(solution)/shard_map/ppermute | solution.py:302
  71.2 1.0 copy-start.1
  79.5 11.0 %collective-permute-start.7 = (bf16[2048,128]{1,0:T(8,128)(2,1)}, bf16[2048,128]{1,0:T(8,128)(2,1)S(1)}, u32[]{:S(2)}, u32[]{:S(2)}) collective-permute-start(bf16[2048,128]{1,0:T(8,128)(2,1)} %get-tuple-element.10), channel_id=1, source_target_pairs={{0,1},{1,0},{2,3},{3,2},{4,5},{5,4},{6,7},{7,6},{8,9},{9,8},{10,11... | collective-permute-start | bytes 1572872 | tf_op jit(solution)/shard_map/ppermute | solution.py:302
  79.5 0.8 copy-start.6
  87.2 12.5 %collective-permute-start.23 = (bf16[1,128,256]{2,1,0:T(8,128)(2,1)S(1)}, bf16[1,128,256]{2,1,0:T(8,128)(2,1)S(1)}, u32[]{:S(2)}, u32[]{:S(2)}) collective-permute-start(bf16[1,128,256]{2,1,0:T(8,128)(2,1)S(1)} %constant_dynamic-slice_fusion.6), channel_id=1, source_target_pairs={{0,14},{2,12},{4,10},{6,8},{8,6},{10,4},{12,2},{14,0},{1,15},{3,13... | collective-permute-start | bytes 196616 | tf_op jit(solution)/shard_map/ppermute | solution.py:287
  90.5 0.8 copy-start.7
  91.3 8.5 %copy-start.4 = (bf16[8,128,256]{2,1,0:T(8,128)(2,1)S(1)}, bf16[8,128,256]{2,1,0:T(8,128)(2,1)}, u32[]{:S(2)}) copy-start(bf16[8,128,256]{2,1,0:T(8,128)(2,1)} %inverse_columns_0.1) | copy-start | bytes 1572868
  98.3 7.6 %collective-permute-start.8 = (bf16[1,128,256]{2,1,0:T(8,128)(2,1)S(1)}, bf16[1,128,256]{2,1,0:T(8,128)(2,1)S(1)}, u32[]{:S(2)}, u32[]{:S(2)}) collective-permute-start(bf16[1,128,256]{2,1,0:T(8,128)(2,1)S(1)} %constant_dynamic-slice_fusion.20), channel_id=1, source_target_pairs={{0,14},{2,12},{4,10},{6,8},{8,6},{10,4},{12,2},{14,0},{1,15},{3,13... | collective-permute-start | bytes 196616 | tf_op jit(solution)/shard_map/ppermute | solution.py:287
  99.8 24.4 %collective-permute-start.29 = (bf16[1,128,256]{2,1,0:T(8,128)(2,1)S(1)}, bf16[1,128,256]{2,1,0:T(8,128)(2,1)S(1)}, u32[]{:S(2)}, u32[]{:S(2)}) collective-permute-start(bf16[1,128,256]{2,1,0:T(8,128)(2,1)S(1)} %get-tuple-element.33), channel_id=1, source_target_pairs={{0,6},{2,4},{4,2},{6,0},{8,14},{10,12},{12,10},{14,8},{1,7},{3,5},... | collective-permute-start | bytes 196616 | tf_op jit(solution)/shard_map/ppermute | solution.py:287
  99.9 22.4 %collective-permute-start.28 = (bf16[1,128,256]{2,1,0:T(8,128)(2,1)S(1)}, bf16[1,128,256]{2,1,0:T(8,128)(2,1)S(1)}, u32[]{:S(2)}, u32[]{:S(2)}) collective-permute-start(bf16[1,128,256]{2,1,0:T(8,128)(2,1)S(1)} %get-tuple-element.34), channel_id=1, source_target_pairs={{0,4},{2,6},{4,0},{6,2},{8,12},{10,14},{12,8},{14,10},{1,5},{3,7},... | collective-permute-start | bytes 196616 | tf_op jit(solution)/shard_map/ppermute | solution.py:287
  102.8 18.8 %collective-permute-start.27 = (bf16[1,128,256]{2,1,0:T(8,128)(2,1)S(1)}, bf16[1,128,256]{2,1,0:T(8,128)(2,1)S(1)}, u32[]{:S(2)}, u32[]{:S(2)}) collective-permute-start(bf16[1,128,256]{2,1,0:T(8,128)(2,1)S(1)} %get-tuple-element.35), channel_id=1, source_target_pairs={{0,10},{2,8},{4,14},{6,12},{8,2},{10,0},{12,6},{14,4},{1,11},{3,9}... | collective-permute-start | bytes 196616 | tf_op jit(solution)/shard_map/ppermute | solution.py:287
  103.7 15.0 %collective-permute-start.26 = (bf16[1,128,256]{2,1,0:T(8,128)(2,1)S(1)}, bf16[1,128,256]{2,1,0:T(8,128)(2,1)S(1)}, u32[]{:S(2)}, u32[]{:S(2)}) collective-permute-start(bf16[1,128,256]{2,1,0:T(8,128)(2,1)S(1)} %get-tuple-element.36), channel_id=1, source_target_pairs={{0,12},{2,14},{4,8},{6,10},{8,4},{10,6},{12,0},{14,2},{1,13},{3,15... | collective-permute-start | bytes 196616 | tf_op jit(solution)/shard_map/ppermute | solution.py:287
  105.9 8.2 %collective-permute-start.24 = (bf16[1,128,256]{2,1,0:T(8,128)(2,1)S(1)}, bf16[1,128,256]{2,1,0:T(8,128)(2,1)S(1)}, u32[]{:S(2)}, u32[]{:S(2)}) collective-permute-start(bf16[1,128,256]{2,1,0:T(8,128)(2,1)S(1)} %get-tuple-element.38), channel_id=1, source_target_pairs={{0,8},{2,10},{4,12},{6,14},{8,0},{10,2},{12,4},{14,6},{1,9},{3,11}... | collective-permute-start | bytes 196616 | tf_op jit(solution)/shard_map/ppermute | solution.py:287
  114.1 4.3 %collective-permute-start.25 = (bf16[1,128,256]{2,1,0:T(8,128)(2,1)S(1)}, bf16[1,128,256]{2,1,0:T(8,128)(2,1)S(1)}, u32[]{:S(2)}, u32[]{:S(2)}) collective-permute-start(bf16[1,128,256]{2,1,0:T(8,128)(2,1)S(1)} %get-tuple-element.37), channel_id=1, source_target_pairs={{0,2},{2,0},{4,6},{6,4},{8,10},{10,8},{12,14},{14,12},{1,3},{3,1},... | collective-permute-start | bytes 196616 | tf_op jit(solution)/shard_map/ppermute | solution.py:287
  118.3 24.7 %collective-permute-start.14 = (bf16[1,128,256]{2,1,0:T(8,128)(2,1)S(1)}, bf16[1,128,256]{2,1,0:T(8,128)(2,1)S(1)}, u32[]{:S(2)}, u32[]{:S(2)}) collective-permute-start(bf16[1,128,256]{2,1,0:T(8,128)(2,1)S(1)} %get-tuple-element.40), channel_id=1, source_target_pairs={{0,6},{2,4},{4,2},{6,0},{8,14},{10,12},{12,10},{14,8},{1,7},{3,5},... | collective-permute-start | bytes 196616 | tf_op jit(solution)/shard_map/ppermute | solution.py:287
  118.7 18.2 %collective-permute-start.13 = (bf16[1,128,256]{2,1,0:T(8,128)(2,1)S(1)}, bf16[1,128,256]{2,1,0:T(8,128)(2,1)S(1)}, u32[]{:S(2)}, u32[]{:S(2)}) collective-permute-start(bf16[1,128,256]{2,1,0:T(8,128)(2,1)S(1)} %get-tuple-element.41), channel_id=1, source_target_pairs={{0,4},{2,6},{4,0},{6,2},{8,12},{10,14},{12,8},{14,10},{1,5},{3,7},... | collective-permute-start | bytes 196616 | tf_op jit(solution)/shard_map/ppermute | solution.py:287
  121.6 14.7 %collective-permute-start.12 = (bf16[1,128,256]{2,1,0:T(8,128)(2,1)S(1)}, bf16[1,128,256]{2,1,0:T(8,128)(2,1)S(1)}, u32[]{:S(2)}, u32[]{:S(2)}) collective-permute-start(bf16[1,128,256]{2,1,0:T(8,128)(2,1)S(1)} %get-tuple-element.42), channel_id=1, source_target_pairs={{0,10},{2,8},{4,14},{6,12},{8,2},{10,0},{12,6},{14,4},{1,11},{3,9}... | collective-permute-start | bytes 196616 | tf_op jit(solution)/shard_map/ppermute | solution.py:287
  122.3 13.4 %collective-permute-start.11 = (bf16[1,128,256]{2,1,0:T(8,128)(2,1)S(1)}, bf16[1,128,256]{2,1,0:T(8,128)(2,1)S(1)}, u32[]{:S(2)}, u32[]{:S(2)}) collective-permute-start(bf16[1,128,256]{2,1,0:T(8,128)(2,1)S(1)} %get-tuple-element.43), channel_id=1, source_target_pairs={{0,12},{2,14},{4,8},{6,10},{8,4},{10,6},{12,0},{14,2},{1,13},{3,15... | collective-permute-start | bytes 196616 | tf_op jit(solution)/shard_map/ppermute | solution.py:287
  124.2 6.6 %collective-permute-start.9 = (bf16[1,128,256]{2,1,0:T(8,128)(2,1)S(1)}, bf16[1,128,256]{2,1,0:T(8,128)(2,1)S(1)}, u32[]{:S(2)}, u32[]{:S(2)}) collective-permute-start(bf16[1,128,256]{2,1,0:T(8,128)(2,1)S(1)} %get-tuple-element.45), channel_id=1, source_target_pairs={{0,8},{2,10},{4,12},{6,14},{8,0},{10,2},{12,4},{14,6},{1,9},{3,11}... | collective-permute-start | bytes 196616 | tf_op jit(solution)/shard_map/ppermute | solution.py:287
  125.5 12.1 %copy-start.5 = (bf16[8,128,256]{2,1,0:T(8,128)(2,1)}, bf16[8,128,256]{2,1,0:T(8,128)(2,1)S(1)}, u32[]{:S(2)}) copy-start(bf16[8,128,256]{2,1,0:T(8,128)(2,1)S(1)} %constant_dynamic-update-slice_fusion) | copy-start | bytes 1572868
  130.8 4.3 %collective-permute-start.10 = (bf16[1,128,256]{2,1,0:T(8,128)(2,1)S(1)}, bf16[1,128,256]{2,1,0:T(8,128)(2,1)S(1)}, u32[]{:S(2)}, u32[]{:S(2)}) collective-permute-start(bf16[1,128,256]{2,1,0:T(8,128)(2,1)S(1)} %get-tuple-element.44), channel_id=1, source_target_pairs={{0,2},{2,0},{4,6},{6,4},{8,10},{10,8},{12,14},{14,12},{1,3},{3,1},... | collective-permute-start | bytes 196616 | tf_op jit(solution)/shard_map/ppermute | solution.py:287

commit v7 on v0

v7 whole, which is shorter than its diff:
```python
import functools
import math

import jax
import jax.numpy as jnp
import ml_dtypes
import numpy as np
from jax import lax
from jax.experimental import pallas as pl
from jax.experimental.pallas import tpu as pltpu
from jax.sharding import PartitionSpec as P

SUBPIX = 16
BLOCK = 512
IMAGE_BLOCK = 256
VMEM_LIMIT = 40 * 1024 * 1024
HBM = pl.BlockSpec(memory_space=pltpu.HBM)
ANYWHERE = pl.BlockSpec(memory_space=pl.ANY)


def packed_freqs(length, cols):
    index = np.arange(length // 2, dtype=np.int32)
    quarter = length // 4
    return 2 * (index % quarter) + index // quarter


def packed_table(length, cols):
    half = length // 2
    freqs = packed_freqs(length, cols)
    positions = np.arange(half, dtype=np.int32)
    turns = freqs[:, None] * positions[None, :] % length
    angles = turns.astype(np.float32) * np.float32(2.0 * math.pi / length)
    factor = np.float32(1.0 / math.sqrt(length))
    cosine = np.cos(angles) * factor
    sine = np.sin(angles) * factor
    sine[0] = np.where(positions % 2 == 0, factor, -factor)
    blocks = np.stack([cosine.reshape(-1, cols, half), sine.reshape(-1, cols, half)], axis=1)
    return blocks.reshape(length, half).astype(ml_dtypes.bfloat16)


def cost(flops, bytes_accessed):
    return pl.CostEstimate(flops=flops, bytes_accessed=bytes_accessed, transcendentals=0)


def start_copies(pairs, sems):
    copies = [
        pltpu.make_async_copy(source, target, sems.at[index])
        for index, (source, target) in enumerate(pairs)
    ]
    for copy in copies:
        copy.start()
    return copies


def wait_copies(copies):
    for copy in copies:
        copy.wait()


def fold(first, second):
    first, second = first.astype(jnp.float32), second.astype(jnp.float32)
    return (first + second).astype(jnp.bfloat16), (first - second).astype(jnp.bfloat16)


def row_kernel(
    images_hbm, table_hbm, out_hbm, images, table, folded, staged, image_sems, table_sems, out_sems
):
    loc_epochs, loc_rows, length = images.shape
    half = length // 2
    devices, _, _, width = staged.shape
    steps = length // BLOCK
    dests = devices // steps
    half_rows = loc_rows // 2
    image_parts = [
        (loc, slice(part * half_rows, (part + 1) * half_rows))
        for loc in range(loc_epochs)
        for part in range(2)
    ]
    image_copies = start_copies(
        [(images_hbm.at[loc, rows], images.at[loc, rows]) for loc, rows in image_parts], image_sems
    )
    table_copies = start_copies(
        [
            (table_hbm.at[:, step * BLOCK : (step + 1) * BLOCK], table.at[step])
            for step in range(steps)
        ],
        table_sems,
    )
    for copy, (loc, rows) in zip(image_copies, image_parts):
        copy.wait()
        at = slice(loc * loc_rows + rows.start, loc * loc_rows + rows.stop)
        folded[0, at], folded[1, at] = fold(images[loc, rows, :half], images[loc, rows, half:])
    out_copies = []
    for step in range(steps):
        table_copies[step].wait()
        pixels = folded[2 * step // steps]
        terms = jnp.dot(pixels, table[step], preferred_element_type=jnp.float32)
        terms = terms.astype(jnp.bfloat16)
        for dest in range(dests):
            for loc in range(loc_epochs):
                staged[step * dests + dest, loc] = terms[
                    loc * loc_rows : (loc + 1) * loc_rows, dest * width : (dest + 1) * width
                ]
        at = pl.ds(step * dests, dests)
        out_copies.append(pltpu.make_async_copy(staged.at[at], out_hbm.at[at], out_sems.at[step]))
        out_copies[-1].start()
    wait_copies(out_copies)


def row_transform(images, table_t, devices):
    loc_epochs, loc_rows, length = images.shape
    half = length // 2
    rows = loc_epochs * loc_rows
    steps = length // BLOCK
    out = (devices, loc_epochs, loc_rows, length // devices)
    return pl.pallas_call(
        row_kernel,
        in_specs=[HBM, HBM],
        out_specs=HBM,
        out_shape=jax.ShapeDtypeStruct(out, jnp.bfloat16),
        scratch_shapes=[
            pltpu.VMEM(images.shape, jnp.bfloat16),
            pltpu.VMEM((steps, half, BLOCK), jnp.bfloat16),
            pltpu.VMEM((2, rows, half), jnp.bfloat16),
            pltpu.VMEM(out, jnp.bfloat16),
            pltpu.SemaphoreType.DMA((2 * loc_epochs,)),
            pltpu.SemaphoreType.DMA((steps,)),
            pltpu.SemaphoreType.DMA((steps,)),
        ],
        compiler_params=pltpu.CompilerParams(vmem_limit_bytes=VMEM_LIMIT),
        cost_estimate=cost(2 * rows * half * length, 2 * half * length + 4 * rows * length),
        name="row_transform",
    )(images, table_t)


def swap_halves(values):
    width = values.shape[1]
    if width % 128 == 0:
        return pltpu.roll(values, width // 2, axis=1)
    return jnp.concatenate([values[:, width // 2 :], values[:, : width // 2]], axis=1)


def ramp_sums(products, coefs, factors, rates, epochs, leads):
    block = products.shape[0]
    width = products.shape[1] // epochs
    cols = width // 2
    groups = block // width
    pairs = rates * epochs
    products = products.reshape(groups, 2, cols, epochs * width)
    even = products[:, 0].reshape(groups * cols, epochs * width)
    odd = products[:, 1].reshape(groups * cols, epochs * width)
    results = []
    for rate in range(rates):
        straight, crossed, lead = [0.0, 0.0], [0.0, 0.0], [0.0, 0.0]
        for epoch in range(epochs):
            pair = rate * epochs + epoch
            even_part = even[:, epoch * width : (epoch + 1) * width]
            odd_part = odd[:, epoch * width : (epoch + 1) * width]
            cos_row = coefs[:, pair : pair + 1]
            sin_row = coefs[:, pairs + pair : pairs + pair + 1]
            turned = (
                cos_row * even_part + sin_row * odd_part,
                cos_row * odd_part - sin_row * even_part,
            )
            lanes = [factors[kind * pairs + pair : kind * pairs + pair + 1, :] for kind in range(4)]
            for which in range(2):
                straight[which] += turned[which] * lanes[0]
                crossed[which] += turned[which] * lanes[1]
                if leads:
                    lead[which] += even_part[:8] * lanes[2 + which]
        even_sum = straight[0] + swap_halves(crossed[0])
        odd_sum = straight[1] + swap_halves(crossed[1])
        if leads:
            lead_sum = lead[0] + swap_halves(lead[1])
            first = lax.broadcasted_iota(jnp.int32, even_sum.shape, 0) == 0
            even_sum = jnp.where(first, lead_sum[0:1], even_sum)
        both = jnp.stack(
            [part.reshape(groups, cols, width) for part in (even_sum, odd_sum)], axis=1
        )
        results.append(both.reshape(block, width))
    return results


def column_kernel(
    epoch_count,
    rates,
    z_any,
    table_hbm,
    coef_any,
    factor_any,
    out_hbm,
    received,
    table,
    coefs,
    factors,
    folded,
    sums,
    staged,
    z_sems,
    table_sems,
    small_sems,
    out_sems,
):
    devices, loc_epochs, loc_rows, width = received.shape
    row_count = devices // epoch_count
    epochs = epoch_count * loc_epochs
    length, half = table.shape
    steps = length // BLOCK
    z_parts = z_sems.shape[0]
    per_part = devices // z_parts
    z_copies = start_copies(
        [
            (z_any.at[pl.ds(part * per_part, per_part)], received.at[pl.ds(part * per_part, per_part)])
            for part in range(z_parts)
        ],
        z_sems,
    )
    small_copies = start_copies([(coef_any, coefs), (factor_any, factors)], small_sems)
    table_copies = start_copies(
        [
            (table_hbm.at[pl.ds(step * BLOCK, BLOCK)], table.at[pl.ds(step * BLOCK, BLOCK)])
            for step in range(steps)
        ],
        table_sems,
    )
    wait_copies(z_copies)
    for row in range(row_count // 2):
        sides = []
        for source in (row, row + row_count // 2):
            parts = [
                received[source * epoch_count + core, loc]
                for core in range(epoch_count)
                for loc in range(loc_epochs)
            ]
            sides.append(jnp.concatenate(parts, axis=1))
        at = slice(row * loc_rows, (row + 1) * loc_rows)
        folded[0, at], folded[1, at] = fold(sides[0], sides[1])
    wait_copies(small_copies)
    for step in range(steps):
        at = slice(step * BLOCK, (step + 1) * BLOCK)
        table_copies[step].wait()
        products = jnp.dot(
            table[at], folded[2 * step // steps], preferred_element_type=jnp.float32
        )
        block_coefs = coefs[step * BLOCK // 2 : (step + 1) * BLOCK // 2]
        results = ramp_sums(products, block_coefs, factors, rates, epochs, step == 0)
        for rate in range(rates):
            sums[rate * width : (rate + 1) * width, at] = results[rate].T.astype(jnp.bfloat16)
    loc_rates = rates // epoch_count
    blocks = max(1, half // BLOCK)
    out_copies = []
    for block in range(blocks):
        at = slice(block * BLOCK, (block + 1) * BLOCK)
        even, odd = [
            jnp.dot(
                sums[:, part * half : (part + 1) * half],
                table[part * half : (part + 1) * half, at],
                preferred_element_type=jnp.float32,
            )
            for part in range(2)
        ]
        rows_here = BLOCK // loc_rows
        for side, back in enumerate((even + odd, even - odd)):
            back = back.astype(jnp.bfloat16)
            first = side * row_count // 2 + block * rows_here
            for row in range(rows_here):
                for rate in range(rates):
                    dest = (first + row) * epoch_count + rate // loc_rates
                    staged[dest, rate % loc_rates] = back[
                        rate * width : (rate + 1) * width, row * loc_rows : (row + 1) * loc_rows
                    ]
            span = pl.ds(first * epoch_count, rows_here * epoch_count)
            out_copies.append(
                pltpu.make_async_copy(
                    staged.at[span], out_hbm.at[span], out_sems.at[2 * block + side]
                )
            )
            out_copies[-1].start()
    wait_copies(out_copies)


def column_stage(spectra, table, coefs, factors, epoch_count, rates):
    devices, loc_epochs, loc_rows, width = spectra.shape
    length, half = table.shape
    epochs = epoch_count * loc_epochs
    steps = length // BLOCK
    out = (devices, rates // epoch_count, width, loc_rows)
    return pl.pallas_call(
        functools.partial(column_kernel, epoch_count, rates),
        in_specs=[ANYWHERE, HBM, ANYWHERE, ANYWHERE],
        out_specs=HBM,
        out_shape=jax.ShapeDtypeStruct(out, jnp.bfloat16),
        scratch_shapes=[
            pltpu.VMEM(spectra.shape, jnp.bfloat16),
            pltpu.VMEM(table.shape, jnp.bfloat16),
            pltpu.VMEM(coefs.shape, jnp.float32),
            pltpu.VMEM(factors.shape, jnp.float32),
            pltpu.VMEM((2, half, epochs * width), jnp.bfloat16),
            pltpu.VMEM((rates * width, length), jnp.bfloat16),
            pltpu.VMEM(out, jnp.bfloat16),
            pltpu.SemaphoreType.DMA((4,)),
            pltpu.SemaphoreType.DMA((steps,)),
            pltpu.SemaphoreType.DMA((2,)),
            pltpu.SemaphoreType.DMA((2 * max(1, half // BLOCK),)),
        ],
        compiler_params=pltpu.CompilerParams(vmem_limit_bytes=VMEM_LIMIT),
        cost_estimate=cost(
            2 * length * half * (epochs + rates) * width, 2 * length * half + 4 * spectra.size
        ),
        name="column_stage",
    )(spectra, table, coefs, factors)


def image_kernel(
    back_any, table_hbm, out_hbm, back, table, left, staged, back_sem, table_sems, out_sems
):
    length, half = table_hbm.shape
    blocks = half // IMAGE_BLOCK
    back_copy = pltpu.make_async_copy(back_any, back, back_sem)
    back_copy.start()
    table_copies = start_copies(
        [
            (table_hbm.at[:, block * IMAGE_BLOCK : (block + 1) * IMAGE_BLOCK], table.at[block])
            for block in range(blocks)
        ],
        table_sems,
    )
    back_copy.wait()
    left[...] = back[...].T
    out_copies = []
    for block in range(blocks):
        table_copies[block].wait()
        even, odd = [
            jnp.dot(
                left[:, part * half : (part + 1) * half],
                table[block, part * half : (part + 1) * half],
                preferred_element_type=jnp.float32,
            )
            for part in range(2)
        ]
        for side, pixels in enumerate((even + odd, even - odd)):
            at = slice(side * half + block * IMAGE_BLOCK, side * half + (block + 1) * IMAGE_BLOCK)
            staged[:, at] = pixels
            out_copies.append(
                pltpu.make_async_copy(
                    staged.at[:, at], out_hbm.at[0, :, at], out_sems.at[2 * block + side]
                )
            )
            out_copies[-1].start()
    wait_copies(out_copies)


def image_rows(back, table):
    rows = back.shape[1]
    length, half = table.shape
    blocks = half // IMAGE_BLOCK
    return pl.pallas_call(
        image_kernel,
        in_specs=[ANYWHERE, HBM],
        out_specs=HBM,
        out_shape=jax.ShapeDtypeStruct((1, rows, length), jnp.float32),
        scratch_shapes=[
            pltpu.VMEM(back.shape, jnp.bfloat16),
            pltpu.VMEM((blocks, length, IMAGE_BLOCK), jnp.bfloat16),
            pltpu.VMEM((rows, length), jnp.bfloat16),
            pltpu.VMEM((rows, length), jnp.float32),
            pltpu.SemaphoreType.DMA,
            pltpu.SemaphoreType.DMA((blocks,)),
            pltpu.SemaphoreType.DMA((2 * blocks,)),
        ],
        compiler_params=pltpu.CompilerParams(vmem_limit_bytes=VMEM_LIMIT),
        cost_estimate=cost(2 * rows * half * length, 2 * half * length + 6 * rows * length),
        name="image_rows",
    )(back, table)


def turn_angle(turns, whole):
    return (turns % whole).astype(jnp.float32) * (2.0 * math.pi / whole)


def row_factors(shift_y, cols, length):
    freqs = jnp.asarray(packed_freqs(length, cols))[:, None]
    angles = turn_angle((freqs - length // 2) * shift_y[None, :], SUBPIX * length)
    return jnp.concatenate(
        [
            jnp.where(freqs == 0, 1.0, 2.0 * jnp.cos(angles)),
            jnp.where(freqs == 0, 0.0, 2.0 * jnp.sin(angles)),
        ],
        axis=1,
    )


def column_factors(shift_y, shift_x, scale, device, devices, cols, length):
    half = length // 2
    shift_y, shift_x = shift_y[:, None], shift_x[:, None]
    lane = jnp.arange(2 * cols, dtype=jnp.int32)[None, :]
    index = device * cols + lane % cols
    freqs = 2 * (index % (half // 2)) + index // (half // 2)
    is_sine = lane >= cols
    paired = freqs == 0
    zero_col = paired & ~is_sine
    angles = turn_angle(shift_x * (freqs - half), SUBPIX * length)
    ramp_cos = jnp.where(paired, scale, 2.0 * scale * jnp.cos(angles))
    ramp_sin = jnp.where(paired, 0.0, 2.0 * scale * jnp.sin(angles))
    ramp_sin = jnp.where(is_sine, ramp_sin, -ramp_sin)
    cos_x = jnp.cos(turn_angle(shift_x, 2 * SUBPIX))
    cos_y = jnp.cos(turn_angle(shift_y, 2 * SUBPIX))
    cos_xy = jnp.cos(turn_angle(shift_x + shift_y, 2 * SUBPIX))
    main = jnp.where(zero_col, cos_y, cos_xy)
    lead = jnp.where(zero_col, 1.0, cos_x)
    return jnp.concatenate([main * ramp_cos, main * ramp_sin, lead * ramp_cos, lead * ramp_sin])


def local(images, rate_vectors, epoch_times):
    _, loc_rows, length = images.shape
    epoch_count = lax.axis_size("epoch")
    devices = lax.axis_size("row") * epoch_count
    device = lax.axis_index("row") * epoch_count + lax.axis_index("epoch")
    rates, epochs = rate_vectors.shape[0], epoch_times.shape[0]
    cols = length // 2 // devices
    table = packed_table(length, cols)
    table_t = jnp.asarray(np.ascontiguousarray(table.T))
    table = jnp.asarray(table)
    period = SUBPIX * length
    shift_y = (rate_vectors[:, 0:1] * epoch_times[None, :] % period).reshape(-1)
    shift_x = (rate_vectors[:, 1:2] * epoch_times[None, :] % period).reshape(-1)
    coefs = row_factors(shift_y, cols, length)
    scale = 1.0 / math.sqrt(epochs)
    factors = column_factors(shift_y, shift_x, scale, device, devices, cols, length)

    def exchange(values):
        return lax.all_to_all(values, ("row", "epoch"), 0, 0, tiled=True)

    spectra = exchange(row_transform(images, table_t, devices))
    back = exchange(column_stage(spectra, table, coefs, factors, epoch_count, rates))
    return image_rows(back.reshape(length, loc_rows), table)


def solution(mesh):
    in_specs = (P(("group", "epoch"), "row", None), P(), P())
    out_specs = P(("group", "epoch"), "row", None)
    return jax.shard_map(local, mesh=mesh, in_specs=in_specs, out_specs=out_specs, check_vma=False)
```

time: 458 us -> 107 us (0.23); the launches traced: 450 us -> 107 us
  other arithmetic: 189 us -> 0.64 us
  local copies, waits for them, and re-layouts: 81.8 us -> 6.54 us
  matrix products: 58.5 us -> 0 us
  waiting for transfers between devices: 93.3 us -> 39.8 us
  blocking collectives: 14.7 us -> 35.9 us
  Pallas kernels: 0 us -> 16.2 us
    convert_element_type x4 -> x0, other arithmetic: 154 us -> none  [the longest x1 71.3 us: dft_tables(): (jnp.cos(angles) * factor).astype(jnp.bfloat16)]
    dot_general x4 -> x0, matrix products: 58.5 us -> none  [the longest x1 22.7 us: local(): jnp.einsum('vetr,wru->wvteu', gathered, stacked, preferred_element_type=j...]
    all_to_all x2 -> x1, waiting for transfers between devices: 93.3 us -> 39.8 us  [exchange(): return lax.all_to_all(values, ('row', 'epoch'), 0, 0, tiled=True)]
    all_to_all x8 -> x0, local copies, waits for them, and re-layouts: 31.5 us -> none  [the longest x3 22.2 us: local(): lax.all_to_all(row_spectrum, 'row', split_axis=0, concat_axis=3, tiled=True)]
    reduce_sum x2 -> x0, other arithmetic: 24.9 us -> none  [one_rate(): summed_re = jnp.sum(real_part * ramp_re - imag_part * ramp_im, axis=1)]
    all_to_all x2 -> x1, blocking collectives: 14.7 us -> 35.9 us  [exchange(): return lax.all_to_all(values, ('row', 'epoch'), 0, 0, tiled=True)]
    convert_element_type x1 -> x0, local copies, waits for them, and re-layouts: 19.1 us -> none  [local(): row_spectrum = (row_terms * sign_wide).astype(jnp.bfloat16)]
    another operation x5 -> x0, local copies, waits for them, and re-layouts: 16.9 us -> none  [the longest x1 14 us: local(): jnp.stack([real_part, imag_part], axis=2).astype(jnp.bfloat16)]
  transfers between devices with their start and end apart: 2 -> 1, of which waited for: 1 -> 1; matrix products, arithmetic and copies ran while one was open for 16% -> 1% of each run, Pallas kernels for 0% -> 0%
where the time goes in v7:
time: 107 us
  waiting for transfers between devices  39.8 us (37%)
  blocking collectives  35.9 us (34%)
  Pallas kernels  16.2 us (15%)
  starting transfers between devices  7.5 us (7%)
  local copies, waits for them, and re-layouts  6.54 us (6%)
    all_to_all x1, waiting for transfers between devices, exchange(): return lax.all_to_all(values, ('row', 'epoch'), 0, 0, tiled=True)  39.8 us
    all_to_all x1, blocking collectives, exchange(): return lax.all_to_all(values, ('row', 'epoch'), 0, 0, tiled=True)  35.9 us
    pallas_call x1, Pallas kernels, column_stage(): pl.pallas_call(functools.partial(column_kernel, epoch_count, rates), in_s...  7.56 us
    all_to_all x1, starting transfers between devices, exchange(): return lax.all_to_all(values, ('row', 'epoch'), 0, 0, tiled=True)  7.5 us
    unnamed x16, local copies, waits for them, and re-layouts  6 us
    pallas_call x1, Pallas kernels, row_transform(): pl.pallas_call(row_kernel, in_specs=[HBM, HBM], out_specs=HBM, out_shape=...  5.01 us
    pallas_call x1, Pallas kernels, image_rows(): pl.pallas_call(image_kernel, in_specs=[ANYWHERE, HBM], out_specs=HBM, out...  3.66 us
  transfers between devices with their start and end apart: 1, of which 1 were waited for; matrix products, arithmetic and copies ran while one was open for 1% of the time, Pallas kernels for 0%

profile of v7, /device:TPU:0, one launch (start us, length us, event | category | flops | bytes accessed | tf_op | source)
XLA Modules:
  0.0 106.8 jit_solution(11996366129699244186)
XLA Ops:
  0.0 0.0 copy-start.2
  0.0 2.2 %copy-done.2 = bf16[1024,2048]{1,0:T(8,128)(2,1)S(1)} copy-done((bf16[1024,2048]{1,0:T(8,128)(2,1)S(1)}, bf16[1024,2048]{1,0:T(8,128)(2,1)}, u32[]{:S(2)}) %copy-start.2) | copy-done | bytes 4194328
  2.2 0.0 copy-start.3
  2.2 1.6 %copy-done.3 = bf16[2,256,2048]{2,1,0:T(8,128)(2,1)S(1)} copy-done((bf16[2,256,2048]{2,1,0:T(8,128)(2,1)S(1)}, bf16[2,256,2048]{2,1,0:T(8,128)(2,1)}, u32[]{:S(2)}) %copy-start.3) | copy-done | bytes 2097176
  3.8 5.0 %row_transform.1 = bf16[16,2,256,128]{3,2,1,0:T(8,128)(2,1)} custom-call(bf16[2,256,2048]{2,1,0:T(8,128)(2,1)S(1)} %copy-done.3, bf16[1024,2048]{1,0:T(8,128)(2,1)S(1)} %copy-done.2), custom_call_target="tpu_custom_call" | custom-call | flops 2147483648 | bytes 8388608 | tf_op jit(solution)/shard_map/row_transform/pallas_call | solution.py:116
  8.8 0.0 copy-start.5
  8.8 0.0 copy-start.7
  8.8 0.0 copy-start.4
  8.8 0.0 copy-start.6
  8.8 7.5 %all-to-all-start = ((bf16[16,2,256,128]{3,2,1,0:T(8,128)(2,1)}), bf16[16,2,256,128]{3,2,1,0:T(8,128)(2,1)S(1)}, u32[]{:S(2)}, u32[]{:S(2)}) async-start(bf16[16,2,256,128]{3,2,1,0:T(8,128)(2,1)} %row_transform.1), calls=%async_computation | async-start | bytes 4194304 | tf_op jit(solution)/shard_map/all_to_all | solution.py:432
  16.4 0.0 copy-done.5
  16.4 0.2 slice_reduce_fusion
  16.6 0.0 copy-done.7
  16.6 0.1 broadcast_multiply_fusion
  16.6 0.1 mul.167
  16.7 0.1 fusion.11
  16.8 0.0 copy-done.4
  16.8 0.0 copy-done.6
  16.8 0.2 multiply_select_fusion.2
  17.0 0.2 copy.7.coef_any
  17.2 0.1 mul.182
  17.4 0.1 fusion.14
  17.5 0.1 select_multiply_fusion.3
  17.6 39.8 %all-to-all-done.z_any = bf16[16,2,256,128]{3,2,1,0:T(8,128)(2,1)S(1)} async-done(((bf16[16,2,256,128]{3,2,1,0:T(8,128)(2,1)}), bf16[16,2,256,128]{3,2,1,0:T(8,128)(2,1)S(1)}, u32[]{:S(2)}, u32[]{:S(2)}) %all-to-all-start) | async-done | bytes 2097184 | tf_op jit(solution)/shard_map/all_to_all | solution.py:432
  57.5 0.0 copy-start
  57.5 2.2 %copy-done = bf16[2048,1024]{1,0:T(8,128)(2,1)S(1)} copy-done((bf16[2048,1024]{1,0:T(8,128)(2,1)S(1)}, bf16[2048,1024]{1,0:T(8,128)(2,1)}, u32[]{:S(2)}) %copy-start) | copy-done | bytes 4194328
  59.7 0.0 copy-start.1
  59.7 7.6 %column_stage.1 = bf16[16,1,128,256]{3,2,1,0:T(8,128)(2,1)S(1)} custom-call(bf16[16,2,256,128]{3,2,1,0:T(8,128)(2,1)S(1)} %all-to-all-done.z_any, bf16[2048,1024]{1,0:T(8,128)(2,1)S(1)} %copy-done, f32[1024,16]{1,0:T(8,128)S(1)} %copy.7.coef_any, f32[32,128]{1,0:T(8,128)S(1)} %pad_maximum_fusion.1.factor_any), custom_call_target="tpu_custom_call" | custom-call | flops 3221225472 | bytes 8388608 | tf_op jit(solution)/shard_map/column_stage/pallas_call | solution.py:288
  67.2 35.9 %all_to_all.10 = bf16[16,1,128,256]{3,2,1,0:T(8,128)(2,1)S(1)} all-to-all(bf16[16,1,128,256]{3,2,1,0:T(8,128)(2,1)S(1)} %column_stage.1), channel_id=1, replica_groups=mesh['group'=2,'row'=8,'epoch'=2] {'row','epoch'}, dimensions={0} | all-to-all | bytes 2097152 | tf_op jit(solution)/shard_map/all_to_all | solution.py:432
  103.1 0.0 copy-done.1
  103.1 3.7 %image_rows.1 = f32[1,256,2048]{2,1,0:T(8,128)} custom-call(bf16[2048,256]{1,0:T(8,128)(2,1)S(1)} %bitcast.1, bf16[2048,1024]{1,0:T(8,128)(2,1)S(1)} %copy-done.1), custom_call_target="tpu_custom_call" | custom-call | flops 1073741824 | bytes 7340032 | tf_op jit(solution)/shard_map/image_rows/pallas_call | solution.py:357
  (6 shorter events, 0.1 us)
Async XLA Ops:
  0.0 2.2 %copy-start.2 = (bf16[1024,2048]{1,0:T(8,128)(2,1)S(1)}, bf16[1024,2048]{1,0:T(8,128)(2,1)}, u32[]{:S(2)}) copy-start(bf16[1024,2048]{1,0:T(8,128)(2,1)} %constant.139.clone.table_hbm) | copy-start | bytes 12582916
  2.2 1.6 %copy-start.3 = (bf16[2,256,2048]{2,1,0:T(8,128)(2,1)S(1)}, bf16[2,256,2048]{2,1,0:T(8,128)(2,1)}, u32[]{:S(2)}) copy-start(bf16[2,256,2048]{2,1,0:T(8,128)(2,1)} %images_hbm.1) | copy-start | bytes 6291460
  8.8 7.6 %copy-start.5 = (s32[2,2]{1,0:T(2,128)S(1)}, s32[2,2]{1,0:T(2,128)}, u32[]{:S(2)}) copy-start(s32[2,2]{1,0:T(2,128)} %param.7) | copy-start | bytes 52
  8.8 7.8 %copy-start.7 = (s32[4]{0:T(128)S(1)}, s32[4]{0:T(128)}, u32[]{:S(2)}) copy-start(s32[4]{0:T(128)} %param.8) | copy-start | bytes 52
  8.8 8.0 %copy-start.4 = (s32[1024]{0:T(1024)S(1)}, s32[1024]{0:T(1024)}, u32[]{:S(2)}) copy-start(s32[1024]{0:T(1024)} %constant.144) | copy-start | bytes 12292
  8.8 8.0 %copy-start.6 = (pred[1024]{0:T(1024)(128)(4,1)S(1)}, pred[1024]{0:T(1024)(128)(4,1)}, u32[]{:S(2)}) copy-start(pred[1024]{0:T(1024)(128)(4,1)} %constant.143) | copy-start | bytes 3076
  8.8 48.6 %all-to-all-start = ((bf16[16,2,256,128]{3,2,1,0:T(8,128)(2,1)}), bf16[16,2,256,128]{3,2,1,0:T(8,128)(2,1)S(1)}, u32[]{:S(2)}, u32[]{:S(2)}) async-start(bf16[16,2,256,128]{3,2,1,0:T(8,128)(2,1)} %row_transform.1), calls=%async_computation | async-start | bytes 4194304 | tf_op jit(solution)/shard_map/all_to_all | solution.py:432
  57.5 2.2 %copy-start = (bf16[2048,1024]{1,0:T(8,128)(2,1)S(1)}, bf16[2048,1024]{1,0:T(8,128)(2,1)}, u32[]{:S(2)}) copy-start(bf16[2048,1024]{1,0:T(8,128)(2,1)} %constant.140.clone.table_hbm) | copy-start | bytes 12582916
  59.7 43.4 %copy-start.1 = (bf16[2048,1024]{1,0:T(8,128)(2,1)S(1)}, bf16[2048,1024]{1,0:T(8,128)(2,1)}, u32[]{:S(2)}) copy-start(bf16[2048,1024]{1,0:T(8,128)(2,1)} %constant.140.clone.table_hbm) | copy-start | bytes 12582916

commit v8 on v7

--- a/solution.py
+++ b/solution.py
@@ -13,7 +13,7 @@
 SUBPIX = 16
 BLOCK = 512
 IMAGE_BLOCK = 256
-VMEM_LIMIT = 40 * 1024 * 1024
+VMEM_LIMIT = 58 * 1024 * 1024
 HBM = pl.BlockSpec(memory_space=pltpu.HBM)
 ANYWHERE = pl.BlockSpec(memory_space=pl.ANY)
 

time: 107 us -> 108 us (level)
  Pallas kernels: 16.2 us -> 21.7 us
  local copies, waits for them, and re-layouts: 6.54 us -> 2.71 us
  waiting for transfers between devices: 39.8 us -> 38.4 us
    unnamed x16 -> x10, local copies, waits for them, and re-layouts: 6 us -> 1.34 us
    pallas_call x1, Pallas kernels: 7.56 us -> 10.1 us  [column_stage(): pl.pallas_call(functools.partial(column_kernel, epoch_count, rates), in_s...]
    pallas_call x1, Pallas kernels: 3.66 us -> 5.27 us  [image_rows(): pl.pallas_call(image_kernel, in_specs=[ANYWHERE, HBM], out_specs=HBM, out...]
    all_to_all x1, waiting for transfers between devices: 39.8 us -> 38.4 us  [exchange(): return lax.all_to_all(values, ('row', 'epoch'), 0, 0, tiled=True)]
    pallas_call x1, Pallas kernels: 5.01 us -> 6.34 us  [row_transform(): pl.pallas_call(row_kernel, in_specs=[HBM, HBM], out_specs=HBM, out_shape=...]
  transfers between devices with their start and end apart: 1 -> 1, of which waited for: 1 -> 1; matrix products, arithmetic and copies ran while one was open for 1% -> 2% of each run, Pallas kernels for 0% -> 0%
where the time goes in v8:
time: 108 us
  waiting for transfers between devices  38.4 us (36%)
  blocking collectives  36.2 us (34%)
  Pallas kernels  21.7 us (20%)
  starting transfers between devices  7.5 us (7%)
  local copies, waits for them, and re-layouts  2.71 us (3%)
  other arithmetic  1.24 us (1%)
    all_to_all x1, waiting for transfers between devices, exchange(): return lax.all_to_all(values, ('row', 'epoch'), 0, 0, tiled=True)  38.4 us
    all_to_all x1, blocking collectives, exchange(): return lax.all_to_all(values, ('row', 'epoch'), 0, 0, tiled=True)  36.2 us
    pallas_call x1, Pallas kernels, column_stage(): pl.pallas_call(functools.partial(column_kernel, epoch_count, rates), in_s...  10.1 us
    all_to_all x1, starting transfers between devices, exchange(): return lax.all_to_all(values, ('row', 'epoch'), 0, 0, tiled=True)  7.5 us
    pallas_call x1, Pallas kernels, row_transform(): pl.pallas_call(row_kernel, in_specs=[HBM, HBM], out_specs=HBM, out_shape=...  6.34 us
    pallas_call x1, Pallas kernels, image_rows(): pl.pallas_call(image_kernel, in_specs=[ANYWHERE, HBM], out_specs=HBM, out...  5.27 us
  transfers between devices with their start and end apart: 1, of which 1 were waited for; matrix products, arithmetic and copies ran while one was open for 2% of the time, Pallas kernels for 0%

profile of v8, /device:TPU:0, one launch (start us, length us, event | category | flops | bytes accessed | tf_op | source)
XLA Modules:
  0.0 107.9 jit_solution(9648927902053015330)
XLA Ops:
  0.0 6.3 %row_transform.1 = bf16[16,2,256,128]{3,2,1,0:T(8,128)(2,1)} custom-call(bf16[2,256,2048]{2,1,0:T(8,128)(2,1)} %images_hbm.1, bf16[1024,2048]{1,0:T(8,128)(2,1)} %constant.139.clone.table_hbm), custom_call_target="tpu_custom_call" | custom-call | flops 2147483648 | bytes 8388608 | tf_op jit(solution)/shard_map/row_transform/pallas_call | solution.py:116
  6.4 0.0 copy-start.2
  6.4 0.0 copy-start.4
  6.4 0.0 copy-start.1
  6.4 0.0 copy-start.3
  6.4 7.5 %all-to-all-start = ((bf16[16,2,256,128]{3,2,1,0:T(8,128)(2,1)}), bf16[16,2,256,128]{3,2,1,0:T(8,128)(2,1)S(1)}, u32[]{:S(2)}, u32[]{:S(2)}) async-start(bf16[16,2,256,128]{3,2,1,0:T(8,128)(2,1)} %row_transform.1), calls=%async_computation | async-start | bytes 4194304 | tf_op jit(solution)/shard_map/all_to_all | solution.py:432
  13.9 0.0 copy-done.2
  13.9 0.2 slice_reduce_fusion
  14.1 0.0 copy-done.4
  14.1 0.1 broadcast_multiply_fusion
  14.2 0.1 mul.167
  14.3 0.1 fusion.11
  14.3 0.0 copy-done.1
  14.3 0.0 copy-done.3
  14.4 0.2 multiply_select_fusion.2
  14.6 1.0 copy.7.coef_any
  15.6 0.1 mul.182
  15.7 0.1 fusion.14
  15.8 0.1 select_multiply_fusion.3
  16.0 0.6 pad_maximum_fusion.1.factor_any
  16.6 38.4 %all-to-all-done.z_any = bf16[16,2,256,128]{3,2,1,0:T(8,128)(2,1)S(1)} async-done(((bf16[16,2,256,128]{3,2,1,0:T(8,128)(2,1)}), bf16[16,2,256,128]{3,2,1,0:T(8,128)(2,1)S(1)}, u32[]{:S(2)}, u32[]{:S(2)}) %all-to-all-start) | async-done | bytes 2097184 | tf_op jit(solution)/shard_map/all_to_all | solution.py:432
  55.0 0.0 copy-start
  55.0 1.3 %copy-done = bf16[16,2,256,128]{3,2,1,0:T(8,128)(2,1)} copy-done((bf16[16,2,256,128]{3,2,1,0:T(8,128)(2,1)}, bf16[16,2,256,128]{3,2,1,0:T(8,128)(2,1)S(1)}, u32[]{:S(2)}) %copy-start) | copy-done | bytes 2097176
  56.3 10.1 %column_stage.1 = bf16[16,1,128,256]{3,2,1,0:T(8,128)(2,1)} custom-call(bf16[16,2,256,128]{3,2,1,0:T(8,128)(2,1)} %copy-done, bf16[2048,1024]{1,0:T(8,128)(2,1)} %constant.140.clone.table_hbm, f32[1024,16]{1,0:T(8,128)} %copy.7.coef_any, f32[32,128]{1,0:T(8,128)} %pad_maximum_fusion.1.factor_any), custom_call_target="tpu_custom_call" | custom-call | flops 3221225472 | bytes 8388608 | tf_op jit(solution)/shard_map/column_stage/pallas_call | solution.py:288
  66.4 36.2 %all_to_all.10 = bf16[16,1,128,256]{3,2,1,0:T(8,128)(2,1)} all-to-all(bf16[16,1,128,256]{3,2,1,0:T(8,128)(2,1)} %column_stage.1), channel_id=1, replica_groups=mesh['group'=2,'row'=8,'epoch'=2] {'row','epoch'}, dimensions={0} | all-to-all | bytes 2097152 | tf_op jit(solution)/shard_map/all_to_all | solution.py:432
  102.6 5.3 %image_rows.1 = f32[1,256,2048]{2,1,0:T(8,128)} custom-call(bf16[2048,256]{1,0:T(8,128)(2,1)} %bitcast.1, bf16[2048,1024]{1,0:T(8,128)(2,1)} %constant.140.clone.table_hbm), custom_call_target="tpu_custom_call" | custom-call | flops 1073741824 | bytes 7340032 | tf_op jit(solution)/shard_map/image_rows/pallas_call | solution.py:357
  (5 shorter events, 0.1 us)
Async XLA Ops:
  6.4 7.6 %copy-start.2 = (s32[2,2]{1,0:T(2,128)S(1)}, s32[2,2]{1,0:T(2,128)}, u32[]{:S(2)}) copy-start(s32[2,2]{1,0:T(2,128)} %param.7) | copy-start | bytes 52
  6.4 7.7 %copy-start.4 = (s32[4]{0:T(128)S(1)}, s32[4]{0:T(128)}, u32[]{:S(2)}) copy-start(s32[4]{0:T(128)} %param.8) | copy-start | bytes 52
  6.4 8.0 %copy-start.1 = (s32[1024]{0:T(1024)S(1)}, s32[1024]{0:T(1024)}, u32[]{:S(2)}) copy-start(s32[1024]{0:T(1024)} %constant.144) | copy-start | bytes 12292
  6.4 8.0 %copy-start.3 = (pred[1024]{0:T(1024)(128)(4,1)S(1)}, pred[1024]{0:T(1024)(128)(4,1)}, u32[]{:S(2)}) copy-start(pred[1024]{0:T(1024)(128)(4,1)} %constant.143) | copy-start | bytes 3076
  6.4 48.6 %all-to-all-start = ((bf16[16,2,256,128]{3,2,1,0:T(8,128)(2,1)}), bf16[16,2,256,128]{3,2,1,0:T(8,128)(2,1)S(1)}, u32[]{:S(2)}, u32[]{:S(2)}) async-start(bf16[16,2,256,128]{3,2,1,0:T(8,128)(2,1)} %row_transform.1), calls=%async_computation | async-start | bytes 4194304 | tf_op jit(solution)/shard_map/all_to_all | solution.py:432
  55.0 1.3 %copy-start = (bf16[16,2,256,128]{3,2,1,0:T(8,128)(2,1)}, bf16[16,2,256,128]{3,2,1,0:T(8,128)(2,1)S(1)}, u32[]{:S(2)}) copy-start(bf16[16,2,256,128]{3,2,1,0:T(8,128)(2,1)S(1)} %all-to-all-done.z_any) | copy-start | bytes 6291460

commit v9 on v8

v9 whole, which is shorter than its diff:
```python
import functools
import math

import jax
import jax.numpy as jnp
import ml_dtypes
import numpy as np
from jax import lax
from jax.experimental import pallas as pl
from jax.experimental.pallas import tpu as pltpu
from jax.sharding import PartitionSpec as P

SUBPIX = 16
GROUP = 128
BLOCK = 512
IMAGE_BLOCK = 256
ROW_CHUNK = 16
MIB = 1024 * 1024
CONTRACT_LAST = (((1,), (1,)), ((), ()))
HBM = pl.BlockSpec(memory_space=pltpu.HBM)
ANYWHERE = pl.BlockSpec(memory_space=pl.ANY)


def packed_table(length):
    half = length // 2
    index = np.arange(half, dtype=np.int32)
    freqs = 2 * (index % (half // 2)) + index // (half // 2)
    positions = np.arange(half, dtype=np.int32)
    turns = freqs[:, None] * positions[None, :] % length
    angles = turns.astype(np.float32) * np.float32(2.0 * math.pi / length)
    factor = np.float32(1.0 / math.sqrt(length))
    cosine = np.cos(angles) * factor
    sine = np.sin(angles) * factor
    sine[0] = np.where(positions % 2 == 0, factor, -factor)
    groups = np.stack([cosine.reshape(-1, GROUP, half), sine.reshape(-1, GROUP, half)], axis=1)
    return groups.reshape(length, half).astype(ml_dtypes.bfloat16)


def cost(flops, bytes_accessed):
    return pl.CostEstimate(flops=flops, bytes_accessed=bytes_accessed, transcendentals=0)


def start_copies(pairs, sems):
    copies = [
        pltpu.make_async_copy(source, target, sems.at[index])
        for index, (source, target) in enumerate(pairs)
    ]
    for copy in copies:
        copy.start()
    return copies


def wait_copies(copies):
    for copy in copies:
        copy.wait()


def fold(first, second):
    first, second = first.astype(jnp.float32), second.astype(jnp.float32)
    return (first + second).astype(jnp.bfloat16), (first - second).astype(jnp.bfloat16)


def row_kernel(
    images_hbm, table_hbm, out_hbm, images, table, folded, staged, image_sems, table_sems, out_sems
):
    loc_epochs, loc_rows, length = images.shape
    half = length // 2
    devices, _, width, _ = staged.shape
    cols = width // 2
    steps = length // BLOCK
    per_step = devices // steps
    per_group = GROUP // cols
    half_rows = loc_rows // 2
    image_parts = [
        (loc, slice(part * half_rows, (part + 1) * half_rows))
        for loc in range(loc_epochs)
        for part in range(2)
    ]
    image_copies = start_copies(
        [(images_hbm.at[loc, rows], images.at[loc, rows]) for loc, rows in image_parts], image_sems
    )
    table_copies = start_copies(
        [
            (table_hbm.at[pl.ds(step * BLOCK, BLOCK)], table.at[pl.ds(step * BLOCK, BLOCK)])
            for step in range(steps)
        ],
        table_sems,
    )
    for copy, (loc, rows) in zip(image_copies, image_parts):
        copy.wait()
        at = slice(loc * loc_rows + rows.start, loc * loc_rows + rows.stop)
        folded[0, at], folded[1, at] = fold(images[loc, rows, :half], images[loc, rows, half:])
    out_copies = []
    for step in range(steps):
        table_copies[step].wait()
        terms = lax.dot_general(
            table[step * BLOCK : (step + 1) * BLOCK],
            folded[2 * step // steps],
            CONTRACT_LAST,
            preferred_element_type=jnp.float32,
        )
        for dest in range(per_step):
            start = dest // per_group * 2 * GROUP + dest % per_group * cols
            parts = [terms[first : first + cols] for first in (start, start + GROUP)]
            block = jnp.concatenate(parts, axis=0).astype(jnp.bfloat16)
            for loc in range(loc_epochs):
                staged[step * per_step + dest, loc] = block[:, loc * loc_rows : (loc + 1) * loc_rows]
        at = pl.ds(step * per_step, per_step)
        out_copies.append(pltpu.make_async_copy(staged.at[at], out_hbm.at[at], out_sems.at[step]))
        out_copies[-1].start()
    wait_copies(out_copies)


def row_transform(images, table, devices):
    loc_epochs, loc_rows, length = images.shape
    half = length // 2
    rows = loc_epochs * loc_rows
    steps = length // BLOCK
    out = (devices, loc_epochs, length // devices, loc_rows)
    return pl.pallas_call(
        row_kernel,
        in_specs=[HBM, HBM],
        out_specs=HBM,
        out_shape=jax.ShapeDtypeStruct(out, jnp.bfloat16),
        scratch_shapes=[
            pltpu.VMEM(images.shape, jnp.bfloat16),
            pltpu.VMEM(table.shape, jnp.bfloat16),
            pltpu.VMEM((2, rows, half), jnp.bfloat16),
            pltpu.VMEM(out, jnp.bfloat16),
            pltpu.SemaphoreType.DMA((2 * loc_epochs,)),
            pltpu.SemaphoreType.DMA((steps,)),
            pltpu.SemaphoreType.DMA((steps,)),
        ],
        compiler_params=pltpu.CompilerParams(vmem_limit_bytes=58 * MIB),
        cost_estimate=cost(2 * rows * half * length, 2 * half * length + 4 * rows * length),
        name="row_transform",
    )(images, table)


def turn_angle(turns, whole):
    return (turns & (whole - 1)).astype(jnp.float32) * (2.0 * math.pi / whole)


def spread_pairs(scalars, lanes):
    pair = lax.broadcasted_iota(jnp.int32, (len(scalars), lanes), 0)
    values = jnp.zeros((len(scalars), lanes), jnp.int32)
    for index, scalar in enumerate(scalars):
        values = jnp.where(pair == index, scalar, values)
    return values


def packed_freqs(index, half):
    return 2 * (index & (half // 2 - 1)) + (index >= half // 2).astype(jnp.int32)


def row_factors(shift_y, half):
    shifts = spread_pairs(shift_y, half)
    freqs = packed_freqs(lax.broadcasted_iota(jnp.int32, shifts.shape, 1), half)
    angles = turn_angle((freqs - half) * shifts, SUBPIX * 2 * half)
    cos_rows = jnp.where(freqs == 0, 1.0, 2.0 * jnp.cos(angles))
    return cos_rows, jnp.where(freqs == 0, 0.0, 2.0 * jnp.sin(angles))


def column_factors(shift_y, shift_x, scale, device, cols, half):
    shifts_y, shifts_x = spread_pairs(shift_y, GROUP), spread_pairs(shift_x, GROUP)
    lane = lax.broadcasted_iota(jnp.int32, shifts_x.shape, 1)
    freqs = packed_freqs(device * cols + (lane & (cols - 1)), half)
    is_sine = (lane & cols) > 0
    paired = freqs == 0
    zero_col = paired & jnp.logical_not(is_sine)
    angles = turn_angle(shifts_x * (freqs - half), SUBPIX * 2 * half)
    ramp_cos = jnp.where(paired, scale, 2.0 * scale * jnp.cos(angles))
    ramp_sin = jnp.where(paired, 0.0, 2.0 * scale * jnp.sin(angles))
    ramp_sin = jnp.where(is_sine, ramp_sin, -ramp_sin)
    cos_x = jnp.cos(turn_angle(shifts_x, 2 * SUBPIX))
    cos_y = jnp.cos(turn_angle(shifts_y, 2 * SUBPIX))
    cos_xy = jnp.cos(turn_angle(shifts_x + shifts_y, 2 * SUBPIX))
    main = jnp.where(zero_col, cos_y, cos_xy)
    lead = jnp.where(zero_col, 1.0, cos_x)
    return jnp.concatenate(
        [main * ramp_cos, main * ramp_sin, lead * ramp_cos, lead * ramp_sin], axis=0
    )


def column_kernel(
    epoch_count,
    rate_smem,
    time_smem,
    z_any,
    table_any,
    out_hbm,
    received,
    table,
    rows_cos,
    rows_sin,
    spread,
    folded,
    products,
    sums,
    staged,
    z_sems,
    table_sems,
    out_sems,
):
    devices, loc_epochs, width, loc_rows = received.shape
    row_count = devices // epoch_count
    epochs = epoch_count * loc_epochs
    rates = rate_smem.shape[0]
    pairs = rates * epochs
    cols = width // 2
    length, half = table.shape
    steps = length // BLOCK
    z_parts = z_sems.shape[0]
    per_part = devices // z_parts
    z_copies = start_copies(
        [
            (z_any.at[pl.ds(part * per_part, per_part)], received.at[pl.ds(part * per_part, per_part)])
            for part in range(z_parts)
        ],
        z_sems,
    )
    table_copies = start_copies(
        [
            (table_any.at[pl.ds(step * BLOCK, BLOCK)], table.at[pl.ds(step * BLOCK, BLOCK)])
            for step in range(steps)
        ],
        table_sems,
    )
    device = lax.axis_index("row") * epoch_count + lax.axis_index("epoch")
    period = SUBPIX * length
    shift_y, shift_x = [
        [
            rate_smem[rate, axis] * time_smem[epoch] & (period - 1)
            for rate in range(rates)
            for epoch in range(epochs)
        ]
        for axis in range(2)
    ]
    rows_cos[...], rows_sin[...] = row_factors(shift_y, half)
    factors = column_factors(shift_y, shift_x, 1.0 / math.sqrt(epochs), device, cols, half).T
    for kind in range(4):
        for pair in range(pairs):
            at = kind * pairs + pair
            spread[kind, pair] = jnp.broadcast_to(factors[:width, at : at + 1], (width, GROUP))

    wait_copies(z_copies)
    per_tile = max(1, GROUP // loc_rows)
    for tile in range(row_count // 2 // per_tile):
        for core in range(epoch_count):
            for loc in range(loc_epochs):
                sides = []
                for side in range(2):
                    first = side * row_count // 2 + tile * per_tile
                    parts = [
                        received[(first + part) * epoch_count + core, loc] for part in range(per_tile)
                    ]
                    sides.append(parts[0] if per_tile == 1 else jnp.concatenate(parts, axis=1))
                at_row = (core * loc_epochs + loc) * width
                at_lane = tile * per_tile * loc_rows
                at = (slice(at_row, at_row + width), slice(at_lane, at_lane + per_tile * loc_rows))
                plus, minus = fold(sides[0], sides[1])
                folded[(0,) + at] = plus
                folded[(1,) + at] = minus

    chunk = min(ROW_CHUNK, cols)

    def add_ramped(step, group):
        tile = (step * BLOCK // 2 // GROUP + group) * GROUP
        at_even = group * 2 * GROUP
        at_odd = at_even + GROUP
        for rate in range(rates):
            for start in range(0, cols, chunk):
                real = slice(start, start + chunk)
                imag = slice(cols + start, cols + start + chunk)
                totals = [[0.0, 0.0], [0.0, 0.0]]
                leads = [0.0, 0.0]
                for epoch in range(epochs):
                    pair = rate * epochs + epoch
                    cos_row = rows_cos[pair : pair + 1, tile : tile + GROUP]
                    sin_row = rows_sin[pair : pair + 1, tile : tile + GROUP]
                    turned, evens = [], []
                    for part in (real, imag):
                        at = slice(epoch * width + part.start, epoch * width + part.stop)
                        even = products[step % 2, at, at_even : at_even + GROUP]
                        odd = products[step % 2, at, at_odd : at_odd + GROUP]
                        turned.append(
                            (cos_row * even + sin_row * odd, cos_row * odd - sin_row * even)
                        )
                        evens.append(even)
                    straight = [spread[0, pair, part] for part in (real, imag)]
                    crossed = [spread[1, pair, part] for part in (real, imag)]
                    for part in range(2):
                        for which in range(2):
                            totals[part][which] += (
                                straight[part] * turned[part][which]
                                + crossed[1 - part] * turned[1 - part][which]
                            )
                        if step == 0 and group == 0:
                            own, other = (real, imag) if part == 0 else (imag, real)
                            leads[part] += (
                                spread[2, pair, own] * evens[part]
                                + spread[3, pair, other] * evens[1 - part]
                            )
                for part, rows in enumerate((real, imag)):
                    even_sum, odd_sum = totals[part]
                    if step == 0 and group == 0:
                        first = lax.broadcasted_iota(jnp.int32, even_sum.shape, 1) == 0
                        even_sum = jnp.where(first, leads[part], even_sum)
                    at = slice(rate * width + rows.start, rate * width + rows.stop)
                    sums[at, step * BLOCK + at_even : step * BLOCK + at_even + GROUP] = even_sum.astype(
                        jnp.bfloat16
                    )
                    sums[at, step * BLOCK + at_odd : step * BLOCK + at_odd + GROUP] = odd_sum.astype(
                        jnp.bfloat16
                    )

    for step in range(steps):
        table_copies[step].wait()
        products[step % 2] = lax.dot_general(
            folded[2 * step // steps],
            table[step * BLOCK : (step + 1) * BLOCK],
            CONTRACT_LAST,
            preferred_element_type=jnp.float32,
        )
        for group in range(BLOCK // 2 // GROUP):
            add_ramped(step, group)

    loc_rates = rates // epoch_count
    blocks = max(1, half // BLOCK)
    out_copies = []
    for block in range(blocks):
        at = slice(block * BLOCK, (block + 1) * BLOCK)
        even, odd = [
            jnp.dot(
                sums[:, part * half : (part + 1) * half],
                table[part * half : (part + 1) * half, at],
                preferred_element_type=jnp.float32,
            )
            for part in range(2)
        ]
        rows_here = BLOCK // loc_rows
        for side, back in enumerate((even + odd, even - odd)):
            back = back.astype(jnp.bfloat16)
            first = side * row_count // 2 + block * rows_here
            for row in range(rows_here):
                for rate in range(rates):
                    dest = (first + row) * epoch_count + rate // loc_rates
                    staged[dest, rate % loc_rates] = back[
                        rate * width : (rate + 1) * width, row * loc_rows : (row + 1) * loc_rows
                    ]
            span = pl.ds(first * epoch_count, rows_here * epoch_count)
            out_copies.append(
                pltpu.make_async_copy(
                    staged.at[span], out_hbm.at[span], out_sems.at[2 * block + side]
                )
            )
            out_copies[-1].start()
    wait_copies(out_copies)


def column_stage(rate_vectors, epoch_times, spectra, table, epoch_count):
    devices, loc_epochs, width, loc_rows = spectra.shape
    length, half = table.shape
    epochs, rates = epoch_times.shape[0], rate_vectors.shape[0]
    steps = length // BLOCK
    out = (devices, rates // epoch_count, width, loc_rows)
    scalars = pl.BlockSpec(memory_space=pltpu.SMEM)
    return pl.pallas_call(
        functools.partial(column_kernel, epoch_count),
        in_specs=[scalars, scalars, ANYWHERE, ANYWHERE],
        out_specs=HBM,
        out_shape=jax.ShapeDtypeStruct(out, jnp.bfloat16),
        scratch_shapes=[
            pltpu.VMEM(spectra.shape, jnp.bfloat16),
            pltpu.VMEM(table.shape, jnp.bfloat16),
            pltpu.VMEM((rates * epochs, half), jnp.float32),
            pltpu.VMEM((rates * epochs, half), jnp.float32),
            pltpu.VMEM((4, rates * epochs, width, GROUP), jnp.float32),
            pltpu.VMEM((2, epochs * width, half), jnp.bfloat16),
            pltpu.VMEM((2, epochs * width, BLOCK), jnp.float32),
            pltpu.VMEM((rates * width, length), jnp.bfloat16),
            pltpu.VMEM(out, jnp.bfloat16),
            pltpu.SemaphoreType.DMA((4,)),
            pltpu.SemaphoreType.DMA((steps,)),
            pltpu.SemaphoreType.DMA((2 * max(1, half // BLOCK),)),
        ],
        compiler_params=pltpu.CompilerParams(vmem_limit_bytes=40 * MIB),
        cost_estimate=cost(
            2 * length * half * (epochs + rates) * width, 2 * length * half + 4 * spectra.size
        ),
        name="column_stage",
    )(rate_vectors, epoch_times, spectra, table)


def image_kernel(
    back_any, table_hbm, out_hbm, back, table, left, staged, back_sem, table_sems, out_sems
):
    length, half = table_hbm.shape
    blocks = half // IMAGE_BLOCK
    back_copy = pltpu.make_async_copy(back_any, back, back_sem)
    back_copy.start()
    table_copies = start_copies(
        [
            (table_hbm.at[:, block * IMAGE_BLOCK : (block + 1) * IMAGE_BLOCK], table.at[block])
            for block in range(blocks)
        ],
        table_sems,
    )
    back_copy.wait()
    width = back.shape[1]
    cols = width // 2
    per_group = GROUP // cols
    for group in range(back.shape[0] // per_group):
        members = [back[group * per_group + place].astype(jnp.float32) for place in range(per_group)]
        parts = [member[:cols] for member in members] + [member[cols:] for member in members]
        whole = jnp.concatenate(parts, axis=0)
        left[:, group * 2 * GROUP : (group + 1) * 2 * GROUP] = whole.T.astype(jnp.bfloat16)
    out_copies = []
    for block in range(blocks):
        table_copies[block].wait()
        even, odd = [
            jnp.dot(
                left[:, part * half : (part + 1) * half],
                table[block, part * half : (part + 1) * half],
                preferred_element_type=jnp.float32,
            )
            for part in range(2)
        ]
        for side, pixels in enumerate((even + odd, even - odd)):
            at = slice(side * half + block * IMAGE_BLOCK, side * half + (block + 1) * IMAGE_BLOCK)
            staged[:, at] = pixels
            out_copies.append(
                pltpu.make_async_copy(
                    staged.at[:, at], out_hbm.at[0, :, at], out_sems.at[2 * block + side]
                )
            )
            out_copies[-1].start()
    wait_copies(out_copies)


def image_rows(back, table):
    rows = back.shape[2]
    length, half = table.shape
    blocks = half // IMAGE_BLOCK
    return pl.pallas_call(
        image_kernel,
        in_specs=[ANYWHERE, ANYWHERE],
        out_specs=HBM,
        out_shape=jax.ShapeDtypeStruct((1, rows, length), jnp.float32),
        scratch_shapes=[
            pltpu.VMEM(back.shape, jnp.bfloat16),
            pltpu.VMEM((blocks, length, IMAGE_BLOCK), jnp.bfloat16),
            pltpu.VMEM((rows, length), jnp.bfloat16),
            pltpu.VMEM((rows, length), jnp.float32),
            pltpu.SemaphoreType.DMA,
            pltpu.SemaphoreType.DMA((blocks,)),
            pltpu.SemaphoreType.DMA((2 * blocks,)),
        ],
        compiler_params=pltpu.CompilerParams(vmem_limit_bytes=40 * MIB),
        cost_estimate=cost(2 * rows * half * length, 2 * half * length + 6 * rows * length),
        name="image_rows",
    )(back, table)


def local(images, rate_vectors, epoch_times):
    _, loc_rows, length = images.shape
    epoch_count = lax.axis_size("epoch")
    devices = lax.axis_size("row") * epoch_count
    table = jnp.asarray(packed_table(length))

    def exchange(values):
        return lax.all_to_all(values, ("row", "epoch"), 0, 0, tiled=True)

    spectra = exchange(row_transform(images, table, devices))
    back = exchange(column_stage(rate_vectors, epoch_times, spectra, table, epoch_count))
    return image_rows(back.reshape(devices, length // devices, loc_rows), table)


def solution(mesh):
    in_specs = (P(("group", "epoch"), "row", None), P(), P())
    out_specs = P(("group", "epoch"), "row", None)
    return jax.shard_map(local, mesh=mesh, in_specs=in_specs, out_specs=out_specs, check_vma=False)
```

time: 108 us -> 104 us (0.963)
  blocking collectives: 36.2 us -> 84.7 us
  waiting for transfers between devices: 38.4 us -> 0 us
  starting transfers between devices: 7.5 us -> 0 us
  Pallas kernels: 21.7 us -> 18.9 us
  local copies, waits for them, and re-layouts: 2.71 us -> 0.01 us
  other arithmetic: 1.24 us -> 0 us
    all_to_all x1 -> x2, blocking collectives: 36.2 us -> 84.7 us  [exchange(): return lax.all_to_all(values, ('row', 'epoch'), 0, 0, tiled=True)]
    all_to_all x1 -> x0, waiting for transfers between devices: 38.4 us -> none  [exchange(): return lax.all_to_all(values, ('row', 'epoch'), 0, 0, tiled=True)]
    all_to_all x1 -> x0, starting transfers between devices: 7.5 us -> none  [exchange(): return lax.all_to_all(values, ('row', 'epoch'), 0, 0, tiled=True)]
    pallas_call x2, Pallas kernels: 15.4 us -> 12.4 us  [the longest x1 8.7 us: column_stage(): pl.pallas_call(functools.partial(column_kernel, epoch_count), in_specs=[s...]
    unnamed x10 -> x6, local copies, waits for them, and re-layouts: 1.34 us -> 0.01 us
  transfers between devices with their start and end apart: 1 -> 0, of which waited for: 1 -> 0; matrix products, arithmetic and copies ran while one was open for 2% -> 0% of each run, Pallas kernels for 0% -> 0%
where the time goes in v9:
time: 104 us
  blocking collectives  84.7 us (81%)
  Pallas kernels  18.9 us (18%)
    all_to_all x2, blocking collectives, exchange(): return lax.all_to_all(values, ('row', 'epoch'), 0, 0, tiled=True)  84.7 us
    pallas_call x1, Pallas kernels, column_stage(): pl.pallas_call(functools.partial(column_kernel, epoch_count), in_specs=[s...  8.7 us
    pallas_call x1, Pallas kernels, row_transform(): pl.pallas_call(row_kernel, in_specs=[HBM, HBM], out_specs=HBM, out_shape=...  6.51 us
    pallas_call x1, Pallas kernels, image_rows(): pl.pallas_call(image_kernel, in_specs=[ANYWHERE, ANYWHERE], out_specs=HBM...  3.67 us

profile of v9, /device:TPU:0, one launch (start us, length us, event | category | flops | bytes accessed | tf_op | source)
XLA Modules:
  0.0 103.6 jit_solution(15494172437707584851)
XLA Ops:
  0.0 0.0 copy-start.1
  0.0 0.0 copy-start.2
  0.0 6.5 %row_transform.1 = bf16[16,2,128,256]{3,2,1,0:T(8,128)(2,1)} custom-call(bf16[2,256,2048]{2,1,0:T(8,128)(2,1)} %images_hbm.1, bf16[2048,1024]{1,0:T(8,128)(2,1)} %constant.2.clone.table_hbm.table_any), custom_call_target="tpu_custom_call" | custom-call | flops 2147483648 | bytes 8388608 | tf_op jit(solution)/shard_map/row_transform/pallas_call | solution.py:120
  6.5 0.0 copy-start
  6.5 54.9 %all_to_all.10.z_any = bf16[16,2,128,256]{3,2,1,0:T(8,128)(2,1)S(1)} all-to-all(bf16[16,2,128,256]{3,2,1,0:T(8,128)(2,1)} %row_transform.1), channel_id=1, replica_groups=mesh['group'=2,'row'=8,'epoch'=2] {'row','epoch'}, dimensions={0} | all-to-all | bytes 4194304 | tf_op jit(solution)/shard_map/all_to_all | solution.py:472
  61.5 0.0 copy-done.1
  61.5 0.0 copy-done.2
  61.5 0.0 copy-done
  61.5 8.7 %column_stage.1 = bf16[16,1,128,256]{3,2,1,0:T(8,128)(2,1)S(1)} custom-call(s32[2,2]{1,0:T(2,128)S(1)} %copy-done.1, s32[4]{0:T(128)S(1)} %copy-done.2, bf16[16,2,128,256]{3,2,1,0:T(8,128)(2,1)S(1)} %all_to_all.10.z_any, bf16[2048,1024]{1,0:T(8,128)(2,1)S(1)} %copy-done), custom_call_target="tpu_custom_call" | custom-call | flops 3221225472 | bytes 8388608 | tf_op jit(solution)/shard_map/column_stage/pallas_call | solution.py:368
  70.2 29.8 %all_to_all.11 = bf16[16,1,128,256]{3,2,1,0:T(8,128)(2,1)S(1)} all-to-all(bf16[16,1,128,256]{3,2,1,0:T(8,128)(2,1)S(1)} %column_stage.1), channel_id=1, replica_groups=mesh['group'=2,'row'=8,'epoch'=2] {'row','epoch'}, dimensions={0} | all-to-all | bytes 2097152 | tf_op jit(solution)/shard_map/all_to_all | solution.py:472
  100.0 3.7 %image_rows.1 = f32[1,256,2048]{2,1,0:T(8,128)} custom-call(bf16[16,128,256]{2,1,0:T(8,128)(2,1)S(1)} %bitcast.1, bf16[2048,1024]{1,0:T(8,128)(2,1)S(1)} %copy-done), custom_call_target="tpu_custom_call" | custom-call | flops 1073741824 | bytes 7340032 | tf_op jit(solution)/shard_map/image_rows/pallas_call | solution.py:445
Async XLA Ops:
  0.0 61.5 %copy-start.1 = (s32[2,2]{1,0:T(2,128)S(1)}, s32[2,2]{1,0:T(2,128)}, u32[]{:S(2)}) copy-start(s32[2,2]{1,0:T(2,128)} %rate_smem.1) | copy-start | bytes 52
  0.0 61.5 %copy-start.2 = (s32[4]{0:T(128)S(1)}, s32[4]{0:T(128)}, u32[]{:S(2)}) copy-start(s32[4]{0:T(128)} %time_smem.1) | copy-start | bytes 52
  6.5 55.0 %copy-start = (bf16[2048,1024]{1,0:T(8,128)(2,1)S(1)}, bf16[2048,1024]{1,0:T(8,128)(2,1)}, u32[]{:S(2)}) copy-start(bf16[2048,1024]{1,0:T(8,128)(2,1)} %constant.2.clone.table_hbm.table_any) | copy-start | bytes 12582916

commit v10 on v9

--- a/solution.py
+++ b/solution.py
@@ -18,7 +18,7 @@
 MIB = 1024 * 1024
 CONTRACT_LAST = (((1,), (1,)), ((), ()))
 HBM = pl.BlockSpec(memory_space=pltpu.HBM)
-ANYWHERE = pl.BlockSpec(memory_space=pl.ANY)
+IN_VMEM = pl.BlockSpec(memory_space=pltpu.VMEM)
 
 
 def packed_table(length):
@@ -40,16 +40,6 @@
     return pl.CostEstimate(flops=flops, bytes_accessed=bytes_accessed, transcendentals=0)
 
 
-def start_copies(pairs, sems):
-    copies = [
-        pltpu.make_async_copy(source, target, sems.at[index])
-        for index, (source, target) in enumerate(pairs)
-    ]
-    for copy in copies:
-        copy.start()
-    return copies
-
-
 def wait_copies(copies):
     for copy in copies:
         copy.wait()
@@ -70,26 +60,26 @@
     steps = length // BLOCK
     per_step = devices // steps
     per_group = GROUP // cols
-    half_rows = loc_rows // 2
-    image_parts = [
-        (loc, slice(part * half_rows, (part + 1) * half_rows))
+    image_copies = [
+        pltpu.make_async_copy(images_hbm.at[loc], images.at[loc], image_sems.at[loc])
         for loc in range(loc_epochs)
-        for part in range(2)
     ]
-    image_copies = start_copies(
-        [(images_hbm.at[loc, rows], images.at[loc, rows]) for loc, rows in image_parts], image_sems
-    )
-    table_copies = start_copies(
-        [
-            (table_hbm.at[pl.ds(step * BLOCK, BLOCK)], table.at[pl.ds(step * BLOCK, BLOCK)])
-            for step in range(steps)
-        ],
-        table_sems,
-    )
-    for copy, (loc, rows) in zip(image_copies, image_parts):
-        copy.wait()
-        at = slice(loc * loc_rows + rows.start, loc * loc_rows + rows.stop)
-        folded[0, at], folded[1, at] = fold(images[loc, rows, :half], images[loc, rows, half:])
+    table_copies = [
+        pltpu.make_async_copy(
+            table_hbm.at[pl.ds(step * BLOCK, BLOCK)],
+            table.at[pl.ds(step * BLOCK, BLOCK)],
+            table_sems.at[step],
+        )
+        for step in range(steps)
+    ]
+    for copy in image_copies + table_copies[:1]:
+        copy.start()
+    for loc in range(loc_epochs):
+        image_copies[loc].wait()
+        at = slice(loc * loc_rows, (loc + 1) * loc_rows)
+        folded[0, at], folded[1, at] = fold(images[loc, :, :half], images[loc, :, half:])
+    for copy in table_copies[1:]:
+        copy.start()
     out_copies = []
     for step in range(steps):
         table_copies[step].wait()
@@ -127,7 +117,7 @@
             pltpu.VMEM(table.shape, jnp.bfloat16),
             pltpu.VMEM((2, rows, half), jnp.bfloat16),
             pltpu.VMEM(out, jnp.bfloat16),
-            pltpu.SemaphoreType.DMA((2 * loc_epochs,)),
+            pltpu.SemaphoreType.DMA((loc_epochs,)),
             pltpu.SemaphoreType.DMA((steps,)),
             pltpu.SemaphoreType.DMA((steps,)),
         ],
@@ -186,11 +176,9 @@
     epoch_count,
     rate_smem,
     time_smem,
-    z_any,
-    table_any,
-    out_hbm,
     received,
     table,
+    out_hbm,
     rows_cos,
     rows_sin,
     spread,
@@ -198,8 +186,6 @@
     products,
     sums,
     staged,
-    z_sems,
-    table_sems,
     out_sems,
 ):
     devices, loc_epochs, width, loc_rows = received.shape
@@ -210,22 +196,6 @@
     cols = width // 2
     length, half = table.shape
     steps = length // BLOCK
-    z_parts = z_sems.shape[0]
-    per_part = devices // z_parts
-    z_copies = start_copies(
-        [
-            (z_any.at[pl.ds(part * per_part, per_part)], received.at[pl.ds(part * per_part, per_part)])
-            for part in range(z_parts)
-        ],
-        z_sems,
-    )
-    table_copies = start_copies(
-        [
-            (table_any.at[pl.ds(step * BLOCK, BLOCK)], table.at[pl.ds(step * BLOCK, BLOCK)])
-            for step in range(steps)
-        ],
-        table_sems,
-    )
     device = lax.axis_index("row") * epoch_count + lax.axis_index("epoch")
     period = SUBPIX * length
     shift_y, shift_x = [
@@ -243,7 +213,6 @@
             at = kind * pairs + pair
             spread[kind, pair] = jnp.broadcast_to(factors[:width, at : at + 1], (width, GROUP))
 
-    wait_copies(z_copies)
     per_tile = max(1, GROUP // loc_rows)
     for tile in range(row_count // 2 // per_tile):
         for core in range(epoch_count):
@@ -315,7 +284,6 @@
                     )
 
     for step in range(steps):
-        table_copies[step].wait()
         products[step % 2] = lax.dot_general(
             folded[2 * step // steps],
             table[step * BLOCK : (step + 1) * BLOCK],
@@ -362,17 +330,14 @@
     devices, loc_epochs, width, loc_rows = spectra.shape
     length, half = table.shape
     epochs, rates = epoch_times.shape[0], rate_vectors.shape[0]
-    steps = length // BLOCK
     out = (devices, rates // epoch_count, width, loc_rows)
     scalars = pl.BlockSpec(memory_space=pltpu.SMEM)
     return pl.pallas_call(
         functools.partial(column_kernel, epoch_count),
-        in_specs=[scalars, scalars, ANYWHERE, ANYWHERE],
+        in_specs=[scalars, scalars, IN_VMEM, IN_VMEM],
         out_specs=HBM,
         out_shape=jax.ShapeDtypeStruct(out, jnp.bfloat16),
         scratch_shapes=[
-            pltpu.VMEM(spectra.shape, jnp.bfloat16),
-            pltpu.VMEM(table.shape, jnp.bfloat16),
             pltpu.VMEM((rates * epochs, half), jnp.float32),
             pltpu.VMEM((rates * epochs, half), jnp.float32),
             pltpu.VMEM((4, rates * epochs, width, GROUP), jnp.float32),
@@ -380,8 +345,6 @@
             pltpu.VMEM((2, epochs * width, BLOCK), jnp.float32),
             pltpu.VMEM((rates * width, length), jnp.bfloat16),
             pltpu.VMEM(out, jnp.bfloat16),
-            pltpu.SemaphoreType.DMA((4,)),
-            pltpu.SemaphoreType.DMA((steps,)),
             pltpu.SemaphoreType.DMA((2 * max(1, half // BLOCK),)),
         ],
         compiler_params=pltpu.CompilerParams(vmem_limit_bytes=40 * MIB),
@@ -392,21 +355,9 @@
     )(rate_vectors, epoch_times, spectra, table)
 
 
-def image_kernel(
-    back_any, table_hbm, out_hbm, back, table, left, staged, back_sem, table_sems, out_sems
-):
-    length, half = table_hbm.shape
+def image_kernel(back, table, out_hbm, left, staged, out_sems):
+    length, half = table.shape
     blocks = half // IMAGE_BLOCK
-    back_copy = pltpu.make_async_copy(back_any, back, back_sem)
-    back_copy.start()
-    table_copies = start_copies(
-        [
-            (table_hbm.at[:, block * IMAGE_BLOCK : (block + 1) * IMAGE_BLOCK], table.at[block])
-            for block in range(blocks)
-        ],
-        table_sems,
-    )
-    back_copy.wait()
     width = back.shape[1]
     cols = width // 2
     per_group = GROUP // cols
@@ -417,11 +368,11 @@
         left[:, group * 2 * GROUP : (group + 1) * 2 * GROUP] = whole.T.astype(jnp.bfloat16)
     out_copies = []
     for block in range(blocks):
-        table_copies[block].wait()
+        at_block = slice(block * IMAGE_BLOCK, (block + 1) * IMAGE_BLOCK)
         even, odd = [
             jnp.dot(
                 left[:, part * half : (part + 1) * half],
-                table[block, part * half : (part + 1) * half],
+                table[part * half : (part + 1) * half, at_block],
                 preferred_element_type=jnp.float32,
             )
             for part in range(2)
@@ -444,16 +395,12 @@
     blocks = half // IMAGE_BLOCK
     return pl.pallas_call(
         image_kernel,
-        in_specs=[ANYWHERE, ANYWHERE],
+        in_specs=[IN_VMEM, IN_VMEM],
         out_specs=HBM,
         out_shape=jax.ShapeDtypeStruct((1, rows, length), jnp.float32),
         scratch_shapes=[
-            pltpu.VMEM(back.shape, jnp.bfloat16),
-            pltpu.VMEM((blocks, length, IMAGE_BLOCK), jnp.bfloat16),
             pltpu.VMEM((rows, length), jnp.bfloat16),
             pltpu.VMEM((rows, length), jnp.float32),
-            pltpu.SemaphoreType.DMA,
-            pltpu.SemaphoreType.DMA((blocks,)),
             pltpu.SemaphoreType.DMA((2 * blocks,)),
         ],
         compiler_params=pltpu.CompilerParams(vmem_limit_bytes=40 * MIB),

time: 104 us -> 99.9 us (0.961)
  Pallas kernels: 18.9 us -> 14.7 us
    pallas_call x1, Pallas kernels: 8.7 us -> 6.35 us  [column_stage(): pl.pallas_call(functools.partial(column_kernel, epoch_count), in_specs=[s...]
    pallas_call x1, Pallas kernels: 3.67 us -> 2.28 us  [image_rows(): pl.pallas_call(image_kernel, in_specs=[IN_VMEM, IN_VMEM], out_specs=HBM,...]
where the time goes in v10:
time: 99.9 us; the launch traced here: 99.4 us
  blocking collectives  84.7 us (85%)
  Pallas kernels  14.7 us (15%)
    all_to_all x2, blocking collectives, exchange(): return lax.all_to_all(values, ('row', 'epoch'), 0, 0, tiled=True)  84.7 us
    pallas_call x1, Pallas kernels, column_stage(): pl.pallas_call(functools.partial(column_kernel, epoch_count), in_specs=[s...  6.35 us
    pallas_call x1, Pallas kernels, row_transform(): pl.pallas_call(row_kernel, in_specs=[HBM, HBM], out_specs=HBM, out_shape=...  6.02 us
    pallas_call x1, Pallas kernels, image_rows(): pl.pallas_call(image_kernel, in_specs=[IN_VMEM, IN_VMEM], out_specs=HBM,...  2.28 us

profile of v10, /device:TPU:0, one launch (start us, length us, event | category | flops | bytes accessed | tf_op | source)
XLA Modules:
  0.0 99.4 jit_solution(7103902575725009620)
XLA Ops:
  0.0 0.0 copy-start.1
  0.0 0.0 copy-start.2
  0.0 6.0 %row_transform.1 = bf16[16,2,128,256]{3,2,1,0:T(8,128)(2,1)} custom-call(bf16[2,256,2048]{2,1,0:T(8,128)(2,1)} %images_hbm.1, bf16[2048,1024]{1,0:T(8,128)(2,1)} %constant.2.clone.table_hbm.table), custom_call_target="tpu_custom_call" | custom-call | flops 2147483648 | bytes 8388608 | tf_op jit(solution)/shard_map/row_transform/pallas_call | solution.py:110
  6.0 0.0 copy-start
  6.0 54.9 %all_to_all.10.received = bf16[16,2,128,256]{3,2,1,0:T(8,128)(2,1)S(1)} all-to-all(bf16[16,2,128,256]{3,2,1,0:T(8,128)(2,1)} %row_transform.1), channel_id=1, replica_groups=mesh['group'=2,'row'=8,'epoch'=2] {'row','epoch'}, dimensions={0} | all-to-all | bytes 4194304 | tf_op jit(solution)/shard_map/all_to_all | solution.py:419
  61.0 0.0 copy-done.1
  61.0 0.0 copy-done.2
  61.0 0.0 copy-done
  61.0 6.4 %column_stage.1 = bf16[16,1,128,256]{3,2,1,0:T(8,128)(2,1)S(1)} custom-call(s32[2,2]{1,0:T(2,128)S(1)} %copy-done.1, s32[4]{0:T(128)S(1)} %copy-done.2, bf16[16,2,128,256]{3,2,1,0:T(8,128)(2,1)S(1)} %all_to_all.10.received, bf16[2048,1024]{1,0:T(8,128)(2,1)S(1)} %copy-done), custom_call_target="tpu_custom_call" | custom-call | flops 3221225472 | bytes 8388608 | tf_op jit(solution)/shard_map/column_stage/pallas_call | solution.py:335
  67.4 29.8 %all_to_all.11 = bf16[16,1,128,256]{3,2,1,0:T(8,128)(2,1)S(1)} all-to-all(bf16[16,1,128,256]{3,2,1,0:T(8,128)(2,1)S(1)} %column_stage.1), channel_id=1, replica_groups=mesh['group'=2,'row'=8,'epoch'=2] {'row','epoch'}, dimensions={0} | all-to-all | bytes 2097152 | tf_op jit(solution)/shard_map/all_to_all | solution.py:419
  97.1 2.3 %image_rows.1 = f32[1,256,2048]{2,1,0:T(8,128)} custom-call(bf16[16,128,256]{2,1,0:T(8,128)(2,1)S(1)} %bitcast.1, bf16[2048,1024]{1,0:T(8,128)(2,1)S(1)} %copy-done), custom_call_target="tpu_custom_call" | custom-call | flops 1073741824 | bytes 7340032 | tf_op jit(solution)/shard_map/image_rows/pallas_call | solution.py:396
Async XLA Ops:
  0.0 61.0 %copy-start.1 = (s32[2,2]{1,0:T(2,128)S(1)}, s32[2,2]{1,0:T(2,128)}, u32[]{:S(2)}) copy-start(s32[2,2]{1,0:T(2,128)} %rate_smem.1) | copy-start | bytes 52
  0.0 61.0 %copy-start.2 = (s32[4]{0:T(128)S(1)}, s32[4]{0:T(128)}, u32[]{:S(2)}) copy-start(s32[4]{0:T(128)} %time_smem.1) | copy-start | bytes 52
  6.0 55.0 %copy-start = (bf16[2048,1024]{1,0:T(8,128)(2,1)S(1)}, bf16[2048,1024]{1,0:T(8,128)(2,1)}, u32[]{:S(2)}) copy-start(bf16[2048,1024]{1,0:T(8,128)(2,1)} %constant.2.clone.table_hbm.table) | copy-start | bytes 12582916

commit v11 on v10

v11 whole, which is shorter than its diff:
```python
import functools
import math

import jax
import jax.numpy as jnp
import ml_dtypes
import numpy as np
from jax import lax
from jax.experimental import pallas as pl
from jax.experimental.pallas import tpu as pltpu
from jax.sharding import PartitionSpec as P

SUBPIX = 16
GROUP = 128
BLOCK = 512
IMAGE_BLOCK = 256
ROW_CHUNK = 16
MIB = 1024 * 1024
CONTRACT_LAST = (((1,), (1,)), ((), ()))
HBM = pl.BlockSpec(memory_space=pltpu.HBM)
IN_VMEM = pl.BlockSpec(memory_space=pltpu.VMEM)


def packed_freqs(index, half, where=jnp.where):
    even = 4 * index - where(index < half // 4, 0, half - 2)
    return where(index < half // 2, even, 2 * index - half + 1)


def packed_tables(length):
    half, quarter = length // 2, length // 4
    freqs = packed_freqs(np.arange(half, dtype=np.int32), half, np.where)
    positions = np.arange(half, dtype=np.int32)
    turns = freqs[:, None] * positions[None, :] % length
    angles = turns.astype(np.float32) * np.float32(2.0 * math.pi / length)
    factor = np.float32(1.0 / math.sqrt(length))
    cosine = np.cos(angles) * factor
    sine = np.sin(angles) * factor
    sine[0] = np.where(positions % 2 == 0, factor, -factor)
    groups = np.stack([cosine.reshape(-1, GROUP, half), sine.reshape(-1, GROUP, half)], axis=1)
    table = groups.reshape(length, half).astype(ml_dtypes.bfloat16)
    return np.ascontiguousarray(table[:half, :quarter]), table[half:]


def cost(flops, bytes_accessed):
    return pl.CostEstimate(flops=flops, bytes_accessed=bytes_accessed, transcendentals=0)


def wait_copies(copies):
    for copy in copies:
        copy.wait()


def fold(quarters):
    first, second, third, fourth = [part.astype(jnp.float32) for part in quarters]
    near, far = first + third, second + fourth
    folds = near + far, near - far, first - third, second - fourth
    return [part.astype(jnp.bfloat16) for part in folds]


def row_kernel(
    images_hbm,
    even_hbm,
    odd_hbm,
    out_hbm,
    images,
    even_table,
    odd_table,
    even_fold,
    odd_fold,
    staged,
    image_sems,
    table_sems,
    out_sems,
):
    loc_epochs, loc_rows, length = images.shape
    half, quarter = length // 2, length // 4
    devices, _, width, _ = staged.shape
    cols = width // 2
    steps = length // BLOCK
    per_step = devices // steps
    per_group = GROUP // cols
    image_copies = [
        pltpu.make_async_copy(images_hbm.at[loc], images.at[loc], image_sems.at[loc])
        for loc in range(loc_epochs)
    ]
    table_copies = [
        pltpu.make_async_copy(
            source.at[pl.ds(block * BLOCK, BLOCK)],
            target.at[pl.ds(block * BLOCK, BLOCK)],
            table_sems.at[first + block],
        )
        for first, source, target in ((0, even_hbm, even_table), (steps // 2, odd_hbm, odd_table))
        for block in range(steps // 2)
    ]
    for copy in image_copies[:1] + table_copies[: steps // 2]:
        copy.start()
    out_copies = []
    for loc in range(loc_epochs):
        image_copies[loc].wait()
        if loc == 0:
            for copy in table_copies[steps // 2 :] + image_copies[1:]:
                copy.start()
        folds = fold([images[loc, :, at * quarter : (at + 1) * quarter] for at in range(4)])
        even_fold[0], even_fold[1] = folds[:2]
        odd_fold[:, :quarter], odd_fold[:, quarter:] = folds[2:]
        for step in range(steps):
            if loc == 0:
                table_copies[step].wait()
            at = slice(step % (steps // 2) * BLOCK, (step % (steps // 2) + 1) * BLOCK)
            if step < steps // 2:
                left, right = even_table[at], even_fold[4 * step // steps]
            else:
                left, right = odd_table[at], odd_fold[...]
            terms = lax.dot_general(left, right, CONTRACT_LAST, preferred_element_type=jnp.float32)
            for dest in range(per_step):
                start = dest // per_group * 2 * GROUP + dest % per_group * cols
                parts = [terms[first : first + cols] for first in (start, start + GROUP)]
                block = jnp.concatenate(parts, axis=0).astype(jnp.bfloat16)
                staged[step * per_step + dest, loc] = block
            at = pl.ds(step * per_step, per_step)
            out_copies.append(
                pltpu.make_async_copy(
                    staged.at[at, loc], out_hbm.at[at, loc], out_sems.at[loc * steps + step]
                )
            )
            out_copies[-1].start()
    wait_copies(out_copies)


def row_transform(images, even_table, odd_table, devices):
    loc_epochs, loc_rows, length = images.shape
    half, quarter = length // 2, length // 4
    rows = loc_epochs * loc_rows
    steps = length // BLOCK
    out = (devices, loc_epochs, length // devices, loc_rows)
    return pl.pallas_call(
        row_kernel,
        in_specs=[HBM, HBM, HBM],
        out_specs=HBM,
        out_shape=jax.ShapeDtypeStruct(out, jnp.bfloat16),
        scratch_shapes=[
            pltpu.VMEM(images.shape, jnp.bfloat16),
            pltpu.VMEM(even_table.shape, jnp.bfloat16),
            pltpu.VMEM(odd_table.shape, jnp.bfloat16),
            pltpu.VMEM((2, loc_rows, quarter), jnp.bfloat16),
            pltpu.VMEM((loc_rows, half), jnp.bfloat16),
            pltpu.VMEM(out, jnp.bfloat16),
            pltpu.SemaphoreType.DMA((loc_epochs,)),
            pltpu.SemaphoreType.DMA((steps,)),
            pltpu.SemaphoreType.DMA((loc_epochs * steps,)),
        ],
        compiler_params=pltpu.CompilerParams(vmem_limit_bytes=58 * MIB),
        cost_estimate=cost(
            2 * rows * (even_table.size + odd_table.size), 3 * half * half + 4 * rows * length
        ),
        name="row_transform",
    )(images, even_table, odd_table)


def turn_angle(turns, whole):
    return (turns & (whole - 1)).astype(jnp.float32) * (2.0 * math.pi / whole)


def spread_pairs(scalars, lanes):
    pair = lax.broadcasted_iota(jnp.int32, (len(scalars), lanes), 0)
    values = jnp.zeros((len(scalars), lanes), jnp.int32)
    for index, scalar in enumerate(scalars):
        values = jnp.where(pair == index, scalar, values)
    return values


def row_factors(shift_y, half):
    shifts = spread_pairs(shift_y, half)
    freqs = packed_freqs(lax.broadcasted_iota(jnp.int32, shifts.shape, 1), half)
    angles = turn_angle((freqs - half) * shifts, SUBPIX * 2 * half)
    cos_rows = jnp.where(freqs == 0, 1.0, 2.0 * jnp.cos(angles))
    return cos_rows, jnp.where(freqs == 0, 0.0, 2.0 * jnp.sin(angles))


def column_factors(shift_y, shift_x, scale, device, cols, half):
    shifts_y, shifts_x = spread_pairs(shift_y, GROUP), spread_pairs(shift_x, GROUP)
    lane = lax.broadcasted_iota(jnp.int32, shifts_x.shape, 1)
    freqs = packed_freqs(device * cols + (lane & (cols - 1)), half)
    is_sine = (lane & cols) > 0
    paired = freqs == 0
    zero_col = paired & jnp.logical_not(is_sine)
    angles = turn_angle(shifts_x * (freqs - half), SUBPIX * 2 * half)
    ramp_cos = jnp.where(paired, scale, 2.0 * scale * jnp.cos(angles))
    ramp_sin = jnp.where(paired, 0.0, 2.0 * scale * jnp.sin(angles))
    ramp_sin = jnp.where(is_sine, ramp_sin, -ramp_sin)
    cos_x = jnp.cos(turn_angle(shifts_x, 2 * SUBPIX))
    cos_y = jnp.cos(turn_angle(shifts_y, 2 * SUBPIX))
    cos_xy = jnp.cos(turn_angle(shifts_x + shifts_y, 2 * SUBPIX))
    main = jnp.where(zero_col, cos_y, cos_xy)
    lead = jnp.where(zero_col, 1.0, cos_x)
    return jnp.concatenate(
        [main * ramp_cos, main * ramp_sin, lead * ramp_cos, lead * ramp_sin], axis=0
    )


def column_kernel(
    epoch_count,
    rate_smem,
    time_smem,
    received,
    even_table,
    odd_table,
    out_hbm,
    rows_cos,
    rows_sin,
    spread,
    even_fold,
    odd_fold,
    products,
    sums,
    staged,
    out_sems,
):
    devices, loc_epochs, width, loc_rows = received.shape
    row_count = devices // epoch_count
    epochs = epoch_count * loc_epochs
    rates = rate_smem.shape[0]
    pairs = rates * epochs
    cols = width // 2
    half, quarter = even_table.shape
    length = 2 * half
    steps = length // BLOCK
    device = lax.axis_index("row") * epoch_count + lax.axis_index("epoch")
    period = SUBPIX * length
    shift_y, shift_x = [
        [
            rate_smem[rate, axis] * time_smem[epoch] & (period - 1)
            for rate in range(rates)
            for epoch in range(epochs)
        ]
        for axis in range(2)
    ]
    per_tile = max(1, GROUP // loc_rows)
    tile_rows = per_tile * loc_rows
    for tile in range(row_count // 4 // per_tile):
        at_lane = slice(tile * tile_rows, (tile + 1) * tile_rows)
        far_lane = slice(quarter + at_lane.start, quarter + at_lane.stop)
        for core in range(epoch_count):
            for loc in range(loc_epochs):
                quarters = []
                for side in range(4):
                    first = side * row_count // 4 + tile * per_tile
                    parts = [
                        received[(first + part) * epoch_count + core, loc] for part in range(per_tile)
                    ]
                    quarters.append(parts[0] if per_tile == 1 else jnp.concatenate(parts, axis=1))
                at_row = (core * loc_epochs + loc) * width
                at = slice(at_row, at_row + width)
                folds = fold(quarters)
                even_fold[0, at, at_lane], even_fold[1, at, at_lane] = folds[:2]
                odd_fold[at, at_lane], odd_fold[at, far_lane] = folds[2:]

    def multiply(step):
        at = slice(step % (steps // 2) * BLOCK, (step % (steps // 2) + 1) * BLOCK)
        if step < steps // 2:
            left, right = even_fold[4 * step // steps], even_table[at]
        else:
            left, right = odd_fold[...], odd_table[at]
        products[step % 2] = lax.dot_general(
            left, right, CONTRACT_LAST, preferred_element_type=jnp.float32
        )

    multiply(0)
    rows_cos[...], rows_sin[...] = row_factors(shift_y, half)
    factors = column_factors(shift_y, shift_x, 1.0 / math.sqrt(epochs), device, cols, half).T
    for kind in range(4):
        for pair in range(pairs):
            at = kind * pairs + pair
            spread[kind, pair] = jnp.broadcast_to(factors[:width, at : at + 1], (width, GROUP))

    chunk = min(ROW_CHUNK, cols)

    def add_ramped(step, group):
        tile = (step * BLOCK // 2 // GROUP + group) * GROUP
        at_even = group * 2 * GROUP
        at_odd = at_even + GROUP
        for rate in range(rates):
            for start in range(0, cols, chunk):
                real = slice(start, start + chunk)
                imag = slice(cols + start, cols + start + chunk)
                totals = [[0.0, 0.0], [0.0, 0.0]]
                leads = [0.0, 0.0]
                for epoch in range(epochs):
                    pair = rate * epochs + epoch
                    cos_row = rows_cos[pair : pair + 1, tile : tile + GROUP]
                    sin_row = rows_sin[pair : pair + 1, tile : tile + GROUP]
                    turned, evens = [], []
                    for part in (real, imag):
                        at = slice(epoch * width + part.start, epoch * width + part.stop)
                        even = products[step % 2, at, at_even : at_even + GROUP]
                        odd = products[step % 2, at, at_odd : at_odd + GROUP]
                        turned.append(
                            (cos_row * even + sin_row * odd, cos_row * odd - sin_row * even)
                        )
                        evens.append(even)
                    straight = [spread[0, pair, part] for part in (real, imag)]
                    crossed = [spread[1, pair, part] for part in (real, imag)]
                    for part in range(2):
                        for which in range(2):
                            totals[part][which] += (
                                straight[part] * turned[part][which]
                                + crossed[1 - part] * turned[1 - part][which]
                            )
                        if step == 0 and group == 0:
                            own, other = (real, imag) if part == 0 else (imag, real)
                            leads[part] += (
                                spread[2, pair, own] * evens[part]
                                + spread[3, pair, other] * evens[1 - part]
                            )
                for part, rows in enumerate((real, imag)):
                    even_sum, odd_sum = totals[part]
                    if step == 0 and group == 0:
                        first = lax.broadcasted_iota(jnp.int32, even_sum.shape, 1) == 0
                        even_sum = jnp.where(first, leads[part], even_sum)
                    at = slice(rate * width + rows.start, rate * width + rows.stop)
                    sums[at, step * BLOCK + at_even : step * BLOCK + at_even + GROUP] = even_sum.astype(
                        jnp.bfloat16
                    )
                    sums[at, step * BLOCK + at_odd : step * BLOCK + at_odd + GROUP] = odd_sum.astype(
                        jnp.bfloat16
                    )

    for step in range(steps):
        if step + 1 < steps:
            multiply(step + 1)
        for group in range(BLOCK // 2 // GROUP):
            add_ramped(step, group)

    loc_rates = rates // epoch_count
    out_copies = []

    def send(side, back):
        back = back.astype(jnp.bfloat16)
        rows_here = quarter // loc_rows
        for row in range(rows_here):
            for rate in range(rates):
                dest = (side * rows_here + row) * epoch_count + rate // loc_rates
                staged[dest, rate % loc_rates] = back[
                    rate * width : (rate + 1) * width, row * loc_rows : (row + 1) * loc_rows
                ]
        span = pl.ds(side * rows_here * epoch_count, rows_here * epoch_count)
        out_copies.append(
            pltpu.make_async_copy(staged.at[span], out_hbm.at[span], out_sems.at[side])
        )
        out_copies[-1].start()

    inverse_parts(sums, even_table, odd_table, slice(0, quarter), quarter, send)
    wait_copies(out_copies)


def inverse_parts(left, even_table, odd_table, at, quarter, send):
    half = 2 * quarter
    far = slice(quarter + at.start, quarter + at.stop)

    def product(first, depth, right):
        return jnp.dot(left[:, first : first + depth], right, preferred_element_type=jnp.float32)

    zero = product(0, quarter, even_table[:quarter, at])
    two = product(quarter, quarter, even_table[quarter:, at])
    for position, even, span in ((0, zero + two, at), (1, zero - two, far)):
        odd = product(half, half, odd_table[:, span])
        send(position, even + odd)
        send(position + 2, even - odd)


def column_stage(rate_vectors, epoch_times, spectra, even_table, odd_table, epoch_count):
    devices, loc_epochs, width, loc_rows = spectra.shape
    half, quarter = even_table.shape
    length = 2 * half
    epochs, rates = epoch_times.shape[0], rate_vectors.shape[0]
    out = (devices, rates // epoch_count, width, loc_rows)
    scalars = pl.BlockSpec(memory_space=pltpu.SMEM)
    return pl.pallas_call(
        functools.partial(column_kernel, epoch_count),
        in_specs=[scalars, scalars, IN_VMEM, IN_VMEM, IN_VMEM],
        out_specs=HBM,
        out_shape=jax.ShapeDtypeStruct(out, jnp.bfloat16),
        scratch_shapes=[
            pltpu.VMEM((rates * epochs, half), jnp.float32),
            pltpu.VMEM((rates * epochs, half), jnp.float32),
            pltpu.VMEM((4, rates * epochs, width, GROUP), jnp.float32),
            pltpu.VMEM((2, epochs * width, quarter), jnp.bfloat16),
            pltpu.VMEM((epochs * width, half), jnp.bfloat16),
            pltpu.VMEM((2, epochs * width, BLOCK), jnp.float32),
            pltpu.VMEM((rates * width, length), jnp.bfloat16),
            pltpu.VMEM(out, jnp.bfloat16),
            pltpu.SemaphoreType.DMA((4,)),
        ],
        compiler_params=pltpu.CompilerParams(vmem_limit_bytes=40 * MIB),
        cost_estimate=cost(
            2 * (even_table.size + odd_table.size) * (epochs + rates) * width,
            3 * half * half + 4 * spectra.size,
        ),
        name="column_stage",
    )(rate_vectors, epoch_times, spectra, even_table, odd_table)


def image_kernel(back, even_table, odd_table, out_hbm, left, staged, out_sems):
    quarter = even_table.shape[1]
    width = back.shape[1]
    cols = width // 2
    per_group = GROUP // cols
    for group in range(back.shape[0] // per_group):
        members = [back[group * per_group + place].astype(jnp.float32) for place in range(per_group)]
        parts = [member[:cols] for member in members] + [member[cols:] for member in members]
        whole = jnp.concatenate(parts, axis=0)
        left[:, group * 2 * GROUP : (group + 1) * 2 * GROUP] = whole.T.astype(jnp.bfloat16)
    out_copies = []
    for block in range(quarter // IMAGE_BLOCK):

        def send(side, pixels):
            start = side * quarter + block * IMAGE_BLOCK
            at = slice(start, start + IMAGE_BLOCK)
            staged[:, at] = pixels
            out_copies.append(
                pltpu.make_async_copy(
                    staged.at[:, at], out_hbm.at[0, :, at], out_sems.at[4 * block + side]
                )
            )
            out_copies[-1].start()

        at = slice(block * IMAGE_BLOCK, (block + 1) * IMAGE_BLOCK)
        inverse_parts(left, even_table, odd_table, at, quarter, send)
    wait_copies(out_copies)


def image_rows(back, even_table, odd_table):
    rows = back.shape[2]
    half, quarter = even_table.shape
    length = 2 * half
    return pl.pallas_call(
        image_kernel,
        in_specs=[IN_VMEM, IN_VMEM, IN_VMEM],
        out_specs=HBM,
        out_shape=jax.ShapeDtypeStruct((1, rows, length), jnp.float32),
        scratch_shapes=[
            pltpu.VMEM((rows, length), jnp.bfloat16),
            pltpu.VMEM((rows, length), jnp.float32),
            pltpu.SemaphoreType.DMA((length // IMAGE_BLOCK,)),
        ],
        compiler_params=pltpu.CompilerParams(vmem_limit_bytes=40 * MIB),
        cost_estimate=cost(
            2 * rows * (even_table.size + odd_table.size), 3 * half * half + 6 * rows * length
        ),
        name="image_rows",
    )(back, even_table, odd_table)


def local(images, rate_vectors, epoch_times):
    _, loc_rows, length = images.shape
    epoch_count = lax.axis_size("epoch")
    devices = lax.axis_size("row") * epoch_count
    even_table, odd_table = [jnp.asarray(part) for part in packed_tables(length)]

    def exchange(values):
        return lax.all_to_all(values, ("row", "epoch"), 0, 0, tiled=True)

    spectra = exchange(row_transform(images, even_table, odd_table, devices))
    back = exchange(
        column_stage(rate_vectors, epoch_times, spectra, even_table, odd_table, epoch_count)
    )
    return image_rows(
        back.reshape(devices, length // devices, loc_rows), even_table, odd_table
    )


def solution(mesh):
    in_specs = (P(("group", "epoch"), "row", None), P(), P())
    out_specs = P(("group", "epoch"), "row", None)
    return jax.shard_map(local, mesh=mesh, in_specs=in_specs, out_specs=out_specs, check_vma=False)
```

time: 99.9 us -> 99.4 us (level)
  no operation moved by 1% of the time
where the time goes in v11:
time: 99.4 us; the launch traced here: 98.9 us
  blocking collectives  84.7 us (85%)
  Pallas kernels  14.1 us (14%)
    all_to_all x2, blocking collectives, exchange(): return lax.all_to_all(values, ('row', 'epoch'), 0, 0, tiled=True)  84.7 us
    pallas_call x1, Pallas kernels, row_transform(): pl.pallas_call(row_kernel, in_specs=[HBM, HBM, HBM], out_specs=HBM, out_s...  6.4 us
    pallas_call x1, Pallas kernels, column_stage(): pl.pallas_call(functools.partial(column_kernel, epoch_count), in_specs=[s...  5.51 us
    pallas_call x1, Pallas kernels, image_rows(): pl.pallas_call(image_kernel, in_specs=[IN_VMEM, IN_VMEM, IN_VMEM], out_sp...  2.16 us

profile of v11, /device:TPU:0, one launch (start us, length us, event | category | flops | bytes accessed | tf_op | source)
XLA Modules:
  0.0 98.9 jit_solution(3755132872749562487)
XLA Ops:
  0.0 6.4 %row_transform.1 = bf16[16,2,128,256]{3,2,1,0:T(8,128)(2,1)} custom-call(bf16[2,256,2048]{2,1,0:T(8,128)(2,1)} %images_hbm.1, bf16[1024,512]{1,0:T(8,128)(2,1)} %constant.4.clone.even_hbm.even_table, bf16[1024,1024]{1,0:T(8,128)(2,1)} %constant.5.clone.odd_hbm.odd_table), custom_call_target="tpu_custom_call" | custom-call | flops 1610612736 | bytes 7340032 | tf_op jit(solution)/shard_map/row_transform/pallas_call | solution.py:136
  6.4 0.0 copy-start
  6.4 0.0 copy-start.1
  6.4 0.0 copy-start.2
  6.4 0.0 copy-start.3
  6.5 55.0 %all_to_all.10.received = bf16[16,2,128,256]{3,2,1,0:T(8,128)(2,1)S(1)} all-to-all(bf16[16,2,128,256]{3,2,1,0:T(8,128)(2,1)} %row_transform.1), channel_id=1, replica_groups=mesh['group'=2,'row'=8,'epoch'=2] {'row','epoch'}, dimensions={0} | all-to-all | bytes 4194304 | tf_op jit(solution)/shard_map/all_to_all | solution.py:461
  61.4 0.0 copy-done
  61.4 0.0 copy-done.1
  61.4 0.0 copy-done.2
  61.4 0.0 copy-done.3
  61.4 5.5 %column_stage.1 = bf16[16,1,128,256]{3,2,1,0:T(8,128)(2,1)S(1)} custom-call(s32[2,2]{1,0:T(2,128)S(1)} %copy-done.2, s32[4]{0:T(128)S(1)} %copy-done.3, bf16[16,2,128,256]{3,2,1,0:T(8,128)(2,1)S(1)} %all_to_all.10.received, bf16[1024,512]{1,0:T(8,128)(2,1)S(1)} %copy-done.1, bf16[1024,1024]{1,0:T(8,128)(2,1)S(1)} %copy-done), custom_call_target="tpu_custom_call" | custom-call | flops 2415919104 | bytes 7340032 | tf_op jit(solution)/shard_map/column_stage/pallas_call | solution.py:378
  66.9 29.7 %all_to_all.11 = bf16[16,1,128,256]{3,2,1,0:T(8,128)(2,1)S(1)} all-to-all(bf16[16,1,128,256]{3,2,1,0:T(8,128)(2,1)S(1)} %column_stage.1), channel_id=1, replica_groups=mesh['group'=2,'row'=8,'epoch'=2] {'row','epoch'}, dimensions={0} | all-to-all | bytes 2097152 | tf_op jit(solution)/shard_map/all_to_all | solution.py:461
  96.7 2.2 %image_rows.1 = f32[1,256,2048]{2,1,0:T(8,128)} custom-call(bf16[16,128,256]{2,1,0:T(8,128)(2,1)S(1)} %bitcast.1, bf16[1024,512]{1,0:T(8,128)(2,1)S(1)} %copy-done.1, bf16[1024,1024]{1,0:T(8,128)(2,1)S(1)} %copy-done), custom_call_target="tpu_custom_call" | custom-call | flops 805306368 | bytes 6291456 | tf_op jit(solution)/shard_map/image_rows/pallas_call | solution.py:436
Async XLA Ops:
  6.4 55.0 %copy-start = (bf16[1024,1024]{1,0:T(8,128)(2,1)S(1)}, bf16[1024,1024]{1,0:T(8,128)(2,1)}, u32[]{:S(2)}) copy-start(bf16[1024,1024]{1,0:T(8,128)(2,1)} %constant.5.clone.odd_hbm.odd_table) | copy-start | bytes 6291460
  6.4 55.0 %copy-start.1 = (bf16[1024,512]{1,0:T(8,128)(2,1)S(1)}, bf16[1024,512]{1,0:T(8,128)(2,1)}, u32[]{:S(2)}) copy-start(bf16[1024,512]{1,0:T(8,128)(2,1)} %constant.4.clone.even_hbm.even_table) | copy-start | bytes 3145732
  6.4 55.0 %copy-start.2 = (s32[2,2]{1,0:T(2,128)S(1)}, s32[2,2]{1,0:T(2,128)}, u32[]{:S(2)}) copy-start(s32[2,2]{1,0:T(2,128)} %rate_smem.1) | copy-start | bytes 52
  6.4 55.0 %copy-start.3 = (s32[4]{0:T(128)S(1)}, s32[4]{0:T(128)}, u32[]{:S(2)}) copy-start(s32[4]{0:T(128)} %time_smem.1) | copy-start | bytes 52

commit v12 on v11

--- a/solution.py
+++ b/solution.py
@@ -45,6 +45,10 @@
     return pl.CostEstimate(flops=flops, bytes_accessed=bytes_accessed, transcendentals=0)
 
 
+def in_space(array, space):
+    return pltpu.with_memory_space_constraint(array, space)
+
+
 def wait_copies(copies):
     for copy in copies:
         copy.wait()
@@ -61,20 +65,18 @@
     images_hbm,
     even_hbm,
     odd_hbm,
-    out_hbm,
+    out_ref,
     images,
     even_table,
     odd_table,
     even_fold,
     odd_fold,
-    staged,
     image_sems,
     table_sems,
-    out_sems,
 ):
     loc_epochs, loc_rows, length = images.shape
     half, quarter = length // 2, length // 4
-    devices, _, width, _ = staged.shape
+    devices, _, width, _ = out_ref.shape
     cols = width // 2
     steps = length // BLOCK
     per_step = devices // steps
@@ -92,14 +94,10 @@
         for first, source, target in ((0, even_hbm, even_table), (steps // 2, odd_hbm, odd_table))
         for block in range(steps // 2)
     ]
-    for copy in image_copies[:1] + table_copies[: steps // 2]:
+    for copy in image_copies[:1] + table_copies + image_copies[1:]:
         copy.start()
-    out_copies = []
     for loc in range(loc_epochs):
         image_copies[loc].wait()
-        if loc == 0:
-            for copy in table_copies[steps // 2 :] + image_copies[1:]:
-                copy.start()
         folds = fold([images[loc, :, at * quarter : (at + 1) * quarter] for at in range(4)])
         even_fold[0], even_fold[1] = folds[:2]
         odd_fold[:, :quarter], odd_fold[:, quarter:] = folds[2:]
@@ -116,15 +114,7 @@
                 start = dest // per_group * 2 * GROUP + dest % per_group * cols
                 parts = [terms[first : first + cols] for first in (start, start + GROUP)]
                 block = jnp.concatenate(parts, axis=0).astype(jnp.bfloat16)
-                staged[step * per_step + dest, loc] = block
-            at = pl.ds(step * per_step, per_step)
-            out_copies.append(
-                pltpu.make_async_copy(
-                    staged.at[at, loc], out_hbm.at[at, loc], out_sems.at[loc * steps + step]
-                )
-            )
-            out_copies[-1].start()
-    wait_copies(out_copies)
+                out_ref[step * per_step + dest, loc] = block
 
 
 def row_transform(images, even_table, odd_table, devices):
@@ -136,25 +126,23 @@
     return pl.pallas_call(
         row_kernel,
         in_specs=[HBM, HBM, HBM],
-        out_specs=HBM,
-        out_shape=jax.ShapeDtypeStruct(out, jnp.bfloat16),
+        out_specs=IN_VMEM,
+        out_shape=pltpu.VMEM(out, jnp.bfloat16),
         scratch_shapes=[
             pltpu.VMEM(images.shape, jnp.bfloat16),
             pltpu.VMEM(even_table.shape, jnp.bfloat16),
             pltpu.VMEM(odd_table.shape, jnp.bfloat16),
             pltpu.VMEM((2, loc_rows, quarter), jnp.bfloat16),
             pltpu.VMEM((loc_rows, half), jnp.bfloat16),
-            pltpu.VMEM(out, jnp.bfloat16),
             pltpu.SemaphoreType.DMA((loc_epochs,)),
             pltpu.SemaphoreType.DMA((steps,)),
-            pltpu.SemaphoreType.DMA((loc_epochs * steps,)),
         ],
-        compiler_params=pltpu.CompilerParams(vmem_limit_bytes=58 * MIB),
+        compiler_params=pltpu.CompilerParams(vmem_limit_bytes=40 * MIB),
         cost_estimate=cost(
             2 * rows * (even_table.size + odd_table.size), 3 * half * half + 4 * rows * length
         ),
         name="row_transform",
-    )(images, even_table, odd_table)
+    )(*(in_space(part, pltpu.HBM) for part in (images, even_table, odd_table)))
 
 
 def turn_angle(turns, whole):
@@ -205,7 +193,7 @@
     received,
     even_table,
     odd_table,
-    out_hbm,
+    out_ref,
     rows_cos,
     rows_sin,
     spread,
@@ -213,8 +201,6 @@
     odd_fold,
     products,
     sums,
-    staged,
-    out_sems,
 ):
     devices, loc_epochs, width, loc_rows = received.shape
     row_count = devices // epoch_count
@@ -332,7 +318,6 @@
             add_ramped(step, group)
 
     loc_rates = rates // epoch_count
-    out_copies = []
 
     def send(side, back):
         back = back.astype(jnp.bfloat16)
@@ -340,17 +325,11 @@
         for row in range(rows_here):
             for rate in range(rates):
                 dest = (side * rows_here + row) * epoch_count + rate // loc_rates
-                staged[dest, rate % loc_rates] = back[
+                out_ref[dest, rate % loc_rates] = back[
                     rate * width : (rate + 1) * width, row * loc_rows : (row + 1) * loc_rows
                 ]
-        span = pl.ds(side * rows_here * epoch_count, rows_here * epoch_count)
-        out_copies.append(
-            pltpu.make_async_copy(staged.at[span], out_hbm.at[span], out_sems.at[side])
-        )
-        out_copies[-1].start()
 
     inverse_parts(sums, even_table, odd_table, slice(0, quarter), quarter, send)
-    wait_copies(out_copies)
 
 
 def inverse_parts(left, even_table, odd_table, at, quarter, send):
@@ -378,8 +357,8 @@
     return pl.pallas_call(
         functools.partial(column_kernel, epoch_count),
         in_specs=[scalars, scalars, IN_VMEM, IN_VMEM, IN_VMEM],
-        out_specs=HBM,
-        out_shape=jax.ShapeDtypeStruct(out, jnp.bfloat16),
+        out_specs=IN_VMEM,
+        out_shape=pltpu.VMEM(out, jnp.bfloat16),
         scratch_shapes=[
             pltpu.VMEM((rates * epochs, half), jnp.float32),
             pltpu.VMEM((rates * epochs, half), jnp.float32),
@@ -388,8 +367,6 @@
             pltpu.VMEM((epochs * width, half), jnp.bfloat16),
             pltpu.VMEM((2, epochs * width, BLOCK), jnp.float32),
             pltpu.VMEM((rates * width, length), jnp.bfloat16),
-            pltpu.VMEM(out, jnp.bfloat16),
-            pltpu.SemaphoreType.DMA((4,)),
         ],
         compiler_params=pltpu.CompilerParams(vmem_limit_bytes=40 * MIB),
         cost_estimate=cost(
@@ -397,7 +374,11 @@
             3 * half * half + 4 * spectra.size,
         ),
         name="column_stage",
-    )(rate_vectors, epoch_times, spectra, even_table, odd_table)
+    )(
+        rate_vectors,
+        epoch_times,
+        *(in_space(part, pltpu.VMEM) for part in (spectra, even_table, odd_table)),
+    )
 
 
 def image_kernel(back, even_table, odd_table, out_hbm, left, staged, out_sems):
@@ -448,7 +429,7 @@
             2 * rows * (even_table.size + odd_table.size), 3 * half * half + 6 * rows * length
         ),
         name="image_rows",
-    )(back, even_table, odd_table)
+    )(*(in_space(part, pltpu.VMEM) for part in (back, even_table, odd_table)))
 
 
 def local(images, rate_vectors, epoch_times):

time: 99.4 us -> 97.7 us (0.983)
  Pallas kernels: 14.1 us -> 12.6 us
    pallas_call x1, Pallas kernels: 6.4 us -> 5.28 us  [row_transform(): pl.pallas_call(row_kernel, in_specs=[HBM, HBM, HBM], out_specs=IN_VMEM, o...]
where the time goes in v12:
time: 97.7 us; the launch traced here: 97.2 us
  blocking collectives  84.5 us (86%)
  Pallas kernels  12.6 us (13%)
    all_to_all x2, blocking collectives, exchange(): return lax.all_to_all(values, ('row', 'epoch'), 0, 0, tiled=True)  84.5 us
    pallas_call x1, Pallas kernels, row_transform(): pl.pallas_call(row_kernel, in_specs=[HBM, HBM, HBM], out_specs=IN_VMEM, o...  5.28 us
    pallas_call x1, Pallas kernels, column_stage(): pl.pallas_call(functools.partial(column_kernel, epoch_count), in_specs=[s...  5.12 us
    pallas_call x1, Pallas kernels, image_rows(): pl.pallas_call(image_kernel, in_specs=[IN_VMEM, IN_VMEM, IN_VMEM], out_sp...  2.18 us

profile of v12, /device:TPU:0, one launch (start us, length us, event | category | flops | bytes accessed | tf_op | source)
XLA Modules:
  0.0 97.2 jit_solution(10854202236867244252)
XLA Ops:
  0.0 5.3 %row_transform.1 = bf16[16,2,128,256]{3,2,1,0:T(8,128)(2,1)S(1)} custom-call(bf16[2,256,2048]{2,1,0:T(8,128)(2,1)} %images_hbm.1, bf16[1024,512]{1,0:T(8,128)(2,1)} %constant.4.clone.even_hbm.even_table, bf16[1024,1024]{1,0:T(8,128)(2,1)} %constant.5.clone.odd_hbm.odd_table), custom_call_target="tpu_custom_call" | custom-call | flops 1610612736 | bytes 7340032 | tf_op jit(solution)/shard_map/row_transform/pallas_call | solution.py:126
  5.3 0.0 copy-start
  5.3 0.0 copy-start.1
  5.3 0.0 copy-start.2
  5.3 0.0 copy-start.3
  5.3 54.7 %all_to_all.10.received = bf16[16,2,128,256]{3,2,1,0:T(8,128)(2,1)S(1)} all-to-all(bf16[16,2,128,256]{3,2,1,0:T(8,128)(2,1)S(1)} %row_transform.1), channel_id=1, replica_groups=mesh['group'=2,'row'=8,'epoch'=2] {'row','epoch'}, dimensions={0} | all-to-all | bytes 4194304 | tf_op jit(solution)/shard_map/all_to_all | solution.py:442
  60.1 0.0 copy-done
  60.1 0.0 copy-done.1
  60.1 0.0 copy-done.2
  60.1 0.0 copy-done.3
  60.1 5.1 %column_stage.1 = bf16[16,1,128,256]{3,2,1,0:T(8,128)(2,1)S(1)} custom-call(s32[2,2]{1,0:T(2,128)S(1)} %copy-done.2, s32[4]{0:T(128)S(1)} %copy-done.3, bf16[16,2,128,256]{3,2,1,0:T(8,128)(2,1)S(1)} %all_to_all.10.received, bf16[1024,512]{1,0:T(8,128)(2,1)S(1)} %copy-done.1, bf16[1024,1024]{1,0:T(8,128)(2,1)S(1)} %copy-done), custom_call_target="tpu_custom_call" | custom-call | flops 2415919104 | bytes 7340032 | tf_op jit(solution)/shard_map/column_stage/pallas_call | solution.py:357
  65.2 29.8 %all_to_all.11 = bf16[16,1,128,256]{3,2,1,0:T(8,128)(2,1)S(1)} all-to-all(bf16[16,1,128,256]{3,2,1,0:T(8,128)(2,1)S(1)} %column_stage.1), channel_id=1, replica_groups=mesh['group'=2,'row'=8,'epoch'=2] {'row','epoch'}, dimensions={0} | all-to-all | bytes 2097152 | tf_op jit(solution)/shard_map/all_to_all | solution.py:442
  95.0 2.2 %image_rows.1 = f32[1,256,2048]{2,1,0:T(8,128)} custom-call(bf16[16,128,256]{2,1,0:T(8,128)(2,1)S(1)} %bitcast.1, bf16[1024,512]{1,0:T(8,128)(2,1)S(1)} %copy-done.1, bf16[1024,1024]{1,0:T(8,128)(2,1)S(1)} %copy-done), custom_call_target="tpu_custom_call" | custom-call | flops 805306368 | bytes 6291456 | tf_op jit(solution)/shard_map/image_rows/pallas_call | solution.py:417
Async XLA Ops:
  5.3 54.8 %copy-start = (bf16[1024,1024]{1,0:T(8,128)(2,1)S(1)}, bf16[1024,1024]{1,0:T(8,128)(2,1)}, u32[]{:S(2)}) copy-start(bf16[1024,1024]{1,0:T(8,128)(2,1)} %constant.5.clone.odd_hbm.odd_table) | copy-start | bytes 6291460
  5.3 54.8 %copy-start.1 = (bf16[1024,512]{1,0:T(8,128)(2,1)S(1)}, bf16[1024,512]{1,0:T(8,128)(2,1)}, u32[]{:S(2)}) copy-start(bf16[1024,512]{1,0:T(8,128)(2,1)} %constant.4.clone.even_hbm.even_table) | copy-start | bytes 3145732
  5.3 54.8 %copy-start.2 = (s32[2,2]{1,0:T(2,128)S(1)}, s32[2,2]{1,0:T(2,128)}, u32[]{:S(2)}) copy-start(s32[2,2]{1,0:T(2,128)} %rate_smem.1) | copy-start | bytes 52
  5.3 54.8 %copy-start.3 = (s32[4]{0:T(128)S(1)}, s32[4]{0:T(128)}, u32[]{:S(2)}) copy-start(s32[4]{0:T(128)} %time_smem.1) | copy-start | bytes 52

commit v13 on v12

--- a/solution.py
+++ b/solution.py
@@ -211,7 +211,7 @@
     half, quarter = even_table.shape
     length = 2 * half
     steps = length // BLOCK
-    device = lax.axis_index("row") * epoch_count + lax.axis_index("epoch")
+    device = lax.axis_index("epoch") * row_count + lax.axis_index("row")
     period = SUBPIX * length
     shift_y, shift_x = [
         [
@@ -232,7 +232,7 @@
                 for side in range(4):
                     first = side * row_count // 4 + tile * per_tile
                     parts = [
-                        received[(first + part) * epoch_count + core, loc] for part in range(per_tile)
+                        received[core * row_count + first + part, loc] for part in range(per_tile)
                     ]
                     quarters.append(parts[0] if per_tile == 1 else jnp.concatenate(parts, axis=1))
                 at_row = (core * loc_epochs + loc) * width
@@ -324,7 +324,7 @@
         rows_here = quarter // loc_rows
         for row in range(rows_here):
             for rate in range(rates):
-                dest = (side * rows_here + row) * epoch_count + rate // loc_rates
+                dest = rate // loc_rates * row_count + side * rows_here + row
                 out_ref[dest, rate % loc_rates] = back[
                     rate * width : (rate + 1) * width, row * loc_rows : (row + 1) * loc_rows
                 ]
@@ -439,7 +439,7 @@
     even_table, odd_table = [jnp.asarray(part) for part in packed_tables(length)]
 
     def exchange(values):
-        return lax.all_to_all(values, ("row", "epoch"), 0, 0, tiled=True)
+        return lax.all_to_all(values, ("epoch", "row"), 0, 0, tiled=True)
 
     spectra = exchange(row_transform(images, even_table, odd_table, devices))
     back = exchange(

time: 97.7 us -> 99.4 us (1.017)
  blocking collectives: 84.5 us -> 86.6 us
    all_to_all x2, blocking collectives: 84.5 us -> 86.6 us  [exchange(): return lax.all_to_all(values, ('epoch', 'row'), 0, 0, tiled=True)]
where the time goes in v13:
time: 99.4 us; the launch traced here: 99.2 us
  blocking collectives  86.6 us (87%)
  Pallas kernels  12.6 us (13%)
    all_to_all x2, blocking collectives, exchange(): return lax.all_to_all(values, ('epoch', 'row'), 0, 0, tiled=True)  86.6 us
    pallas_call x1, Pallas kernels, row_transform(): pl.pallas_call(row_kernel, in_specs=[HBM, HBM, HBM], out_specs=IN_VMEM, o...  5.28 us
    pallas_call x1, Pallas kernels, column_stage(): pl.pallas_call(functools.partial(column_kernel, epoch_count), in_specs=[s...  5.1 us
    pallas_call x1, Pallas kernels, image_rows(): pl.pallas_call(image_kernel, in_specs=[IN_VMEM, IN_VMEM, IN_VMEM], out_sp...  2.19 us

profile of v13, /device:TPU:0, one launch (start us, length us, event | category | flops | bytes accessed | tf_op | source)
XLA Modules:
  0.0 99.2 jit_solution(7091137652936307092)
XLA Ops:
  0.0 5.3 %row_transform.1 = bf16[16,2,128,256]{3,2,1,0:T(8,128)(2,1)S(1)} custom-call(bf16[2,256,2048]{2,1,0:T(8,128)(2,1)} %images_hbm.1, bf16[1024,512]{1,0:T(8,128)(2,1)} %constant.4.clone.even_hbm.even_table, bf16[1024,1024]{1,0:T(8,128)(2,1)} %constant.5.clone.odd_hbm.odd_table), custom_call_target="tpu_custom_call" | custom-call | flops 1610612736 | bytes 7340032 | tf_op jit(solution)/shard_map/row_transform/pallas_call | solution.py:126
  5.3 0.0 copy-start
  5.3 0.0 copy-start.1
  5.3 0.0 copy-start.2
  5.3 0.0 copy-start.3
  5.3 56.9 %all_to_all.10.received = bf16[16,2,128,256]{3,2,1,0:T(8,128)(2,1)S(1)} all-to-all(bf16[16,2,128,256]{3,2,1,0:T(8,128)(2,1)S(1)} %row_transform.1), channel_id=1, replica_groups=mesh['group'=2,'row'=8,'epoch'=2] {'epoch','row'}, dimensions={0} | all-to-all | bytes 4194304 | tf_op jit(solution)/shard_map/all_to_all | solution.py:442
  62.3 0.0 copy-done
  62.3 0.0 copy-done.1
  62.3 0.0 copy-done.2
  62.3 0.0 copy-done.3
  62.3 5.1 %column_stage.1 = bf16[16,1,128,256]{3,2,1,0:T(8,128)(2,1)S(1)} custom-call(s32[2,2]{1,0:T(2,128)S(1)} %copy-done.2, s32[4]{0:T(128)S(1)} %copy-done.3, bf16[16,2,128,256]{3,2,1,0:T(8,128)(2,1)S(1)} %all_to_all.10.received, bf16[1024,512]{1,0:T(8,128)(2,1)S(1)} %copy-done.1, bf16[1024,1024]{1,0:T(8,128)(2,1)S(1)} %copy-done), custom_call_target="tpu_custom_call" | custom-call | flops 2415919104 | bytes 7340032 | tf_op jit(solution)/shard_map/column_stage/pallas_call | solution.py:357
  67.4 29.6 %all_to_all.11 = bf16[16,1,128,256]{3,2,1,0:T(8,128)(2,1)S(1)} all-to-all(bf16[16,1,128,256]{3,2,1,0:T(8,128)(2,1)S(1)} %column_stage.1), channel_id=1, replica_groups=mesh['group'=2,'row'=8,'epoch'=2] {'epoch','row'}, dimensions={0} | all-to-all | bytes 2097152 | tf_op jit(solution)/shard_map/all_to_all | solution.py:442
  97.0 2.2 %image_rows.1 = f32[1,256,2048]{2,1,0:T(8,128)} custom-call(bf16[16,128,256]{2,1,0:T(8,128)(2,1)S(1)} %bitcast.1, bf16[1024,512]{1,0:T(8,128)(2,1)S(1)} %copy-done.1, bf16[1024,1024]{1,0:T(8,128)(2,1)S(1)} %copy-done), custom_call_target="tpu_custom_call" | custom-call | flops 805306368 | bytes 6291456 | tf_op jit(solution)/shard_map/image_rows/pallas_call | solution.py:417
Async XLA Ops:
  5.3 57.0 %copy-start = (bf16[1024,1024]{1,0:T(8,128)(2,1)S(1)}, bf16[1024,1024]{1,0:T(8,128)(2,1)}, u32[]{:S(2)}) copy-start(bf16[1024,1024]{1,0:T(8,128)(2,1)} %constant.5.clone.odd_hbm.odd_table) | copy-start | bytes 6291460
  5.3 57.0 %copy-start.1 = (bf16[1024,512]{1,0:T(8,128)(2,1)S(1)}, bf16[1024,512]{1,0:T(8,128)(2,1)}, u32[]{:S(2)}) copy-start(bf16[1024,512]{1,0:T(8,128)(2,1)} %constant.4.clone.even_hbm.even_table) | copy-start | bytes 3145732
  5.3 57.0 %copy-start.2 = (s32[2,2]{1,0:T(2,128)S(1)}, s32[2,2]{1,0:T(2,128)}, u32[]{:S(2)}) copy-start(s32[2,2]{1,0:T(2,128)} %rate_smem.1) | copy-start | bytes 52
  5.3 57.0 %copy-start.3 = (s32[4]{0:T(128)S(1)}, s32[4]{0:T(128)}, u32[]{:S(2)}) copy-start(s32[4]{0:T(128)} %time_smem.1) | copy-start | bytes 52

commit v14 on v12

--- a/solution.py
+++ b/solution.py
@@ -79,7 +79,6 @@
     devices, _, width, _ = out_ref.shape
     cols = width // 2
     steps = length // BLOCK
-    per_step = devices // steps
     per_group = GROUP // cols
     image_copies = [
         pltpu.make_async_copy(images_hbm.at[loc], images.at[loc], image_sems.at[loc])
@@ -101,20 +100,19 @@
         folds = fold([images[loc, :, at * quarter : (at + 1) * quarter] for at in range(4)])
         even_fold[0], even_fold[1] = folds[:2]
         odd_fold[:, :quarter], odd_fold[:, quarter:] = folds[2:]
-        for step in range(steps):
+        for step, rows in enumerate((BLOCK, BLOCK, half)):
             if loc == 0:
-                table_copies[step].wait()
-            at = slice(step % (steps // 2) * BLOCK, (step % (steps // 2) + 1) * BLOCK)
+                wait_copies(table_copies[step : step + rows // BLOCK])
             if step < steps // 2:
-                left, right = even_table[at], even_fold[4 * step // steps]
+                left, right = even_table[step * BLOCK : (step + 1) * BLOCK], even_fold[step]
             else:
-                left, right = odd_table[at], odd_fold[...]
+                left, right = odd_table[...], odd_fold[...]
             terms = lax.dot_general(left, right, CONTRACT_LAST, preferred_element_type=jnp.float32)
-            for dest in range(per_step):
+            for dest in range(rows // width):
                 start = dest // per_group * 2 * GROUP + dest % per_group * cols
                 parts = [terms[first : first + cols] for first in (start, start + GROUP)]
                 block = jnp.concatenate(parts, axis=0).astype(jnp.bfloat16)
-                out_ref[step * per_step + dest, loc] = block
+                out_ref[step * BLOCK // width + dest, loc] = block
 
 
 def row_transform(images, even_table, odd_table, devices):
@@ -191,6 +189,8 @@
     rate_smem,
     time_smem,
     received,
+    even_turned,
+    odd_turned,
     even_table,
     odd_table,
     out_ref,
@@ -244,12 +244,10 @@
     def multiply(step):
         at = slice(step % (steps // 2) * BLOCK, (step % (steps // 2) + 1) * BLOCK)
         if step < steps // 2:
-            left, right = even_fold[4 * step // steps], even_table[at]
+            left, right = even_fold[4 * step // steps], even_turned[:, at]
         else:
-            left, right = odd_fold[...], odd_table[at]
-        products[step % 2] = lax.dot_general(
-            left, right, CONTRACT_LAST, preferred_element_type=jnp.float32
-        )
+            left, right = odd_fold[...], odd_turned[:, at]
+        products[step % 2] = jnp.dot(left, right, preferred_element_type=jnp.float32)
 
     multiply(0)
     rows_cos[...], rows_sin[...] = row_factors(shift_y, half)
@@ -347,16 +345,16 @@
         send(position + 2, even - odd)
 
 
-def column_stage(rate_vectors, epoch_times, spectra, even_table, odd_table, epoch_count):
+def column_stage(rate_vectors, epoch_times, spectra, turned_tables, tables, epoch_count):
     devices, loc_epochs, width, loc_rows = spectra.shape
-    half, quarter = even_table.shape
+    half, quarter = tables[0].shape
     length = 2 * half
     epochs, rates = epoch_times.shape[0], rate_vectors.shape[0]
     out = (devices, rates // epoch_count, width, loc_rows)
     scalars = pl.BlockSpec(memory_space=pltpu.SMEM)
     return pl.pallas_call(
         functools.partial(column_kernel, epoch_count),
-        in_specs=[scalars, scalars, IN_VMEM, IN_VMEM, IN_VMEM],
+        in_specs=[scalars, scalars] + [IN_VMEM] * 5,
         out_specs=IN_VMEM,
         out_shape=pltpu.VMEM(out, jnp.bfloat16),
         scratch_shapes=[
@@ -370,24 +368,25 @@
         ],
         compiler_params=pltpu.CompilerParams(vmem_limit_bytes=40 * MIB),
         cost_estimate=cost(
-            2 * (even_table.size + odd_table.size) * (epochs + rates) * width,
-            3 * half * half + 4 * spectra.size,
+            3 * half * half * (epochs + rates) * width, 6 * half * half + 4 * spectra.size
         ),
         name="column_stage",
     )(
         rate_vectors,
         epoch_times,
-        *(in_space(part, pltpu.VMEM) for part in (spectra, even_table, odd_table)),
+        *(in_space(part, pltpu.VMEM) for part in (spectra, *turned_tables, *tables)),
     )
 
 
 def image_kernel(back, even_table, odd_table, out_hbm, left, staged, out_sems):
     quarter = even_table.shape[1]
-    width = back.shape[1]
+    _, width, rows = back.shape
     cols = width // 2
     per_group = GROUP // cols
     for group in range(back.shape[0] // per_group):
-        members = [back[group * per_group + place].astype(jnp.float32) for place in range(per_group)]
+        members = [back[group * per_group + place] for place in range(per_group)]
+        if cols % 16 != 0 or rows % 128 != 0:
+            members = [member.astype(jnp.float32) for member in members]
         parts = [member[:cols] for member in members] + [member[cols:] for member in members]
         whole = jnp.concatenate(parts, axis=0)
         left[:, group * 2 * GROUP : (group + 1) * 2 * GROUP] = whole.T.astype(jnp.bfloat16)
@@ -436,18 +435,18 @@
     _, loc_rows, length = images.shape
     epoch_count = lax.axis_size("epoch")
     devices = lax.axis_size("row") * epoch_count
-    even_table, odd_table = [jnp.asarray(part) for part in packed_tables(length)]
+    tables = packed_tables(length)
+    turned_tables = [jnp.asarray(np.ascontiguousarray(part.T)) for part in tables]
+    tables = [jnp.asarray(part) for part in tables]
 
     def exchange(values):
         return lax.all_to_all(values, ("row", "epoch"), 0, 0, tiled=True)
 
-    spectra = exchange(row_transform(images, even_table, odd_table, devices))
+    spectra = exchange(row_transform(images, *tables, devices))
     back = exchange(
-        column_stage(rate_vectors, epoch_times, spectra, even_table, odd_table, epoch_count)
+        column_stage(rate_vectors, epoch_times, spectra, turned_tables, tables, epoch_count)
     )
-    return image_rows(
-        back.reshape(devices, length // devices, loc_rows), even_table, odd_table
-    )
+    return image_rows(back.reshape(devices, length // devices, loc_rows), *tables)
 
 
 def solution(mesh):

time: 97.7 us -> 98.2 us (level)
  no operation moved by 1% of the time
where the time goes in v14:
time: 98.2 us; the launch traced here: 97.7 us
  blocking collectives  84.5 us (86%)
  Pallas kernels  13.1 us (13%)
    all_to_all x2, blocking collectives, exchange(): return lax.all_to_all(values, ('row', 'epoch'), 0, 0, tiled=True)  84.5 us
    pallas_call x1, Pallas kernels, row_transform(): pl.pallas_call(row_kernel, in_specs=[HBM, HBM, HBM], out_specs=IN_VMEM, o...  5.85 us
    pallas_call x1, Pallas kernels, column_stage(): pl.pallas_call(functools.partial(column_kernel, epoch_count), in_specs=[s...  5.12 us
    pallas_call x1, Pallas kernels, image_rows(): pl.pallas_call(image_kernel, in_specs=[IN_VMEM, IN_VMEM, IN_VMEM], out_sp...  2.12 us

profile of v14, /device:TPU:0, one launch (start us, length us, event | category | flops | bytes accessed | tf_op | source)
XLA Modules:
  0.0 97.7 jit_solution(11236324884582835014)
XLA Ops:
  0.0 0.0 copy-start.2
  0.0 0.0 copy-start.4
  0.0 0.0 copy-start.5
  0.0 5.8 %row_transform.1 = bf16[16,2,128,256]{3,2,1,0:T(8,128)(2,1)S(1)} custom-call(bf16[2,256,2048]{2,1,0:T(8,128)(2,1)} %images_hbm.1, bf16[1024,512]{1,0:T(8,128)(2,1)} %constant.10.clone.even_hbm.even_table, bf16[1024,1024]{1,0:T(8,128)(2,1)} %constant.11.clone.odd_hbm.odd_table), custom_call_target="tpu_custom_call" | custom-call | flops 1610612736 | bytes 7340032 | tf_op jit(solution)/shard_map/row_transform/pallas_call | solution.py:124
  5.9 0.0 copy-start
  5.9 0.0 copy-start.1
  5.9 0.0 copy-start.3
  5.9 54.7 %all_to_all.10.received = bf16[16,2,128,256]{3,2,1,0:T(8,128)(2,1)S(1)} all-to-all(bf16[16,2,128,256]{3,2,1,0:T(8,128)(2,1)S(1)} %row_transform.1), channel_id=1, replica_groups=mesh['group'=2,'row'=8,'epoch'=2] {'row','epoch'}, dimensions={0} | all-to-all | bytes 4194304 | tf_op jit(solution)/shard_map/all_to_all | solution.py:443
  60.6 0.0 copy-done.2
  60.6 0.0 copy-done.4
  60.6 0.0 copy-done.5
  60.7 0.0 copy-done
  60.7 0.0 copy-done.1
  60.7 0.0 copy-done.3
  60.7 5.1 %column_stage.1 = bf16[16,1,128,256]{3,2,1,0:T(8,128)(2,1)S(1)} custom-call(s32[2,2]{1,0:T(2,128)S(1)} %copy-done.4, s32[4]{0:T(128)S(1)} %copy-done.5, bf16[16,2,128,256]{3,2,1,0:T(8,128)(2,1)S(1)} %all_to_all.10.received, bf16[512,1024]{1,0:T(8,128)(2,1)S(1)} %copy-done.3, bf16[1024,1024]{1,0:T(8,128)(2,1)S(1)} %copy-done.2, ...), custom_call_target="tpu_custom_call" | custom-call | flops 2415919104 | bytes 10485760 | tf_op jit(solution)/shard_map/column_stage/pallas_call | solution.py:355
  65.8 29.8 %all_to_all.11 = bf16[16,1,128,256]{3,2,1,0:T(8,128)(2,1)S(1)} all-to-all(bf16[16,1,128,256]{3,2,1,0:T(8,128)(2,1)S(1)} %column_stage.1), channel_id=1, replica_groups=mesh['group'=2,'row'=8,'epoch'=2] {'row','epoch'}, dimensions={0} | all-to-all | bytes 2097152 | tf_op jit(solution)/shard_map/all_to_all | solution.py:443
  95.6 2.1 %image_rows.1 = f32[1,256,2048]{2,1,0:T(8,128)} custom-call(bf16[16,128,256]{2,1,0:T(8,128)(2,1)S(1)} %bitcast.1, bf16[1024,512]{1,0:T(8,128)(2,1)S(1)} %copy-done.1, bf16[1024,1024]{1,0:T(8,128)(2,1)S(1)} %copy-done), custom_call_target="tpu_custom_call" | custom-call | flops 805306368 | bytes 6291456 | tf_op jit(solution)/shard_map/image_rows/pallas_call | solution.py:416
Async XLA Ops:
  0.0 60.6 %copy-start.2 = (bf16[1024,1024]{1,0:T(8,128)(2,1)S(1)}, bf16[1024,1024]{1,0:T(8,128)(2,1)}, u32[]{:S(2)}) copy-start(bf16[1024,1024]{1,0:T(8,128)(2,1)} %constant.9.clone.odd_turned) | copy-start | bytes 6291460
  0.0 60.6 %copy-start.4 = (s32[2,2]{1,0:T(2,128)S(1)}, s32[2,2]{1,0:T(2,128)}, u32[]{:S(2)}) copy-start(s32[2,2]{1,0:T(2,128)} %rate_smem.1) | copy-start | bytes 52
  0.0 60.6 %copy-start.5 = (s32[4]{0:T(128)S(1)}, s32[4]{0:T(128)}, u32[]{:S(2)}) copy-start(s32[4]{0:T(128)} %time_smem.1) | copy-start | bytes 52
  5.9 54.8 %copy-start = (bf16[1024,1024]{1,0:T(8,128)(2,1)S(1)}, bf16[1024,1024]{1,0:T(8,128)(2,1)}, u32[]{:S(2)}) copy-start(bf16[1024,1024]{1,0:T(8,128)(2,1)} %constant.11.clone.odd_hbm.odd_table) | copy-start | bytes 6291460
  5.9 54.8 %copy-start.1 = (bf16[1024,512]{1,0:T(8,128)(2,1)S(1)}, bf16[1024,512]{1,0:T(8,128)(2,1)}, u32[]{:S(2)}) copy-start(bf16[1024,512]{1,0:T(8,128)(2,1)} %constant.10.clone.even_hbm.even_table) | copy-start | bytes 3145732
  5.9 54.8 %copy-start.3 = (bf16[512,1024]{1,0:T(8,128)(2,1)S(1)}, bf16[512,1024]{1,0:T(8,128)(2,1)}, u32[]{:S(2)}) copy-start(bf16[512,1024]{1,0:T(8,128)(2,1)} %constant.8.clone.even_turned) | copy-start | bytes 3145732

commit v15 on v12

--- a/solution.py
+++ b/solution.py
@@ -55,10 +55,9 @@
 
 
 def fold(quarters):
-    first, second, third, fourth = [part.astype(jnp.float32) for part in quarters]
+    first, second, third, fourth = quarters
     near, far = first + third, second + fourth
-    folds = near + far, near - far, first - third, second - fourth
-    return [part.astype(jnp.bfloat16) for part in folds]
+    return near + far, near - far, first - third, second - fourth
 
 
 def row_kernel(
@@ -383,11 +382,13 @@
 
 def image_kernel(back, even_table, odd_table, out_hbm, left, staged, out_sems):
     quarter = even_table.shape[1]
-    width = back.shape[1]
+    _, width, rows = back.shape
     cols = width // 2
     per_group = GROUP // cols
     for group in range(back.shape[0] // per_group):
-        members = [back[group * per_group + place].astype(jnp.float32) for place in range(per_group)]
+        members = [back[group * per_group + place] for place in range(per_group)]
+        if cols % 16 != 0 or rows % 128 != 0:
+            members = [member.astype(jnp.float32) for member in members]
         parts = [member[:cols] for member in members] + [member[cols:] for member in members]
         whole = jnp.concatenate(parts, axis=0)
         left[:, group * 2 * GROUP : (group + 1) * 2 * GROUP] = whole.T.astype(jnp.bfloat16)

time: 97.7 us -> 97.4 us (level)
  no operation moved by 1% of the time
where the time goes in v15:
time: 97.4 us; the launch traced here: 96.9 us
  blocking collectives  84.5 us (87%)
  Pallas kernels  12.3 us (13%)
    all_to_all x2, blocking collectives, exchange(): return lax.all_to_all(values, ('row', 'epoch'), 0, 0, tiled=True)  84.5 us
    pallas_call x1, Pallas kernels, row_transform(): pl.pallas_call(row_kernel, in_specs=[HBM, HBM, HBM], out_specs=IN_VMEM, o...  5.13 us
    pallas_call x1, Pallas kernels, column_stage(): pl.pallas_call(functools.partial(column_kernel, epoch_count), in_specs=[s...  5.04 us
    pallas_call x1, Pallas kernels, image_rows(): pl.pallas_call(image_kernel, in_specs=[IN_VMEM, IN_VMEM, IN_VMEM], out_sp...  2.13 us

profile of v15, /device:TPU:0, one launch (start us, length us, event | category | flops | bytes accessed | tf_op | source)
XLA Modules:
  0.0 96.9 jit_solution(3160421591053767329)
XLA Ops:
  0.0 5.1 %row_transform.1 = bf16[16,2,128,256]{3,2,1,0:T(8,128)(2,1)S(1)} custom-call(bf16[2,256,2048]{2,1,0:T(8,128)(2,1)} %images_hbm.1, bf16[1024,512]{1,0:T(8,128)(2,1)} %constant.4.clone.even_hbm.even_table, bf16[1024,1024]{1,0:T(8,128)(2,1)} %constant.5.clone.odd_hbm.odd_table), custom_call_target="tpu_custom_call" | custom-call | flops 1610612736 | bytes 7340032 | tf_op jit(solution)/shard_map/row_transform/pallas_call | solution.py:125
  5.1 0.0 copy-start
  5.2 0.0 copy-start.1
  5.2 0.0 copy-start.2
  5.2 0.0 copy-start.3
  5.2 54.7 %all_to_all.10.received = bf16[16,2,128,256]{3,2,1,0:T(8,128)(2,1)S(1)} all-to-all(bf16[16,2,128,256]{3,2,1,0:T(8,128)(2,1)S(1)} %row_transform.1), channel_id=1, replica_groups=mesh['group'=2,'row'=8,'epoch'=2] {'row','epoch'}, dimensions={0} | all-to-all | bytes 4194304 | tf_op jit(solution)/shard_map/all_to_all | solution.py:443
  59.9 0.0 copy-done
  59.9 0.0 copy-done.1
  59.9 0.0 copy-done.2
  59.9 0.0 copy-done.3
  60.0 5.0 %column_stage.1 = bf16[16,1,128,256]{3,2,1,0:T(8,128)(2,1)S(1)} custom-call(s32[2,2]{1,0:T(2,128)S(1)} %copy-done.2, s32[4]{0:T(128)S(1)} %copy-done.3, bf16[16,2,128,256]{3,2,1,0:T(8,128)(2,1)S(1)} %all_to_all.10.received, bf16[1024,512]{1,0:T(8,128)(2,1)S(1)} %copy-done.1, bf16[1024,1024]{1,0:T(8,128)(2,1)S(1)} %copy-done), custom_call_target="tpu_custom_call" | custom-call | flops 2415919104 | bytes 7340032 | tf_op jit(solution)/shard_map/column_stage/pallas_call | solution.py:356
  65.0 29.7 %all_to_all.11 = bf16[16,1,128,256]{3,2,1,0:T(8,128)(2,1)S(1)} all-to-all(bf16[16,1,128,256]{3,2,1,0:T(8,128)(2,1)S(1)} %column_stage.1), channel_id=1, replica_groups=mesh['group'=2,'row'=8,'epoch'=2] {'row','epoch'}, dimensions={0} | all-to-all | bytes 2097152 | tf_op jit(solution)/shard_map/all_to_all | solution.py:443
  94.7 2.1 %image_rows.1 = f32[1,256,2048]{2,1,0:T(8,128)} custom-call(bf16[16,128,256]{2,1,0:T(8,128)(2,1)S(1)} %bitcast.1, bf16[1024,512]{1,0:T(8,128)(2,1)S(1)} %copy-done.1, bf16[1024,1024]{1,0:T(8,128)(2,1)S(1)} %copy-done), custom_call_target="tpu_custom_call" | custom-call | flops 805306368 | bytes 6291456 | tf_op jit(solution)/shard_map/image_rows/pallas_call | solution.py:418
Async XLA Ops:
  5.1 54.8 %copy-start = (bf16[1024,1024]{1,0:T(8,128)(2,1)S(1)}, bf16[1024,1024]{1,0:T(8,128)(2,1)}, u32[]{:S(2)}) copy-start(bf16[1024,1024]{1,0:T(8,128)(2,1)} %constant.5.clone.odd_hbm.odd_table) | copy-start | bytes 6291460
  5.2 54.8 %copy-start.1 = (bf16[1024,512]{1,0:T(8,128)(2,1)S(1)}, bf16[1024,512]{1,0:T(8,128)(2,1)}, u32[]{:S(2)}) copy-start(bf16[1024,512]{1,0:T(8,128)(2,1)} %constant.4.clone.even_hbm.even_table) | copy-start | bytes 3145732
  5.2 54.8 %copy-start.2 = (s32[2,2]{1,0:T(2,128)S(1)}, s32[2,2]{1,0:T(2,128)}, u32[]{:S(2)}) copy-start(s32[2,2]{1,0:T(2,128)} %rate_smem.1) | copy-start | bytes 52
  5.2 54.8 %copy-start.3 = (s32[4]{0:T(128)S(1)}, s32[4]{0:T(128)}, u32[]{:S(2)}) copy-start(s32[4]{0:T(128)} %time_smem.1) | copy-start | bytes 52

commit v16 on v15

--- a/solution.py
+++ b/solution.py
@@ -185,6 +185,19 @@
     )
 
 
+def aligned(value, multiple):
+    return value if isinstance(value, int) else pl.multiple_of(value, multiple)
+
+
+def loop_over(count, body):
+    pl.loop(0, count)(body)
+
+
+def unroll_over(count, body):
+    for index in range(count):
+        body(index)
+
+
 def column_kernel(
     epoch_count,
     rate_smem,
@@ -251,7 +264,9 @@
         )
 
     multiply(0)
-    rows_cos[...], rows_sin[...] = row_factors(shift_y, half)
+    for target, values in zip((rows_cos, rows_sin), row_factors(shift_y, half)):
+        for pair in range(pairs):
+            target[pair] = values[pair : pair + 1]
     factors = column_factors(shift_y, shift_x, 1.0 / math.sqrt(epochs), device, cols, half).T
     for kind in range(4):
         for pair in range(pairs):
@@ -260,61 +275,71 @@
 
     chunk = min(ROW_CHUNK, cols)
 
-    def add_ramped(step, group):
-        tile = (step * BLOCK // 2 // GROUP + group) * GROUP
-        at_even = group * 2 * GROUP
-        at_odd = at_even + GROUP
-        for rate in range(rates):
-            for start in range(0, cols, chunk):
-                real = slice(start, start + chunk)
-                imag = slice(cols + start, cols + start + chunk)
-                totals = [[0.0, 0.0], [0.0, 0.0]]
-                leads = [0.0, 0.0]
-                for epoch in range(epochs):
-                    pair = rate * epochs + epoch
-                    cos_row = rows_cos[pair : pair + 1, tile : tile + GROUP]
-                    sin_row = rows_sin[pair : pair + 1, tile : tile + GROUP]
-                    turned, evens = [], []
-                    for part in (real, imag):
-                        at = slice(epoch * width + part.start, epoch * width + part.stop)
-                        even = products[step % 2, at, at_even : at_even + GROUP]
-                        odd = products[step % 2, at, at_odd : at_odd + GROUP]
-                        turned.append(
-                            (cos_row * even + sin_row * odd, cos_row * odd - sin_row * even)
-                        )
-                        evens.append(even)
-                    straight = [spread[0, pair, part] for part in (real, imag)]
-                    crossed = [spread[1, pair, part] for part in (real, imag)]
-                    for part in range(2):
-                        for which in range(2):
-                            totals[part][which] += (
-                                straight[part] * turned[part][which]
-                                + crossed[1 - part] * turned[1 - part][which]
-                            )
-                        if step == 0 and group == 0:
-                            own, other = (real, imag) if part == 0 else (imag, real)
-                            leads[part] += (
-                                spread[2, pair, own] * evens[part]
-                                + spread[3, pair, other] * evens[1 - part]
-                            )
-                for part, rows in enumerate((real, imag)):
-                    even_sum, odd_sum = totals[part]
-                    if step == 0 and group == 0:
-                        first = lax.broadcasted_iota(jnp.int32, even_sum.shape, 1) == 0
-                        even_sum = jnp.where(first, leads[part], even_sum)
-                    at = slice(rate * width + rows.start, rate * width + rows.stop)
-                    sums[at, step * BLOCK + at_even : step * BLOCK + at_even + GROUP] = even_sum.astype(
-                        jnp.bfloat16
+    chunks = cols // chunk
+    repeat = loop_over if chunk == ROW_CHUNK else unroll_over
+    groups = BLOCK // 2 // GROUP
+
+    def place(index):
+        rate, part = index // chunks, index % chunks
+        return rate, aligned(part * chunk, chunk), aligned(cols + part * chunk, chunk)
+
+    def add_ramped(step, index):
+        group, index = index // (rates * chunks), index % (rates * chunks)
+        rate, real, imag = place(index)
+        tile = aligned((step * groups + group) * GROUP, GROUP)
+        at_even = aligned(group * 2 * GROUP, GROUP)
+        at_odd = aligned(at_even + GROUP, GROUP)
+        totals = [[0.0, 0.0], [0.0, 0.0]]
+        for epoch in range(epochs):
+            pair = rate * epochs + epoch
+            cos_row = rows_cos[pair, :, pl.ds(tile, GROUP)]
+            sin_row = rows_sin[pair, :, pl.ds(tile, GROUP)]
+            turned = []
+            for start in (real, imag):
+                at = pl.ds(aligned(epoch * width + start, chunk), chunk)
+                even = products[step % 2, at, pl.ds(at_even, GROUP)]
+                odd = products[step % 2, at, pl.ds(at_odd, GROUP)]
+                turned.append((cos_row * even + sin_row * odd, cos_row * odd - sin_row * even))
+            straight = [spread[0, pair, pl.ds(start, chunk)] for start in (real, imag)]
+            crossed = [spread[1, pair, pl.ds(start, chunk)] for start in (real, imag)]
+            for part in range(2):
+                for which in range(2):
+                    totals[part][which] += (
+                        straight[part] * turned[part][which]
+                        + crossed[1 - part] * turned[1 - part][which]
                     )
-                    sums[at, step * BLOCK + at_odd : step * BLOCK + at_odd + GROUP] = odd_sum.astype(
-                        jnp.bfloat16
-                    )
+        for part, start in enumerate((real, imag)):
+            at = pl.ds(aligned(rate * width + start, chunk), chunk)
+            for which, lane in enumerate((at_even, at_odd)):
+                lane = aligned(step * BLOCK + lane, GROUP)
+                sums[at, pl.ds(lane, GROUP)] = totals[part][which].astype(jnp.bfloat16)
+
+    def replace_lead(index):
+        rate, real, imag = place(index)
+        leads = [0.0, 0.0]
+        for epoch in range(epochs):
+            pair = rate * epochs + epoch
+            evens = [
+                products[0, pl.ds(aligned(epoch * width + start, chunk), chunk), :GROUP]
+                for start in (real, imag)
+            ]
+            for part, (own, other) in enumerate(((real, imag), (imag, real))):
+                leads[part] += (
+                    spread[2, pair, pl.ds(own, chunk)] * evens[part]
+                    + spread[3, pair, pl.ds(other, chunk)] * evens[1 - part]
+                )
+        for part, start in enumerate((real, imag)):
+            at = pl.ds(aligned(rate * width + start, chunk), chunk)
+            first = lax.broadcasted_iota(jnp.int32, leads[part].shape, 1) == 0
+            kept = sums[at, :GROUP].astype(jnp.float32)
+            sums[at, :GROUP] = jnp.where(first, leads[part], kept).astype(jnp.bfloat16)
 
     for step in range(steps):
+        repeat(groups * rates * chunks, functools.partial(add_ramped, step))
+        if step == 0:
+            repeat(rates * chunks, replace_lead)
         if step + 1 < steps:
             multiply(step + 1)
-        for group in range(BLOCK // 2 // GROUP):
-            add_ramped(step, group)
 
     loc_rates = rates // epoch_count
 
@@ -359,8 +384,8 @@
         out_specs=IN_VMEM,
         out_shape=pltpu.VMEM(out, jnp.bfloat16),
         scratch_shapes=[
-            pltpu.VMEM((rates * epochs, half), jnp.float32),
-            pltpu.VMEM((rates * epochs, half), jnp.float32),
+            pltpu.VMEM((rates * epochs, 1, half), jnp.float32),
+            pltpu.VMEM((rates * epochs, 1, half), jnp.float32),
             pltpu.VMEM((4, rates * epochs, width, GROUP), jnp.float32),
             pltpu.VMEM((2, epochs * width, quarter), jnp.bfloat16),
             pltpu.VMEM((epochs * width, half), jnp.bfloat16),

time: 97.4 us -> 101 us (1.037)
  Pallas kernels: 12.3 us -> 15.4 us
    pallas_call x1, Pallas kernels: 5.04 us -> 8.18 us  [column_stage(): pl.pallas_call(functools.partial(column_kernel, epoch_count), in_specs=[s...]
where the time goes in v16:
time: 101 us; the launch traced here: 100 us
  blocking collectives  84.5 us (84%)
  Pallas kernels  15.4 us (15%)
    all_to_all x2, blocking collectives, exchange(): return lax.all_to_all(values, ('row', 'epoch'), 0, 0, tiled=True)  84.5 us
    pallas_call x1, Pallas kernels, column_stage(): pl.pallas_call(functools.partial(column_kernel, epoch_count), in_specs=[s...  8.18 us
    pallas_call x1, Pallas kernels, row_transform(): pl.pallas_call(row_kernel, in_specs=[HBM, HBM, HBM], out_specs=IN_VMEM, o...  5.13 us
    pallas_call x1, Pallas kernels, image_rows(): pl.pallas_call(image_kernel, in_specs=[IN_VMEM, IN_VMEM, IN_VMEM], out_sp...  2.12 us

profile of v16, /device:TPU:0, one launch (start us, length us, event | category | flops | bytes accessed | tf_op | source)
XLA Modules:
  0.0 100.0 jit_solution(1026999263655361909)
XLA Ops:
  0.0 5.1 %row_transform.1 = bf16[16,2,128,256]{3,2,1,0:T(8,128)(2,1)S(1)} custom-call(bf16[2,256,2048]{2,1,0:T(8,128)(2,1)} %images_hbm.1, bf16[1024,512]{1,0:T(8,128)(2,1)} %constant.4.clone.even_hbm.even_table, bf16[1024,1024]{1,0:T(8,128)(2,1)} %constant.5.clone.odd_hbm.odd_table), custom_call_target="tpu_custom_call" | custom-call | flops 1610612736 | bytes 7340032 | tf_op jit(solution)/shard_map/row_transform/pallas_call | solution.py:125
  5.1 0.0 copy-start
  5.2 0.0 copy-start.1
  5.2 0.0 copy-start.2
  5.2 0.0 copy-start.3
  5.2 54.7 %all_to_all.10.received = bf16[16,2,128,256]{3,2,1,0:T(8,128)(2,1)S(1)} all-to-all(bf16[16,2,128,256]{3,2,1,0:T(8,128)(2,1)S(1)} %row_transform.1), channel_id=1, replica_groups=mesh['group'=2,'row'=8,'epoch'=2] {'row','epoch'}, dimensions={0} | all-to-all | bytes 4194304 | tf_op jit(solution)/shard_map/all_to_all | solution.py:468
  59.9 0.0 copy-done
  59.9 0.0 copy-done.1
  59.9 0.0 copy-done.2
  59.9 0.0 copy-done.3
  60.0 8.2 %column_stage.1 = bf16[16,1,128,256]{3,2,1,0:T(8,128)(2,1)S(1)} custom-call(s32[2,2]{1,0:T(2,128)S(1)} %copy-done.2, s32[4]{0:T(128)S(1)} %copy-done.3, bf16[16,2,128,256]{3,2,1,0:T(8,128)(2,1)S(1)} %all_to_all.10.received, bf16[1024,512]{1,0:T(8,128)(2,1)S(1)} %copy-done.1, bf16[1024,1024]{1,0:T(8,128)(2,1)S(1)} %copy-done), custom_call_target="tpu_custom_call" | custom-call | flops 2415919104 | bytes 7340032 | tf_op jit(solution)/shard_map/column_stage/pallas_call | solution.py:381
  68.1 29.7 %all_to_all.11 = bf16[16,1,128,256]{3,2,1,0:T(8,128)(2,1)S(1)} all-to-all(bf16[16,1,128,256]{3,2,1,0:T(8,128)(2,1)S(1)} %column_stage.1), channel_id=1, replica_groups=mesh['group'=2,'row'=8,'epoch'=2] {'row','epoch'}, dimensions={0} | all-to-all | bytes 2097152 | tf_op jit(solution)/shard_map/all_to_all | solution.py:468
  97.9 2.1 %image_rows.1 = f32[1,256,2048]{2,1,0:T(8,128)} custom-call(bf16[16,128,256]{2,1,0:T(8,128)(2,1)S(1)} %bitcast.1, bf16[1024,512]{1,0:T(8,128)(2,1)S(1)} %copy-done.1, bf16[1024,1024]{1,0:T(8,128)(2,1)S(1)} %copy-done), custom_call_target="tpu_custom_call" | custom-call | flops 805306368 | bytes 6291456 | tf_op jit(solution)/shard_map/image_rows/pallas_call | solution.py:443
Async XLA Ops:
  5.1 54.8 %copy-start = (bf16[1024,1024]{1,0:T(8,128)(2,1)S(1)}, bf16[1024,1024]{1,0:T(8,128)(2,1)}, u32[]{:S(2)}) copy-start(bf16[1024,1024]{1,0:T(8,128)(2,1)} %constant.5.clone.odd_hbm.odd_table) | copy-start | bytes 6291460
  5.2 54.8 %copy-start.1 = (bf16[1024,512]{1,0:T(8,128)(2,1)S(1)}, bf16[1024,512]{1,0:T(8,128)(2,1)}, u32[]{:S(2)}) copy-start(bf16[1024,512]{1,0:T(8,128)(2,1)} %constant.4.clone.even_hbm.even_table) | copy-start | bytes 3145732
  5.2 54.8 %copy-start.2 = (s32[2,2]{1,0:T(2,128)S(1)}, s32[2,2]{1,0:T(2,128)}, u32[]{:S(2)}) copy-start(s32[2,2]{1,0:T(2,128)} %rate_smem.1) | copy-start | bytes 52
  5.2 54.8 %copy-start.3 = (s32[4]{0:T(128)S(1)}, s32[4]{0:T(128)}, u32[]{:S(2)}) copy-start(s32[4]{0:T(128)} %time_smem.1) | copy-start | bytes 52

commit v17 on v15

--- a/solution.py
+++ b/solution.py
@@ -15,6 +15,7 @@
 BLOCK = 512
 IMAGE_BLOCK = 256
 ROW_CHUNK = 16
+PIECES = 4
 MIB = 1024 * 1024
 CONTRACT_LAST = (((1,), (1,)), ((), ()))
 HBM = pl.BlockSpec(memory_space=pltpu.HBM)
@@ -80,29 +81,33 @@
     steps = length // BLOCK
     per_step = devices // steps
     per_group = GROUP // cols
+    def copies(source, target, sems, pieces):
+        rows = source.shape[0] // pieces
+        spans = [pl.ds(piece * rows, rows) for piece in range(pieces)]
+        return [
+            pltpu.make_async_copy(source.at[span], target.at[span], sems.at[piece])
+            for piece, span in enumerate(spans)
+        ]
+
+    pieces = max(1, min(PIECES, loc_rows // 16))
     image_copies = [
-        pltpu.make_async_copy(images_hbm.at[loc], images.at[loc], image_sems.at[loc])
+        copies(images_hbm.at[loc], images.at[loc], image_sems.at[loc], 1 if loc else pieces)
         for loc in range(loc_epochs)
     ]
-    table_copies = [
-        pltpu.make_async_copy(
-            source.at[pl.ds(block * BLOCK, BLOCK)],
-            target.at[pl.ds(block * BLOCK, BLOCK)],
-            table_sems.at[first + block],
-        )
-        for first, source, target in ((0, even_hbm, even_table), (steps // 2, odd_hbm, odd_table))
-        for block in range(steps // 2)
-    ]
-    for copy in image_copies[:1] + table_copies + image_copies[1:]:
+    even_copies = copies(even_hbm, even_table, table_sems.at[0], PIECES)
+    odd_copies = copies(odd_hbm, odd_table, table_sems.at[1], 2)
+    halfway = PIECES // 2
+    table_copies = [even_copies[:halfway], even_copies[halfway:], odd_copies[:1], odd_copies[1:]]
+    for copy in image_copies[0] + even_copies + odd_copies + sum(image_copies[1:], []):
         copy.start()
     for loc in range(loc_epochs):
-        image_copies[loc].wait()
+        wait_copies(image_copies[loc])
         folds = fold([images[loc, :, at * quarter : (at + 1) * quarter] for at in range(4)])
         even_fold[0], even_fold[1] = folds[:2]
         odd_fold[:, :quarter], odd_fold[:, quarter:] = folds[2:]
         for step in range(steps):
             if loc == 0:
-                table_copies[step].wait()
+                wait_copies(table_copies[step])
             at = slice(step % (steps // 2) * BLOCK, (step % (steps // 2) + 1) * BLOCK)
             if step < steps // 2:
                 left, right = even_table[at], even_fold[4 * step // steps]
@@ -133,8 +138,8 @@
             pltpu.VMEM(odd_table.shape, jnp.bfloat16),
             pltpu.VMEM((2, loc_rows, quarter), jnp.bfloat16),
             pltpu.VMEM((loc_rows, half), jnp.bfloat16),
-            pltpu.SemaphoreType.DMA((loc_epochs,)),
-            pltpu.SemaphoreType.DMA((steps,)),
+            pltpu.SemaphoreType.DMA((loc_epochs, PIECES)),
+            pltpu.SemaphoreType.DMA((2, PIECES)),
         ],
         compiler_params=pltpu.CompilerParams(vmem_limit_bytes=40 * MIB),
         cost_estimate=cost(
@@ -144,8 +149,24 @@
     )(*(in_space(part, pltpu.HBM) for part in (images, even_table, odd_table)))
 
 
-def turn_angle(turns, whole):
-    return (turns & (whole - 1)).astype(jnp.float32) * (2.0 * math.pi / whole)
+def cos_sin(turns, whole):
+    quarter, eighth = whole // 4, whole // 8
+    shifted = (turns + eighth) & (whole - 1)
+    quadrant = shifted >> (quarter.bit_length() - 1)
+    angle = ((shifted & (quarter - 1)) - eighth).astype(jnp.float32) * (2.0 * math.pi / whole)
+    square = angle * angle
+    sine, cosine = 1.0 / 362880.0, 1.0 / 40320.0
+    for divisor in (-5040.0, 120.0, -6.0, 1.0):
+        sine = sine * square + 1.0 / divisor
+    for divisor in (-720.0, 24.0, -2.0, 1.0):
+        cosine = cosine * square + 1.0 / divisor
+    sine = sine * angle
+    odd = (quadrant & 1) == 1
+    first, second = jnp.where(odd, sine, cosine), jnp.where(odd, cosine, sine)
+    return (
+        jnp.where(((quadrant + 1) & 2) == 2, -first, first),
+        jnp.where(quadrant >= 2, -second, second),
+    )
 
 
 def spread_pairs(scalars, lanes):
@@ -159,9 +180,8 @@
 def row_factors(shift_y, half):
     shifts = spread_pairs(shift_y, half)
     freqs = packed_freqs(lax.broadcasted_iota(jnp.int32, shifts.shape, 1), half)
-    angles = turn_angle((freqs - half) * shifts, SUBPIX * 2 * half)
-    cos_rows = jnp.where(freqs == 0, 1.0, 2.0 * jnp.cos(angles))
-    return cos_rows, jnp.where(freqs == 0, 0.0, 2.0 * jnp.sin(angles))
+    cosine, sine = cos_sin((freqs - half) * shifts, SUBPIX * 2 * half)
+    return jnp.where(freqs == 0, 1.0, 2.0 * cosine), jnp.where(freqs == 0, 0.0, 2.0 * sine)
 
 
 def column_factors(shift_y, shift_x, scale, device, cols, half):
@@ -171,13 +191,13 @@
     is_sine = (lane & cols) > 0
     paired = freqs == 0
     zero_col = paired & jnp.logical_not(is_sine)
-    angles = turn_angle(shifts_x * (freqs - half), SUBPIX * 2 * half)
-    ramp_cos = jnp.where(paired, scale, 2.0 * scale * jnp.cos(angles))
-    ramp_sin = jnp.where(paired, 0.0, 2.0 * scale * jnp.sin(angles))
+    cosine, sine = cos_sin(shifts_x * (freqs - half), SUBPIX * 2 * half)
+    ramp_cos = jnp.where(paired, scale, 2.0 * scale * cosine)
+    ramp_sin = jnp.where(paired, 0.0, 2.0 * scale * sine)
     ramp_sin = jnp.where(is_sine, ramp_sin, -ramp_sin)
-    cos_x = jnp.cos(turn_angle(shifts_x, 2 * SUBPIX))
-    cos_y = jnp.cos(turn_angle(shifts_y, 2 * SUBPIX))
-    cos_xy = jnp.cos(turn_angle(shifts_x + shifts_y, 2 * SUBPIX))
+    cos_x, cos_y, cos_xy = [
+        cos_sin(shifts, 2 * SUBPIX)[0] for shifts in (shifts_x, shifts_y, shifts_x + shifts_y)
+    ]
     main = jnp.where(zero_col, cos_y, cos_xy)
     lead = jnp.where(zero_col, 1.0, cos_x)
     return jnp.concatenate(

time: 97.4 us -> 97.3 us (level)
  no operation moved by 1% of the time
where the time goes in v17:
time: 97.3 us; the launch traced here: 96.8 us
  blocking collectives  84.5 us (87%)
  Pallas kernels  12.2 us (13%)
    all_to_all x2, blocking collectives, exchange(): return lax.all_to_all(values, ('row', 'epoch'), 0, 0, tiled=True)  84.5 us
    pallas_call x1, Pallas kernels, row_transform(): pl.pallas_call(row_kernel, in_specs=[HBM, HBM, HBM], out_specs=IN_VMEM, o...  5.18 us
    pallas_call x1, Pallas kernels, column_stage(): pl.pallas_call(functools.partial(column_kernel, epoch_count), in_specs=[s...  4.93 us
    pallas_call x1, Pallas kernels, image_rows(): pl.pallas_call(image_kernel, in_specs=[IN_VMEM, IN_VMEM, IN_VMEM], out_sp...  2.12 us

profile of v17, /device:TPU:0, one launch (start us, length us, event | category | flops | bytes accessed | tf_op | source)
XLA Modules:
  0.0 96.8 jit_solution(9451713060340778483)
XLA Ops:
  0.0 5.2 %row_transform.1 = bf16[16,2,128,256]{3,2,1,0:T(8,128)(2,1)S(1)} custom-call(bf16[2,256,2048]{2,1,0:T(8,128)(2,1)} %images_hbm.1, bf16[1024,512]{1,0:T(8,128)(2,1)} %constant.4.clone.even_hbm.even_table, bf16[1024,1024]{1,0:T(8,128)(2,1)} %constant.5.clone.odd_hbm.odd_table), custom_call_target="tpu_custom_call" | custom-call | flops 1610612736 | bytes 7340032 | tf_op jit(solution)/shard_map/row_transform/pallas_call | solution.py:130
  5.2 0.0 copy-start
  5.2 0.0 copy-start.1
  5.2 0.0 copy-start.2
  5.2 0.0 copy-start.3
  5.2 54.7 %all_to_all.10.received = bf16[16,2,128,256]{3,2,1,0:T(8,128)(2,1)S(1)} all-to-all(bf16[16,2,128,256]{3,2,1,0:T(8,128)(2,1)S(1)} %row_transform.1), channel_id=1, replica_groups=mesh['group'=2,'row'=8,'epoch'=2] {'row','epoch'}, dimensions={0} | all-to-all | bytes 4194304 | tf_op jit(solution)/shard_map/all_to_all | solution.py:463
  60.0 0.0 copy-done
  60.0 0.0 copy-done.1
  60.0 0.0 copy-done.2
  60.0 0.0 copy-done.3
  60.0 4.9 %column_stage.1 = bf16[16,1,128,256]{3,2,1,0:T(8,128)(2,1)S(1)} custom-call(s32[2,2]{1,0:T(2,128)S(1)} %copy-done.2, s32[4]{0:T(128)S(1)} %copy-done.3, bf16[16,2,128,256]{3,2,1,0:T(8,128)(2,1)S(1)} %all_to_all.10.received, bf16[1024,512]{1,0:T(8,128)(2,1)S(1)} %copy-done.1, bf16[1024,1024]{1,0:T(8,128)(2,1)S(1)} %copy-done), custom_call_target="tpu_custom_call" | custom-call | flops 2415919104 | bytes 7340032 | tf_op jit(solution)/shard_map/column_stage/pallas_call | solution.py:376
  64.9 29.8 %all_to_all.11 = bf16[16,1,128,256]{3,2,1,0:T(8,128)(2,1)S(1)} all-to-all(bf16[16,1,128,256]{3,2,1,0:T(8,128)(2,1)S(1)} %column_stage.1), channel_id=1, replica_groups=mesh['group'=2,'row'=8,'epoch'=2] {'row','epoch'}, dimensions={0} | all-to-all | bytes 2097152 | tf_op jit(solution)/shard_map/all_to_all | solution.py:463
  94.7 2.1 %image_rows.1 = f32[1,256,2048]{2,1,0:T(8,128)} custom-call(bf16[16,128,256]{2,1,0:T(8,128)(2,1)S(1)} %bitcast.1, bf16[1024,512]{1,0:T(8,128)(2,1)S(1)} %copy-done.1, bf16[1024,1024]{1,0:T(8,128)(2,1)S(1)} %copy-done), custom_call_target="tpu_custom_call" | custom-call | flops 805306368 | bytes 6291456 | tf_op jit(solution)/shard_map/image_rows/pallas_call | solution.py:438
Async XLA Ops:
  5.2 54.8 %copy-start = (bf16[1024,1024]{1,0:T(8,128)(2,1)S(1)}, bf16[1024,1024]{1,0:T(8,128)(2,1)}, u32[]{:S(2)}) copy-start(bf16[1024,1024]{1,0:T(8,128)(2,1)} %constant.5.clone.odd_hbm.odd_table) | copy-start | bytes 6291460
  5.2 54.8 %copy-start.1 = (bf16[1024,512]{1,0:T(8,128)(2,1)S(1)}, bf16[1024,512]{1,0:T(8,128)(2,1)}, u32[]{:S(2)}) copy-start(bf16[1024,512]{1,0:T(8,128)(2,1)} %constant.4.clone.even_hbm.even_table) | copy-start | bytes 3145732
  5.2 54.8 %copy-start.2 = (s32[2,2]{1,0:T(2,128)S(1)}, s32[2,2]{1,0:T(2,128)}, u32[]{:S(2)}) copy-start(s32[2,2]{1,0:T(2,128)} %rate_smem.1) | copy-start | bytes 52
  5.2 54.8 %copy-start.3 = (s32[4]{0:T(128)S(1)}, s32[4]{0:T(128)}, u32[]{:S(2)}) copy-start(s32[4]{0:T(128)} %time_smem.1) | copy-start | bytes 52

commit v18 on v17

--- a/solution.py
+++ b/solution.py
@@ -13,7 +13,7 @@
 SUBPIX = 16
 GROUP = 128
 BLOCK = 512
-IMAGE_BLOCK = 256
+IMAGE_BLOCK = 512
 ROW_CHUNK = 16
 PIECES = 4
 MIB = 1024 * 1024
@@ -91,34 +91,35 @@
 
     pieces = max(1, min(PIECES, loc_rows // 16))
     image_copies = [
-        copies(images_hbm.at[loc], images.at[loc], image_sems.at[loc], 1 if loc else pieces)
+        copies(images_hbm.at[loc], images.at[loc], image_sems.at[loc], pieces)
         for loc in range(loc_epochs)
     ]
     even_copies = copies(even_hbm, even_table, table_sems.at[0], PIECES)
     odd_copies = copies(odd_hbm, odd_table, table_sems.at[1], 2)
     halfway = PIECES // 2
     table_copies = [even_copies[:halfway], even_copies[halfway:], odd_copies[:1], odd_copies[1:]]
-    for copy in image_copies[0] + even_copies + odd_copies + sum(image_copies[1:], []):
+    for copy in sum(image_copies, []) + even_copies + odd_copies:
         copy.start()
     for loc in range(loc_epochs):
         wait_copies(image_copies[loc])
-        folds = fold([images[loc, :, at * quarter : (at + 1) * quarter] for at in range(4)])
-        even_fold[0], even_fold[1] = folds[:2]
-        odd_fold[:, :quarter], odd_fold[:, quarter:] = folds[2:]
-        for step in range(steps):
-            if loc == 0:
-                wait_copies(table_copies[step])
-            at = slice(step % (steps // 2) * BLOCK, (step % (steps // 2) + 1) * BLOCK)
-            if step < steps // 2:
-                left, right = even_table[at], even_fold[4 * step // steps]
-            else:
-                left, right = odd_table[at], odd_fold[...]
-            terms = lax.dot_general(left, right, CONTRACT_LAST, preferred_element_type=jnp.float32)
-            for dest in range(per_step):
-                start = dest // per_group * 2 * GROUP + dest % per_group * cols
-                parts = [terms[first : first + cols] for first in (start, start + GROUP)]
-                block = jnp.concatenate(parts, axis=0).astype(jnp.bfloat16)
-                out_ref[step * per_step + dest, loc] = block
+        at = slice(loc * loc_rows, (loc + 1) * loc_rows)
+        folds = fold([images[loc, :, part * quarter : (part + 1) * quarter] for part in range(4)])
+        even_fold[0, at], even_fold[1, at] = folds[:2]
+        odd_fold[at, :quarter], odd_fold[at, quarter:] = folds[2:]
+    for step in range(steps):
+        wait_copies(table_copies[step])
+        at = slice(step % (steps // 2) * BLOCK, (step % (steps // 2) + 1) * BLOCK)
+        if step < steps // 2:
+            left, right = even_table[at], even_fold[4 * step // steps]
+        else:
+            left, right = odd_table[at], odd_fold[...]
+        terms = lax.dot_general(left, right, CONTRACT_LAST, preferred_element_type=jnp.float32)
+        for dest in range(per_step):
+            start = dest // per_group * 2 * GROUP + dest % per_group * cols
+            parts = [terms[first : first + cols] for first in (start, start + GROUP)]
+            block = jnp.concatenate(parts, axis=0).astype(jnp.bfloat16)
+            for loc in range(loc_epochs):
+                out_ref[step * per_step + dest, loc] = block[:, loc * loc_rows : (loc + 1) * loc_rows]
 
 
 def row_transform(images, even_table, odd_table, devices):
@@ -136,8 +137,8 @@
             pltpu.VMEM(images.shape, jnp.bfloat16),
             pltpu.VMEM(even_table.shape, jnp.bfloat16),
             pltpu.VMEM(odd_table.shape, jnp.bfloat16),
-            pltpu.VMEM((2, loc_rows, quarter), jnp.bfloat16),
-            pltpu.VMEM((loc_rows, half), jnp.bfloat16),
+            pltpu.VMEM((2, rows, quarter), jnp.bfloat16),
+            pltpu.VMEM((rows, half), jnp.bfloat16),
             pltpu.SemaphoreType.DMA((loc_epochs, PIECES)),
             pltpu.SemaphoreType.DMA((2, PIECES)),
         ],

time: 97.3 us -> 97 us (level)
  no operation moved by 1% of the time
where the time goes in v18:
time: 97 us; the launch traced here: 96.5 us
  blocking collectives  84.5 us (87%)
  Pallas kernels  11.9 us (12%)
    all_to_all x2, blocking collectives, exchange(): return lax.all_to_all(values, ('row', 'epoch'), 0, 0, tiled=True)  84.5 us
    pallas_call x1, Pallas kernels, column_stage(): pl.pallas_call(functools.partial(column_kernel, epoch_count), in_specs=[s...  4.93 us
    pallas_call x1, Pallas kernels, row_transform(): pl.pallas_call(row_kernel, in_specs=[HBM, HBM, HBM], out_specs=IN_VMEM, o...  4.86 us
    pallas_call x1, Pallas kernels, image_rows(): pl.pallas_call(image_kernel, in_specs=[IN_VMEM, IN_VMEM, IN_VMEM], out_sp...  2.11 us

profile of v18, /device:TPU:0, one launch (start us, length us, event | category | flops | bytes accessed | tf_op | source)
XLA Modules:
  0.0 96.5 jit_solution(6420760490678831896)
XLA Ops:
  0.0 4.9 %row_transform.1 = bf16[16,2,128,256]{3,2,1,0:T(8,128)(2,1)S(1)} custom-call(bf16[2,256,2048]{2,1,0:T(8,128)(2,1)} %images_hbm.1, bf16[1024,512]{1,0:T(8,128)(2,1)} %constant.4.clone.even_hbm.even_table, bf16[1024,1024]{1,0:T(8,128)(2,1)} %constant.5.clone.odd_hbm.odd_table), custom_call_target="tpu_custom_call" | custom-call | flops 1610612736 | bytes 7340032 | tf_op jit(solution)/shard_map/row_transform/pallas_call | solution.py:131
  4.9 0.0 copy-start
  4.9 0.0 copy-start.1
  4.9 0.0 copy-start.2
  4.9 0.0 copy-start.3
  4.9 54.7 %all_to_all.10.received = bf16[16,2,128,256]{3,2,1,0:T(8,128)(2,1)S(1)} all-to-all(bf16[16,2,128,256]{3,2,1,0:T(8,128)(2,1)S(1)} %row_transform.1), channel_id=1, replica_groups=mesh['group'=2,'row'=8,'epoch'=2] {'row','epoch'}, dimensions={0} | all-to-all | bytes 4194304 | tf_op jit(solution)/shard_map/all_to_all | solution.py:464
  59.6 0.0 copy-done
  59.7 0.0 copy-done.1
  59.7 0.0 copy-done.2
  59.7 0.0 copy-done.3
  59.7 4.9 %column_stage.1 = bf16[16,1,128,256]{3,2,1,0:T(8,128)(2,1)S(1)} custom-call(s32[2,2]{1,0:T(2,128)S(1)} %copy-done.2, s32[4]{0:T(128)S(1)} %copy-done.3, bf16[16,2,128,256]{3,2,1,0:T(8,128)(2,1)S(1)} %all_to_all.10.received, bf16[1024,512]{1,0:T(8,128)(2,1)S(1)} %copy-done.1, bf16[1024,1024]{1,0:T(8,128)(2,1)S(1)} %copy-done), custom_call_target="tpu_custom_call" | custom-call | flops 2415919104 | bytes 7340032 | tf_op jit(solution)/shard_map/column_stage/pallas_call | solution.py:377
  64.6 29.7 %all_to_all.11 = bf16[16,1,128,256]{3,2,1,0:T(8,128)(2,1)S(1)} all-to-all(bf16[16,1,128,256]{3,2,1,0:T(8,128)(2,1)S(1)} %column_stage.1), channel_id=1, replica_groups=mesh['group'=2,'row'=8,'epoch'=2] {'row','epoch'}, dimensions={0} | all-to-all | bytes 2097152 | tf_op jit(solution)/shard_map/all_to_all | solution.py:464
  94.3 2.1 %image_rows.1 = f32[1,256,2048]{2,1,0:T(8,128)} custom-call(bf16[16,128,256]{2,1,0:T(8,128)(2,1)S(1)} %bitcast.1, bf16[1024,512]{1,0:T(8,128)(2,1)S(1)} %copy-done.1, bf16[1024,1024]{1,0:T(8,128)(2,1)S(1)} %copy-done), custom_call_target="tpu_custom_call" | custom-call | flops 805306368 | bytes 6291456 | tf_op jit(solution)/shard_map/image_rows/pallas_call | solution.py:439
Async XLA Ops:
  4.9 54.8 %copy-start = (bf16[1024,1024]{1,0:T(8,128)(2,1)S(1)}, bf16[1024,1024]{1,0:T(8,128)(2,1)}, u32[]{:S(2)}) copy-start(bf16[1024,1024]{1,0:T(8,128)(2,1)} %constant.5.clone.odd_hbm.odd_table) | copy-start | bytes 6291460
  4.9 54.8 %copy-start.1 = (bf16[1024,512]{1,0:T(8,128)(2,1)S(1)}, bf16[1024,512]{1,0:T(8,128)(2,1)}, u32[]{:S(2)}) copy-start(bf16[1024,512]{1,0:T(8,128)(2,1)} %constant.4.clone.even_hbm.even_table) | copy-start | bytes 3145732
  4.9 54.8 %copy-start.2 = (s32[2,2]{1,0:T(2,128)S(1)}, s32[2,2]{1,0:T(2,128)}, u32[]{:S(2)}) copy-start(s32[2,2]{1,0:T(2,128)} %rate_smem.1) | copy-start | bytes 52
  4.9 54.8 %copy-start.3 = (s32[4]{0:T(128)S(1)}, s32[4]{0:T(128)}, u32[]{:S(2)}) copy-start(s32[4]{0:T(128)} %time_smem.1) | copy-start | bytes 52

commit v19 on v18

--- a/solution.py
+++ b/solution.py
@@ -22,14 +22,15 @@
 IN_VMEM = pl.BlockSpec(memory_space=pltpu.VMEM)
 
 
-def packed_freqs(index, half, where=jnp.where):
-    even = 4 * index - where(index < half // 4, 0, half - 2)
-    return where(index < half // 2, even, 2 * index - half + 1)
+def packed_freqs(index, half):
+    count = half // 4
+    kind = index >> (count.bit_length() - 1)
+    return 4 * (index & (count - 1)) + 2 * (kind & 1) + (kind >> 1)
 
 
 def packed_tables(length):
     half, quarter = length // 2, length // 4
-    freqs = packed_freqs(np.arange(half, dtype=np.int32), half, np.where)
+    freqs = packed_freqs(np.arange(half, dtype=np.int32), half)
     positions = np.arange(half, dtype=np.int32)
     turns = freqs[:, None] * positions[None, :] % length
     angles = turns.astype(np.float32) * np.float32(2.0 * math.pi / length)
@@ -69,8 +70,7 @@
     images,
     even_table,
     odd_table,
-    even_fold,
-    odd_fold,
+    folded,
     image_sems,
     table_sems,
 ):
@@ -95,7 +95,7 @@
         for loc in range(loc_epochs)
     ]
     even_copies = copies(even_hbm, even_table, table_sems.at[0], PIECES)
-    odd_copies = copies(odd_hbm, odd_table, table_sems.at[1], 2)
+    odd_copies = copies(odd_hbm.at[:, :quarter], odd_table, table_sems.at[1], 2)
     halfway = PIECES // 2
     table_copies = [even_copies[:halfway], even_copies[halfway:], odd_copies[:1], odd_copies[1:]]
     for copy in sum(image_copies, []) + even_copies + odd_copies:
@@ -104,19 +104,27 @@
         wait_copies(image_copies[loc])
         at = slice(loc * loc_rows, (loc + 1) * loc_rows)
         folds = fold([images[loc, :, part * quarter : (part + 1) * quarter] for part in range(4)])
-        even_fold[0, at], even_fold[1, at] = folds[:2]
-        odd_fold[at, :quarter], odd_fold[at, quarter:] = folds[2:]
+        for part in range(4):
+            folded[part, at] = folds[part]
     for step in range(steps):
         wait_copies(table_copies[step])
         at = slice(step % (steps // 2) * BLOCK, (step % (steps // 2) + 1) * BLOCK)
-        if step < steps // 2:
-            left, right = even_table[at], even_fold[4 * step // steps]
-        else:
-            left, right = odd_table[at], odd_fold[...]
-        terms = lax.dot_general(left, right, CONTRACT_LAST, preferred_element_type=jnp.float32)
+        left = (even_table if step < steps // 2 else odd_table)[at]
+        sources = [step] if step < steps // 2 else [2, 3]
+        terms = [
+            lax.dot_general(
+                left, folded[source], CONTRACT_LAST, preferred_element_type=jnp.float32
+            )
+            for source in sources
+        ]
         for dest in range(per_step):
             start = dest // per_group * 2 * GROUP + dest % per_group * cols
-            parts = [terms[first : first + cols] for first in (start, start + GROUP)]
+            cosine, sine = [slice(first, first + cols) for first in (start, start + GROUP)]
+            parts = [terms[0][cosine], terms[0][sine]]
+            if step == 2:
+                parts = [parts[0] - terms[1][sine], parts[1] + terms[1][cosine]]
+            if step == 3:
+                parts = [parts[0] + terms[1][sine], parts[1] - terms[1][cosine]]
             block = jnp.concatenate(parts, axis=0).astype(jnp.bfloat16)
             for loc in range(loc_epochs):
                 out_ref[step * per_step + dest, loc] = block[:, loc * loc_rows : (loc + 1) * loc_rows]
@@ -136,9 +144,8 @@
         scratch_shapes=[
             pltpu.VMEM(images.shape, jnp.bfloat16),
             pltpu.VMEM(even_table.shape, jnp.bfloat16),
-            pltpu.VMEM(odd_table.shape, jnp.bfloat16),
-            pltpu.VMEM((2, rows, quarter), jnp.bfloat16),
-            pltpu.VMEM((rows, half), jnp.bfloat16),
+            pltpu.VMEM(even_table.shape, jnp.bfloat16),
+            pltpu.VMEM((4, rows, quarter), jnp.bfloat16),
             pltpu.SemaphoreType.DMA((loc_epochs, PIECES)),
             pltpu.SemaphoreType.DMA((2, PIECES)),
         ],

time: 97 us -> 96.8 us (level)
  no operation moved by 1% of the time
where the time goes in v19:
time: 96.8 us; the launch traced here: 96.3 us
  blocking collectives  84.5 us (87%)
  Pallas kernels  11.7 us (12%)
    all_to_all x2, blocking collectives, exchange(): return lax.all_to_all(values, ('row', 'epoch'), 0, 0, tiled=True)  84.5 us
    pallas_call x1, Pallas kernels, column_stage(): pl.pallas_call(functools.partial(column_kernel, epoch_count), in_specs=[s...  4.91 us
    pallas_call x1, Pallas kernels, row_transform(): pl.pallas_call(row_kernel, in_specs=[HBM, HBM, HBM], out_specs=IN_VMEM, o...  4.72 us
    pallas_call x1, Pallas kernels, image_rows(): pl.pallas_call(image_kernel, in_specs=[IN_VMEM, IN_VMEM, IN_VMEM], out_sp...  2.1 us

profile of v19, /device:TPU:0, one launch (start us, length us, event | category | flops | bytes accessed | tf_op | source)
XLA Modules:
  0.0 96.3 jit_solution(9208664713507805248)
XLA Ops:
  0.0 4.7 %row_transform.1 = bf16[16,2,128,256]{3,2,1,0:T(8,128)(2,1)S(1)} custom-call(bf16[2,256,2048]{2,1,0:T(8,128)(2,1)} %images_hbm.1, bf16[1024,512]{1,0:T(8,128)(2,1)} %constant.4.clone.even_hbm.even_table, bf16[1024,1024]{1,0:T(8,128)(2,1)} %constant.5.clone.odd_hbm.odd_table), custom_call_target="tpu_custom_call" | custom-call | flops 1610612736 | bytes 7340032 | tf_op jit(solution)/shard_map/row_transform/pallas_call | solution.py:139
  4.7 0.0 copy-start
  4.7 0.0 copy-start.1
  4.8 0.0 copy-start.2
  4.8 0.0 copy-start.3
  4.8 54.7 %all_to_all.10.received = bf16[16,2,128,256]{3,2,1,0:T(8,128)(2,1)S(1)} all-to-all(bf16[16,2,128,256]{3,2,1,0:T(8,128)(2,1)S(1)} %row_transform.1), channel_id=1, replica_groups=mesh['group'=2,'row'=8,'epoch'=2] {'row','epoch'}, dimensions={0} | all-to-all | bytes 4194304 | tf_op jit(solution)/shard_map/all_to_all | solution.py:471
  59.5 0.0 copy-done
  59.5 0.0 copy-done.1
  59.5 0.0 copy-done.2
  59.5 0.0 copy-done.3
  59.5 4.9 %column_stage.1 = bf16[16,1,128,256]{3,2,1,0:T(8,128)(2,1)S(1)} custom-call(s32[2,2]{1,0:T(2,128)S(1)} %copy-done.2, s32[4]{0:T(128)S(1)} %copy-done.3, bf16[16,2,128,256]{3,2,1,0:T(8,128)(2,1)S(1)} %all_to_all.10.received, bf16[1024,512]{1,0:T(8,128)(2,1)S(1)} %copy-done.1, bf16[1024,1024]{1,0:T(8,128)(2,1)S(1)} %copy-done), custom_call_target="tpu_custom_call" | custom-call | flops 2415919104 | bytes 7340032 | tf_op jit(solution)/shard_map/column_stage/pallas_call | solution.py:384
  64.5 29.8 %all_to_all.11 = bf16[16,1,128,256]{3,2,1,0:T(8,128)(2,1)S(1)} all-to-all(bf16[16,1,128,256]{3,2,1,0:T(8,128)(2,1)S(1)} %column_stage.1), channel_id=1, replica_groups=mesh['group'=2,'row'=8,'epoch'=2] {'row','epoch'}, dimensions={0} | all-to-all | bytes 2097152 | tf_op jit(solution)/shard_map/all_to_all | solution.py:471
  94.2 2.1 %image_rows.1 = f32[1,256,2048]{2,1,0:T(8,128)} custom-call(bf16[16,128,256]{2,1,0:T(8,128)(2,1)S(1)} %bitcast.1, bf16[1024,512]{1,0:T(8,128)(2,1)S(1)} %copy-done.1, bf16[1024,1024]{1,0:T(8,128)(2,1)S(1)} %copy-done), custom_call_target="tpu_custom_call" | custom-call | flops 805306368 | bytes 6291456 | tf_op jit(solution)/shard_map/image_rows/pallas_call | solution.py:446
Async XLA Ops:
  4.7 54.8 %copy-start = (bf16[1024,1024]{1,0:T(8,128)(2,1)S(1)}, bf16[1024,1024]{1,0:T(8,128)(2,1)}, u32[]{:S(2)}) copy-start(bf16[1024,1024]{1,0:T(8,128)(2,1)} %constant.5.clone.odd_hbm.odd_table) | copy-start | bytes 6291460
  4.7 54.8 %copy-start.1 = (bf16[1024,512]{1,0:T(8,128)(2,1)S(1)}, bf16[1024,512]{1,0:T(8,128)(2,1)}, u32[]{:S(2)}) copy-start(bf16[1024,512]{1,0:T(8,128)(2,1)} %constant.4.clone.even_hbm.even_table) | copy-start | bytes 3145732
  4.8 54.8 %copy-start.2 = (s32[2,2]{1,0:T(2,128)S(1)}, s32[2,2]{1,0:T(2,128)}, u32[]{:S(2)}) copy-start(s32[2,2]{1,0:T(2,128)} %rate_smem.1) | copy-start | bytes 52
  4.8 54.8 %copy-start.3 = (s32[4]{0:T(128)S(1)}, s32[4]{0:T(128)}, u32[]{:S(2)}) copy-start(s32[4]{0:T(128)} %time_smem.1) | copy-start | bytes 52

commit v20 on v19

--- a/solution.py
+++ b/solution.py
@@ -228,6 +228,7 @@
     odd_fold,
     products,
     sums,
+    parts,
 ):
     devices, loc_epochs, width, loc_rows = received.shape
     row_count = devices // epoch_count
@@ -258,10 +259,10 @@
                 quarters = []
                 for side in range(4):
                     first = side * row_count // 4 + tile * per_tile
-                    parts = [
+                    blocks = [
                         received[(first + part) * epoch_count + core, loc] for part in range(per_tile)
                     ]
-                    quarters.append(parts[0] if per_tile == 1 else jnp.concatenate(parts, axis=1))
+                    quarters.append(blocks[0] if per_tile == 1 else jnp.concatenate(blocks, axis=1))
                 at_row = (core * loc_epochs + loc) * width
                 at = slice(at_row, at_row + width)
                 folds = fold(quarters)
@@ -338,9 +339,22 @@
                         jnp.bfloat16
                     )
 
+    def invert(step):
+        at = slice(step % (steps // 2) * BLOCK, (step % (steps // 2) + 1) * BLOCK)
+        table = even_table if step < steps // 2 else odd_table
+        for side in range(table.shape[1] // quarter):
+            yield jnp.dot(
+                sums[:, step * BLOCK : (step + 1) * BLOCK],
+                table[at, side * quarter : (side + 1) * quarter],
+                preferred_element_type=jnp.float32,
+            )
+
     for step in range(steps):
         if step + 1 < steps:
             multiply(step + 1)
+        if step > 0:
+            for side, part in enumerate(invert(step - 1)):
+                parts[step - 1 + side] = part
         for group in range(BLOCK // 2 // GROUP):
             add_ramped(step, group)
 
@@ -356,7 +370,11 @@
                     rate * width : (rate + 1) * width, row * loc_rows : (row + 1) * loc_rows
                 ]
 
-    inverse_parts(sums, even_table, odd_table, slice(0, quarter), quarter, send)
+    for side, part in enumerate(invert(steps - 1)):
+        even = parts[0] + parts[1] if side == 0 else parts[0] - parts[1]
+        odd = parts[2 + side] + part
+        send(side, even + odd)
+        send(side + 2, even - odd)
 
 
 def inverse_parts(left, even_table, odd_table, at, quarter, send):
@@ -394,6 +412,7 @@
             pltpu.VMEM((epochs * width, half), jnp.bfloat16),
             pltpu.VMEM((2, epochs * width, BLOCK), jnp.float32),
             pltpu.VMEM((rates * width, length), jnp.bfloat16),
+            pltpu.VMEM((4, rates * width, quarter), jnp.float32),
         ],
         compiler_params=pltpu.CompilerParams(vmem_limit_bytes=40 * MIB),
         cost_estimate=cost(

time: 96.8 us -> 96.9 us (level)
  no operation moved by 1% of the time
where the time goes in v20:
time: 96.9 us; the launch traced here: 96.4 us
  blocking collectives  84.5 us (87%)
  Pallas kernels  11.8 us (12%)
    all_to_all x2, blocking collectives, exchange(): return lax.all_to_all(values, ('row', 'epoch'), 0, 0, tiled=True)  84.5 us
    pallas_call x1, Pallas kernels, column_stage(): pl.pallas_call(functools.partial(column_kernel, epoch_count), in_specs=[s...  4.99 us
    pallas_call x1, Pallas kernels, row_transform(): pl.pallas_call(row_kernel, in_specs=[HBM, HBM, HBM], out_specs=IN_VMEM, o...  4.72 us
    pallas_call x1, Pallas kernels, image_rows(): pl.pallas_call(image_kernel, in_specs=[IN_VMEM, IN_VMEM, IN_VMEM], out_sp...  2.1 us

profile of v20, /device:TPU:0, one launch (start us, length us, event | category | flops | bytes accessed | tf_op | source)
XLA Modules:
  0.0 96.4 jit_solution(26089269490002436)
XLA Ops:
  0.0 4.7 %row_transform.1 = bf16[16,2,128,256]{3,2,1,0:T(8,128)(2,1)S(1)} custom-call(bf16[2,256,2048]{2,1,0:T(8,128)(2,1)} %images_hbm.1, bf16[1024,512]{1,0:T(8,128)(2,1)} %constant.4.clone.even_hbm.even_table, bf16[1024,1024]{1,0:T(8,128)(2,1)} %constant.5.clone.odd_hbm.odd_table), custom_call_target="tpu_custom_call" | custom-call | flops 1610612736 | bytes 7340032 | tf_op jit(solution)/shard_map/row_transform/pallas_call | solution.py:139
  4.7 0.0 copy-start
  4.7 0.0 copy-start.1
  4.8 0.0 copy-start.2
  4.8 0.0 copy-start.3
  4.8 54.7 %all_to_all.10.received = bf16[16,2,128,256]{3,2,1,0:T(8,128)(2,1)S(1)} all-to-all(bf16[16,2,128,256]{3,2,1,0:T(8,128)(2,1)S(1)} %row_transform.1), channel_id=1, replica_groups=mesh['group'=2,'row'=8,'epoch'=2] {'row','epoch'}, dimensions={0} | all-to-all | bytes 4194304 | tf_op jit(solution)/shard_map/all_to_all | solution.py:490
  59.5 0.0 copy-done
  59.5 0.0 copy-done.1
  59.5 0.0 copy-done.2
  59.5 0.0 copy-done.3
  59.5 5.0 %column_stage.1 = bf16[16,1,128,256]{3,2,1,0:T(8,128)(2,1)S(1)} custom-call(s32[2,2]{1,0:T(2,128)S(1)} %copy-done.2, s32[4]{0:T(128)S(1)} %copy-done.3, bf16[16,2,128,256]{3,2,1,0:T(8,128)(2,1)S(1)} %all_to_all.10.received, bf16[1024,512]{1,0:T(8,128)(2,1)S(1)} %copy-done.1, bf16[1024,1024]{1,0:T(8,128)(2,1)S(1)} %copy-done), custom_call_target="tpu_custom_call" | custom-call | flops 2415919104 | bytes 7340032 | tf_op jit(solution)/shard_map/column_stage/pallas_call | solution.py:402
  64.5 29.8 %all_to_all.11 = bf16[16,1,128,256]{3,2,1,0:T(8,128)(2,1)S(1)} all-to-all(bf16[16,1,128,256]{3,2,1,0:T(8,128)(2,1)S(1)} %column_stage.1), channel_id=1, replica_groups=mesh['group'=2,'row'=8,'epoch'=2] {'row','epoch'}, dimensions={0} | all-to-all | bytes 2097152 | tf_op jit(solution)/shard_map/all_to_all | solution.py:490
  94.3 2.1 %image_rows.1 = f32[1,256,2048]{2,1,0:T(8,128)} custom-call(bf16[16,128,256]{2,1,0:T(8,128)(2,1)S(1)} %bitcast.1, bf16[1024,512]{1,0:T(8,128)(2,1)S(1)} %copy-done.1, bf16[1024,1024]{1,0:T(8,128)(2,1)S(1)} %copy-done), custom_call_target="tpu_custom_call" | custom-call | flops 805306368 | bytes 6291456 | tf_op jit(solution)/shard_map/image_rows/pallas_call | solution.py:465
Async XLA Ops:
  4.7 54.8 %copy-start = (bf16[1024,1024]{1,0:T(8,128)(2,1)S(1)}, bf16[1024,1024]{1,0:T(8,128)(2,1)}, u32[]{:S(2)}) copy-start(bf16[1024,1024]{1,0:T(8,128)(2,1)} %constant.5.clone.odd_hbm.odd_table) | copy-start | bytes 6291460
  4.7 54.8 %copy-start.1 = (bf16[1024,512]{1,0:T(8,128)(2,1)S(1)}, bf16[1024,512]{1,0:T(8,128)(2,1)}, u32[]{:S(2)}) copy-start(bf16[1024,512]{1,0:T(8,128)(2,1)} %constant.4.clone.even_hbm.even_table) | copy-start | bytes 3145732
  4.8 54.8 %copy-start.2 = (s32[2,2]{1,0:T(2,128)S(1)}, s32[2,2]{1,0:T(2,128)}, u32[]{:S(2)}) copy-start(s32[2,2]{1,0:T(2,128)} %rate_smem.1) | copy-start | bytes 52
  4.8 54.8 %copy-start.3 = (s32[4]{0:T(128)S(1)}, s32[4]{0:T(128)}, u32[]{:S(2)}) copy-start(s32[4]{0:T(128)} %time_smem.1) | copy-start | bytes 52

commit v21 on v19

--- a/solution.py
+++ b/solution.py
@@ -149,7 +149,7 @@
             pltpu.SemaphoreType.DMA((loc_epochs, PIECES)),
             pltpu.SemaphoreType.DMA((2, PIECES)),
         ],
-        compiler_params=pltpu.CompilerParams(vmem_limit_bytes=40 * MIB),
+        compiler_params=pltpu.CompilerParams(vmem_limit_bytes=32 * MIB),
         cost_estimate=cost(
             2 * rows * (even_table.size + odd_table.size), 3 * half * half + 4 * rows * length
         ),
@@ -213,31 +213,31 @@
     )
 
 
-def column_kernel(
+def prepare_kernel(
     epoch_count,
     rate_smem,
     time_smem,
-    received,
+    even_hbm,
+    odd_hbm,
+    after,
     even_table,
     odd_table,
-    out_ref,
     rows_cos,
     rows_sin,
     spread,
-    even_fold,
-    odd_fold,
-    products,
-    sums,
+    sems,
 ):
-    devices, loc_epochs, width, loc_rows = received.shape
-    row_count = devices // epoch_count
-    epochs = epoch_count * loc_epochs
-    rates = rate_smem.shape[0]
+    del after
+    even_copy = pltpu.make_async_copy(even_hbm, even_table, sems.at[0])
+    odd_copy = pltpu.make_async_copy(odd_hbm, odd_table, sems.at[1])
+    even_copy.start()
+    odd_copy.start()
+    rates, epochs = rate_smem.shape[0], time_smem.shape[0]
     pairs = rates * epochs
+    width = spread.shape[2]
     cols = width // 2
-    half, quarter = even_table.shape
+    half = even_table.shape[0]
     length = 2 * half
-    steps = length // BLOCK
     device = lax.axis_index("row") * epoch_count + lax.axis_index("epoch")
     period = SUBPIX * length
     shift_y, shift_x = [
@@ -248,6 +248,66 @@
         ]
         for axis in range(2)
     ]
+    rows_cos[...], rows_sin[...] = row_factors(shift_y, half)
+    factors = column_factors(shift_y, shift_x, 1.0 / math.sqrt(epochs), device, cols, half).T
+    for kind in range(4):
+        for pair in range(pairs):
+            at = kind * pairs + pair
+            spread[kind, pair] = jnp.broadcast_to(factors[:width, at : at + 1], (width, GROUP))
+    even_copy.wait()
+    odd_copy.wait()
+
+
+def prepare(rate_vectors, epoch_times, even_table, odd_table, after, epoch_count, width):
+    pairs = rate_vectors.shape[0] * epoch_times.shape[0]
+    scalars = pl.BlockSpec(memory_space=pltpu.SMEM)
+    half = even_table.shape[0]
+    return pl.pallas_call(
+        functools.partial(prepare_kernel, epoch_count),
+        in_specs=[scalars, scalars, HBM, HBM, pl.BlockSpec(memory_space=pl.ANY)],
+        out_specs=[IN_VMEM] * 5,
+        out_shape=[
+            pltpu.VMEM(even_table.shape, jnp.bfloat16),
+            pltpu.VMEM(odd_table.shape, jnp.bfloat16),
+            pltpu.VMEM((pairs, half), jnp.float32),
+            pltpu.VMEM((pairs, half), jnp.float32),
+            pltpu.VMEM((4, pairs, width, GROUP), jnp.float32),
+        ],
+        scratch_shapes=[pltpu.SemaphoreType.DMA((2,))],
+        compiler_params=pltpu.CompilerParams(vmem_limit_bytes=24 * MIB),
+        cost_estimate=cost(10 * MIB, 4 * MIB),
+        name="prepare",
+    )(
+        rate_vectors,
+        epoch_times,
+        in_space(even_table, pltpu.HBM),
+        in_space(odd_table, pltpu.HBM),
+        after,
+    )
+
+
+def column_kernel(
+    epoch_count,
+    rates,
+    received,
+    even_table,
+    odd_table,
+    rows_cos,
+    rows_sin,
+    spread,
+    out_ref,
+    even_fold,
+    odd_fold,
+    products,
+    sums,
+):
+    devices, loc_epochs, width, loc_rows = received.shape
+    row_count = devices // epoch_count
+    epochs = epoch_count * loc_epochs
+    cols = width // 2
+    half, quarter = even_table.shape
+    length = 2 * half
+    steps = length // BLOCK
     per_tile = max(1, GROUP // loc_rows)
     tile_rows = per_tile * loc_rows
     for tile in range(row_count // 4 // per_tile):
@@ -279,13 +339,6 @@
         )
 
     multiply(0)
-    rows_cos[...], rows_sin[...] = row_factors(shift_y, half)
-    factors = column_factors(shift_y, shift_x, 1.0 / math.sqrt(epochs), device, cols, half).T
-    for kind in range(4):
-        for pair in range(pairs):
-            at = kind * pairs + pair
-            spread[kind, pair] = jnp.broadcast_to(factors[:width, at : at + 1], (width, GROUP))
-
     chunk = min(ROW_CHUNK, cols)
 
     def add_ramped(step, group):
@@ -374,38 +427,30 @@
         send(position + 2, even - odd)
 
 
-def column_stage(rate_vectors, epoch_times, spectra, even_table, odd_table, epoch_count):
+def column_stage(spectra, prepared, epoch_count, rates):
     devices, loc_epochs, width, loc_rows = spectra.shape
-    half, quarter = even_table.shape
+    half, quarter = prepared[0].shape
     length = 2 * half
-    epochs, rates = epoch_times.shape[0], rate_vectors.shape[0]
+    epochs = epoch_count * loc_epochs
     out = (devices, rates // epoch_count, width, loc_rows)
-    scalars = pl.BlockSpec(memory_space=pltpu.SMEM)
     return pl.pallas_call(
-        functools.partial(column_kernel, epoch_count),
-        in_specs=[scalars, scalars, IN_VMEM, IN_VMEM, IN_VMEM],
+        functools.partial(column_kernel, epoch_count, rates),
+        in_specs=[IN_VMEM] * 6,
         out_specs=IN_VMEM,
         out_shape=pltpu.VMEM(out, jnp.bfloat16),
         scratch_shapes=[
-            pltpu.VMEM((rates * epochs, half), jnp.float32),
-            pltpu.VMEM((rates * epochs, half), jnp.float32),
-            pltpu.VMEM((4, rates * epochs, width, GROUP), jnp.float32),
             pltpu.VMEM((2, epochs * width, quarter), jnp.bfloat16),
             pltpu.VMEM((epochs * width, half), jnp.bfloat16),
             pltpu.VMEM((2, epochs * width, BLOCK), jnp.float32),
             pltpu.VMEM((rates * width, length), jnp.bfloat16),
         ],
-        compiler_params=pltpu.CompilerParams(vmem_limit_bytes=40 * MIB),
+        compiler_params=pltpu.CompilerParams(vmem_limit_bytes=32 * MIB),
         cost_estimate=cost(
-            2 * (even_table.size + odd_table.size) * (epochs + rates) * width,
+            3 * half * half * (epochs + rates) * width,
             3 * half * half + 4 * spectra.size,
         ),
         name="column_stage",
-    )(
-        rate_vectors,
-        epoch_times,
-        *(in_space(part, pltpu.VMEM) for part in (spectra, even_table, odd_table)),
-    )
+    )(*(in_space(part, pltpu.VMEM) for part in (spectra, *prepared)))
 
 
 def image_kernel(back, even_table, odd_table, out_hbm, left, staged, out_sems):
@@ -453,7 +498,7 @@
             pltpu.VMEM((rows, length), jnp.float32),
             pltpu.SemaphoreType.DMA((length // IMAGE_BLOCK,)),
         ],
-        compiler_params=pltpu.CompilerParams(vmem_limit_bytes=40 * MIB),
+        compiler_params=pltpu.CompilerParams(vmem_limit_bytes=32 * MIB),
         cost_estimate=cost(
             2 * rows * (even_table.size + odd_table.size), 3 * half * half + 6 * rows * length
         ),
@@ -470,13 +515,19 @@
     def exchange(values):
         return lax.all_to_all(values, ("row", "epoch"), 0, 0, tiled=True)
 
-    spectra = exchange(row_transform(images, even_table, odd_table, devices))
-    back = exchange(
-        column_stage(rate_vectors, epoch_times, spectra, even_table, odd_table, epoch_count)
+    row_spectra = row_transform(images, even_table, odd_table, devices)
+    prepared = prepare(
+        rate_vectors,
+        epoch_times,
+        even_table,
+        odd_table,
+        row_spectra,
+        epoch_count,
+        length // devices,
     )
-    return image_rows(
-        back.reshape(devices, length // devices, loc_rows), even_table, odd_table
-    )
+    spectra = exchange(row_spectra)
+    back = exchange(column_stage(spectra, prepared, epoch_count, rate_vectors.shape[0]))
+    return image_rows(back.reshape(devices, length // devices, loc_rows), *prepared[:2])
 
 
 def solution(mesh):

time: 96.8 us -> 100 us (1.033)
  blocking collectives: 84.5 us -> 35.9 us
  waiting for transfers between devices: 0 us -> 37.3 us
  starting transfers between devices: 0 us -> 7.42 us
  Pallas kernels: 11.7 us -> 15.9 us
  local copies, waits for them, and re-layouts: 0.03 us -> 2.91 us
    all_to_all x2 -> x1, blocking collectives: 84.5 us -> 35.9 us  [exchange(): return lax.all_to_all(values, ('row', 'epoch'), 0, 0, tiled=True)]
    all_to_all x0 -> x1, waiting for transfers between devices: none -> 37.3 us  [exchange(): return lax.all_to_all(values, ('row', 'epoch'), 0, 0, tiled=True)]
    all_to_all x0 -> x1, starting transfers between devices: none -> 7.42 us  [exchange(): return lax.all_to_all(values, ('row', 'epoch'), 0, 0, tiled=True)]
    unnamed x8, local copies, waits for them, and re-layouts: 0.03 us -> 2.91 us
    pallas_call x1 -> x2, Pallas kernels: 4.91 us -> 7.76 us  [the longest x1 5.21 us: column_stage(): pl.pallas_call(functools.partial(column_kernel, epoch_count, rates), in_s...]
    pallas_call x1, Pallas kernels: 4.72 us -> 6.04 us  [row_transform(): pl.pallas_call(row_kernel, in_specs=[HBM, HBM, HBM], out_specs=IN_VMEM, o...]
  transfers between devices with their start and end apart: 0 -> 1, of which waited for: 0 -> 1; matrix products, arithmetic and copies ran while one was open for 0% -> 0% of each run, Pallas kernels for 0% -> 3%
where the time goes in v21:
time: 100 us; the launch traced here: 99.4 us
  waiting for transfers between devices  37.3 us (37%)
  blocking collectives  35.9 us (36%)
  Pallas kernels  15.9 us (16%)
  starting transfers between devices  7.42 us (7%)
  local copies, waits for them, and re-layouts  2.91 us (3%)
    all_to_all x1, waiting for transfers between devices, exchange(): return lax.all_to_all(values, ('row', 'epoch'), 0, 0, tiled=True)  37.3 us
    all_to_all x1, blocking collectives, exchange(): return lax.all_to_all(values, ('row', 'epoch'), 0, 0, tiled=True)  35.9 us
    all_to_all x1, starting transfers between devices, exchange(): return lax.all_to_all(values, ('row', 'epoch'), 0, 0, tiled=True)  7.42 us
    pallas_call x1, Pallas kernels, row_transform(): pl.pallas_call(row_kernel, in_specs=[HBM, HBM, HBM], out_specs=IN_VMEM, o...  6.04 us
    pallas_call x1, Pallas kernels, column_stage(): pl.pallas_call(functools.partial(column_kernel, epoch_count, rates), in_s...  5.21 us
    unnamed x8, local copies, waits for them, and re-layouts  2.91 us
    pallas_call x1, Pallas kernels, prepare(): pl.pallas_call(functools.partial(prepare_kernel, epoch_count), in_specs=[...  2.55 us
    pallas_call x1, Pallas kernels, image_rows(): pl.pallas_call(image_kernel, in_specs=[IN_VMEM, IN_VMEM, IN_VMEM], out_sp...  2.09 us
  transfers between devices with their start and end apart: 1, of which 1 were waited for; matrix products, arithmetic and copies ran while one was open for 0% of the time, Pallas kernels for 3%

profile of v21, /device:TPU:0, one launch (start us, length us, event | category | flops | bytes accessed | tf_op | source)
XLA Modules:
  0.0 99.4 jit_solution(453871113830646146)
XLA Ops:
  0.0 6.0 %row_transform.1.after = bf16[16,2,128,256]{3,2,1,0:T(8,128)(2,1)} custom-call(bf16[2,256,2048]{2,1,0:T(8,128)(2,1)} %images_hbm.1, bf16[1024,512]{1,0:T(8,128)(2,1)} %constant.4.clone.even_hbm, bf16[1024,1024]{1,0:T(8,128)(2,1)} %constant.5.clone.odd_hbm), custom_call_target="tpu_custom_call" | custom-call | flops 1610612736 | bytes 7340032 | tf_op jit(solution)/shard_map/row_transform/pallas_call | solution.py:139
  6.0 0.0 copy-start
  6.1 0.0 copy-start.1
  6.1 7.4 %all-to-all-start = ((bf16[16,2,128,256]{3,2,1,0:T(8,128)(2,1)}), bf16[16,2,128,256]{3,2,1,0:T(8,128)(2,1)}, u32[]{:S(2)}, u32[]{:S(2)}) async-start(bf16[16,2,128,256]{3,2,1,0:T(8,128)(2,1)} %row_transform.1.after), calls=%async_computation | async-start | bytes 4194304 | tf_op jit(solution)/shard_map/all_to_all | solution.py:516
  13.5 0.0 copy-done
  13.5 0.0 copy-done.1
  13.5 2.6 %prepare.1 = (bf16[1024,512]{1,0:T(8,128)(2,1)S(1)}, bf16[1024,1024]{1,0:T(8,128)(2,1)S(1)}, f32[8,1024]{1,0:T(8,128)S(1)}, f32[8,1024]{1,0:T(8,128)S(1)}, f32[4,8,128,128]{3,2,1,0:T(8,128)S(1)}) custom-call(s32[2,2]{1,0:T(2,128)S(1)} %copy-done, s32[4]{0:T(128)S(1)} %copy-done.1, bf16[1024,512]{1,0:T(8,128)(2,1)} %constant.4.clone.even_hbm, ...), custom_call_target="tpu_custom_call" | custom-call | flops 10485760 | bytes 4194304 | tf_op jit(solution)/shard_map/prepare/pallas_call | solution.py:265
  16.1 0.0 copy-start.2
  16.1 1.3 %copy-done.2 = f32[4,8,128,128]{3,2,1,0:T(8,128)} copy-done((f32[4,8,128,128]{3,2,1,0:T(8,128)}, f32[4,8,128,128]{3,2,1,0:T(8,128)S(1)}, u32[]{:S(2)}) %copy-start.2) | copy-done | bytes 2097176
  17.4 37.3 %all-to-all-done.received = bf16[16,2,128,256]{3,2,1,0:T(8,128)(2,1)} async-done(((bf16[16,2,128,256]{3,2,1,0:T(8,128)(2,1)}), bf16[16,2,128,256]{3,2,1,0:T(8,128)(2,1)}, u32[]{:S(2)}, u32[]{:S(2)}) %all-to-all-start) | async-done | bytes 2097184 | tf_op jit(solution)/shard_map/all_to_all | solution.py:516
  54.7 0.0 copy-start.3
  54.7 1.6 %copy-done.3 = f32[4,8,128,128]{3,2,1,0:T(8,128)S(1)} copy-done((f32[4,8,128,128]{3,2,1,0:T(8,128)S(1)}, f32[4,8,128,128]{3,2,1,0:T(8,128)}, u32[]{:S(2)}) %copy-start.3) | copy-done | bytes 2097176
  56.2 5.2 %column_stage.1 = bf16[16,1,128,256]{3,2,1,0:T(8,128)(2,1)S(1)} custom-call(bf16[16,2,128,256]{3,2,1,0:T(8,128)(2,1)} %all-to-all-done.received, bf16[1024,512]{1,0:T(8,128)(2,1)S(1)} %get-tuple-element.10.even_table, bf16[1024,1024]{1,0:T(8,128)(2,1)S(1)} %get-tuple-element.11.odd_table, f32[8,1024]{1,0:T(8,128)S(1)} %get-tuple-element.12.rows_cos, ...), custom_call_target="tpu_custom_call" | custom-call | flops 2415919104 | bytes 7340032 | tf_op jit(solution)/shard_map/column_stage/pallas_call | solution.py:436
  61.5 35.9 %all_to_all.10 = bf16[16,1,128,256]{3,2,1,0:T(8,128)(2,1)S(1)} all-to-all(bf16[16,1,128,256]{3,2,1,0:T(8,128)(2,1)S(1)} %column_stage.1), channel_id=1, replica_groups=mesh['group'=2,'row'=8,'epoch'=2] {'row','epoch'}, dimensions={0} | all-to-all | bytes 2097152 | tf_op jit(solution)/shard_map/all_to_all | solution.py:516
  97.3 2.1 %image_rows.1 = f32[1,256,2048]{2,1,0:T(8,128)} custom-call(bf16[16,128,256]{2,1,0:T(8,128)(2,1)S(1)} %bitcast.1, bf16[1024,512]{1,0:T(8,128)(2,1)S(1)} %get-tuple-element.10.even_table, bf16[1024,1024]{1,0:T(8,128)(2,1)S(1)} %get-tuple-element.11.odd_table), custom_call_target="tpu_custom_call" | custom-call | flops 805306368 | bytes 6291456 | tf_op jit(solution)/shard_map/image_rows/pallas_call | solution.py:491
Async XLA Ops:
  6.0 7.4 %copy-start = (s32[2,2]{1,0:T(2,128)S(1)}, s32[2,2]{1,0:T(2,128)}, u32[]{:S(2)}) copy-start(s32[2,2]{1,0:T(2,128)} %rate_smem.1) | copy-start | bytes 52
  6.1 7.4 %copy-start.1 = (s32[4]{0:T(128)S(1)}, s32[4]{0:T(128)}, u32[]{:S(2)}) copy-start(s32[4]{0:T(128)} %time_smem.1) | copy-start | bytes 52
  6.1 48.6 %all-to-all-start = ((bf16[16,2,128,256]{3,2,1,0:T(8,128)(2,1)}), bf16[16,2,128,256]{3,2,1,0:T(8,128)(2,1)}, u32[]{:S(2)}, u32[]{:S(2)}) async-start(bf16[16,2,128,256]{3,2,1,0:T(8,128)(2,1)} %row_transform.1.after), calls=%async_computation | async-start | bytes 4194304 | tf_op jit(solution)/shard_map/all_to_all | solution.py:516
  16.1 1.3 %copy-start.2 = (f32[4,8,128,128]{3,2,1,0:T(8,128)}, f32[4,8,128,128]{3,2,1,0:T(8,128)S(1)}, u32[]{:S(2)}) copy-start(f32[4,8,128,128]{3,2,1,0:T(8,128)S(1)} %get-tuple-element.14.spread) | copy-start | bytes 6291460
  54.7 1.6 %copy-start.3 = (f32[4,8,128,128]{3,2,1,0:T(8,128)S(1)}, f32[4,8,128,128]{3,2,1,0:T(8,128)}, u32[]{:S(2)}) copy-start(f32[4,8,128,128]{3,2,1,0:T(8,128)} %copy-done.2) | copy-start | bytes 6291460

commit v22 on v19

--- a/solution.py
+++ b/solution.py
@@ -98,10 +98,13 @@
     odd_copies = copies(odd_hbm.at[:, :quarter], odd_table, table_sems.at[1], 2)
     halfway = PIECES // 2
     table_copies = [even_copies[:halfway], even_copies[halfway:], odd_copies[:1], odd_copies[1:]]
-    for copy in sum(image_copies, []) + even_copies + odd_copies:
+    for copy in sum(image_copies, []) + even_copies:
         copy.start()
     for loc in range(loc_epochs):
         wait_copies(image_copies[loc])
+        if loc == loc_epochs - 1:
+            for copy in odd_copies:
+                copy.start()
         at = slice(loc * loc_rows, (loc + 1) * loc_rows)
         folds = fold([images[loc, :, part * quarter : (part + 1) * quarter] for part in range(4)])
         for part in range(4):
@@ -292,51 +295,53 @@
         tile = (step * BLOCK // 2 // GROUP + group) * GROUP
         at_even = group * 2 * GROUP
         at_odd = at_even + GROUP
-        for rate in range(rates):
-            for start in range(0, cols, chunk):
-                real = slice(start, start + chunk)
-                imag = slice(cols + start, cols + start + chunk)
-                totals = [[0.0, 0.0], [0.0, 0.0]]
-                leads = [0.0, 0.0]
-                for epoch in range(epochs):
+        for start in range(0, cols, chunk):
+            real = slice(start, start + chunk)
+            imag = slice(cols + start, cols + start + chunk)
+            totals = [[[0.0, 0.0], [0.0, 0.0]] for _ in range(rates)]
+            leads = [[0.0, 0.0] for _ in range(rates)]
+            for epoch in range(epochs):
+                loaded = []
+                for part in (real, imag):
+                    at = slice(epoch * width + part.start, epoch * width + part.stop)
+                    loaded.append(
+                        [
+                            products[step % 2, at, first : first + GROUP]
+                            for first in (at_even, at_odd)
+                        ]
+                    )
+                for rate in range(rates):
                     pair = rate * epochs + epoch
                     cos_row = rows_cos[pair : pair + 1, tile : tile + GROUP]
                     sin_row = rows_sin[pair : pair + 1, tile : tile + GROUP]
-                    turned, evens = [], []
-                    for part in (real, imag):
-                        at = slice(epoch * width + part.start, epoch * width + part.stop)
-                        even = products[step % 2, at, at_even : at_even + GROUP]
-                        odd = products[step % 2, at, at_odd : at_odd + GROUP]
-                        turned.append(
-                            (cos_row * even + sin_row * odd, cos_row * odd - sin_row * even)
-                        )
-                        evens.append(even)
+                    turned = [
+                        (cos_row * even + sin_row * odd, cos_row * odd - sin_row * even)
+                        for even, odd in loaded
+                    ]
                     straight = [spread[0, pair, part] for part in (real, imag)]
                     crossed = [spread[1, pair, part] for part in (real, imag)]
                     for part in range(2):
                         for which in range(2):
-                            totals[part][which] += (
+                            totals[rate][part][which] += (
                                 straight[part] * turned[part][which]
                                 + crossed[1 - part] * turned[1 - part][which]
                             )
                         if step == 0 and group == 0:
                             own, other = (real, imag) if part == 0 else (imag, real)
-                            leads[part] += (
-                                spread[2, pair, own] * evens[part]
-                                + spread[3, pair, other] * evens[1 - part]
+                            leads[rate][part] += (
+                                spread[2, pair, own] * loaded[part][0]
+                                + spread[3, pair, other] * loaded[1 - part][0]
                             )
+            for rate in range(rates):
                 for part, rows in enumerate((real, imag)):
-                    even_sum, odd_sum = totals[part]
+                    even_sum, odd_sum = totals[rate][part]
                     if step == 0 and group == 0:
                         first = lax.broadcasted_iota(jnp.int32, even_sum.shape, 1) == 0
-                        even_sum = jnp.where(first, leads[part], even_sum)
+                        even_sum = jnp.where(first, leads[rate][part], even_sum)
                     at = slice(rate * width + rows.start, rate * width + rows.stop)
-                    sums[at, step * BLOCK + at_even : step * BLOCK + at_even + GROUP] = even_sum.astype(
-                        jnp.bfloat16
-                    )
-                    sums[at, step * BLOCK + at_odd : step * BLOCK + at_odd + GROUP] = odd_sum.astype(
-                        jnp.bfloat16
-                    )
+                    for values, lane in ((even_sum, at_even), (odd_sum, at_odd)):
+                        lane = step * BLOCK + lane
+                        sums[at, lane : lane + GROUP] = values.astype(jnp.bfloat16)
 
     for step in range(steps):
         if step + 1 < steps:

time: 96.8 us -> 96.6 us (level)
  no operation moved by 1% of the time
where the time goes in v22:
time: 96.6 us; the launch traced here: 96.1 us
  blocking collectives  84.5 us (87%)
  Pallas kernels  11.5 us (12%)
    all_to_all x2, blocking collectives, exchange(): return lax.all_to_all(values, ('row', 'epoch'), 0, 0, tiled=True)  84.5 us
    pallas_call x1, Pallas kernels, column_stage(): pl.pallas_call(functools.partial(column_kernel, epoch_count), in_specs=[s...  4.92 us
    pallas_call x1, Pallas kernels, row_transform(): pl.pallas_call(row_kernel, in_specs=[HBM, HBM, HBM], out_specs=IN_VMEM, o...  4.48 us
    pallas_call x1, Pallas kernels, image_rows(): pl.pallas_call(image_kernel, in_specs=[IN_VMEM, IN_VMEM, IN_VMEM], out_sp...  2.1 us

profile of v22, /device:TPU:0, one launch (start us, length us, event | category | flops | bytes accessed | tf_op | source)
XLA Modules:
  0.0 96.1 jit_solution(10219841937481820742)
XLA Ops:
  0.0 4.5 %row_transform.1 = bf16[16,2,128,256]{3,2,1,0:T(8,128)(2,1)S(1)} custom-call(bf16[2,256,2048]{2,1,0:T(8,128)(2,1)} %images_hbm.1, bf16[1024,512]{1,0:T(8,128)(2,1)} %constant.4.clone.even_hbm.even_table, bf16[1024,1024]{1,0:T(8,128)(2,1)} %constant.5.clone.odd_hbm.odd_table), custom_call_target="tpu_custom_call" | custom-call | flops 1610612736 | bytes 7340032 | tf_op jit(solution)/shard_map/row_transform/pallas_call | solution.py:142
  4.5 0.0 copy-start
  4.5 0.0 copy-start.1
  4.5 0.0 copy-start.2
  4.5 0.0 copy-start.3
  4.5 54.7 %all_to_all.10.received = bf16[16,2,128,256]{3,2,1,0:T(8,128)(2,1)S(1)} all-to-all(bf16[16,2,128,256]{3,2,1,0:T(8,128)(2,1)S(1)} %row_transform.1), channel_id=1, replica_groups=mesh['group'=2,'row'=8,'epoch'=2] {'row','epoch'}, dimensions={0} | all-to-all | bytes 4194304 | tf_op jit(solution)/shard_map/all_to_all | solution.py:476
  59.3 0.0 copy-done
  59.3 0.0 copy-done.1
  59.3 0.0 copy-done.2
  59.3 0.0 copy-done.3
  59.3 4.9 %column_stage.1 = bf16[16,1,128,256]{3,2,1,0:T(8,128)(2,1)S(1)} custom-call(s32[2,2]{1,0:T(2,128)S(1)} %copy-done.2, s32[4]{0:T(128)S(1)} %copy-done.3, bf16[16,2,128,256]{3,2,1,0:T(8,128)(2,1)S(1)} %all_to_all.10.received, bf16[1024,512]{1,0:T(8,128)(2,1)S(1)} %copy-done.1, bf16[1024,1024]{1,0:T(8,128)(2,1)S(1)} %copy-done), custom_call_target="tpu_custom_call" | custom-call | flops 2415919104 | bytes 7340032 | tf_op jit(solution)/shard_map/column_stage/pallas_call | solution.py:389
  64.2 29.7 %all_to_all.11 = bf16[16,1,128,256]{3,2,1,0:T(8,128)(2,1)S(1)} all-to-all(bf16[16,1,128,256]{3,2,1,0:T(8,128)(2,1)S(1)} %column_stage.1), channel_id=1, replica_groups=mesh['group'=2,'row'=8,'epoch'=2] {'row','epoch'}, dimensions={0} | all-to-all | bytes 2097152 | tf_op jit(solution)/shard_map/all_to_all | solution.py:476
  94.0 2.1 %image_rows.1 = f32[1,256,2048]{2,1,0:T(8,128)} custom-call(bf16[16,128,256]{2,1,0:T(8,128)(2,1)S(1)} %bitcast.1, bf16[1024,512]{1,0:T(8,128)(2,1)S(1)} %copy-done.1, bf16[1024,1024]{1,0:T(8,128)(2,1)S(1)} %copy-done), custom_call_target="tpu_custom_call" | custom-call | flops 805306368 | bytes 6291456 | tf_op jit(solution)/shard_map/image_rows/pallas_call | solution.py:451
Async XLA Ops:
  4.5 54.8 %copy-start = (bf16[1024,1024]{1,0:T(8,128)(2,1)S(1)}, bf16[1024,1024]{1,0:T(8,128)(2,1)}, u32[]{:S(2)}) copy-start(bf16[1024,1024]{1,0:T(8,128)(2,1)} %constant.5.clone.odd_hbm.odd_table) | copy-start | bytes 6291460
  4.5 54.8 %copy-start.1 = (bf16[1024,512]{1,0:T(8,128)(2,1)S(1)}, bf16[1024,512]{1,0:T(8,128)(2,1)}, u32[]{:S(2)}) copy-start(bf16[1024,512]{1,0:T(8,128)(2,1)} %constant.4.clone.even_hbm.even_table) | copy-start | bytes 3145732
  4.5 54.8 %copy-start.2 = (s32[2,2]{1,0:T(2,128)S(1)}, s32[2,2]{1,0:T(2,128)}, u32[]{:S(2)}) copy-start(s32[2,2]{1,0:T(2,128)} %rate_smem.1) | copy-start | bytes 52
  4.5 54.8 %copy-start.3 = (s32[4]{0:T(128)S(1)}, s32[4]{0:T(128)}, u32[]{:S(2)}) copy-start(s32[4]{0:T(128)} %time_smem.1) | copy-start | bytes 52

commit v23 on v22

--- a/solution.py
+++ b/solution.py
@@ -14,7 +14,7 @@
 GROUP = 128
 BLOCK = 512
 IMAGE_BLOCK = 512
-ROW_CHUNK = 16
+ROW_CHUNK = 32
 PIECES = 4
 MIB = 1024 * 1024
 CONTRACT_LAST = (((1,), (1,)), ((), ()))
@@ -98,12 +98,12 @@
     odd_copies = copies(odd_hbm.at[:, :quarter], odd_table, table_sems.at[1], 2)
     halfway = PIECES // 2
     table_copies = [even_copies[:halfway], even_copies[halfway:], odd_copies[:1], odd_copies[1:]]
-    for copy in sum(image_copies, []) + even_copies:
+    for copy in sum(image_copies, []) + table_copies[0]:
         copy.start()
     for loc in range(loc_epochs):
         wait_copies(image_copies[loc])
-        if loc == loc_epochs - 1:
-            for copy in odd_copies:
+        if loc == 0:
+            for copy in sum(table_copies[1:], []):
                 copy.start()
         at = slice(loc * loc_rows, (loc + 1) * loc_rows)
         folds = fold([images[loc, :, part * quarter : (part + 1) * quarter] for part in range(4)])

time: 96.6 us -> 96.8 us (level)
  no operation moved by 1% of the time
where the time goes in v23:
time: 96.8 us; the launch traced here: 96.3 us
  blocking collectives  84.5 us (87%)
  Pallas kernels  11.7 us (12%)
    all_to_all x2, blocking collectives, exchange(): return lax.all_to_all(values, ('row', 'epoch'), 0, 0, tiled=True)  84.5 us
    pallas_call x1, Pallas kernels, column_stage(): pl.pallas_call(functools.partial(column_kernel, epoch_count), in_specs=[s...  5.14 us
    pallas_call x1, Pallas kernels, row_transform(): pl.pallas_call(row_kernel, in_specs=[HBM, HBM, HBM], out_specs=IN_VMEM, o...  4.44 us
    pallas_call x1, Pallas kernels, image_rows(): pl.pallas_call(image_kernel, in_specs=[IN_VMEM, IN_VMEM, IN_VMEM], out_sp...  2.1 us

profile of v23, /device:TPU:0, one launch (start us, length us, event | category | flops | bytes accessed | tf_op | source)
XLA Modules:
  0.0 96.3 jit_solution(1781512064419589913)
XLA Ops:
  0.0 4.4 %row_transform.1 = bf16[16,2,128,256]{3,2,1,0:T(8,128)(2,1)S(1)} custom-call(bf16[2,256,2048]{2,1,0:T(8,128)(2,1)} %images_hbm.1, bf16[1024,512]{1,0:T(8,128)(2,1)} %constant.4.clone.even_hbm.even_table, bf16[1024,1024]{1,0:T(8,128)(2,1)} %constant.5.clone.odd_hbm.odd_table), custom_call_target="tpu_custom_call" | custom-call | flops 1610612736 | bytes 7340032 | tf_op jit(solution)/shard_map/row_transform/pallas_call | solution.py:142
  4.4 0.0 copy-start
  4.5 0.0 copy-start.1
  4.5 0.0 copy-start.2
  4.5 0.0 copy-start.3
  4.5 54.7 %all_to_all.10.received = bf16[16,2,128,256]{3,2,1,0:T(8,128)(2,1)S(1)} all-to-all(bf16[16,2,128,256]{3,2,1,0:T(8,128)(2,1)S(1)} %row_transform.1), channel_id=1, replica_groups=mesh['group'=2,'row'=8,'epoch'=2] {'row','epoch'}, dimensions={0} | all-to-all | bytes 4194304 | tf_op jit(solution)/shard_map/all_to_all | solution.py:476
  59.2 0.0 copy-done
  59.2 0.0 copy-done.1
  59.2 0.0 copy-done.2
  59.2 0.0 copy-done.3
  59.3 5.1 %column_stage.1 = bf16[16,1,128,256]{3,2,1,0:T(8,128)(2,1)S(1)} custom-call(s32[2,2]{1,0:T(2,128)S(1)} %copy-done.2, s32[4]{0:T(128)S(1)} %copy-done.3, bf16[16,2,128,256]{3,2,1,0:T(8,128)(2,1)S(1)} %all_to_all.10.received, bf16[1024,512]{1,0:T(8,128)(2,1)S(1)} %copy-done.1, bf16[1024,1024]{1,0:T(8,128)(2,1)S(1)} %copy-done), custom_call_target="tpu_custom_call" | custom-call | flops 2415919104 | bytes 7340032 | tf_op jit(solution)/shard_map/column_stage/pallas_call | solution.py:389
  64.4 29.8 %all_to_all.11 = bf16[16,1,128,256]{3,2,1,0:T(8,128)(2,1)S(1)} all-to-all(bf16[16,1,128,256]{3,2,1,0:T(8,128)(2,1)S(1)} %column_stage.1), channel_id=1, replica_groups=mesh['group'=2,'row'=8,'epoch'=2] {'row','epoch'}, dimensions={0} | all-to-all | bytes 2097152 | tf_op jit(solution)/shard_map/all_to_all | solution.py:476
  94.2 2.1 %image_rows.1 = f32[1,256,2048]{2,1,0:T(8,128)} custom-call(bf16[16,128,256]{2,1,0:T(8,128)(2,1)S(1)} %bitcast.1, bf16[1024,512]{1,0:T(8,128)(2,1)S(1)} %copy-done.1, bf16[1024,1024]{1,0:T(8,128)(2,1)S(1)} %copy-done), custom_call_target="tpu_custom_call" | custom-call | flops 805306368 | bytes 6291456 | tf_op jit(solution)/shard_map/image_rows/pallas_call | solution.py:451
Async XLA Ops:
  4.4 54.8 %copy-start = (bf16[1024,1024]{1,0:T(8,128)(2,1)S(1)}, bf16[1024,1024]{1,0:T(8,128)(2,1)}, u32[]{:S(2)}) copy-start(bf16[1024,1024]{1,0:T(8,128)(2,1)} %constant.5.clone.odd_hbm.odd_table) | copy-start | bytes 6291460
  4.5 54.8 %copy-start.1 = (bf16[1024,512]{1,0:T(8,128)(2,1)S(1)}, bf16[1024,512]{1,0:T(8,128)(2,1)}, u32[]{:S(2)}) copy-start(bf16[1024,512]{1,0:T(8,128)(2,1)} %constant.4.clone.even_hbm.even_table) | copy-start | bytes 3145732
  4.5 54.8 %copy-start.2 = (s32[2,2]{1,0:T(2,128)S(1)}, s32[2,2]{1,0:T(2,128)}, u32[]{:S(2)}) copy-start(s32[2,2]{1,0:T(2,128)} %rate_smem.1) | copy-start | bytes 52
  4.5 54.8 %copy-start.3 = (s32[4]{0:T(128)S(1)}, s32[4]{0:T(128)}, u32[]{:S(2)}) copy-start(s32[4]{0:T(128)} %time_smem.1) | copy-start | bytes 52

commit v24 on v23

--- a/solution.py
+++ b/solution.py
@@ -14,7 +14,7 @@
 GROUP = 128
 BLOCK = 512
 IMAGE_BLOCK = 512
-ROW_CHUNK = 32
+ROW_CHUNK = 16
 PIECES = 4
 MIB = 1024 * 1024
 CONTRACT_LAST = (((1,), (1,)), ((), ()))
@@ -473,7 +473,9 @@
     even_table, odd_table = [jnp.asarray(part) for part in packed_tables(length)]
 
     def exchange(values):
-        return lax.all_to_all(values, ("row", "epoch"), 0, 0, tiled=True)
+        blocks = values.reshape(devices, -1, loc_rows)
+        received = lax.all_to_all(blocks, ("row", "epoch"), 0, 0, tiled=True)
+        return received.reshape(values.shape)
 
     spectra = exchange(row_transform(images, even_table, odd_table, devices))
     back = exchange(

time: 96.8 us -> 96.6 us (level)
  no operation moved by 1% of the time
where the time goes in v24:
time: 96.6 us; the launch traced here: 96 us
  blocking collectives  84.5 us (87%)
  Pallas kernels  11.5 us (12%)
    all_to_all x2, blocking collectives, exchange(): received = lax.all_to_all(blocks, ('row', 'epoch'), 0, 0, tiled=True)  84.5 us
    pallas_call x1, Pallas kernels, column_stage(): pl.pallas_call(functools.partial(column_kernel, epoch_count), in_specs=[s...  4.91 us
    pallas_call x1, Pallas kernels, row_transform(): pl.pallas_call(row_kernel, in_specs=[HBM, HBM, HBM], out_specs=IN_VMEM, o...  4.44 us
    pallas_call x1, Pallas kernels, image_rows(): pl.pallas_call(image_kernel, in_specs=[IN_VMEM, IN_VMEM, IN_VMEM], out_sp...  2.1 us

profile of v24, /device:TPU:0, one launch (start us, length us, event | category | flops | bytes accessed | tf_op | source)
XLA Modules:
  0.0 96.0 jit_solution(18219638977143272633)
XLA Ops:
  0.0 4.4 %row_transform.1 = bf16[16,2,128,256]{3,2,1,0:T(8,128)(2,1)S(1)} custom-call(bf16[2,256,2048]{2,1,0:T(8,128)(2,1)} %images_hbm.1, bf16[1024,512]{1,0:T(8,128)(2,1)} %constant.4.clone.even_hbm.even_table, bf16[1024,1024]{1,0:T(8,128)(2,1)} %constant.5.clone.odd_hbm.odd_table), custom_call_target="tpu_custom_call" | custom-call | flops 1610612736 | bytes 7340032 | tf_op jit(solution)/shard_map/row_transform/pallas_call | solution.py:142
  4.4 0.0 copy-start
  4.5 0.0 copy-start.1
  4.5 0.0 copy-start.2
  4.5 0.0 copy-start.3
  4.5 54.7 %all_to_all.10 = bf16[16,256,256]{2,1,0:T(8,128)(2,1)S(1)} all-to-all(bf16[16,256,256]{2,1,0:T(8,128)(2,1)S(1)} %bitcast.3), channel_id=1, replica_groups=mesh['group'=2,'row'=8,'epoch'=2] {'row','epoch'}, dimensions={0} | all-to-all | bytes 4194304 | tf_op jit(solution)/shard_map/all_to_all | solution.py:477
  59.2 0.0 copy-done
  59.2 0.0 copy-done.1
  59.2 0.0 copy-done.2
  59.2 0.0 copy-done.3
  59.3 4.9 %column_stage.1 = bf16[16,1,128,256]{3,2,1,0:T(8,128)(2,1)S(1)} custom-call(s32[2,2]{1,0:T(2,128)S(1)} %copy-done.2, s32[4]{0:T(128)S(1)} %copy-done.3, bf16[16,2,128,256]{3,2,1,0:T(8,128)(2,1)S(1)} %bitcast.4, bf16[1024,512]{1,0:T(8,128)(2,1)S(1)} %copy-done.1, bf16[1024,1024]{1,0:T(8,128)(2,1)S(1)} %copy-done), custom_call_target="tpu_custom_call" | custom-call | flops 2415919104 | bytes 7340032 | tf_op jit(solution)/shard_map/column_stage/pallas_call | solution.py:389
  64.2 29.8 %all_to_all.11.back = bf16[16,128,256]{2,1,0:T(8,128)(2,1)S(1)} all-to-all(bf16[16,128,256]{2,1,0:T(8,128)(2,1)S(1)} %bitcast.5), channel_id=1, replica_groups=mesh['group'=2,'row'=8,'epoch'=2] {'row','epoch'}, dimensions={0} | all-to-all | bytes 2097152 | tf_op jit(solution)/shard_map/all_to_all | solution.py:477
  93.9 2.1 %image_rows.1 = f32[1,256,2048]{2,1,0:T(8,128)} custom-call(bf16[16,128,256]{2,1,0:T(8,128)(2,1)S(1)} %all_to_all.11.back, bf16[1024,512]{1,0:T(8,128)(2,1)S(1)} %copy-done.1, bf16[1024,1024]{1,0:T(8,128)(2,1)S(1)} %copy-done), custom_call_target="tpu_custom_call" | custom-call | flops 805306368 | bytes 6291456 | tf_op jit(solution)/shard_map/image_rows/pallas_call | solution.py:451
Async XLA Ops:
  4.4 54.8 %copy-start = (bf16[1024,1024]{1,0:T(8,128)(2,1)S(1)}, bf16[1024,1024]{1,0:T(8,128)(2,1)}, u32[]{:S(2)}) copy-start(bf16[1024,1024]{1,0:T(8,128)(2,1)} %constant.5.clone.odd_hbm.odd_table) | copy-start | bytes 6291460
  4.5 54.8 %copy-start.1 = (bf16[1024,512]{1,0:T(8,128)(2,1)S(1)}, bf16[1024,512]{1,0:T(8,128)(2,1)}, u32[]{:S(2)}) copy-start(bf16[1024,512]{1,0:T(8,128)(2,1)} %constant.4.clone.even_hbm.even_table) | copy-start | bytes 3145732
  4.5 54.8 %copy-start.2 = (s32[2,2]{1,0:T(2,128)S(1)}, s32[2,2]{1,0:T(2,128)}, u32[]{:S(2)}) copy-start(s32[2,2]{1,0:T(2,128)} %rate_smem.1) | copy-start | bytes 52
  4.5 54.8 %copy-start.3 = (s32[4]{0:T(128)S(1)}, s32[4]{0:T(128)}, u32[]{:S(2)}) copy-start(s32[4]{0:T(128)} %time_smem.1) | copy-start | bytes 52

commit v25 on v23

--- a/solution.py
+++ b/solution.py
@@ -14,7 +14,7 @@
 GROUP = 128
 BLOCK = 512
 IMAGE_BLOCK = 512
-ROW_CHUNK = 32
+ROW_CHUNK = 16
 PIECES = 4
 MIB = 1024 * 1024
 CONTRACT_LAST = (((1,), (1,)), ((), ()))
@@ -227,6 +227,7 @@
     rows_cos,
     rows_sin,
     spread,
+    columns,
     even_fold,
     odd_fold,
     products,
@@ -284,7 +285,8 @@
     multiply(0)
     rows_cos[...], rows_sin[...] = row_factors(shift_y, half)
     factors = column_factors(shift_y, shift_x, 1.0 / math.sqrt(epochs), device, cols, half).T
-    for kind in range(4):
+    columns[...] = factors
+    for kind in range(2):
         for pair in range(pairs):
             at = kind * pairs + pair
             spread[kind, pair] = jnp.broadcast_to(factors[:width, at : at + 1], (width, GROUP))
@@ -328,9 +330,11 @@
                             )
                         if step == 0 and group == 0:
                             own, other = (real, imag) if part == 0 else (imag, real)
+                            at_own = 2 * pairs + pair
+                            at_other = 3 * pairs + pair
                             leads[rate][part] += (
-                                spread[2, pair, own] * loaded[part][0]
-                                + spread[3, pair, other] * loaded[1 - part][0]
+                                columns[own, at_own : at_own + 1] * loaded[part][0][:, :1]
+                                + columns[other, at_other : at_other + 1] * loaded[1 - part][0][:, :1]
                             )
             for rate in range(rates):
                 for part, rows in enumerate((real, imag)):
@@ -394,7 +398,8 @@
         scratch_shapes=[
             pltpu.VMEM((rates * epochs, half), jnp.float32),
             pltpu.VMEM((rates * epochs, half), jnp.float32),
-            pltpu.VMEM((4, rates * epochs, width, GROUP), jnp.float32),
+            pltpu.VMEM((2, rates * epochs, width, GROUP), jnp.float32),
+            pltpu.VMEM((GROUP, 4 * rates * epochs), jnp.float32),
             pltpu.VMEM((2, epochs * width, quarter), jnp.bfloat16),
             pltpu.VMEM((epochs * width, half), jnp.bfloat16),
             pltpu.VMEM((2, epochs * width, BLOCK), jnp.float32),

time: 96.8 us -> 96.6 us (level)
  no operation moved by 1% of the time
where the time goes in v25:
time: 96.6 us; the launch traced here: 96.1 us
  blocking collectives  84.5 us (87%)
  Pallas kernels  11.5 us (12%)
    all_to_all x2, blocking collectives, exchange(): return lax.all_to_all(values, ('row', 'epoch'), 0, 0, tiled=True)  84.5 us
    pallas_call x1, Pallas kernels, column_stage(): pl.pallas_call(functools.partial(column_kernel, epoch_count), in_specs=[s...  4.94 us
    pallas_call x1, Pallas kernels, row_transform(): pl.pallas_call(row_kernel, in_specs=[HBM, HBM, HBM], out_specs=IN_VMEM, o...  4.44 us
    pallas_call x1, Pallas kernels, image_rows(): pl.pallas_call(image_kernel, in_specs=[IN_VMEM, IN_VMEM, IN_VMEM], out_sp...  2.11 us

profile of v25, /device:TPU:0, one launch (start us, length us, event | category | flops | bytes accessed | tf_op | source)
XLA Modules:
  0.0 96.1 jit_solution(10130268916401751175)
XLA Ops:
  0.0 4.4 %row_transform.1 = bf16[16,2,128,256]{3,2,1,0:T(8,128)(2,1)S(1)} custom-call(bf16[2,256,2048]{2,1,0:T(8,128)(2,1)} %images_hbm.1, bf16[1024,512]{1,0:T(8,128)(2,1)} %constant.4.clone.even_hbm.even_table, bf16[1024,1024]{1,0:T(8,128)(2,1)} %constant.5.clone.odd_hbm.odd_table), custom_call_target="tpu_custom_call" | custom-call | flops 1610612736 | bytes 7340032 | tf_op jit(solution)/shard_map/row_transform/pallas_call | solution.py:142
  4.4 0.0 copy-start
  4.5 0.0 copy-start.1
  4.5 0.0 copy-start.2
  4.5 0.0 copy-start.3
  4.5 54.7 %all_to_all.10.received = bf16[16,2,128,256]{3,2,1,0:T(8,128)(2,1)S(1)} all-to-all(bf16[16,2,128,256]{3,2,1,0:T(8,128)(2,1)S(1)} %row_transform.1), channel_id=1, replica_groups=mesh['group'=2,'row'=8,'epoch'=2] {'row','epoch'}, dimensions={0} | all-to-all | bytes 4194304 | tf_op jit(solution)/shard_map/all_to_all | solution.py:481
  59.2 0.0 copy-done
  59.2 0.0 copy-done.1
  59.2 0.0 copy-done.2
  59.2 0.0 copy-done.3
  59.3 4.9 %column_stage.1 = bf16[16,1,128,256]{3,2,1,0:T(8,128)(2,1)S(1)} custom-call(s32[2,2]{1,0:T(2,128)S(1)} %copy-done.2, s32[4]{0:T(128)S(1)} %copy-done.3, bf16[16,2,128,256]{3,2,1,0:T(8,128)(2,1)S(1)} %all_to_all.10.received, bf16[1024,512]{1,0:T(8,128)(2,1)S(1)} %copy-done.1, bf16[1024,1024]{1,0:T(8,128)(2,1)S(1)} %copy-done), custom_call_target="tpu_custom_call" | custom-call | flops 2415919104 | bytes 7340032 | tf_op jit(solution)/shard_map/column_stage/pallas_call | solution.py:393
  64.2 29.8 %all_to_all.11 = bf16[16,1,128,256]{3,2,1,0:T(8,128)(2,1)S(1)} all-to-all(bf16[16,1,128,256]{3,2,1,0:T(8,128)(2,1)S(1)} %column_stage.1), channel_id=1, replica_groups=mesh['group'=2,'row'=8,'epoch'=2] {'row','epoch'}, dimensions={0} | all-to-all | bytes 2097152 | tf_op jit(solution)/shard_map/all_to_all | solution.py:481
  94.0 2.1 %image_rows.1 = f32[1,256,2048]{2,1,0:T(8,128)} custom-call(bf16[16,128,256]{2,1,0:T(8,128)(2,1)S(1)} %bitcast.1, bf16[1024,512]{1,0:T(8,128)(2,1)S(1)} %copy-done.1, bf16[1024,1024]{1,0:T(8,128)(2,1)S(1)} %copy-done), custom_call_target="tpu_custom_call" | custom-call | flops 805306368 | bytes 6291456 | tf_op jit(solution)/shard_map/image_rows/pallas_call | solution.py:456
Async XLA Ops:
  4.4 54.8 %copy-start = (bf16[1024,1024]{1,0:T(8,128)(2,1)S(1)}, bf16[1024,1024]{1,0:T(8,128)(2,1)}, u32[]{:S(2)}) copy-start(bf16[1024,1024]{1,0:T(8,128)(2,1)} %constant.5.clone.odd_hbm.odd_table) | copy-start | bytes 6291460
  4.5 54.8 %copy-start.1 = (bf16[1024,512]{1,0:T(8,128)(2,1)S(1)}, bf16[1024,512]{1,0:T(8,128)(2,1)}, u32[]{:S(2)}) copy-start(bf16[1024,512]{1,0:T(8,128)(2,1)} %constant.4.clone.even_hbm.even_table) | copy-start | bytes 3145732
  4.5 54.8 %copy-start.2 = (s32[2,2]{1,0:T(2,128)S(1)}, s32[2,2]{1,0:T(2,128)}, u32[]{:S(2)}) copy-start(s32[2,2]{1,0:T(2,128)} %rate_smem.1) | copy-start | bytes 52
  4.5 54.8 %copy-start.3 = (s32[4]{0:T(128)S(1)}, s32[4]{0:T(128)}, u32[]{:S(2)}) copy-start(s32[4]{0:T(128)} %time_smem.1) | copy-start | bytes 52

commit v26 on v22

--- a/solution.py
+++ b/solution.py
@@ -15,7 +15,7 @@
 BLOCK = 512
 IMAGE_BLOCK = 512
 ROW_CHUNK = 16
-PIECES = 4
+PIECES = 8
 MIB = 1024 * 1024
 CONTRACT_LAST = (((1,), (1,)), ((), ()))
 HBM = pl.BlockSpec(memory_space=pltpu.HBM)

time: 96.6 us -> 96.9 us (level)
  no operation moved by 1% of the time
where the time goes in v26:
time: 96.9 us; the launch traced here: 96.4 us
  blocking collectives  84.5 us (87%)
  Pallas kernels  11.8 us (12%)
    all_to_all x2, blocking collectives, exchange(): return lax.all_to_all(values, ('row', 'epoch'), 0, 0, tiled=True)  84.5 us
    pallas_call x1, Pallas kernels, column_stage(): pl.pallas_call(functools.partial(column_kernel, epoch_count), in_specs=[s...  4.92 us
    pallas_call x1, Pallas kernels, row_transform(): pl.pallas_call(row_kernel, in_specs=[HBM, HBM, HBM], out_specs=IN_VMEM, o...  4.76 us
    pallas_call x1, Pallas kernels, image_rows(): pl.pallas_call(image_kernel, in_specs=[IN_VMEM, IN_VMEM, IN_VMEM], out_sp...  2.1 us

profile of v26, /device:TPU:0, one launch (start us, length us, event | category | flops | bytes accessed | tf_op | source)
XLA Modules:
  0.0 96.4 jit_solution(15962410981813370618)
XLA Ops:
  0.0 4.8 %row_transform.1 = bf16[16,2,128,256]{3,2,1,0:T(8,128)(2,1)S(1)} custom-call(bf16[2,256,2048]{2,1,0:T(8,128)(2,1)} %images_hbm.1, bf16[1024,512]{1,0:T(8,128)(2,1)} %constant.4.clone.even_hbm.even_table, bf16[1024,1024]{1,0:T(8,128)(2,1)} %constant.5.clone.odd_hbm.odd_table), custom_call_target="tpu_custom_call" | custom-call | flops 1610612736 | bytes 7340032 | tf_op jit(solution)/shard_map/row_transform/pallas_call | solution.py:142
  4.8 0.0 copy-start
  4.8 0.0 copy-start.1
  4.8 0.0 copy-start.2
  4.8 0.0 copy-start.3
  4.8 54.7 %all_to_all.10.received = bf16[16,2,128,256]{3,2,1,0:T(8,128)(2,1)S(1)} all-to-all(bf16[16,2,128,256]{3,2,1,0:T(8,128)(2,1)S(1)} %row_transform.1), channel_id=1, replica_groups=mesh['group'=2,'row'=8,'epoch'=2] {'row','epoch'}, dimensions={0} | all-to-all | bytes 4194304 | tf_op jit(solution)/shard_map/all_to_all | solution.py:476
  59.6 0.0 copy-done
  59.6 0.0 copy-done.1
  59.6 0.0 copy-done.2
  59.6 0.0 copy-done.3
  59.6 4.9 %column_stage.1 = bf16[16,1,128,256]{3,2,1,0:T(8,128)(2,1)S(1)} custom-call(s32[2,2]{1,0:T(2,128)S(1)} %copy-done.2, s32[4]{0:T(128)S(1)} %copy-done.3, bf16[16,2,128,256]{3,2,1,0:T(8,128)(2,1)S(1)} %all_to_all.10.received, bf16[1024,512]{1,0:T(8,128)(2,1)S(1)} %copy-done.1, bf16[1024,1024]{1,0:T(8,128)(2,1)S(1)} %copy-done), custom_call_target="tpu_custom_call" | custom-call | flops 2415919104 | bytes 7340032 | tf_op jit(solution)/shard_map/column_stage/pallas_call | solution.py:389
  64.5 29.7 %all_to_all.11 = bf16[16,1,128,256]{3,2,1,0:T(8,128)(2,1)S(1)} all-to-all(bf16[16,1,128,256]{3,2,1,0:T(8,128)(2,1)S(1)} %column_stage.1), channel_id=1, replica_groups=mesh['group'=2,'row'=8,'epoch'=2] {'row','epoch'}, dimensions={0} | all-to-all | bytes 2097152 | tf_op jit(solution)/shard_map/all_to_all | solution.py:476
  94.2 2.1 %image_rows.1 = f32[1,256,2048]{2,1,0:T(8,128)} custom-call(bf16[16,128,256]{2,1,0:T(8,128)(2,1)S(1)} %bitcast.1, bf16[1024,512]{1,0:T(8,128)(2,1)S(1)} %copy-done.1, bf16[1024,1024]{1,0:T(8,128)(2,1)S(1)} %copy-done), custom_call_target="tpu_custom_call" | custom-call | flops 805306368 | bytes 6291456 | tf_op jit(solution)/shard_map/image_rows/pallas_call | solution.py:451
Async XLA Ops:
  4.8 54.8 %copy-start = (bf16[1024,1024]{1,0:T(8,128)(2,1)S(1)}, bf16[1024,1024]{1,0:T(8,128)(2,1)}, u32[]{:S(2)}) copy-start(bf16[1024,1024]{1,0:T(8,128)(2,1)} %constant.5.clone.odd_hbm.odd_table) | copy-start | bytes 6291460
  4.8 54.8 %copy-start.1 = (bf16[1024,512]{1,0:T(8,128)(2,1)S(1)}, bf16[1024,512]{1,0:T(8,128)(2,1)}, u32[]{:S(2)}) copy-start(bf16[1024,512]{1,0:T(8,128)(2,1)} %constant.4.clone.even_hbm.even_table) | copy-start | bytes 3145732
  4.8 54.8 %copy-start.2 = (s32[2,2]{1,0:T(2,128)S(1)}, s32[2,2]{1,0:T(2,128)}, u32[]{:S(2)}) copy-start(s32[2,2]{1,0:T(2,128)} %rate_smem.1) | copy-start | bytes 52
  4.8 54.8 %copy-start.3 = (s32[4]{0:T(128)S(1)}, s32[4]{0:T(128)}, u32[]{:S(2)}) copy-start(s32[4]{0:T(128)} %time_smem.1) | copy-start | bytes 52
